TPU v7x, 256 devices: a whole 4x4x8 slice. The times are simulated.
256 devices in a mesh: gx: 4 (over x), gy: 4 (over z_hi, core), gz: 16 (over z_lo, y).
Axes of the slice: x: 4, y: 4, z: 8 (z_hi: 2, z_lo: 4; z = z_hi * 4 + z_lo), core: 2. Of those that a mesh axis runs over, the one named last changes fastest.
Arguments:
- charges: float32 [98304, 128], P(('gx', 'gy', 'gz')), may hold values from -6 to 6
- counts: int32 [98304], P(('gx', 'gy', 'gz')), may hold values from 1 to 128
- slots: int32 [98304], P(('gx', 'gy', 'gz')), may hold values from 0 to 511, as said below
- spline: bfloat16 [98304, 3, 4, 128], P(('gx', 'gy', 'gz')), may hold values from 0.049804688 to 1
- kernel_fine: float32 [5, 5, 5], replicated, may hold values from -0.6 to 0.6
- kernel_mid: float32 [5, 5, 5], replicated, may hold values from -0.6 to 0.6
- kernel_coarse: float32 [5, 5, 5], replicated, may hold values from -0.6 to 0.6
Outputs:
- potential: float32 [128, 128, 512], P('gx', 'gy', 'gz')
Inputs may be any that keep to these rules, and one draw needn't show every extreme that they name: Within the 384 cells of one grid block the slots are distinct.
All inputs are finite; a program needn't handle non-finite values.
Results may differ from a plain program's by a relative error of at most 0.0003.
Values sent between devices are 32-bit elements; how exact they have to be, the bound alone decides.
No kernel may reach another device: no remote copies, remote signals or barrier semaphores. Data moves between devices by JAX's collectives and lax.ppermute only.
A program may use at most 64 MiB of HBM per device.

v0:
```python
import math

import jax
import jax.numpy as jnp
from jax import lax
from jax.sharding import PartitionSpec as P

BX = 32
BY = 32


WEIGHTS = (0.125, 0.5, 0.75, 0.5, 0.125)
PRECISION_HIGH = lax.Precision.HIGHEST


def extended_2(x, sides, width):
    for axis, dim in sides:
        size, length = (lax.axis_size(axis), x.shape[dim])
        up = [(i, (i + 1) % size) for i in range(size - 1)]
        down = [(j, i) for i, j in up]
        last = lax.slice_in_dim(x, length - width, length, axis=dim)
        first = lax.slice_in_dim(x, 0, width, axis=dim)
        before = lax.ppermute(last, axis, up)
        after = lax.ppermute(first, axis, down)
        x = jnp.concatenate([before, x, after], axis=dim)
    return x


def pad_along(values, along, margin):
    spec = [(0, 0)] * values.ndim
    spec[along] = (margin, margin)
    return jnp.pad(values, spec)


def restrict_from(values, along, shift_amount, amount):
    summed = WEIGHTS[0] * lax.slice_in_dim(
        values, shift_amount, shift_amount + 2 * amount - 1, 2, along
    )
    for shift in range(1, 5):
        summed = summed + WEIGHTS[shift] * lax.slice_in_dim(
            values, shift_amount + shift, shift_amount + shift + 2 * amount - 1, 2, along
        )
    return summed


def restrict_along(values, along):
    return restrict_from(pad_along(values, along, 2), along, 0, values.shape[along] // 2)


def prolong_framed(framed, along):
    length = framed.shape[along]
    middle = lax.slice_in_dim(framed, 1, length - 1, 1, along)
    lowered = lax.slice_in_dim(framed, 0, length - 2, 1, along)
    raised = lax.slice_in_dim(framed, 2, length, 1, along)
    even_rows = 0.75 * middle + 0.125 * (lowered + raised)
    odd_rows = 0.5 * (middle + raised)
    joined = jnp.stack([even_rows, odd_rows], axis=along + 1)
    target = list(middle.shape)
    target[along] = 2 * target[along]
    return joined.reshape(target)


def prolong_along(values, along):
    return prolong_framed(pad_along(values, along, 1), along)


def spline_weight(offsets):
    summed = jnp.zeros(offsets.shape, jnp.float32)
    for position in range(5):
        summed = summed + WEIGHTS[position] * (offsets == position).astype(jnp.float32)
    return summed


def direct_stencil(padded, kernel, out_shape):
    summed = jnp.zeros(out_shape, jnp.float32)
    for shift_x in range(5):
        for shift_y in range(5):
            for shift_z in range(5):
                summed = (
                    summed
                    + kernel[shift_x, shift_y, shift_z]
                    * padded[
                        shift_x : shift_x + out_shape[0],
                        shift_y : shift_y + out_shape[1],
                        shift_z : shift_z + out_shape[2],
                    ]
                )
    return summed


def green_block(target_x, target_y, target_z, source, flat):
    delta = target_x[:, None] - source[0][None, :]
    dist = delta * delta
    delta = target_y[:, None] - source[1][None, :]
    dist = dist + delta * delta
    delta = target_z[:, None] - source[2][None, :]
    dist = dist + delta * delta
    green = 0.0625 / jnp.sqrt(1.0 + dist)
    return jnp.dot(green, flat, precision=PRECISION_HIGH)


def grid_points(indices, size_y, size_z):
    return jnp.stack(
        [indices // (size_y * size_z), indices // size_z % size_y, indices % size_z]
    ).astype(jnp.float32)


def potentials_at(targets, source, flat):
    amount = targets.shape[1]
    block_len = math.gcd(amount, 32)
    blocked = targets.reshape(3, amount // block_len, block_len).transpose(1, 0, 2)

    def one_block(target):
        return green_block(target[0], target[1], target[2], source, flat)

    return lax.map(one_block, blocked).reshape(amount)


def shards(charges, counts, slots, spline, kernel_fine, kernel_mid, kernel_coarse):
    n_gx = lax.axis_size("gx")
    n_gy = lax.axis_size("gy")
    n_gz = lax.axis_size("gz")
    groups = n_gx * n_gy
    depth = 2 * groups
    half_x = BX // 2
    half_y = BY // 2
    lane = lax.axis_index(("gx", "gy"))
    zslab = lax.axis_index("gz")
    live = (lax.broadcasted_iota(jnp.int32, charges.shape, 1) < counts[:, None]).astype(jnp.float32)
    weighted = charges * live
    splines = spline.astype(jnp.float32)
    cross_product = (splines[:, 0][:, :, None, :] * splines[:, 1][:, None, :, :]).reshape(
        splines.shape[0], 16, splines.shape[3]
    )
    vertical_column = splines[:, 2] * weighted[:, None, :]
    local_patches = jnp.einsum(
        "fjl,fgl->fjg", cross_product, vertical_column, precision=PRECISION_HIGH
    ).reshape(splines.shape[0], 64)
    slot_count = BX // 4 * (BY // 4) * (depth // 4)
    blocks = jnp.zeros((slot_count, 64), jnp.float32).at[slots].add(local_patches)
    fine = (
        blocks.reshape(BX // 4, BY // 4, depth // 4, 4, 4, 4)
        .transpose(0, 3, 1, 4, 2, 5)
        .reshape(BX, BY, depth)
    )
    padded = extended_2(fine, (("gx", 0), ("gy", 1), ("gz", 2)), 6)
    side = 6
    rows = depth + 4
    region = padded[side - 2 : side + BX + 2, side - 2 : side + BY + 2, 4 : depth + 8]
    differ = lax.broadcasted_iota(jnp.int32, (rows, depth), 0) - lax.broadcasted_iota(
        jnp.int32, (rows, depth), 1
    )
    one_hot_rows = (differ[:, :, None] == jnp.arange(5, dtype=jnp.int32)[None, None, :]).astype(
        jnp.float32
    )
    table = jnp.einsum(
        "kjc,abc->kabj", one_hot_rows, kernel_fine, precision=PRECISION_HIGH
    ).reshape(rows, 25 * depth)
    product = jnp.dot(
        region.reshape((BX + 4) * (BY + 4), rows), table, precision=PRECISION_HIGH
    ).reshape(BX + 4, BY + 4, 25, depth)
    near_first = jnp.zeros((BX, BY, depth), jnp.float32)
    for shift_x in range(5):
        for shift_y in range(5):
            near_first = (
                near_first
                + product[shift_x : shift_x + BX, shift_y : shift_y + BY, shift_x * 5 + shift_y, :]
            )
    second_ext = restrict_from(padded, 0, side - 2, half_x)
    second_ext = restrict_from(second_ext, 1, side - 2, half_y)
    second_ext = restrict_from(second_ext, 2, 0, groups + 4)
    global_plane = zslab * groups + jnp.arange(groups + 4, dtype=jnp.int32) - 2
    inside = ((global_plane >= 0) & (global_plane < groups * n_gz)).astype(jnp.float32)
    second_ext = second_ext * inside[None, None, :]
    stacked = jnp.stack([second_ext[:, :, shift : shift + groups] for shift in range(5)], axis=-1)
    received = lax.all_to_all(stacked, ("gx", "gy"), split_axis=2, concat_axis=0, tiled=True)
    size_x2 = n_gx * half_x
    size_y2 = n_gy * half_y
    stacked_planes = (
        received.reshape(n_gx, n_gy, half_x, half_y, 5)
        .transpose(0, 2, 1, 3, 4)
        .reshape(size_x2, size_y2, 5)
    )
    framed_two = jnp.pad(stacked_planes, ((2, 2), (2, 2), (0, 0)))
    near_second = direct_stencil(framed_two, kernel_mid, (size_x2, size_y2, 1))[:, :, 0]
    shrunk = restrict_along(restrict_along(stacked_planes, 0), 1)
    candidate = WEIGHTS[0] * shrunk[:, :, 0]
    for shift in range(1, 5):
        candidate = candidate + WEIGHTS[shift] * shrunk[:, :, shift]
    size_x3 = size_x2 // 2
    size_y3 = size_y2 // 2
    size_z3 = n_gz * groups // 2
    plane = zslab * groups + lane
    start_three = plane // 2 - 1
    start_four = start_three // 2 - 1
    pieces = lax.all_gather(candidate[None], ("gx", "gy", "gz"), axis=0, tiled=True)
    arranged = pieces.reshape(groups // 2, 2, n_gz, size_x3, size_y3)[:, 0]
    arranged = arranged.transpose(1, 0, 2, 3).reshape(size_z3, size_x3, size_y3)
    third = arranged.transpose(1, 2, 0)
    fourth = restrict_along(restrict_along(restrict_along(third, 0), 1), 2)
    padded_three = jnp.pad(third, ((2, 2), (2, 2), (4, 4)))
    window_three = lax.dynamic_slice_in_dim(padded_three, start_three + 2, 7, 2)
    size_x4, size_y4, size_z4 = fourth.shape
    points = size_x4 * size_y4 * size_z4
    flat = fourth.reshape(points)
    source = grid_points(jnp.arange(points, dtype=jnp.int32), size_y4, size_z4)
    count_t = size_x4 * size_y4 * 4
    tidx = jnp.arange(count_t, dtype=jnp.int32)
    targets = jnp.stack([tidx // (4 * size_y4), tidx // 4 % size_y4, start_four + tidx % 4]).astype(
        jnp.float32
    )
    window_four = potentials_at(targets, source, flat).reshape(size_x4, size_y4, 4)
    planes_four = start_four + jnp.arange(4, dtype=jnp.int32)
    window_four = (
        window_four
        * ((planes_four >= 0) & (planes_four < size_z4)).astype(jnp.float32)[None, None, :]
    )
    near_third = direct_stencil(window_three, kernel_coarse, (size_x3, size_y3, 3))
    raised_four = prolong_along(prolong_along(window_four, 0), 1)
    planes_three = start_three + jnp.arange(3, dtype=jnp.int32)
    keys_34 = planes_three[:, None] - 2 * (start_four + jnp.arange(4, dtype=jnp.int32))[None, :] + 2
    part_three = jnp.einsum(
        "xyl,jl->xyj", raised_four, spline_weight(keys_34), precision=PRECISION_HIGH
    )
    mask_three = ((planes_three >= 0) & (planes_three < size_z3)).astype(jnp.float32)
    third_total = (near_third + part_three) * mask_three[None, None, :]
    keys_23 = plane - 2 * planes_three + 2
    squeezed = jnp.einsum(
        "xyj,j->xy", third_total, spline_weight(keys_23), precision=PRECISION_HIGH
    )
    second_total = near_second + prolong_along(prolong_along(squeezed, 0), 1)
    framed = jnp.pad(second_total, 1)

    def cut_tile(target):
        return lax.dynamic_slice(
            framed, (target // n_gy * half_x, target % n_gy * half_y), (half_x + 2, half_y + 2)
        )

    tiles = jax.vmap(cut_tile)(jnp.arange(groups, dtype=jnp.int32))
    returned = lax.all_to_all(tiles, ("gx", "gy"), split_axis=0, concat_axis=0, tiled=True)
    level_block = returned.transpose(1, 2, 0)
    extended = extended_2(level_block, (("gz", 2),), 1)
    raised = prolong_framed(prolong_framed(prolong_framed(extended, 0), 1), 2)
    return near_first + raised


def solution(mesh):
    return jax.shard_map(
        shards,
        mesh=mesh,
        in_specs=(
            P(("gx", "gy", "gz"), None),
            P(("gx", "gy", "gz")),
            P(("gx", "gy", "gz")),
            P(("gx", "gy", "gz"), None, None, None),
            P(),
            P(),
            P(),
        ),
        out_specs=P("gx", "gy", "gz"),
        check_vma=False,
    )
```

profile of v0, /device:TPU:32, one launch (start us, length us, event | category | flops | bytes accessed | tf_op | source)
XLA Modules:
  0.0 1204.3 jit_solution(10828840761259656192)
XLA Ops:
  10.7 5.0 fusion.24
  19.3 7.6 copy.235
  26.9 3.3 reshape.495
  31.5 4.8 collective-permute-start
  49.3 8.5 collective-permute-done.3
  60.6 5.4 collective-permute-start.5
  67.9 7.4 collective-permute-done.4
  86.1 11.7 all-to-all-start
  99.7 8.3 all-to-all-done
  117.1 702.8 %all-gather.3.cloned.1.call-done = f32[8192,32,1]{1,0,2:T(8,128)} async-done(((f32[32,32,1]{1,0,2:T(8,128)}), f32[8192,32,1]{1,0,2:T(8,128)}) %all-gather.3.cloned.1.call-update) | async-done | bytes 1048592 | tf_op jit(solution)/shard_map/all_gather | solution.py:196
  838.4 85.3 %while.11 = (s32[]{:T(128)}, f32[32,32]{1,0:T(8,128)S(1)}, f32[32,3,32]{2,1,0:T(4,128)S(1)}, f32[3,16384]{1,0:T(4,128)S(1)}, f32[16384]{0:T(1024)S(1)}, /*index=5*/s32[]{:T(128)}, s32[]{:T(128)}) while((s32[]{:T(128)}, f32[32,32]{1,0:T(8,128)S(1)}, f32[32,3,32]{2,1,0:T(4,128)S(1)}, f32[3,16384]{1,0:T(4,128)S(1)}, f32[16384]{0:T(1024)S(1)}, ...), condition=%wide.region_2.3_spmd, body=%wide.region_1.2_spmd.sunk | while | flops 11534338 | bytes 657757 | solution.py:116
  838.6 2.4 fusion.698
  841.2 2.4 fusion.698
  843.9 2.4 fusion.698
  851.9 2.4 fusion.698
  854.5 2.4 fusion.698
  862.5 2.4 fusion.698
  873.1 2.4 fusion.698
  883.8 2.4 fusion.698
  891.7 2.4 fusion.698
  894.4 2.4 fusion.698
  902.4 2.4 fusion.698
  905.0 2.4 fusion.698
  913.0 2.4 fusion.698
  924.7 108.6 %fusion.22 = f32[32,32,3]{2,1,0:T(8,128)S(1)} fusion(f32[32,32,4]{1,2,0:T(4,128)S(1)} %copy.271, s32[]{:T(128)S(6)} %add.1745, s32[]{:T(128)S(6)} %add.1717, f32[32,32,128]{2,1,0:T(8,128)S(1)} %bitcast.590, s32[]{:T(128)S(6)} %add.1718, s32[]{:T(128)S(6)} %add.1714, s32[]{:T(128)S(6)} %add.1715, s32[]{:T(128)S(6)} %add.1716, s32[]{:T(128)S(6)} %add.1727, ...), kind=kOutput, calls=%fused_computation.157 | convolution fusion | flops 918720 | bytes 553536 | tf_op jit(solution)/shard_map/xyl,jl->xyj/dot_general | solution.py:222
  1035.8 79.1 %bitcast_add_fusion = f32[64,64]{1,0:T(8,128)S(1)} fusion(f32[64,64]{1,0:T(8,128)S(1)} %copy.277, f32[64,64,5]{1,0,2:T(8,128)S(1)} %copy-done.2, f32[]{:T(128)} %bitcast.165, f32[]{:T(128)} %bitcast.164, f32[]{:T(128)} %bitcast.163, f32[]{:T(128)} %bitcast.162, f32[]{:T(128)} %bitcast.161, f32[]{:T(128)} %bitcast.160, f32[]{:T(128)} %bitcast.159, ...), kind=kLoop, calls=%fused_computation.929 | loop fusion | flops 1024000 | bytes 377332 | tf_op jit(solution)/shard_map/add | solution.py:231
  1115.0 31.8 %while.12 = (s32[]{:T(128)}, f32[66,66]{1,0:T(8,128)S(1)}, s32[16,2]{0,1:T(2,128)S(1)}, f32[16,18,18]{2,1,0:T(8,128)S(1)}, s32[]{:T(128)}) while((s32[]{:T(128)}, f32[66,66]{1,0:T(8,128)S(1)}, s32[16,2]{0,1:T(2,128)S(1)}, f32[16,18,18]{2,1,0:T(8,128)S(1)}, s32[]{:T(128)}) %tuple.300), condition=%wide.while_cond, body=%wide.while_body.sunk | while | flops 2 | bytes 24693 | solution.py:235
  1147.5 5.5 all-to-all-start.1
  1153.6 9.5 all-to-all-done.1
  1165.9 6.0 collective-permute-start.7
  1171.9 14.7 %fusion.26 = f32[36,36,25,32]{1,3,2,0:T(8,128)} fusion(f32[25,32,36,1]{2,1,0,3:T(8,128)S(1)} %bitcast.594, f32[44,44,44]{2,1,0:T(8,128)S(1)} %pad_maximum_fusion.1), kind=kOutput, calls=%fused_computation.166 | convolution fusion | flops 447897600 | bytes 5294080 | tf_op jit(solution)/shard_map/dot_general | solution.py:159
  1188.7 7.6 fusion.277
  (385 shorter events, 160.5 us)
Async XLA Ops:
  6.5 1146.5 %copy-start = (f32[5,5,5]{2,1,0:T(8,128)S(1)}, f32[5,5,5]{2,1,0:T(8,128)}, u32[]{:S(2)}) copy-start(f32[5,5,5]{2,1,0:T(8,128)} %param.13) | copy-start | bytes 1504
  8.8 0.9 copy-start.6
  8.8 0.9 copy-start.12
  26.9 9.5 copy-start.4
  26.9 13.8 %copy-start.5 = (f32[5,5,5]{2,1,0:T(8,128)S(1)}, f32[5,5,5]{2,1,0:T(8,128)}, u32[]{:S(2)}) copy-start(f32[5,5,5]{2,1,0:T(8,128)} %param.15) | copy-start | bytes 1504
  30.2 16.4 %collective-permute-start.1 = (f32[6,32,32]{2,1,0:T(8,128)S(1)}, f32[6,32,32]{2,1,0:T(8,128)S(1)}, u32[]{:S(2)}, u32[]{:S(2)}) collective-permute-start(f32[6,32,32]{2,1,0:T(8,128)S(1)} %get-tuple-element.77), channel_id=1, source_target_pairs={{64,0},{128,64},{192,128},{65,1},{129,65},{193,129},{66,2},{130,66... | collective-permute-start | bytes 73736 | tf_op jit(solution)/shard_map/ppermute | solution.py:24
  31.5 15.0 %collective-permute-start = (f32[6,32,32]{2,1,0:T(8,128)S(1)}, f32[6,32,32]{2,1,0:T(8,128)S(1)}, u32[]{:S(2)}, u32[]{:S(2)}) collective-permute-start(f32[6,32,32]{2,1,0:T(8,128)S(1)} %get-tuple-element.78), channel_id=1, source_target_pairs={{0,64},{64,128},{128,192},{1,65},{65,129},{129,193},{2,66},{66,130... | collective-permute-start | bytes 73736 | tf_op jit(solution)/shard_map/ppermute | solution.py:23
  46.6 2.6 collective-permute-start.2
  47.9 9.8 collective-permute-start.3
  60.6 15.2 %collective-permute-start.5 = (f32[44,44,6]{1,0,2:T(8,128)}, f32[44,44,6]{1,0,2:T(8,128)S(1)}, u32[]{:S(2)}, u32[]{:S(2)}) collective-permute-start(f32[44,44,6]{1,0,2:T(8,128)} %copy.237), channel_id=1, source_target_pairs={{1,0},{2,1},{3,2},{4,3},{5,4},{6,5},{7,6},{8,7},{9,8},{10,9},{11,1... | collective-permute-start | bytes 139400 | tf_op jit(solution)/shard_map/ppermute | solution.py:24
  65.9 9.4 collective-permute-start.4
  86.1 21.8 %all-to-all-start = ((f32[16,1,1280]{2,1,0:T(1,128)}), f32[16,1,1280]{2,1,0:T(1,128)S(1)}, u32[]{:S(2)}, u32[]{:S(2)}) async-start(f32[16,1,1280]{2,1,0:T(1,128)} %reshape.563), calls=%async_computation | async-start | bytes 163840 | tf_op jit(solution)/shard_map/all_to_all | solution.py:176
  97.8 722.0 %all-gather.3.cloned.1.call-start = ((), (), s32[]{:S(2)}) async-start(), calls=%async_computation.2 | async-start | bytes 4210688 | tf_op jit(solution)/shard_map/all_gather | solution.py:196
  109.9 6.9 copy-start.8
  109.9 6.9 copy-start.9
  109.9 6.9 copy-start.10
  110.2 0.7 copy-start.1
  825.9 12.5 %copy-start.11 = (f32[32,32]{1,0:T(8,128)S(1)}, f32[32,32]{1,0:T(8,128)}, u32[]{:S(2)}) copy-start(f32[32,32]{1,0:T(8,128)} %custom-call.2) | copy-start | bytes 12292
  923.7 1.0 copy-start.3
  923.7 1.0 copy-start.13
  923.7 1.0 copy-start.14
  924.7 111.1 %copy-start.2 = (f32[64,64,5]{1,0,2:T(8,128)S(1)}, f32[64,64,5]{1,0,2:T(8,128)}, u32[]{:S(2)}) copy-start(f32[64,64,5]{1,0,2:T(8,128)} %copy-done.1) | copy-start | bytes 245764
  1033.3 81.7 %copy-start.7 = (f32[16,18,18]{2,1,0:T(8,128)S(1)}, f32[16,18,18]{2,1,0:T(8,128)}, u32[]{:S(2)}) copy-start(f32[16,18,18]{2,1,0:T(8,128)} %custom-call.3) | copy-start | bytes 62212
  1147.5 15.5 %all-to-all-start.1 = ((f32[16,1,324]{2,1,0:T(1,128)}), f32[16,1,324]{2,1,0:T(1,128)S(1)}, u32[]{:S(2)}, u32[]{:S(2)}) async-start(f32[16,1,324]{2,1,0:T(1,128)} %reshape.565), calls=%async_computation.1 | async-start | bytes 49152 | tf_op jit(solution)/shard_map/all_to_all | solution.py:240
  1163.9 22.7 %collective-permute-start.6 = (f32[18,18,1]{1,0,2:T(8,128)S(1)}, f32[18,18,1]{1,0,2:T(8,128)S(1)}, u32[]{:S(2)}, u32[]{:S(2)}) collective-permute-start(f32[18,18,1]{1,0,2:T(8,128)S(1)} %get-tuple-element.85), channel_id=1, source_target_pairs={{0,1},{1,2},{2,3},{3,4},{4,5},{5,6},{6,7},{7,8},{8,9},{9,10},{10,1... | collective-permute-start | bytes 3896 | tf_op jit(solution)/shard_map/ppermute | solution.py:23
  1165.9 20.8 %collective-permute-start.7 = (f32[18,18,1]{1,0,2:T(8,128)S(1)}, f32[18,18,1]{1,0,2:T(8,128)S(1)}, u32[]{:S(2)}, u32[]{:S(2)}) collective-permute-start(f32[18,18,1]{1,0,2:T(8,128)S(1)} %get-tuple-element.86), channel_id=1, source_target_pairs={{1,0},{2,1},{3,2},{4,3},{5,4},{6,5},{7,6},{8,7},{9,8},{10,9},{11,1... | collective-permute-start | bytes 3896 | tf_op jit(solution)/shard_map/ppermute | solution.py:24
Sparse Core Ops, SparseCore 0:
  115.6 704.1 all-gather.2
where the time goes:
time: 1220 us; the launch traced here: 1200 us
  waiting for transfers between devices  736 us (60%)
  matrix products  209 us (17%)
  other arithmetic  101 us (8%)
  local copies, waits for them, and re-layouts  99.4 us (8%)
  starting transfers between devices  41.7 us (3%)
  between operations  14.8 us (1%)
    all_gather x1, waiting for transfers between devices, shards(): lax.all_gather(candidate[None], ('gx', 'gy', 'gz'), axis=0, tiled=True)  703 us
    dot_general x1, matrix products, shards(): jnp.einsum('xyl,jl->xyj', raised_four, spline_weight(keys_34), precision=...  109 us
    add x1, other arithmetic, shards(): second_total = near_second + prolong_along(prolong_along(squeezed, 0), 1)  79.1 us
    dot_general x32, matrix products, green_block(): return jnp.dot(green, flat, precision=PRECISION_HIGH)  78 us
    gather x48, local copies, waits for them, and re-layouts  31.8 us
  transfers between devices with their start and end apart: 11, of which 5 were waited for; matrix products, arithmetic and copies ran while one was open for 2% of the time, Pallas kernels for 0%

commit v1 on v0

v1 whole, which is shorter than its diff:
```python
import jax
import jax.numpy as jnp
import numpy as np
from jax import lax
from jax.experimental import pallas as pl
from jax.experimental.pallas import tpu as pltpu
from jax.sharding import PartitionSpec as P

W = (0.125, 0.5, 0.75, 0.5, 0.125)
F32 = jnp.float32
BF16 = jnp.bfloat16
CELLS = 384
ATOMS = 128
SPAN_2 = 18
SPAN_3 = 11
SPAN_4 = 7
SEC = 32
THI = 64
VMEM = pl.BlockSpec(memory_space=pltpu.VMEM)
SMEM = pl.BlockSpec(memory_space=pltpu.SMEM)


def weight(t):
    return W[t] if 0 <= t <= 4 else 0.0


def table(rows, columns, offset, turned):
    out = np.zeros((128, 128), np.float32)
    for r in range(rows):
        for c in range(columns):
            out[r, c] = weight(c - 2 * r + offset if turned else r - 2 * c + offset)
    return out


REST_2 = table(32, SPAN_2, 4, False)
REST_3 = table(SPAN_2, SPAN_3, 3, False)
PROL_2 = table(SPAN_3, SPAN_2, 3, True)
PROL_1 = table(SPAN_2, 32, 4, True)


def near_codes(shape, mains, lows, highs, group, outs):
    codes = np.full(shape, 99, np.int32)
    for start, count, first in (mains, lows, highs):
        for a in range(5):
            for k in range(count):
                for b in range(5):
                    for zo in range(outs):
                        c = first + k - zo
                        if 0 <= c <= 4:
                            codes[start + a * count + k, b * group + zo] = 5 * a + c
    return codes


CODES_1 = near_codes((256, 256), (0, 32, 2), (160, 2, 0), (192, 2, 34), 32, 32)
CODES_2 = near_codes((256, 128), (0, 18, 2), (128, 4, 0), (160, 4, 18), 24, 18)
CODES_3 = near_codes((128, 128), (0, 11, 2), (64, 5, 0), (96, 5, 10), 16, 11)


def spread_table():
    out = np.zeros((512, 64), np.float32)
    for r in range(512):
        out[r, r // 32 * 4 + r % 4] = 1.0
    return out


def composite(first, last):
    p3 = np.array([[weight(i - 2 * j + 3) for j in range(7)] for i in range(11)])
    p2 = np.array([[weight(i - 2 * j + 3) for j in range(11)] for i in range(18)])
    p1 = np.array([[weight(i - 2 * j + 4) for j in range(18)] for i in range(32)])
    m4, m3, m2 = np.ones(7), np.ones(11), np.ones(18)
    if first:
        m4[0] = m3[0] = m2[0] = 0
    if last:
        m4[5:] = 0
        m3[9:] = 0
        m2[17:] = 0
    return (p1 * m2) @ (p2 * m3) @ (p3 * m4)


def composites():
    qx = np.zeros((4, 32, 8), np.float32)
    qy = np.zeros((4, 32, 128), np.float32)
    qz = np.zeros((4, 128, 128), np.float32)
    for v in range(4):
        q = composite(v % 2 == 1, v >= 2)
        qx[v, :, :7] = q
        for lane in range(64):
            if lane // 8 < 7:
                qy[v, :, lane] = q[:, lane // 8]
            if lane % 8 < 7:
                qz[v, lane, :32] = q[:, lane % 8]
    return qx, qy, qz


def split(x):
    high = x.astype(BF16)
    return high, (x - high.astype(F32)).astype(BF16)


def dot(a, b):
    return jnp.dot(a, b, preferred_element_type=F32)


def dot_exact(x, right):
    high, low = split(x)
    return dot(high, right) + dot(low, right)


def dot_split(x, right_high, right_low):
    high, low = split(x)
    return dot(high, right_high) + (dot(low, right_high) + dot(high, right_low))


def iota(shape, dim):
    return lax.broadcasted_iota(jnp.int32, shape, dim)


def roll(x, shift, axis=None):
    axis = x.ndim - 1 if axis is None else axis
    shift = shift % x.shape[axis]
    return x if shift == 0 else pltpu.roll(x, shift, axis)


def lanes_of(x, low, count):
    lane = iota(x.shape, x.ndim - 1)
    return jnp.where((lane >= low) & (lane < low + count), x, 0.0)


def as_rows(x):
    return x.reshape(x.shape[0] * x.shape[1], x.shape[2])


def taps(pieces):
    total = None
    for factor, value in pieces:
        term = value if factor == 1.0 else factor * value
        total = term if total is None else total + term
    return total


def restrict_planes(read, span, size, offset):
    planes = []
    for p in range(span):
        planes.append(
            taps([(W[t], read(2 * p + t - offset)) for t in range(5) if 0 <= 2 * p + t - offset < size])
        )
    return planes


def place():
    sizes = [lax.axis_size(a) for a in ("gx", "gy", "gz")]
    index = [lax.axis_index(a) for a in ("gx", "gy", "gz")]
    return index, sizes


def inside_mask(shape, spans, high, place_of):
    index, sizes = place_of
    keep = None
    for dim in range(3):
        at = iota(shape, dim)
        low = jnp.where(index[dim] == 0, 1, 0)
        top = jnp.where(index[dim] == sizes[dim] - 1, high, spans)
        part = (at >= low) & (at < top)
        keep = part if keep is None else keep & part
    return keep


def deposit_kernel(
    charges, counts, slots, spline, spread, rest_2, rest_3,
    packed, fourth, to_high, to_low,
    wide, patch, fine, buf_2, buf_3, buf_4,
):
    where = place()
    index, sizes = where
    wide[...] = spline[...].astype(F32)
    alive = iota((ATOMS, CELLS), 0) < counts[...]
    weighted = jnp.where(alive, charges[...].T, 0.0)
    for chunk in range(CELLS // 128):
        lanes = slice(128 * chunk, 128 * chunk + 128)

        def column(d, i):
            return wide[pl.ds(chunk * 128 * 12 + 4 * d + i, 128, stride=12), :].T

        charge = weighted[:, lanes]
        depth = [charge * column(2, k) for k in range(4)]
        ys = [column(1, j) for j in range(4)]
        for i in range(4):
            xs = column(0, i)
            for j in range(4):
                cross = xs * ys[j]
                for k in range(4):
                    patch[16 * i + 4 * j + k : 16 * i + 4 * j + k + 1, lanes] = jnp.sum(
                        cross * depth[k], axis=0, keepdims=True
                    )
    slot = slots[...]
    high, low = split(patch[...])
    fits = (iota((512, CELLS), 0) // 4 % 8) == slot % 8
    spread_high = jnp.where(fits, dot(spread[...], high), 0.0).astype(BF16)
    spread_low = jnp.where(fits, dot(spread[...], low), 0.0).astype(BF16)
    hot = (iota((64, CELLS), 0) == slot // 8).astype(BF16)
    nt = (((1,), (1,)), ((), ()))
    placed = lax.dot_general(hot, spread_high, nt, preferred_element_type=F32) + lax.dot_general(
        hot, spread_low, nt, preferred_element_type=F32
    )
    for i in range(4):
        for j in range(4):
            rows = lanes_of(roll(placed[:, 128 * i : 128 * i + 128], -32 * j), 0, 32)
            for sx in range(8):
                fine[4 * sx + i, pl.ds(j, 8, stride=4), :] = rows[8 * sx : 8 * sx + 8]

    buf_2[...] = jnp.zeros_like(buf_2)
    buf_3[...] = jnp.zeros_like(buf_3)
    buf_4[...] = jnp.zeros_like(buf_4)
    for p, plane in enumerate(restrict_planes(lambda x: fine[x], SPAN_2, 32, 4)):
        buf_2[p, 4:36, :] = plane
    second = taps([(W[t], buf_2[:, pl.ds(t, 24, stride=2), :]) for t in range(5)])
    second = dot_exact(as_rows(second), rest_2[...]).reshape(SPAN_2, 24, 128)
    second = jnp.where(inside_mask(second.shape, SPAN_2, 17, where), second, 0.0)
    for p, plane in enumerate(restrict_planes(lambda x: second[x], SPAN_3, SPAN_2, 3)):
        buf_3[p, 3:27, :] = plane
    third = taps([(W[t], buf_3[:, pl.ds(t, 16, stride=2), :]) for t in range(5)])
    third = dot_exact(as_rows(third), rest_3[...]).reshape(SPAN_3, 16, 128)
    third = jnp.where(inside_mask(third.shape, SPAN_3, 9, where), third, 0.0)
    for p, plane in enumerate(restrict_planes(lambda x: third[x], SPAN_4, SPAN_3, 3)):
        buf_4[p, 3:19, :] = plane
    last = taps([(W[t], buf_4[:, pl.ds(t, 8, stride=2), :]) for t in range(5)])
    row, column = iota((128, 128), 0), iota((128, 128), 1)
    t = 8 * index[2] + row + 1 - 2 * column
    rest_4 = jnp.zeros((128, 128), F32)
    for tap in range(5):
        rest_4 = jnp.where(t == tap, W[tap], rest_4)
    rest_4 = jnp.where((row < SPAN_3) & (column < 4 * sizes[2]), rest_4, 0.0).astype(BF16)
    last = dot_exact(as_rows(last), rest_4).reshape(SPAN_4, 8, 128)
    y_at = iota(last.shape, 1) + 4 * index[1] - 1
    x_at = iota(last.shape, 0) + 4 * index[0] - 1
    legal = (y_at >= 0) & (y_at < 4 * sizes[1]) & (x_at >= 0) & (x_at < 4 * sizes[0])
    last = jnp.where(legal & (iota(last.shape, 1) < SPAN_4), last, 0.0)
    halves = []
    for half in range(2):
        total = jnp.zeros_like(last)
        for by in range(sizes[1]):
            shift = 4 * by - 1 - 8 * half
            if -8 < shift < 8:
                moved = roll(last, shift, 1)
                at = iota(last.shape, 1)
                moved = jnp.where((at >= shift) & (at < 8 + shift), moved, 0.0)
                total = total + jnp.where(index[1] == by, moved, 0.0)
        halves.append(total)
    fourth[...] = halves[0] + roll(halves[1], 64)

    packed[...] = fine[...]
    packed[0:SPAN_2, 0:24, :] += roll(second, SEC)
    packed[0:SPAN_3, 0:16, :] += roll(third, THI)
    lane = iota((5, 32, 128), 2)
    to_low[...] = packed[0:5]
    to_high[...] = (
        jnp.where((lane >= SEC) & (lane < THI), packed[14:19], 0.0)
        + jnp.where(lane >= THI, packed[6:11], 0.0)
    )
    to_high[0:2] += lanes_of(packed[30:32], 0, 32)


def widen_x_kernel(packed, from_low, from_high, out, to_high, to_low):
    out[0:2] = jnp.zeros((2, 32, 128), F32)
    out[34:36] = jnp.zeros((2, 32, 128), F32)
    out[2:34] = packed[...]
    low, high = from_low[...], from_high[...]
    first = lanes_of(low[2:5], SEC, 96)
    out[0:2] = low[0:2]
    out[2:5] += first
    out[34:36] += lanes_of(high[0:2], 0, 32)
    out[18:22] += lanes_of(high[0:4], SEC, 32)
    out[10:15] += lanes_of(high, THI, 64)
    def pack(fine_at, second_at, third_at):
        def rows(start, count, first, planes, low, width):
            slab = out[first : first + planes, start : start + 8, :]
            row = iota(slab.shape, 1)
            return jnp.where(row < count, lanes_of(slab, low, width), 0.0)

        base = rows(fine_at, 2, 0, 18, 0, 32) + rows(second_at, 4, 0, 18, SEC, 32)
        base = base + rows(third_at, 5, 0, 18, THI, 32)
        other = roll(rows(fine_at, 2, 18, 18, 0, 32), 2, 1)
        extra = roll(rows(second_at, 4, 18, 4, SEC, 32), 64)
        return base + other, extra

    for ref, at in ((to_low, (0, 0, 0)), (to_high, (24, 14, 6))):
        if at[0] == 24:
            body, extra = pack_high(out)
        else:
            body, extra = pack(*at)
        ref[...] = body
        ref[0:4] += extra


def pack_high(out):
    def rows(start, count, skip, first, planes, low, width):
        slab = out[first : first + planes, start : start + 8, :]
        slab = roll(slab, -skip, 1)
        row = iota(slab.shape, 1)
        return jnp.where(row < count, lanes_of(slab, low, width), 0.0)

    base = rows(24, 2, 6, 0, 18, 0, 32) + rows(14, 4, 0, 0, 18, SEC, 32) + rows(6, 5, 0, 0, 18, THI, 32)
    other = roll(rows(24, 2, 6, 18, 18, 0, 32), 2, 1)
    extra = roll(rows(14, 4, 0, 18, 4, SEC, 32), 64)
    return base + other, extra


def widen_y_kernel(wide_x, from_low, from_high, out, to_high, to_low):
    out[...] = jnp.zeros_like(out)
    out[:, 2:34, :] = wide_x[...]

    def parts(ref):
        body = ref[...]
        row = iota(body.shape, 1)
        fine_low = jnp.where(row < 2, lanes_of(body, 0, 32), 0.0)
        fine_far = roll(lanes_of(body, 0, 32), -2, 1)
        fine_far = jnp.where(row < 2, fine_far, 0.0)
        second = lanes_of(body, SEC, 32)
        far = lanes_of(roll(body[0:4], -64), SEC, 32)
        third = lanes_of(body, THI, 32)
        return fine_low, fine_far, second, far, third

    for ref, at in ((from_low, (0, 0, 0)), (from_high, (34, 18, 10))):
        fine_low, fine_far, second, far, third = parts(ref)
        out[0:18, at[0] : at[0] + 2, :] += fine_low[:, 0:2]
        out[18:36, at[0] : at[0] + 2, :] += fine_far[:, 0:2]
        out[0:18, at[1] : at[1] + 4, :] += second[:, 0:4]
        out[18:22, at[1] : at[1] + 4, :] += far[:, 0:4]
        out[0:18, at[2] : at[2] + 5, :] += third[:, 0:5]

    for ref, at in ((to_low, (0, 0, 0)), (to_high, (30, 14, 6))):
        for base, rows, planes, count, start in (
            (0, 40, 36, 2, at[0]),
            (40, 24, 22, 4, SEC + at[1]),
            (64, 16, 15, 5, THI + at[2]),
        ):
            total = jnp.zeros((rows, 128), F32)
            for x in range(planes):
                total = total + lanes_of(roll(out[x, 0:rows, :], count * x - start), count * x, count)
            ref[base : base + rows, :] = total


def build_bands(kernel, codes):
    lanes = codes.shape[1]
    group = {256: 32, 128: 24}[lanes] if codes.shape[0] == 256 else 16
    block = iota((8, lanes), 1) // group
    total = jnp.zeros(codes.shape, F32)
    code = codes[...]
    for a in range(5):
        for c in range(5):
            row = jnp.zeros((8, lanes), F32)
            for b in range(5):
                row = jnp.where(block == b, kernel[a, b, c], row)
            total = jnp.where(code == 5 * a + c, row[0:1], total)
    return split(total)


def tables_kernel(
    after, kernel_1, kernel_2, kernel_3, codes_1, codes_2, codes_3,
    green_high, green_low, b1h, b1l, b2h, b2l, b3h, b3l,
):
    index, sizes = place()
    for kernel, codes, high_ref, low_ref in (
        (kernel_1, codes_1, b1h, b1l),
        (kernel_2, codes_2, b2h, b2l),
        (kernel_3, codes_3, b3h, b3l),
    ):
        high, low = build_bands(kernel, codes)
        high_ref[...] = high
        low_ref[...] = low
    row, lane = iota((128, 128), 0), iota((128, 128), 1)
    target_y = 4 * index[1] - 1 + lane // 8 % 8
    target_z = 4 * index[2] - 1 + lane % 8
    delta_z = (target_z - row % 64).astype(F32)
    plain = delta_z * delta_z + 1.0
    for s in range(8):
        delta_y = (target_y - (s + 8 * (row // 64))).astype(F32)
        base = plain + delta_y * delta_y
        for pair in range(8):
            delta_x = (2 * pair + lane // 64).astype(F32)
            green = 0.0625 * lax.rsqrt(base + delta_x * delta_x)
            high, low = split(green)
            green_high[128 * s : 128 * s + 128, 128 * pair : 128 * pair + 128] = high
            green_low[128 * s : 128 * s + 128, 128 * pair : 128 * pair + 128] = low


def prolong_rows(source, target, count, whole):
    size = target.shape[1] // 2
    q0 = source[:, 0:size, :]
    q1 = source[:, 1 : size + 1, :]
    q2 = source[:, 2 : size + 2, :]
    even = 0.75 * q1 + 0.125 * (q0 + q2)
    odd = 0.5 * (q0 + q1) if whole else 0.5 * (q1 + q2)
    target[:, pl.ds(1 if whole else 0, size, stride=2), :] = even
    target[:, pl.ds(0 if whole else 1, size, stride=2), :] = odd


def prolong_plane(read, p, whole):
    half = p // 2
    if (p % 2 == 1) == whole:
        return 0.75 * read(half + 1) + 0.125 * (read(half) + read(half + 2))
    first = half if whole else half + 1
    return 0.5 * (read(first) + read(first + 1))


def near_kernel(
    wide, from_low, from_high, b1h, b1l, b2h, b2l, b3h, b3l, prol_2, prol_1,
    out,
    near_1, near_2, near_3, tall_3, tall_3y, tall_2, tall_2y,
):
    where = place()
    low_msg, high_msg = from_low[...], from_high[...]

    def halo(x, rows, base, count, low_at, high_at):
        low = roll(low_msg[base : base + rows], low_at - count * x)
        high = roll(high_msg[base : base + rows], high_at - count * x)
        return lanes_of(low, low_at, 5 * count) + lanes_of(high, high_at, 5 * count)

    planes = [lanes_of(wide[x, 0:16, :], THI, 11) for x in range(15)]
    left = []
    for x in range(SPAN_3):
        main = taps([(1.0, roll(planes[x + a], 11 * a - THI)) for a in range(5)])
        left.append(main + halo(x, 16, 64, 5, 64, 96))
    left = jnp.concatenate(left, axis=0)
    near_3[...] = jnp.zeros_like(near_3)
    near_3[:, 0:16, :] = dot_split(left, b3h[...], b3l[...]).reshape(SPAN_3, 16, 128)
    third = taps([(1.0, roll(near_3[:, b : b + 16, :], -16 * b)) for b in range(5)])
    third = jnp.where(inside_mask(third.shape, SPAN_3, 9, where), third, 0.0)
    tall_3[...] = jnp.zeros_like(tall_3)
    tall_3[:, 0:16, :] = dot_exact(as_rows(third), prol_2[...]).reshape(SPAN_3, 16, 128)
    prolong_rows(tall_3, tall_3y, SPAN_2, True)

    planes = [lanes_of(wide[x, 0:24, :], SEC, 18) for x in range(22)]
    left_a, left_b = [], []
    for x in range(SPAN_2):
        left_a.append(taps([(1.0, roll(planes[x + a], 18 * a - SEC)) for a in range(5)]))
        left_b.append(halo(x, 24, 40, 4, 0, 32))
    left = jnp.concatenate(
        [jnp.concatenate(left_a, axis=0), jnp.concatenate(left_b, axis=0)], axis=1
    )
    near_2[...] = jnp.zeros_like(near_2)
    near_2[:, 0:24, :] = dot_split(left, b2h[...], b2l[...]).reshape(SPAN_2, 24, 128)
    second = taps([(1.0, roll(near_2[:, b : b + 24, :], -24 * b)) for b in range(5)])
    raised = jnp.stack(
        [prolong_plane(lambda x: tall_3y[x], p, True) for p in range(SPAN_2)], axis=0
    )
    second = jnp.where(inside_mask(second.shape, SPAN_2, 17, where), second + raised, 0.0)
    tall_2[...] = jnp.zeros_like(tall_2)
    tall_2[:, 0:24, :] = dot_exact(as_rows(second), prol_1[...]).reshape(SPAN_2, 24, 128)
    prolong_rows(tall_2, tall_2y, 32, False)

    planes = [lanes_of(wide[x], 0, 32) for x in range(36)]
    left_a, left_b = [], []
    for x in range(32):
        left_a.append(taps([(1.0, roll(planes[x + a], 32 * a)) for a in range(4)]))
        left_b.append(planes[x + 4] + halo(x, 40, 0, 2, 32, 64))
    left = jnp.concatenate(
        [jnp.concatenate(left_a, axis=0), jnp.concatenate(left_b, axis=0)], axis=1
    )
    near_1[...] = dot_split(left, b1h[...], b1l[...]).reshape(32, 40, 256)
    for x in range(32):
        first = taps(
            [(1.0, roll(near_1[x, b : b + 32, 0:128], -32 * b)) for b in range(4)]
            + [(1.0, near_1[x, 4:36, 128:256])]
        )
        out[x] = first + prolong_plane(lambda q: tall_2y[q], x, False)


def top_kernel(
    base, piece_0, piece_1, piece_2, piece_3, green_high, green_low, qx, qy, qz_high, qz_low,
    out,
    fourth,
):
    index, sizes = place()
    fourth[...] = jnp.zeros_like(fourth)
    for step, piece in enumerate((piece_0, piece_1, piece_2, piece_3)[: sizes[0]]):
        source = jnp.bitwise_xor(index[0], step)
        for r in range(SPAN_4):
            at = 4 * source + 3 + r
            fourth[at] = fourth[at] + piece[r]
    total = jnp.zeros((32, 1024), F32)
    extra = jnp.zeros((16, 1024), F32)
    for s in range(0, 8, 2):
        left = jnp.concatenate([fourth[4:20, s, :], fourth[4:20, s + 1, :]], axis=1)
        high, low = split(left)
        rows = slice(128 * s, 128 * s + 256)
        total = total + dot(jnp.concatenate([high, low], axis=0), green_high[rows, :])
        extra = extra + dot(high, green_low[rows, :])
    sums = total[0:16] + (total[16:32] + extra)
    row, lane = iota((16, 128), 0), iota((16, 128), 1)
    tops = []
    target_y = 4 * index[1] - 1 + lane // 8 % 8
    target_z = 4 * index[2] - 1 + lane % 8
    legal = (target_y >= 0) & (target_y < 4 * sizes[1]) & (target_z >= 0) & (target_z < 4 * sizes[2])
    legal = legal & (lane < 64)
    for tx in range(SPAN_4):
        target_x = 4 * index[0] - 1 + tx
        apart = jnp.abs(target_x - row)
        picked = jnp.zeros((16, 128), F32)
        for pair in range(8):
            picked = jnp.where(
                apart == 2 * pair + lane // 64, sums[:, 128 * pair : 128 * pair + 128], picked
            )
        picked = picked + roll(picked, 64)
        fits = legal & (target_x >= 0) & (target_x < 4 * sizes[0])
        tops.append(jnp.sum(jnp.where(fits, picked, 0.0), axis=0, keepdims=True))
    variant = [
        jnp.where(index[d] == 0, 1, 0) + jnp.where(index[d] == sizes[d] - 1, 2, 0) for d in range(3)
    ]
    spread_x = qx[variant[0]]
    raised = None
    for tx in range(SPAN_4):
        term = spread_x[:, tx : tx + 1] * tops[tx]
        raised = term if raised is None else raised + term
    spread = raised[:, None, :] * qy[variant[1]][None, :, :]
    far = dot_split(as_rows(spread), qz_high[variant[2]], qz_low[variant[2]])
    out[...] = (base[...] + far.reshape(32, 32, 128))[:, :, 0:32]


def call(kernel, outs, ins, scratch=(), megabytes=16, flops=1000000, spaces=None):
    spaces = spaces or {}
    return pl.pallas_call(
        kernel,
        out_shape=outs,
        in_specs=[spaces.get(i, VMEM) for i in range(len(ins))],
        out_specs=jax.tree.map(lambda _: VMEM, outs),
        scratch_shapes=list(scratch),
        compiler_params=pltpu.CompilerParams(vmem_limit_bytes=megabytes * 2**20),
        cost_estimate=pl.CostEstimate(flops=flops, bytes_accessed=2**21, transcendentals=0),
    )(*ins)


def shape(*dims, dtype=F32):
    return jax.ShapeDtypeStruct(dims, dtype)


def halo_pair(to_high, to_low, axis):
    size = lax.axis_size(axis)
    up = [(i, i + 1) for i in range(size - 1)]
    down = [(i + 1, i) for i in range(size - 1)]
    return lax.ppermute(to_high, axis, up), lax.ppermute(to_low, axis, down)


def partners(value, axis, stride):
    size = lax.axis_size(axis)
    got = []
    for step in range(1, min(4, size // stride)):
        got.append(lax.ppermute(value, axis, [(i, i ^ (step * stride)) for i in range(size)]))
    return got


def shards(charges, counts, slots, spline, kernel_fine, kernel_mid, kernel_coarse):
    cells = charges.shape[0]
    table_shapes = (shape(*CODES_1.shape, dtype=BF16), shape(*CODES_2.shape, dtype=BF16), shape(*CODES_3.shape, dtype=BF16))
    packed, fourth, to_high, to_low = call(
        deposit_kernel,
        (shape(32, 32, 128), shape(SPAN_4, 8, 128), shape(5, 32, 128), shape(5, 32, 128)),
        (
            charges,
            counts.reshape(1, cells),
            slots.reshape(1, cells),
            spline.reshape(cells * 12, ATOMS),
            jnp.asarray(spread_table(), BF16),
            jnp.asarray(REST_2, BF16),
            jnp.asarray(REST_3, BF16),
        ),
        (
            pltpu.VMEM((cells * 12, 128), F32),
            pltpu.VMEM((64, cells), F32),
            pltpu.VMEM((32, 32, 128), F32),
            pltpu.VMEM((SPAN_2, 56, 128), F32),
            pltpu.VMEM((SPAN_3, 40, 128), F32),
            pltpu.VMEM((SPAN_4, 24, 128), F32),
        ),
    )
    value = fourth
    size_z = lax.axis_size("gz")
    stride = 1
    while stride < size_z:
        for got in partners(value, "gz", stride):
            value = value + got
        stride *= 4
    for got in partners(value, "gy", 1):
        value = value + got
    pieces = [value] + partners(value, "gx", 1)
    while len(pieces) < 4:
        pieces.append(value)
    from_low, from_high = halo_pair(to_high, to_low, "gx")
    wide_x, to_high, to_low = call(
        widen_x_kernel,
        (shape(36, 32, 128), shape(18, 8, 128), shape(18, 8, 128)),
        (packed, from_low, from_high),
    )
    from_low, from_high = halo_pair(to_high, to_low, "gy")
    wide_y, to_high, to_low = call(
        widen_y_kernel,
        (shape(36, 40, 128), shape(80, 128), shape(80, 128)),
        (wide_x, from_low, from_high),
    )
    from_low, from_high = halo_pair(to_high, to_low, "gz")
    tables = call(
        tables_kernel,
        (shape(1024, 1024, dtype=BF16), shape(1024, 1024, dtype=BF16))
        + tuple(s for s in table_shapes for _ in range(2)),
        (
            fourth, kernel_fine, kernel_mid, kernel_coarse,
            jnp.asarray(CODES_1), jnp.asarray(CODES_2), jnp.asarray(CODES_3),
        ),
        spaces={1: SMEM, 2: SMEM, 3: SMEM, 0: pl.BlockSpec(memory_space=pl.ANY)},
    )
    base = call(
        near_kernel,
        shape(32, 32, 128),
        (
            wide_y, from_low, from_high, *tables[2:],
            jnp.asarray(PROL_2, BF16), jnp.asarray(PROL_1, BF16),
        ),
        (
            pltpu.VMEM((32, 40, 256), F32),
            pltpu.VMEM((SPAN_2, 32, 128), F32),
            pltpu.VMEM((SPAN_3, 24, 128), F32),
            pltpu.VMEM((SPAN_3, 24, 128), F32),
            pltpu.VMEM((SPAN_3, 24, 128), F32),
            pltpu.VMEM((SPAN_2, 32, 128), F32),
            pltpu.VMEM((SPAN_2, 32, 128), F32),
        ),
    )
    qx, qy, qz = composites()
    qz_high = jnp.asarray(qz).astype(BF16)
    qz_low = jnp.asarray(qz - np.asarray(qz.astype(BF16)).astype(np.float32)).astype(BF16)
    return call(
        top_kernel,
        shape(32, 32, 32),
        (base, *pieces, *tables[:2], jnp.asarray(qx), jnp.asarray(qy), qz_high, qz_low),
        (pltpu.VMEM((28, 8, 128), F32),),
    )


def solution(mesh):
    return jax.shard_map(
        shards,
        mesh=mesh,
        in_specs=(
            P(("gx", "gy", "gz"), None),
            P(("gx", "gy", "gz")),
            P(("gx", "gy", "gz")),
            P(("gx", "gy", "gz"), None, None, None),
            P(),
            P(),
            P(),
        ),
        out_specs=P("gx", "gy", "gz"),
        check_vma=False,
    )
```

time: 1220 us -> 63.1 us (0.05)
  the two profiles are of different devices: /device:TPU:32 before, /device:TPU:39 now
where the time goes in v1:
time: 63.1 us; the launch traced here: 62.7 us
  starting transfers between devices  42.1 us (67%)
  Pallas kernels  12.7 us (20%)
  local copies, waits for them, and re-layouts  6.05 us (10%)
  waiting for transfers between devices  1.42 us (2%)
    ppermute x6, starting transfers between devices, halo_pair(): return (lax.ppermute(to_high, axis, up), lax.ppermute(to_low, axis, down))  24.1 us
    ppermute x12, starting transfers between devices, partners(): lax.ppermute(value, axis, [(i, i ^ step * stride) for i in range(size)])  17.9 us
    pallas_call x6, Pallas kernels, call(): pl.pallas_call(kernel, out_shape=outs, in_specs=[spaces.get(i, VMEM) for...  12.7 us
    unnamed x34, local copies, waits for them, and re-layouts  4.68 us
    ppermute x6, waiting for transfers between devices, halo_pair(): return (lax.ppermute(to_high, axis, up), lax.ppermute(to_low, axis, down))  1.39 us
  transfers between devices with their start and end apart: 18, of which 1 were waited for; matrix products, arithmetic and copies ran while one was open for 0% of the time, Pallas kernels for 12%

profile of v1, /device:TPU:39, one launch (start us, length us, event | category | flops | bytes accessed | tf_op | source)
XLA Modules:
  0.0 62.7 jit_solution(2303440938464189478)
XLA Ops:
  0.0 0.7 %reshape.9.counts = s32[1,384]{1,0:T(1,128)S(1)} reshape(s32[384]{0:T(512)} %param.20) | data formatting | bytes 3072 | tf_op jit(solution)/shard_map/reshape | solution.py:560
  0.7 0.7 %reshape.10.slots = s32[1,384]{1,0:T(1,128)S(1)} reshape(s32[384]{0:T(512)} %param.21) | data formatting | bytes 3072 | tf_op jit(solution)/shard_map/reshape | solution.py:561
  1.4 1.3 %copy-done = bf16[384,3,4,128]{3,2,1,0:T(4,128)(2,1)S(1)} copy-done((bf16[384,3,4,128]{3,2,1,0:T(4,128)(2,1)S(1)}, bf16[384,3,4,128]{3,2,1,0:T(4,128)(2,1)}, u32[]{:S(2)}) %copy-start) | copy-done | bytes 1179672
  2.6 0.9 %copy-done.2 = f32[384,128]{1,0:T(8,128)S(1)} copy-done((f32[384,128]{1,0:T(8,128)S(1)}, f32[384,128]{1,0:T(8,128)}, u32[]{:S(2)}) %copy-start.2) | copy-done | bytes 196632
  3.6 0.9 %copy-done.6 = bf16[512,64]{1,0:T(8,128)(2,1)S(1)} copy-done((bf16[512,64]{1,0:T(8,128)(2,1)S(1)}, bf16[512,64]{1,0:T(8,128)(2,1)}, u32[]{:S(2)}) %copy-start.6) | copy-done | bytes 65560
  4.5 0.8 %copy-done.12 = bf16[128,128]{1,0:T(8,128)(2,1)S(1)} copy-done((bf16[128,128]{1,0:T(8,128)(2,1)S(1)}, bf16[128,128]{1,0:T(8,128)(2,1)}, u32[]{:S(2)}) %copy-start.12) | copy-done | bytes 32792
  5.2 0.8 %copy-done.13 = bf16[128,128]{1,0:T(8,128)(2,1)S(1)} copy-done((bf16[128,128]{1,0:T(8,128)(2,1)S(1)}, bf16[128,128]{1,0:T(8,128)(2,1)}, u32[]{:S(2)}) %copy-start.13) | copy-done | bytes 32792
  6.0 0.0 copy-start.10
  6.0 3.1 %shard_map.181 = (f32[32,32,128]{2,1,0:T(8,128)S(1)}, f32[7,8,128]{2,1,0:T(8,128)S(1)}, f32[5,32,128]{2,1,0:T(8,128)S(1)}, f32[5,32,128]{2,1,0:T(8,128)S(1)}) custom-call(f32[384,128]{1,0:T(8,128)S(1)} %copy-done.2, s32[1,384]{1,0:T(1,128)S(1)} %reshape.9.counts, s32[1,384]{1,0:T(1,128)S(1)} %reshape.10.slots, bf16[4608,128]{1,0:T(8,128)(2,1)S(1)} %bitcast.1, ...), custom_call_target="tpu_custom_call" | custom-call | flops 1000000 | bytes 2097152 | tf_op jit(solution)/shard_map/pallas_call | solution.py:522
  9.2 2.8 %collective-permute-start.8 = (f32[7,8,128]{2,1,0:T(8,128)S(1)}, f32[7,8,128]{2,1,0:T(8,128)S(1)}, u32[]{:S(2)}, u32[]{:S(2)}) collective-permute-start(f32[7,8,128]{2,1,0:T(8,128)S(1)} %get-tuple-element.32.after), channel_id=1, source_target_pairs={{0,3},{1,2},{2,1},{3,0},{4,7},{5,6},{6,5},{7,4},{8,11},{9,10},{10,... | collective-permute-start | bytes 86024 | tf_op jit(solution)/shard_map/ppermute | solution.py:548
  12.0 0.3 collective-permute-start.7
  12.3 0.3 collective-permute-start.6
  12.7 1.3 %collective-permute-start = (f32[5,32,128]{2,1,0:T(8,128)S(1)}, f32[5,32,128]{2,1,0:T(8,128)S(1)}, u32[]{:S(2)}, u32[]{:S(2)}) collective-permute-start(f32[5,32,128]{2,1,0:T(8,128)S(1)} %get-tuple-element.24), channel_id=1, source_target_pairs={{0,64},{64,128},{128,192},{1,65},{65,129},{129,193},{2,66},{66,130... | collective-permute-start | bytes 245768 | tf_op jit(solution)/shard_map/ppermute | solution.py:541
  13.9 4.0 %collective-permute-start.1 = (f32[5,32,128]{2,1,0:T(8,128)S(1)}, f32[5,32,128]{2,1,0:T(8,128)S(1)}, u32[]{:S(2)}, u32[]{:S(2)}) collective-permute-start(f32[5,32,128]{2,1,0:T(8,128)S(1)} %get-tuple-element.25), channel_id=1, source_target_pairs={{64,0},{128,64},{192,128},{65,1},{129,65},{193,129},{66,2},{130,66... | collective-permute-start | bytes 245768 | tf_op jit(solution)/shard_map/ppermute | solution.py:541
  18.0 1.7 %collective-permute-start.11 = (f32[7,8,128]{2,1,0:T(8,128)S(1)}, f32[7,8,128]{2,1,0:T(8,128)S(1)}, u32[]{:S(2)}, u32[]{:S(2)}) collective-permute-start(f32[7,8,128]{2,1,0:T(8,128)S(1)} %add_add_fusion.2), channel_id=1, source_target_pairs={{0,12},{1,13},{2,14},{3,15},{4,8},{5,9},{6,10},{7,11},{8,4},{9,5},... | collective-permute-start | bytes 86024 | tf_op jit(solution)/shard_map/ppermute | solution.py:548
  19.8 1.5 %collective-permute-start.10 = (f32[7,8,128]{2,1,0:T(8,128)S(1)}, f32[7,8,128]{2,1,0:T(8,128)S(1)}, u32[]{:S(2)}, u32[]{:S(2)}) collective-permute-start(f32[7,8,128]{2,1,0:T(8,128)S(1)} %add_add_fusion.2), channel_id=1, source_target_pairs={{0,8},{1,9},{2,10},{3,11},{4,12},{5,13},{6,14},{7,15},{8,0},{9,1},... | collective-permute-start | bytes 86024 | tf_op jit(solution)/shard_map/ppermute | solution.py:548
  21.2 1.1 %collective-permute-start.9 = (f32[7,8,128]{2,1,0:T(8,128)S(1)}, f32[7,8,128]{2,1,0:T(8,128)S(1)}, u32[]{:S(2)}, u32[]{:S(2)}) collective-permute-start(f32[7,8,128]{2,1,0:T(8,128)S(1)} %add_add_fusion.2), channel_id=1, source_target_pairs={{0,4},{1,5},{2,6},{3,7},{4,0},{5,1},{6,2},{7,3},{8,12},{9,13},{10,... | collective-permute-start | bytes 86024 | tf_op jit(solution)/shard_map/ppermute | solution.py:548
  22.3 0.1 shard_map.182
  22.4 9.0 %collective-permute-start.2 = (f32[18,8,128]{2,1,0:T(8,128)S(1)}, f32[18,8,128]{2,1,0:T(8,128)S(1)}, u32[]{:S(2)}, u32[]{:S(2)}) collective-permute-start(f32[18,8,128]{2,1,0:T(8,128)S(1)} %get-tuple-element.27), channel_id=1, source_target_pairs={{0,16},{16,32},{32,48},{1,17},{17,33},{33,49},{2,18},{18,34},{34,5... | collective-permute-start | bytes 221192 | tf_op jit(solution)/shard_map/ppermute | solution.py:541
  31.5 1.9 %collective-permute-start.3 = (f32[18,8,128]{2,1,0:T(8,128)S(1)}, f32[18,8,128]{2,1,0:T(8,128)S(1)}, u32[]{:S(2)}, u32[]{:S(2)}) collective-permute-start(f32[18,8,128]{2,1,0:T(8,128)S(1)} %get-tuple-element.28), channel_id=1, source_target_pairs={{16,0},{32,16},{48,32},{17,1},{33,17},{49,33},{18,2},{34,18},{50,3... | collective-permute-start | bytes 221192 | tf_op jit(solution)/shard_map/ppermute | solution.py:541
  33.4 5.7 %collective-permute-start.14 = (f32[7,8,128]{2,1,0:T(8,128)S(1)}, f32[7,8,128]{2,1,0:T(8,128)S(1)}, u32[]{:S(2)}, u32[]{:S(2)}) collective-permute-start(f32[7,8,128]{2,1,0:T(8,128)S(1)} %add_add_fusion.1), channel_id=1, source_target_pairs={{0,48},{16,32},{32,16},{48,0},{1,49},{17,33},{33,17},{49,1},{2,50}... | collective-permute-start | bytes 86024 | tf_op jit(solution)/shard_map/ppermute | solution.py:548
  39.2 0.5 collective-permute-start.12
  39.7 1.4 %collective-permute-done.3.from_high = f32[18,8,128]{2,1,0:T(8,128)S(1)} collective-permute-done((f32[18,8,128]{2,1,0:T(8,128)S(1)}, f32[18,8,128]{2,1,0:T(8,128)S(1)}, u32[]{:S(2)}, u32[]{:S(2)}) %collective-permute-start.3) | collective-permute-done | bytes 73760 | tf_op jit(solution)/shard_map/ppermute | solution.py:541
  41.1 0.7 %shard_map.183 = (f32[36,40,128]{2,1,0:T(8,128)S(1)}, f32[80,128]{1,0:T(8,128)S(1)}, f32[80,128]{1,0:T(8,128)S(1)}) custom-call(f32[36,32,128]{2,1,0:T(8,128)S(1)} %get-tuple-element.26.wide_x, f32[18,8,128]{2,1,0:T(8,128)S(1)} %collective-permute-done.2.from_low, f32[18,8,128]{2,1,0:T(8,128)S(1)} %collective-permute-done.3.from_high), custom_call_target="tpu_custom_call" | custom-call | flops 1000000 | bytes 2097152 | tf_op jit(solution)/shard_map/pallas_call | solution.py:522
  41.8 3.2 %collective-permute-start.4 = (f32[80,128]{1,0:T(8,128)S(1)}, f32[80,128]{1,0:T(8,128)S(1)}, u32[]{:S(2)}, u32[]{:S(2)}) collective-permute-start(f32[80,128]{1,0:T(8,128)S(1)} %get-tuple-element.30), channel_id=1, source_target_pairs={{0,1},{1,2},{2,3},{3,4},{4,5},{5,6},{6,7},{7,8},{8,9},{9,10},{10,1... | collective-permute-start | bytes 122888 | tf_op jit(solution)/shard_map/ppermute | solution.py:541
  45.0 4.7 %collective-permute-start.5 = (f32[80,128]{1,0:T(8,128)S(1)}, f32[80,128]{1,0:T(8,128)S(1)}, u32[]{:S(2)}, u32[]{:S(2)}) collective-permute-start(f32[80,128]{1,0:T(8,128)S(1)} %get-tuple-element.31), channel_id=1, source_target_pairs={{1,0},{2,1},{3,2},{4,3},{5,4},{6,5},{7,6},{8,7},{9,8},{10,9},{11,1... | collective-permute-start | bytes 122888 | tf_op jit(solution)/shard_map/ppermute | solution.py:541
  49.8 0.6 %collective-permute-start.15 = (f32[7,8,128]{2,1,0:T(8,128)S(1)}, f32[7,8,128]{2,1,0:T(8,128)S(1)}, u32[]{:S(2)}, u32[]{:S(2)}) collective-permute-start(f32[7,8,128]{2,1,0:T(8,128)S(1)} %add_add_fusion.piece_0), channel_id=1, source_target_pairs={{0,64},{64,0},{128,192},{192,128},{1,65},{65,1},{129,193},{193,129... | collective-permute-start | bytes 86024 | tf_op jit(solution)/shard_map/ppermute | solution.py:548
  50.4 0.7 %collective-permute-start.16 = (f32[7,8,128]{2,1,0:T(8,128)S(1)}, f32[7,8,128]{2,1,0:T(8,128)S(1)}, u32[]{:S(2)}, u32[]{:S(2)}) collective-permute-start(f32[7,8,128]{2,1,0:T(8,128)S(1)} %add_add_fusion.piece_0), channel_id=1, source_target_pairs={{0,128},{64,192},{128,0},{192,64},{1,129},{65,193},{129,1},{193,65... | collective-permute-start | bytes 86024 | tf_op jit(solution)/shard_map/ppermute | solution.py:548
  51.1 2.6 %collective-permute-start.17 = (f32[7,8,128]{2,1,0:T(8,128)S(1)}, f32[7,8,128]{2,1,0:T(8,128)S(1)}, u32[]{:S(2)}, u32[]{:S(2)}) collective-permute-start(f32[7,8,128]{2,1,0:T(8,128)S(1)} %add_add_fusion.piece_0), channel_id=1, source_target_pairs={{0,192},{64,128},{128,64},{192,0},{1,193},{65,129},{129,65},{193,1... | collective-permute-start | bytes 86024 | tf_op jit(solution)/shard_map/ppermute | solution.py:548
  53.7 3.9 %shard_map.184 = (bf16[1024,1024]{1,0:T(8,128)(2,1)S(1)}, bf16[1024,1024]{1,0:T(8,128)(2,1)S(1)}, bf16[256,256]{1,0:T(8,128)(2,1)S(1)}, bf16[256,256]{1,0:T(8,12...) custom-call(f32[7,8,128]{2,1,0:T(8,128)S(1)} %get-tuple-element.32.a, ...), custom_call_target="tpu_custom_call" | custom-call | flops 1000000 | bytes 2097152 | tf_op jit(solution)/shard_map/pallas_call | solution.py:522
  57.7 2.9 %shard_map.185.base = f32[32,32,128]{2,1,0:T(8,128)S(1)} custom-call(f32[36,40,128]{2,1,0:T(8,128)S(1)} %get-tuple-element.29.wide, f32[80,128]{1,0:T(8,128)S(1)} %collective-permute-done.4.from_low, f32[80,128]{1,0:T(8,128)S(1)} %collective-permute-done.5.from_high, bf16[256,256]{1,0:T(8,128)(2,1)S(1)} %get-tuple-element.33.b1h, ...), custom_call_target="tpu_custom_call" | custom-call | flops 1000000 | bytes 2097152 | tf_op jit(solution)/shard_map/pallas_call | solution.py:522
  60.7 2.0 %shard_map.186 = f32[32,32,32]{2,1,0:T(8,128)} custom-call(f32[32,32,128]{2,1,0:T(8,128)S(1)} %shard_map.185.base, f32[7,8,128]{2,1,0:T(8,128)S(1)} %add_add_fusion.piece_0, f32[7,8,128]{2,1,0:T(8,128)S(1)} %collective-permute-done.15.piece_1, f32[7,8,128]{2,1,0:T(8,128)S(1)} %collective-permute-done.16.piece_2, ...), custom_call_target="tpu_custom_call" | custom-call | flops 1000000 | bytes 2097152 | tf_op jit(solution)/shard_map/pallas_call | solution.py:522
  (49 shorter events, 0.2 us)
Async XLA Ops:
  1.4 1.3 %copy-start = (bf16[384,3,4,128]{3,2,1,0:T(4,128)(2,1)S(1)}, bf16[384,3,4,128]{3,2,1,0:T(4,128)(2,1)}, u32[]{:S(2)}) copy-start(bf16[384,3,4,128]{3,2,1,0:T(4,128)(2,1)} %param.22) | copy-start | bytes 3538948
  2.6 0.9 %copy-start.2 = (f32[384,128]{1,0:T(8,128)S(1)}, f32[384,128]{1,0:T(8,128)}, u32[]{:S(2)}) copy-start(f32[384,128]{1,0:T(8,128)} %charges.1) | copy-start | bytes 589828
  6.0 47.7 %copy-start.1 = (s32[256,256]{1,0:T(8,128)S(1)}, s32[256,256]{1,0:T(8,128)}, u32[]{:S(2)}) copy-start(s32[256,256]{1,0:T(8,128)} %constant.27.clone.codes_1) | copy-start | bytes 786436
  6.0 47.7 %copy-start.5 = (s32[256,128]{1,0:T(8,128)S(1)}, s32[256,128]{1,0:T(8,128)}, u32[]{:S(2)}) copy-start(s32[256,128]{1,0:T(8,128)} %constant.28.clone.codes_2) | copy-start | bytes 393220
  6.0 47.7 %copy-start.9 = (s32[128,128]{1,0:T(8,128)S(1)}, s32[128,128]{1,0:T(8,128)}, u32[]{:S(2)}) copy-start(s32[128,128]{1,0:T(8,128)} %constant.29.clone.codes_3) | copy-start | bytes 196612
  6.0 47.7 %copy-start.14 = (f32[5,5,5]{2,1,0:T(8,128)S(1)}, f32[5,5,5]{2,1,0:T(8,128)}, u32[]{:S(2)}) copy-start(f32[5,5,5]{2,1,0:T(8,128)} %kernel_1.1) | copy-start | bytes 1504
  6.0 47.7 %copy-start.15 = (f32[5,5,5]{2,1,0:T(8,128)S(1)}, f32[5,5,5]{2,1,0:T(8,128)}, u32[]{:S(2)}) copy-start(f32[5,5,5]{2,1,0:T(8,128)} %kernel_2.1) | copy-start | bytes 1504
  6.0 47.7 %copy-start.16 = (f32[5,5,5]{2,1,0:T(8,128)S(1)}, f32[5,5,5]{2,1,0:T(8,128)}, u32[]{:S(2)}) copy-start(f32[5,5,5]{2,1,0:T(8,128)} %kernel_3.1) | copy-start | bytes 1504
  6.0 51.7 %copy-start.10 = (bf16[128,128]{1,0:T(8,128)(2,1)S(1)}, bf16[128,128]{1,0:T(8,128)(2,1)}, u32[]{:S(2)}) copy-start(bf16[128,128]{1,0:T(8,128)(2,1)} %constant.30.clone.prol_2) | copy-start | bytes 98308
  6.0 51.7 %copy-start.11 = (bf16[128,128]{1,0:T(8,128)(2,1)S(1)}, bf16[128,128]{1,0:T(8,128)(2,1)}, u32[]{:S(2)}) copy-start(bf16[128,128]{1,0:T(8,128)(2,1)} %constant.31.clone.prol_1) | copy-start | bytes 98308
  9.2 8.8 %collective-permute-start.8 = (f32[7,8,128]{2,1,0:T(8,128)S(1)}, f32[7,8,128]{2,1,0:T(8,128)S(1)}, u32[]{:S(2)}, u32[]{:S(2)}) collective-permute-start(f32[7,8,128]{2,1,0:T(8,128)S(1)} %get-tuple-element.32.after), channel_id=1, source_target_pairs={{0,3},{1,2},{2,1},{3,0},{4,7},{5,6},{6,5},{7,4},{8,11},{9,10},{10,... | collective-permute-start | bytes 86024 | tf_op jit(solution)/shard_map/ppermute | solution.py:548
  12.0 6.0 %collective-permute-start.7 = (f32[7,8,128]{2,1,0:T(8,128)S(1)}, f32[7,8,128]{2,1,0:T(8,128)S(1)}, u32[]{:S(2)}, u32[]{:S(2)}) collective-permute-start(f32[7,8,128]{2,1,0:T(8,128)S(1)} %get-tuple-element.32.after), channel_id=1, source_target_pairs={{0,2},{1,3},{2,0},{3,1},{4,6},{5,7},{6,4},{7,5},{8,10},{9,11},{10,... | collective-permute-start | bytes 86024 | tf_op jit(solution)/shard_map/ppermute | solution.py:548
  12.3 5.6 %collective-permute-start.6 = (f32[7,8,128]{2,1,0:T(8,128)S(1)}, f32[7,8,128]{2,1,0:T(8,128)S(1)}, u32[]{:S(2)}, u32[]{:S(2)}) collective-permute-start(f32[7,8,128]{2,1,0:T(8,128)S(1)} %get-tuple-element.32.after), channel_id=1, source_target_pairs={{0,1},{1,0},{2,3},{3,2},{4,5},{5,4},{6,7},{7,6},{8,9},{9,8},{10,11... | collective-permute-start | bytes 86024 | tf_op jit(solution)/shard_map/ppermute | solution.py:548
  12.7 9.7 %collective-permute-start = (f32[5,32,128]{2,1,0:T(8,128)S(1)}, f32[5,32,128]{2,1,0:T(8,128)S(1)}, u32[]{:S(2)}, u32[]{:S(2)}) collective-permute-start(f32[5,32,128]{2,1,0:T(8,128)S(1)} %get-tuple-element.24), channel_id=1, source_target_pairs={{0,64},{64,128},{128,192},{1,65},{65,129},{129,193},{2,66},{66,130... | collective-permute-start | bytes 245768 | tf_op jit(solution)/shard_map/ppermute | solution.py:541
  13.9 8.4 %collective-permute-start.1 = (f32[5,32,128]{2,1,0:T(8,128)S(1)}, f32[5,32,128]{2,1,0:T(8,128)S(1)}, u32[]{:S(2)}, u32[]{:S(2)}) collective-permute-start(f32[5,32,128]{2,1,0:T(8,128)S(1)} %get-tuple-element.25), channel_id=1, source_target_pairs={{64,0},{128,64},{192,128},{65,1},{129,65},{193,129},{66,2},{130,66... | collective-permute-start | bytes 245768 | tf_op jit(solution)/shard_map/ppermute | solution.py:541
  18.0 42.6 %copy-start.3 = (bf16[4,128,128]{2,1,0:T(8,128)(2,1)S(1)}, bf16[4,128,128]{2,1,0:T(8,128)(2,1)}, u32[]{:S(2)}) copy-start(bf16[4,128,128]{2,1,0:T(8,128)(2,1)} %constant.40.qz_high) | copy-start | bytes 393220
  18.0 42.6 %copy-start.4 = (bf16[4,128,128]{2,1,0:T(8,128)(2,1)S(1)}, bf16[4,128,128]{2,1,0:T(8,128)(2,1)}, u32[]{:S(2)}) copy-start(bf16[4,128,128]{2,1,0:T(8,128)(2,1)} %constant.41.qz_low) | copy-start | bytes 393220
  18.0 42.6 %copy-start.7 = (f32[4,32,8]{2,1,0:T(8,128)S(1)}, f32[4,32,8]{2,1,0:T(8,128)}, u32[]{:S(2)}) copy-start(f32[4,32,8]{2,1,0:T(8,128)} %constant.34.clone.qx) | copy-start | bytes 12292
  18.0 42.6 %copy-start.8 = (f32[4,32,128]{2,1,0:T(8,128)S(1)}, f32[4,32,128]{2,1,0:T(8,128)}, u32[]{:S(2)}) copy-start(f32[4,32,128]{2,1,0:T(8,128)} %constant.35.clone.qy) | copy-start | bytes 196612
  18.0 15.4 %collective-permute-start.11 = (f32[7,8,128]{2,1,0:T(8,128)S(1)}, f32[7,8,128]{2,1,0:T(8,128)S(1)}, u32[]{:S(2)}, u32[]{:S(2)}) collective-permute-start(f32[7,8,128]{2,1,0:T(8,128)S(1)} %add_add_fusion.2), channel_id=1, source_target_pairs={{0,12},{1,13},{2,14},{3,15},{4,8},{5,9},{6,10},{7,11},{8,4},{9,5},... | collective-permute-start | bytes 86024 | tf_op jit(solution)/shard_map/ppermute | solution.py:548
  19.8 13.6 %collective-permute-start.10 = (f32[7,8,128]{2,1,0:T(8,128)S(1)}, f32[7,8,128]{2,1,0:T(8,128)S(1)}, u32[]{:S(2)}, u32[]{:S(2)}) collective-permute-start(f32[7,8,128]{2,1,0:T(8,128)S(1)} %add_add_fusion.2), channel_id=1, source_target_pairs={{0,8},{1,9},{2,10},{3,11},{4,12},{5,13},{6,14},{7,15},{8,0},{9,1},... | collective-permute-start | bytes 86024 | tf_op jit(solution)/shard_map/ppermute | solution.py:548
  21.2 12.2 %collective-permute-start.9 = (f32[7,8,128]{2,1,0:T(8,128)S(1)}, f32[7,8,128]{2,1,0:T(8,128)S(1)}, u32[]{:S(2)}, u32[]{:S(2)}) collective-permute-start(f32[7,8,128]{2,1,0:T(8,128)S(1)} %add_add_fusion.2), channel_id=1, source_target_pairs={{0,4},{1,5},{2,6},{3,7},{4,0},{5,1},{6,2},{7,3},{8,12},{9,13},{10,... | collective-permute-start | bytes 86024 | tf_op jit(solution)/shard_map/ppermute | solution.py:548
  22.4 17.2 %collective-permute-start.2 = (f32[18,8,128]{2,1,0:T(8,128)S(1)}, f32[18,8,128]{2,1,0:T(8,128)S(1)}, u32[]{:S(2)}, u32[]{:S(2)}) collective-permute-start(f32[18,8,128]{2,1,0:T(8,128)S(1)} %get-tuple-element.27), channel_id=1, source_target_pairs={{0,16},{16,32},{32,48},{1,17},{17,33},{33,49},{2,18},{18,34},{34,5... | collective-permute-start | bytes 221192 | tf_op jit(solution)/shard_map/ppermute | solution.py:541
  31.5 9.6 %collective-permute-start.3 = (f32[18,8,128]{2,1,0:T(8,128)S(1)}, f32[18,8,128]{2,1,0:T(8,128)S(1)}, u32[]{:S(2)}, u32[]{:S(2)}) collective-permute-start(f32[18,8,128]{2,1,0:T(8,128)S(1)} %get-tuple-element.28), channel_id=1, source_target_pairs={{16,0},{32,16},{48,32},{17,1},{33,17},{49,33},{18,2},{34,18},{50,3... | collective-permute-start | bytes 221192 | tf_op jit(solution)/shard_map/ppermute | solution.py:541
  33.4 16.3 %collective-permute-start.14 = (f32[7,8,128]{2,1,0:T(8,128)S(1)}, f32[7,8,128]{2,1,0:T(8,128)S(1)}, u32[]{:S(2)}, u32[]{:S(2)}) collective-permute-start(f32[7,8,128]{2,1,0:T(8,128)S(1)} %add_add_fusion.1), channel_id=1, source_target_pairs={{0,48},{16,32},{32,16},{48,0},{1,49},{17,33},{33,17},{49,1},{2,50}... | collective-permute-start | bytes 86024 | tf_op jit(solution)/shard_map/ppermute | solution.py:548
  39.2 10.6 %collective-permute-start.13 = (f32[7,8,128]{2,1,0:T(8,128)S(1)}, f32[7,8,128]{2,1,0:T(8,128)S(1)}, u32[]{:S(2)}, u32[]{:S(2)}) collective-permute-start(f32[7,8,128]{2,1,0:T(8,128)S(1)} %add_add_fusion.1), channel_id=1, source_target_pairs={{0,32},{16,48},{32,0},{48,16},{1,33},{17,49},{33,1},{49,17},{2,34}... | collective-permute-start | bytes 86024 | tf_op jit(solution)/shard_map/ppermute | solution.py:548
  39.2 10.6 %collective-permute-start.12 = (f32[7,8,128]{2,1,0:T(8,128)S(1)}, f32[7,8,128]{2,1,0:T(8,128)S(1)}, u32[]{:S(2)}, u32[]{:S(2)}) collective-permute-start(f32[7,8,128]{2,1,0:T(8,128)S(1)} %add_add_fusion.1), channel_id=1, source_target_pairs={{0,16},{16,0},{32,48},{48,32},{1,17},{17,1},{33,49},{49,33},{2,18}... | collective-permute-start | bytes 86024 | tf_op jit(solution)/shard_map/ppermute | solution.py:548
  41.8 15.9 %collective-permute-start.4 = (f32[80,128]{1,0:T(8,128)S(1)}, f32[80,128]{1,0:T(8,128)S(1)}, u32[]{:S(2)}, u32[]{:S(2)}) collective-permute-start(f32[80,128]{1,0:T(8,128)S(1)} %get-tuple-element.30), channel_id=1, source_target_pairs={{0,1},{1,2},{2,3},{3,4},{4,5},{5,6},{6,7},{7,8},{8,9},{9,10},{10,1... | collective-permute-start | bytes 122888 | tf_op jit(solution)/shard_map/ppermute | solution.py:541
  45.0 12.7 %collective-permute-start.5 = (f32[80,128]{1,0:T(8,128)S(1)}, f32[80,128]{1,0:T(8,128)S(1)}, u32[]{:S(2)}, u32[]{:S(2)}) collective-permute-start(f32[80,128]{1,0:T(8,128)S(1)} %get-tuple-element.31), channel_id=1, source_target_pairs={{1,0},{2,1},{3,2},{4,3},{5,4},{6,5},{7,6},{8,7},{9,8},{10,9},{11,1... | collective-permute-start | bytes 122888 | tf_op jit(solution)/shard_map/ppermute | solution.py:541
  49.8 10.8 %collective-permute-start.15 = (f32[7,8,128]{2,1,0:T(8,128)S(1)}, f32[7,8,128]{2,1,0:T(8,128)S(1)}, u32[]{:S(2)}, u32[]{:S(2)}) collective-permute-start(f32[7,8,128]{2,1,0:T(8,128)S(1)} %add_add_fusion.piece_0), channel_id=1, source_target_pairs={{0,64},{64,0},{128,192},{192,128},{1,65},{65,1},{129,193},{193,129... | collective-permute-start | bytes 86024 | tf_op jit(solution)/shard_map/ppermute | solution.py:548
  50.4 10.2 %collective-permute-start.16 = (f32[7,8,128]{2,1,0:T(8,128)S(1)}, f32[7,8,128]{2,1,0:T(8,128)S(1)}, u32[]{:S(2)}, u32[]{:S(2)}) collective-permute-start(f32[7,8,128]{2,1,0:T(8,128)S(1)} %add_add_fusion.piece_0), channel_id=1, source_target_pairs={{0,128},{64,192},{128,0},{192,64},{1,129},{65,193},{129,1},{193,65... | collective-permute-start | bytes 86024 | tf_op jit(solution)/shard_map/ppermute | solution.py:548
  51.1 9.5 %collective-permute-start.17 = (f32[7,8,128]{2,1,0:T(8,128)S(1)}, f32[7,8,128]{2,1,0:T(8,128)S(1)}, u32[]{:S(2)}, u32[]{:S(2)}) collective-permute-start(f32[7,8,128]{2,1,0:T(8,128)S(1)} %add_add_fusion.piece_0), channel_id=1, source_target_pairs={{0,192},{64,128},{128,64},{192,0},{1,193},{65,129},{129,65},{193,1... | collective-permute-start | bytes 86024 | tf_op jit(solution)/shard_map/ppermute | solution.py:548
  (3 other events, 2.4 us)

commit v2 on v1

v2 whole, which is shorter than its diff:
```python
import jax
import jax.numpy as jnp
import numpy as np
from jax import lax
from jax.experimental import pallas as pl
from jax.experimental.pallas import tpu as pltpu
from jax.sharding import PartitionSpec as P

W = (0.125, 0.5, 0.75, 0.5, 0.125)
F32 = jnp.float32
BF16 = jnp.bfloat16
CELLS = 384
ATOMS = 128
SPAN_2 = 18
SPAN_3 = 11
SPAN_4 = 7
SEC = 32
THI = 64
VMEM = pl.BlockSpec(memory_space=pltpu.VMEM)
SMEM = pl.BlockSpec(memory_space=pltpu.SMEM)
HBM = pl.BlockSpec(memory_space=pltpu.HBM)


def weight(t):
    return W[t] if 0 <= t <= 4 else 0.0


def table(rows, columns, offset, turned):
    out = np.zeros((128, 128), np.float32)
    for r in range(rows):
        for c in range(columns):
            out[r, c] = weight(c - 2 * r + offset if turned else r - 2 * c + offset)
    return out


PROL_2 = table(SPAN_3, SPAN_2, 3, True)
PROL_1 = table(SPAN_2, 32, 4, True)


BANDS = (
    (256, 256, ((0, 32, 2), (160, 2, 0), (192, 2, 34)), 32, 32),
    (256, 128, ((0, 18, 2), (128, 4, 0), (160, 4, 18)), 24, 18),
    (128, 128, ((0, 11, 2), (64, 5, 0), (96, 5, 10)), 16, 11),
)
DIVIDE = {32: (1, 5), 2: (1, 1), 18: (57, 10), 4: (1, 2), 11: (94, 10), 5: (52, 8), 24: (43, 10), 16: (1, 4)}


def composite(first, last):
    p3 = np.array([[weight(i - 2 * j + 3) for j in range(7)] for i in range(11)])
    p2 = np.array([[weight(i - 2 * j + 3) for j in range(11)] for i in range(18)])
    p1 = np.array([[weight(i - 2 * j + 4) for j in range(18)] for i in range(32)])
    m4, m3, m2 = np.ones(7), np.ones(11), np.ones(18)
    if first:
        m4[0] = m3[0] = m2[0] = 0
    if last:
        m4[5:] = 0
        m3[9:] = 0
        m2[17:] = 0
    return (p1 * m2) @ (p2 * m3) @ (p3 * m4)


def composites():
    qx = np.zeros((4, 32, 128), np.float32)
    qy = np.zeros((4, 32, 128), np.float32)
    qz = np.zeros((4, 128, 128), np.float32)
    for v in range(4):
        q = composite(v % 2 == 1, v >= 2)
        for lane in range(64):
            if lane // 8 < 7 and lane % 8 < 7:
                qx[v, :, lane] = q[:, lane // 8]
                qy[v, :, lane] = q[:, lane % 8]
        for row in range(128):
            if row % 8 < 7:
                qz[v, row, :32] = q[:, row % 8]
    return qx, qy, qz


def split(x):
    high = x.astype(BF16)
    return high, (x - high.astype(F32)).astype(BF16)


def dot(a, b):
    return jnp.dot(a, b, preferred_element_type=F32)


def dot_exact(x, right):
    high, low = split(x)
    return dot(high, right) + dot(low, right)


def dot_split(x, right_high, right_low):
    high, low = split(x)
    return dot(high, right_high) + (dot(low, right_high) + dot(high, right_low))


def iota(shape, dim):
    return lax.broadcasted_iota(jnp.int32, shape, dim)


def roll(x, shift, axis=None):
    axis = x.ndim - 1 if axis is None else axis
    shift = shift % x.shape[axis]
    return x if shift == 0 else pltpu.roll(x, shift, axis)


def lanes_of(x, low, count):
    lane = iota(x.shape, x.ndim - 1)
    return jnp.where((lane >= low) & (lane < low + count), x, 0.0)


def as_rows(x):
    return x.reshape(x.shape[0] * x.shape[1], x.shape[2])


def taps(pieces):
    total = None
    for factor, value in pieces:
        term = value if factor == 1.0 else factor * value
        total = term if total is None else total + term
    return total


def restrict_planes(read, span, size, offset):
    planes = []
    for p in range(span):
        planes.append(
            taps([(W[t], read(2 * p + t - offset)) for t in range(5) if 0 <= 2 * p + t - offset < size])
        )
    return planes


def place():
    sizes = [lax.axis_size(a) for a in ("gx", "gy", "gz")]
    index = [lax.axis_index(a) for a in ("gx", "gy", "gz")]
    return index, sizes


def inside_mask(shape, spans, high, place_of):
    index, sizes = place_of
    keep = None
    for dim in range(3):
        at = iota(shape, dim)
        low = jnp.where(index[dim] == 0, 1, 0)
        top = jnp.where(index[dim] == sizes[dim] - 1, high, spans)
        part = (at >= low) & (at < top)
        keep = part if keep is None else keep & part
    return keep


def nearest(index):
    even = lax.rem(index, 2) == 0
    return even, index == 1, index == 2


def deposit_kernel(
    codes, charges_hbm, spline_hbm,
    packed, raw_out, face,
    charges, spline, wide, patch, fine, buf_2, buf_3, buf_4, second_ref, third_ref, sems,
):
    where = place()
    index, sizes = where
    part = CELLS * 12 // 3
    copies = [pltpu.make_async_copy(charges_hbm, charges, sems.at[3])]
    for chunk in range(3):
        rows = slice(part * chunk, part * chunk + part)
        copies.append(
            pltpu.make_async_copy(spline_hbm.at[rows, :], spline.at[rows, :], sems.at[chunk])
        )
    for copy in copies:
        copy.start()
    buf_2[...] = jnp.zeros_like(buf_2)
    buf_3[...] = jnp.zeros_like(buf_3)
    buf_4[...] = jnp.zeros_like(buf_4)
    row, column = iota((512, 64), 0), iota((512, 64), 1)
    spread = (row // 32 * 4 + row % 4 == column).astype(F32).astype(BF16)
    row, column = iota((128, 128), 0), iota((128, 128), 1)

    def restriction(rows, columns, offset):
        t = row - 2 * column + offset
        out = jnp.zeros((128, 128), F32)
        for tap in range(5):
            out = jnp.where(t == tap, W[tap], out)
        return jnp.where((row < rows) & (column < columns), out, 0.0).astype(BF16)

    rest_2 = restriction(32, SPAN_2, 4)
    rest_3 = restriction(SPAN_2, SPAN_3, 3)
    rest_4 = restriction(SPAN_3, SPAN_4, 3)
    slot = lax.shift_right_logical(codes[...].reshape(1, CELLS), 8)
    fits = (iota((512, CELLS), 0) // 4 % 8) == slot % 8
    hot = (iota((64, CELLS), 0) == slot // 8).astype(F32).astype(BF16)
    copies[0].wait()
    alive = iota((ATOMS, CELLS), 0) < (codes[...].reshape(1, CELLS) & 255)
    weighted = jnp.where(alive, charges[...].T, 0.0)
    for chunk in range(CELLS // 128):
        lanes = slice(128 * chunk, 128 * chunk + 128)
        copies[1 + chunk].wait()
        rows = slice(part * chunk, part * chunk + part)
        wide[rows, :] = spline[rows, :].astype(F32)

        def column_of(d, i):
            return wide[pl.ds(chunk * part + 4 * d + i, 128, stride=12), :].T

        charge = weighted[:, lanes]
        depth = [charge * column_of(2, k) for k in range(4)]
        ys = [column_of(1, j) for j in range(4)]
        for i in range(4):
            xs = column_of(0, i)
            for j in range(4):
                cross = xs * ys[j]
                for k in range(4):
                    patch[16 * i + 4 * j + k : 16 * i + 4 * j + k + 1, lanes] = jnp.sum(
                        cross * depth[k], axis=0, keepdims=True
                    )
    high, low = split(patch[...])
    spread_high = jnp.where(fits, dot(spread, high), 0.0).astype(BF16)
    spread_low = jnp.where(fits, dot(spread, low), 0.0).astype(BF16)
    nt = (((1,), (1,)), ((), ()))
    placed = lax.dot_general(hot, spread_high, nt, preferred_element_type=F32) + lax.dot_general(
        hot, spread_low, nt, preferred_element_type=F32
    )
    for i in range(4):
        for j in range(4):
            rows = lanes_of(roll(placed[:, 128 * i : 128 * i + 128], -32 * j), 0, 32)
            for sx in range(8):
                fine[4 * sx + i, pl.ds(j, 8, stride=4), :] = rows[8 * sx : 8 * sx + 8]

    for p, plane in enumerate(restrict_planes(lambda x: fine[x], SPAN_2, 32, 4)):
        buf_2[p, 4:36, :] = plane
    second = taps([(W[t], buf_2[:, pl.ds(t, 24, stride=2), :]) for t in range(5)])
    second = dot_exact(as_rows(second), rest_2).reshape(SPAN_2, 24, 128)
    second = jnp.where(inside_mask(second.shape, SPAN_2, 17, where), second, 0.0)
    second_ref[...] = second
    for p, plane in enumerate(restrict_planes(lambda x: second[x], SPAN_3, SPAN_2, 3)):
        buf_3[p, 3:27, :] = plane
    third = taps([(W[t], buf_3[:, pl.ds(t, 16, stride=2), :]) for t in range(5)])
    third = dot_exact(as_rows(third), rest_3).reshape(SPAN_3, 16, 128)
    third = jnp.where(inside_mask(third.shape, SPAN_3, 9, where), third, 0.0)
    third_ref[...] = third
    for p, plane in enumerate(restrict_planes(lambda x: third[x], SPAN_4, SPAN_3, 3)):
        buf_4[p, 3:19, :] = plane
    last = taps([(W[t], buf_4[:, pl.ds(t, 8, stride=2), :]) for t in range(5)])
    last = dot_exact(as_rows(last), rest_4).reshape(SPAN_4, 8, 128)
    last = jnp.where(inside_mask(last.shape, SPAN_4, 5, where), last, 0.0)
    raw = taps([(1.0, roll(last[x], 8 * x)) for x in range(SPAN_4)])
    raw_out[...] = raw

    packed[...] = fine[...]
    packed[0:SPAN_2, 0:24, :] += roll(second, SEC)
    packed[0:SPAN_3, 0:16, :] += roll(third, THI)
    even, _, _ = nearest(index[1])
    low = pack_y(packed, (0, 0, 0))
    high = pack_y(packed, (30, 14, 6))
    for v in range(5):
        face[8 * v : 8 * v + 8, :] = jnp.where(even, high[v], low[v])
        face[40 + 8 * v : 48 + 8 * v, :] = jnp.where(even, low[v], high[v])
    face[80:88, :] = raw


def spot_1(p):
    return p // 16, p % 16 // 4 * 2, p % 4 * 32


def spot_2(p):
    return 2 + p // 14, p % 14 // 7 * 4, p % 7 * 18


def spot_3(p):
    return 4, 0, p * 11


LEVELS = ((32, 2, 0, 32, spot_1), (SPAN_2, 4, SEC, 18, spot_2), (SPAN_3, 5, THI, 11, spot_3))


def pack_y(source, at):
    tiles = [jnp.zeros((8, 128), F32) for _ in range(5)]
    row, at_lane = iota((8, 128), 0), iota((8, 128), 1)
    for (planes, count, lane, width, spot), start in zip(LEVELS, at):
        for p in range(planes):
            v, r, to = spot(p)
            if start == 30:
                slab = roll(source[p, 24:32, :], r - 6, 0)
            else:
                slab = roll(source[p, start : start + 8, :], r, 0)
            slab = roll(slab, to - lane)
            keep = (row >= r) & (row < r + count) & (at_lane >= to) & (at_lane < to + width)
            tiles[v] = jnp.where(keep, slab, tiles[v])
    return tiles


def place_y(tile, index):
    tall = jnp.concatenate([tile, jnp.zeros((8, 128), F32)], axis=0)
    tall = pltpu.roll(tall, lax.rem(4 * index + 15, 16), 0)
    return tall[0:8] + roll(tall[8:16], 64)


def relay_kernel(raw, got, out):
    index, _ = place()
    out[0:40, :] = got[40:80, :]
    partner = jnp.bitwise_xor(index[1], 1)
    out[40:48, :] = place_y(raw[...], index[1]) + place_y(got[80:88, :], partner)


def widen_y_kernel(packed, own, got_1, got_2, after, out, raw_out, face_1, face_3):
    index, _ = place()
    even, one, two = nearest(index[1])
    total = own[40:48, :] + got_2[40:48, :]
    raw_out[...] = total
    out[...] = jnp.zeros_like(out)
    out[:, 2:34, :] = packed[...]
    a, b = got_1[0:40, :], got_2[0:40, :]
    low = jnp.where(even, 0.0, a) + jnp.where(two, b, 0.0)
    high = jnp.where(even, a, 0.0) + jnp.where(one, b, 0.0)
    for face, at in ((low, (0, 0, 0)), (high, (34, 18, 10))):
        for (planes, count, lane, width, spot), start in zip(LEVELS, at):
            for p in range(planes):
                v, r, to = spot(p)
                slab = roll(roll(face[8 * v : 8 * v + 8], -r, 0), lane - to)
                slab = lanes_of(slab, lane, width)
                out[p, start : start + count, :] += slab[0:count]
    even, one, _ = nearest(index[0])
    for ref, to_high in ((face_1, even), (face_3, one)):
        f = jnp.where(to_high, 30, 0)
        s = jnp.where(to_high, 14, 0)
        t = jnp.where(to_high, 6, 0)
        ref[0:40, :] = lanes_of(out[f], 0, 32) + lanes_of(roll(out[f + 1], 32), 32, 32)
        ref[0:16, :] += taps(
            [(1.0, lanes_of(roll(out[t + k, 0:16, :], 11 * k), THI + 11 * k, 11)) for k in range(5)]
        )
        ref[40:64, :] = taps(
            [(1.0, lanes_of(roll(out[s + k, 0:24, :], 18 * k - SEC), 18 * k, 18)) for k in range(4)]
        )
        ref[64:72, :] = total


def widen_x_kernel(wide_y, own, got_1, got_3, got_2, after, out, raw_out, face_1, face_2):
    index, _ = place()
    even, one, two = nearest(index[0])
    total = None
    lane = iota((16, 128), 1)
    for step, tile in ((0, own[...]), (1, got_1[64:72, :]), (2, got_2[...]), (3, got_3[64:72, :])):
        tall = jnp.concatenate([tile, roll(tile, 64)], axis=0)
        tall = jnp.where(lane < 64, tall, 0.0)
        at = lax.rem(32 * jnp.bitwise_xor(index[0], step) + 120, 128)
        moved = pltpu.roll(tall, at, 1)
        total = moved if total is None else total + moved
    raw_out[...] = total
    a, b = got_1[...], got_3[...]
    low = jnp.where(even, 0.0, a) + jnp.where(two, b, 0.0)
    high = jnp.where(even, a, 0.0) + jnp.where(one, b, 0.0)
    out[0:2] = jnp.zeros((2, 40, 128), F32)
    out[34:36] = jnp.zeros((2, 40, 128), F32)
    out[2:34] = wide_y[...]
    for face, at in ((low, (0, 0, 0)), (high, (34, 18, 10))):
        for k in range(2):
            out[at[0] + k] += lanes_of(roll(face[0:40], -32 * k), 0, 32)
        for k in range(4):
            out[at[1] + k, 0:24, :] += lanes_of(roll(face[40:64], SEC - 18 * k), SEC, 18)
        for k in range(5):
            out[at[2] + k, 0:16, :] += lanes_of(roll(face[0:16], -11 * k), THI, 11)
    even, _, _ = nearest(index[2])
    for base, rows, planes, count, lane in ((0, 40, 36, 2, 0), (40, 24, 22, 4, SEC), (64, 16, 15, 5, THI)):
        at = {2: 30, 4: 14, 5: 6}[count]
        sums = [jnp.zeros((rows, 128), F32) for _ in range(2)]
        for x in range(planes):
            slab = out[x, 0:rows, :]
            for n, start in enumerate((lane, lane + at)):
                sums[n] = sums[n] + lanes_of(roll(slab, count * x - start), count * x, count)
        face_1[base : base + rows, :] = jnp.where(even, sums[1], sums[0])
        face_2[base : base + rows, :] = jnp.where(even, sums[0], sums[1])
    face_1[80:96, :] = total


def window_kernel(own, got_1, got_2, got_3, out):
    index, _ = place()
    pieces = (own[...], got_1[80:96, :], got_2[...], got_3[...])
    for group in range(4):
        total = None
        for step, piece in enumerate(pieces):
            apart = taps(
                [(1.0, lanes_of(roll(piece, 24 * q - 32 * group), 32 * q, 8)) for q in range(4)]
            )
            at = 4 * lax.rem(jnp.bitwise_xor(index[2], step), 4)
            moved = pltpu.roll(apart, at, 1)
            total = moved if total is None else total + moved
        out[group] = total


def divided(n, d):
    factor, bits = DIVIDE[d]
    return lax.shift_right_logical(n * factor, bits)


def build_bands(kernel, band):
    rows, columns, runs, group, outs = band
    row = iota((rows, 128), 0)
    shift = jnp.full((rows, 128), 99, jnp.int32)
    point = jnp.full((rows, 128), 99, jnp.int32)
    for start, count, offset in runs:
        at = row - start
        a = divided(at, count)
        inside = (at >= 0) & (at < 5 * count)
        shift = jnp.where(inside, a, shift)
        point = jnp.where(inside, offset + at - a * count, point)
    chosen = (shift == iota((rows, 128), 1)).astype(F32).astype(BF16)
    column = iota((8, columns), 1)
    block = divided(column, group)
    out_at = (column - block * group)[0:1]
    block = jnp.where((column - block * group) < outs, block, 9)
    sub = iota((8, columns), 0)
    entry = jnp.concatenate([point] * (columns // 128), axis=1) - out_at
    total_high = jnp.zeros((rows, columns), F32)
    total_low = jnp.zeros((rows, columns), F32)
    for c in range(5):
        source = jnp.zeros((8, columns), F32)
        for b in range(5):
            column_of = jnp.zeros((8, columns), F32)
            for a in range(5):
                column_of = jnp.where(sub == a, kernel[a, b, c], column_of)
            source = jnp.where(block == b, column_of, source)
        source = jnp.concatenate([source, jnp.zeros((120, columns), F32)], axis=0)
        high, low = split(source)
        fits = entry == c
        total_high = jnp.where(fits, dot(chosen, high), total_high)
        total_low = jnp.where(fits, dot(chosen, low), total_low)
    return total_high.astype(BF16), total_low.astype(BF16)


def bands_kernel(kernel_1, kernel_2, kernel_3, b1h, b1l, b2h, b2l, b3h, b3l):
    outs = ((b1h, b1l), (b2h, b2l), (b3h, b3l))
    for kernel, band, (high_ref, low_ref) in zip((kernel_1, kernel_2, kernel_3), BANDS, outs):
        high, low = build_bands(kernel, band)
        high_ref[...] = high
        low_ref[...] = low


def green_kernel(factors, green_high, green_low, rise, block_high, block_low):
    index, sizes = place()
    row, lane = iota((64, 128), 0), iota((64, 128), 1)
    delta_x = (lane // 8).astype(F32)
    delta_z = (4 * index[2] - 1 + lane % 8 - row).astype(F32)
    plain = delta_z * delta_z + (1.0 + delta_x * delta_x)
    for apart in range(18):
        high, low = split(0.0625 * lax.rsqrt(plain + float(apart * apart)))
        block_high[apart] = high
        block_low[apart] = low
    for ty in range(SPAN_4):
        columns = slice(128 * ty, 128 * ty + 128)
        for sy in range(16):
            apart = jnp.abs(4 * index[1] - 1 + ty - sy)
            first = sy % 8 * 128 + sy // 8 * 64
            green_high[first : first + 64, columns] = block_high[apart]
            green_low[first : first + 64, columns] = block_low[apart]
    variant = [
        jnp.where(index[d] == 0, 1, 0) + jnp.where(index[d] == sizes[d] - 1, 2, 0) for d in range(3)
    ]
    factor_x, factor_y = factors[variant[0]], factors[4 + variant[1]]
    kept = as_rows(factor_x[:, None, :] * factor_y[None, :, :])
    high, low = split(kept)
    rise[:, 0:128] = (high.astype(F32) + roll(low.astype(F32), 64)).astype(BF16)
    rise[:, 128:256] = high


def prolong_rows(source, target, count, whole):
    size = target.shape[1] // 2
    q0 = source[:, 0:size, :]
    q1 = source[:, 1 : size + 1, :]
    q2 = source[:, 2 : size + 2, :]
    even = 0.75 * q1 + 0.125 * (q0 + q2)
    odd = 0.5 * (q0 + q1) if whole else 0.5 * (q1 + q2)
    target[:, pl.ds(1 if whole else 0, size, stride=2), :] = even
    target[:, pl.ds(0 if whole else 1, size, stride=2), :] = odd


def prolong_plane(read, p, whole):
    half = p // 2
    if (p % 2 == 1) == whole:
        return 0.75 * read(half + 1) + 0.125 * (read(half) + read(half + 2))
    first = half if whole else half + 1
    return 0.5 * (read(first) + read(first + 1))


def near_kernel(
    wide, got_1, got_2, b1h, b1l, b2h, b2l, b3h, b3l, prol_2, prol_1,
    out,
    near_1, near_2, near_3, tall_3, tall_3y, tall_2, tall_2y,
):
    where = place()
    index, sizes = where
    even, _, _ = nearest(index[2])
    swapped, matched = got_1[0:80, :], got_2[...]
    low_msg = jnp.where(index[2] == 0, 0.0, jnp.where(even, matched, swapped))
    high_msg = jnp.where(index[2] == sizes[2] - 1, 0.0, jnp.where(even, swapped, matched))

    def halo(x, rows, base, count, low_at, high_at):
        low = roll(low_msg[base : base + rows], low_at - count * x)
        high = roll(high_msg[base : base + rows], high_at - count * x)
        return lanes_of(low, low_at, 5 * count) + lanes_of(high, high_at, 5 * count)

    planes = [lanes_of(wide[x, 0:16, :], THI, 11) for x in range(15)]
    left = []
    for x in range(SPAN_3):
        main = taps([(1.0, roll(planes[x + a], 11 * a - THI)) for a in range(5)])
        left.append(main + halo(x, 16, 64, 5, 64, 96))
    left = jnp.concatenate(left, axis=0)
    near_3[...] = jnp.zeros_like(near_3)
    near_3[:, 0:16, :] = dot_split(left, b3h[...], b3l[...]).reshape(SPAN_3, 16, 128)
    third = taps([(1.0, roll(near_3[:, b : b + 16, :], -16 * b)) for b in range(5)])
    third = jnp.where(inside_mask(third.shape, SPAN_3, 9, where), third, 0.0)
    tall_3[...] = jnp.zeros_like(tall_3)
    tall_3[:, 0:16, :] = dot_exact(as_rows(third), prol_2[...]).reshape(SPAN_3, 16, 128)
    prolong_rows(tall_3, tall_3y, SPAN_2, True)

    planes = [lanes_of(wide[x, 0:24, :], SEC, 18) for x in range(22)]
    left_a, left_b = [], []
    for x in range(SPAN_2):
        left_a.append(taps([(1.0, roll(planes[x + a], 18 * a - SEC)) for a in range(5)]))
        left_b.append(halo(x, 24, 40, 4, 0, 32))
    left = jnp.concatenate(
        [jnp.concatenate(left_a, axis=0), jnp.concatenate(left_b, axis=0)], axis=1
    )
    near_2[...] = jnp.zeros_like(near_2)
    near_2[:, 0:24, :] = dot_split(left, b2h[...], b2l[...]).reshape(SPAN_2, 24, 128)
    second = taps([(1.0, roll(near_2[:, b : b + 24, :], -24 * b)) for b in range(5)])
    raised = jnp.stack(
        [prolong_plane(lambda x: tall_3y[x], p, True) for p in range(SPAN_2)], axis=0
    )
    second = jnp.where(inside_mask(second.shape, SPAN_2, 17, where), second + raised, 0.0)
    tall_2[...] = jnp.zeros_like(tall_2)
    tall_2[:, 0:24, :] = dot_exact(as_rows(second), prol_1[...]).reshape(SPAN_2, 24, 128)
    prolong_rows(tall_2, tall_2y, 32, False)

    planes = [lanes_of(wide[x], 0, 32) for x in range(36)]
    left_a, left_b = [], []
    for x in range(32):
        left_a.append(taps([(1.0, roll(planes[x + a], 32 * a)) for a in range(4)]))
        left_b.append(planes[x + 4] + halo(x, 40, 0, 2, 32, 64))
    left = jnp.concatenate(
        [jnp.concatenate(left_a, axis=0), jnp.concatenate(left_b, axis=0)], axis=1
    )
    near_1[...] = dot_split(left, b1h[...], b1l[...]).reshape(32, 40, 256)
    for x in range(32):
        first = taps(
            [(1.0, roll(near_1[x, b : b + 32, 0:128], -32 * b)) for b in range(4)]
            + [(1.0, near_1[x, 4:36, 128:256])]
        )
        out[x] = first + prolong_plane(lambda q: tall_2y[q], x, False)


def top_kernel(
    base, piece_0, piece_1, piece_2, piece_3, green_high, green_low, rise, qz,
    out,
    fourth,
):
    index, sizes = place()
    lane = iota((8, 128), 1)
    sources = [lax.rem(16 * (jnp.bitwise_xor(index[2], 4 * s) // 4) + 127, 128) for s in range(4)]
    for x in range(16):
        total = None
        for piece, at in zip((piece_0, piece_1, piece_2, piece_3), sources):
            kept = lanes_of(piece[x // 4], 32 * (x % 4), 32)
            moved = pltpu.roll(kept, lax.rem(at + 128 - 32 * (x % 4), 128), 1)
            total = moved if total is None else total + moved
        total = total + roll(total, 64)
        fourth[x] = jnp.where(lane < 64, total[0:8], total[8:16])
    total = jnp.zeros((32, 128 * SPAN_4), F32)
    extra = jnp.zeros((16, 128 * SPAN_4), F32)
    for s in range(0, 8, 2):
        left = jnp.concatenate([fourth[:, s, :], fourth[:, s + 1, :]], axis=1)
        high, low = split(left)
        rows = slice(128 * s, 128 * s + 256)
        total = total + dot(jnp.concatenate([high, low], axis=0), green_high[rows, :])
        extra = extra + dot(high, green_low[rows, :])
    sums = total[0:16] + (total[16:32] + extra)
    row, lane = iota((16, 128), 0), iota((16, 128), 1)
    tops = []
    for tx in range(SPAN_4):
        keep = jnp.abs(4 * index[0] - 1 + tx - row) == lane // 8
        for ty in range(SPAN_4):
            picked = jnp.where(keep, sums[:, 128 * ty : 128 * ty + 128], 0.0)
            tops.append(jnp.sum(picked, axis=0, keepdims=True))
        tops.append(jnp.zeros((1, 128), F32))
    tops = jnp.concatenate(tops + [jnp.zeros((8, 128), F32)], axis=0)
    variant = jnp.where(index[2] == 0, 1, 0) + jnp.where(index[2] == sizes[2] - 1, 2, 0)
    high, low = split(dot_split(tops, qz[variant], qz[4 + variant]))
    right = jnp.concatenate([high, high, low, jnp.zeros_like(low)], axis=0)
    far = dot(rise[...], right)
    out[...] = (base[...] + far.reshape(32, 32, 128))[:, :, 0:32]


def call(kernel, outs, ins, scratch=(), megabytes=16, flops=1000000, spaces=None):
    spaces = spaces or {}
    return pl.pallas_call(
        kernel,
        out_shape=outs,
        in_specs=[spaces.get(i, VMEM) for i in range(len(ins))],
        out_specs=jax.tree.map(lambda _: VMEM, outs),
        scratch_shapes=list(scratch),
        compiler_params=pltpu.CompilerParams(vmem_limit_bytes=megabytes * 2**20),
        cost_estimate=pl.CostEstimate(flops=flops, bytes_accessed=2**21, transcendentals=0),
    )(*ins)


def shape(*dims, dtype=F32):
    return jax.ShapeDtypeStruct(dims, dtype)


def exchange(values, axis, steps):
    size = lax.axis_size(axis)
    return [
        lax.ppermute(value, axis, [(i, i ^ step) for i in range(size)])
        for value, step in zip(values, steps)
    ]


def match(value, axis):
    size = lax.axis_size(axis)
    pairs = [(0, 0), (size - 1, size - 1)]
    for i in range(1, size - 1, 2):
        pairs += [(i, i + 1), (i + 1, i)]
    return lax.ppermute(value, axis, pairs)


ANY = pl.BlockSpec(memory_space=pl.ANY)


def shards(charges, counts, slots, spline, kernel_fine, kernel_mid, kernel_coarse):
    cells = charges.shape[0]
    packed, raw, face = call(
        deposit_kernel,
        (shape(32, 32, 128), shape(8, 128), shape(88, 128)),
        (256 * slots + counts, charges, spline.reshape(cells * 12, ATOMS)),
        (
            pltpu.VMEM((cells, ATOMS), F32),
            pltpu.VMEM((cells * 12, 128), BF16),
            pltpu.VMEM((cells * 12, 128), F32),
            pltpu.VMEM((64, cells), F32),
            pltpu.VMEM((32, 32, 128), F32),
            pltpu.VMEM((SPAN_2, 56, 128), F32),
            pltpu.VMEM((SPAN_3, 40, 128), F32),
            pltpu.VMEM((SPAN_4, 24, 128), F32),
            pltpu.VMEM((SPAN_2, 24, 128), F32),
            pltpu.VMEM((SPAN_3, 16, 128), F32),
            pltpu.SemaphoreType.DMA((4,)),
        ),
        spaces={1: HBM, 2: HBM},
        megabytes=53,
    )
    (got_1,) = exchange((face,), "gy", (1,))
    relay = call(relay_kernel, shape(48, 128), (raw, got_1))
    (got_2,) = exchange((relay,), "gy", (2,))
    qx, qy, qz = composites()
    qz_high = qz.astype(BF16)
    qz_low = (qz - qz_high.astype(np.float32)).astype(BF16)
    green_high, green_low, rise = call(
        green_kernel,
        (
            shape(1024, 128 * SPAN_4, dtype=BF16),
            shape(1024, 128 * SPAN_4, dtype=BF16),
            shape(1024, 256, dtype=BF16),
        ),
        (jnp.asarray(np.concatenate([qx, qy])),),
        (pltpu.VMEM((18, 64, 128), BF16), pltpu.VMEM((18, 64, 128), BF16)),
    )
    wide_y, raw, face_1, face_3 = call(
        widen_y_kernel,
        (shape(32, 40, 128), shape(8, 128), shape(72, 128), shape(72, 128)),
        (packed, relay, got_1, got_2, rise),
        spaces={4: ANY},
    )
    got_1, got_3, got_2 = exchange((face_1, face_3, raw), "gx", (1, 3, 2))
    bands = call(
        bands_kernel,
        tuple(shape(band[0], band[1], dtype=BF16) for band in BANDS for _ in range(2)),
        (kernel_fine, kernel_mid, kernel_coarse),
        spaces={0: SMEM, 1: SMEM, 2: SMEM},
    )
    wide_x, raw, face_1, face_2 = call(
        widen_x_kernel,
        (shape(36, 40, 128), shape(16, 128), shape(96, 128), shape(80, 128)),
        (wide_y, raw, got_1, got_3, got_2, bands[0]),
        spaces={5: ANY},
    )
    got_1, got_3, got_2 = exchange((face_1, raw, raw), "gz", (1, 3, 2))
    matched = match(face_2, "gz")
    window = call(window_kernel, shape(4, 16, 128), (raw, got_1, got_2, got_3))
    pieces = [window] + exchange((window, window, window), "gz", (4, 8, 12))
    base = call(
        near_kernel,
        shape(32, 32, 128),
        (wide_x, got_1, matched, *bands, jnp.asarray(PROL_2, BF16), jnp.asarray(PROL_1, BF16)),
        (
            pltpu.VMEM((32, 40, 256), F32),
            pltpu.VMEM((SPAN_2, 32, 128), F32),
            pltpu.VMEM((SPAN_3, 24, 128), F32),
            pltpu.VMEM((SPAN_3, 24, 128), F32),
            pltpu.VMEM((SPAN_3, 24, 128), F32),
            pltpu.VMEM((SPAN_2, 32, 128), F32),
            pltpu.VMEM((SPAN_2, 32, 128), F32),
        ),
    )
    return call(
        top_kernel,
        shape(32, 32, 32),
        (base, *pieces, green_high, green_low, rise, jnp.asarray(np.concatenate([qz_high, qz_low]))),
        (pltpu.VMEM((16, 8, 128), F32),),
    )


def solution(mesh):
    return jax.shard_map(
        shards,
        mesh=mesh,
        in_specs=(
            P(("gx", "gy", "gz"), None),
            P(("gx", "gy", "gz")),
            P(("gx", "gy", "gz")),
            P(("gx", "gy", "gz"), None, None, None),
            P(),
            P(),
            P(),
        ),
        out_specs=P("gx", "gy", "gz"),
        check_vma=False,
    )
```

time: 63.1 us -> 48.6 us (0.77)
  the two profiles are of different devices: /device:TPU:39 before, /device:TPU:32 now
where the time goes in v2:
time: 48.6 us; the launch traced here: 48.3 us
  starting transfers between devices  22.8 us (47%)
  Pallas kernels  14.6 us (30%)
  waiting for transfers between devices  8.21 us (17%)
  local copies, waits for them, and re-layouts  1.86 us (4%)
  other arithmetic  0.7 us (1%)
    ppermute x11, starting transfers between devices, exchange(): lax.ppermute(value, axis, [(i, i ^ step) for i in range(size)])  18.3 us
    pallas_call x9, Pallas kernels, call(): pl.pallas_call(kernel, out_shape=outs, in_specs=[spaces.get(i, VMEM) for...  14.6 us
    ppermute x11, waiting for transfers between devices, exchange(): lax.ppermute(value, axis, [(i, i ^ step) for i in range(size)])  8.21 us
    ppermute x1, starting transfers between devices, match(): return lax.ppermute(value, axis, pairs)  4.52 us
    unnamed x16, local copies, waits for them, and re-layouts  1.86 us
  transfers between devices with their start and end apart: 12, of which 6 were waited for; matrix products, arithmetic and copies ran while one was open for 0% of the time, Pallas kernels for 13%

profile of v2, /device:TPU:32, one launch (start us, length us, event | category | flops | bytes accessed | tf_op | source)
XLA Modules:
  0.0 48.3 jit_solution(11000355822578960593)
XLA Ops:
  0.0 0.7 %multiply_add_fusion.codes = s32[384]{0:T(512)S(1)} fusion(s32[384]{0:T(512)} %param.12, s32[384]{0:T(512)} %param.13), kind=kLoop, calls=%fused_computation | loop fusion | flops 768 | bytes 4608 | tf_op jit(solution)/shard_map/add | solution.py:632
  0.7 0.9 %copy-done.1 = f32[384,128]{1,0:T(8,128)S(1)} copy-done((f32[384,128]{1,0:T(8,128)S(1)}, f32[384,128]{1,0:T(8,128)}, u32[]{:S(2)}) %copy-start.1) | copy-done | bytes 196632
  1.6 0.0 copy-start.4
  1.7 4.7 %shard_map.109 = (f32[32,32,128]{2,1,0:T(8,128)S(1)}, f32[8,128]{1,0:T(8,128)S(1)}, f32[88,128]{1,0:T(8,128)S(1)}) custom-call(s32[384]{0:T(512)S(1)} %multiply_add_fusion.codes, f32[384,128]{1,0:T(8,128)S(1)} %copy-done.1, bf16[4608,128]{1,0:T(8,128)(2,1)} %bitcast.1), custom_call_target="tpu_custom_call" | custom-call | flops 1000000 | bytes 2097152 | tf_op jit(solution)/shard_map/pallas_call | solution.py:593
  6.3 0.1 collective-permute-start
  6.4 1.2 %collective-permute-done.got.got_1 = f32[88,128]{1,0:T(8,128)S(1)} collective-permute-done((f32[88,128]{1,0:T(8,128)S(1)}, f32[88,128]{1,0:T(8,128)S(1)}, u32[]{:S(2)}, u32[]{:S(2)}) %collective-permute-start) | collective-permute-done | bytes 45088 | tf_op jit(solution)/shard_map/ppermute | solution.py:611
  7.6 0.1 shard_map.110.own
  7.7 6.3 %collective-permute-start.1 = (f32[48,128]{1,0:T(8,128)S(1)}, f32[48,128]{1,0:T(8,128)S(1)}, u32[]{:S(2)}, u32[]{:S(2)}) collective-permute-start(f32[48,128]{1,0:T(8,128)S(1)} %shard_map.110.own), channel_id=1, source_target_pairs={{0,32},{16,48},{32,0},{48,16},{1,33},{17,49},{33,1},{49,17},{2,34}... | collective-permute-start | bytes 73736 | tf_op jit(solution)/shard_map/ppermute | solution.py:611
  14.0 0.9 %copy-done.2 = f32[8,32,128]{2,1,0:T(8,128)S(1)} copy-done((f32[8,32,128]{2,1,0:T(8,128)S(1)}, f32[8,32,128]{2,1,0:T(8,128)}, u32[]{:S(2)}) %copy-start.2) | copy-done | bytes 131096
  14.9 1.0 %shard_map.111 = (bf16[1024,896]{1,0:T(8,128)(2,1)S(1)}, bf16[1024,896]{1,0:T(8,128)(2,1)S(1)}, bf16[1024,256]{1,0:T(8,128)(2,1)S(1)}) custom-call(f32[8,32,128]{2,1,0:T(8,128)S(1)} %copy-done.2), custom_call_target="tpu_custom_call" | custom-call | flops 1000000 | bytes 2097152 | tf_op jit(solution)/shard_map/pallas_call | solution.py:593
  15.9 0.0 copy-start
  15.9 0.3 shard_map.112
  16.3 1.6 %collective-permute-start.2 = (f32[72,128]{1,0:T(8,128)S(1)}, f32[72,128]{1,0:T(8,128)S(1)}, u32[]{:S(2)}, u32[]{:S(2)}) collective-permute-start(f32[72,128]{1,0:T(8,128)S(1)} %get-tuple-element.31), channel_id=1, source_target_pairs={{0,64},{64,0},{128,192},{192,128},{1,65},{65,1},{129,193},{193,129... | collective-permute-start | bytes 110600 | tf_op jit(solution)/shard_map/ppermute | solution.py:611
  17.8 2.1 %collective-permute-start.3 = (f32[72,128]{1,0:T(8,128)S(1)}, f32[72,128]{1,0:T(8,128)S(1)}, u32[]{:S(2)}, u32[]{:S(2)}) collective-permute-start(f32[72,128]{1,0:T(8,128)S(1)} %get-tuple-element.32), channel_id=1, source_target_pairs={{0,192},{64,128},{128,64},{192,0},{1,193},{65,129},{129,65},{193,1... | collective-permute-start | bytes 110600 | tf_op jit(solution)/shard_map/ppermute | solution.py:611
  19.9 0.6 %collective-permute-start.4 = (f32[8,128]{1,0:T(8,128)S(1)}, f32[8,128]{1,0:T(8,128)S(1)}, u32[]{:S(2)}, u32[]{:S(2)}) collective-permute-start(f32[8,128]{1,0:T(8,128)S(1)} %get-tuple-element.30.own), channel_id=1, source_target_pairs={{0,128},{64,192},{128,0},{192,64},{1,129},{65,193},{129,1},{193,65... | collective-permute-start | bytes 12296 | tf_op jit(solution)/shard_map/ppermute | solution.py:611
  20.6 2.3 %shard_map.113 = (bf16[256,256]{1,0:T(8,128)(2,1)S(1)}, bf16[256,256]{1,0:T(8,128)(2,1)S(1)}, bf16[256,128]{1,0:T(8,128)(2,1)S(1)}, bf16[256,128]{1,0:T(8,128)(2...) custom-call(f32[5,5,5]{2,1,0:T(8,128)S(1)} %copy-done.5, f32[5,5,5]{2,1,0:T(8,128)S(1)} %copy-done.6, ...), custom_call_target="tpu_custom_call" | custom-call | flops 1000000 | bytes 2097152 | tf_op jit(solution)/shard_map/pallas_call | solution.py:593
  22.9 2.1 %collective-permute-done.4.got_2 = f32[8,128]{1,0:T(8,128)S(1)} collective-permute-done((f32[8,128]{1,0:T(8,128)S(1)}, f32[8,128]{1,0:T(8,128)S(1)}, u32[]{:S(2)}, u32[]{:S(2)}) %collective-permute-start.4) | collective-permute-done | bytes 4128 | tf_op jit(solution)/shard_map/ppermute | solution.py:611
  25.1 0.7 %shard_map.114 = (f32[36,40,128]{2,1,0:T(8,128)S(1)}, f32[16,128]{1,0:T(8,128)S(1)}, f32[96,128]{1,0:T(8,128)S(1)}, f32[80,128]{1,0:T(8,128)S(1)}) custom-call(f32[32,40,128]{2,1,0:T(8,128)S(1)} %get-tuple-element.29.wide_y, f32[8,128]{1,0:T(8,128)S(1)} %get-tuple-element.30.own, f32[72,128]{1,0:T(8,128)S(1)} %collective-permute-done.2.got_1, ...), custom_call_target="tpu_custom_call" | custom-call | flops 1000000 | bytes 2097152 | tf_op jit(solution)/shard_map/pallas_call | solution.py:593
  25.8 1.7 %collective-permute-start.5 = (f32[96,128]{1,0:T(8,128)S(1)}, f32[96,128]{1,0:T(8,128)S(1)}, u32[]{:S(2)}, u32[]{:S(2)}) collective-permute-start(f32[96,128]{1,0:T(8,128)S(1)} %get-tuple-element.35), channel_id=1, source_target_pairs={{0,1},{1,0},{2,3},{3,2},{4,5},{5,4},{6,7},{7,6},{8,9},{9,8},{10,11... | collective-permute-start | bytes 147464 | tf_op jit(solution)/shard_map/ppermute | solution.py:611
  27.5 4.5 %collective-permute-start.6 = (f32[80,128]{1,0:T(8,128)S(1)}, f32[80,128]{1,0:T(8,128)S(1)}, u32[]{:S(2)}, u32[]{:S(2)}) collective-permute-start(f32[80,128]{1,0:T(8,128)S(1)} %get-tuple-element.36), channel_id=1, source_target_pairs={{0,0},{15,15},{1,2},{2,1},{3,4},{4,3},{5,6},{6,5},{7,8},{8,7},{9,1... | collective-permute-start | bytes 122888 | tf_op jit(solution)/shard_map/ppermute | solution.py:621
  32.0 1.7 %collective-permute-start.8 = (f32[16,128]{1,0:T(8,128)S(1)}, f32[16,128]{1,0:T(8,128)S(1)}, u32[]{:S(2)}, u32[]{:S(2)}) collective-permute-start(f32[16,128]{1,0:T(8,128)S(1)} %get-tuple-element.42.own), channel_id=1, source_target_pairs={{0,3},{1,2},{2,1},{3,0},{4,7},{5,6},{6,5},{7,4},{8,11},{9,10},{10,... | collective-permute-start | bytes 24584 | tf_op jit(solution)/shard_map/ppermute | solution.py:611
  33.7 0.7 %collective-permute-start.7 = (f32[16,128]{1,0:T(8,128)S(1)}, f32[16,128]{1,0:T(8,128)S(1)}, u32[]{:S(2)}, u32[]{:S(2)}) collective-permute-start(f32[16,128]{1,0:T(8,128)S(1)} %get-tuple-element.42.own), channel_id=1, source_target_pairs={{0,2},{1,3},{2,0},{3,1},{4,6},{5,7},{6,4},{7,5},{8,10},{9,11},{10,... | collective-permute-start | bytes 24584 | tf_op jit(solution)/shard_map/ppermute | solution.py:611
  34.4 2.6 %collective-permute-done.8.got_3 = f32[16,128]{1,0:T(8,128)S(1)} collective-permute-done((f32[16,128]{1,0:T(8,128)S(1)}, f32[16,128]{1,0:T(8,128)S(1)}, u32[]{:S(2)}, u32[]{:S(2)}) %collective-permute-start.8) | collective-permute-done | bytes 8224 | tf_op jit(solution)/shard_map/ppermute | solution.py:611
  36.9 1.9 %collective-permute-done.7.got_2 = f32[16,128]{1,0:T(8,128)S(1)} collective-permute-done((f32[16,128]{1,0:T(8,128)S(1)}, f32[16,128]{1,0:T(8,128)S(1)}, u32[]{:S(2)}, u32[]{:S(2)}) %collective-permute-start.7) | collective-permute-done | bytes 8224 | tf_op jit(solution)/shard_map/ppermute | solution.py:611
  38.9 0.4 shard_map.116.piece_0
  39.3 1.9 %collective-permute-start.11 = (f32[4,16,128]{2,1,0:T(8,128)S(1)}, f32[4,16,128]{2,1,0:T(8,128)S(1)}, u32[]{:S(2)}, u32[]{:S(2)}) collective-permute-start(f32[4,16,128]{2,1,0:T(8,128)S(1)} %shard_map.116.piece_0), channel_id=1, source_target_pairs={{0,12},{1,13},{2,14},{3,15},{4,8},{5,9},{6,10},{7,11},{8,4},{9,5},... | collective-permute-start | bytes 98312 | tf_op jit(solution)/shard_map/ppermute | solution.py:611
  41.1 1.0 %collective-permute-start.10 = (f32[4,16,128]{2,1,0:T(8,128)S(1)}, f32[4,16,128]{2,1,0:T(8,128)S(1)}, u32[]{:S(2)}, u32[]{:S(2)}) collective-permute-start(f32[4,16,128]{2,1,0:T(8,128)S(1)} %shard_map.116.piece_0), channel_id=1, source_target_pairs={{0,8},{1,9},{2,10},{3,11},{4,12},{5,13},{6,14},{7,15},{8,0},{9,1},... | collective-permute-start | bytes 98312 | tf_op jit(solution)/shard_map/ppermute | solution.py:611
  42.1 0.7 %collective-permute-start.9 = (f32[4,16,128]{2,1,0:T(8,128)S(1)}, f32[4,16,128]{2,1,0:T(8,128)S(1)}, u32[]{:S(2)}, u32[]{:S(2)}) collective-permute-start(f32[4,16,128]{2,1,0:T(8,128)S(1)} %shard_map.116.piece_0), channel_id=1, source_target_pairs={{0,4},{1,5},{2,6},{3,7},{4,0},{5,1},{6,2},{7,3},{8,12},{9,13},{10,... | collective-permute-start | bytes 98312 | tf_op jit(solution)/shard_map/ppermute | solution.py:611
  42.8 2.8 %shard_map.115.base = f32[32,32,128]{2,1,0:T(8,128)S(1)} custom-call(f32[36,40,128]{2,1,0:T(8,128)S(1)} %get-tuple-element.34.wide, f32[96,128]{1,0:T(8,128)S(1)} %collective-permute-done.5.got_1, f32[80,128]{1,0:T(8,128)S(1)} %collective-permute-done.6.got_2, bf16[256,256]{1,0:T(8,128)(2,1)S(1)} %get-tuple-element.33.after.b1h, ...), custom_call_target="tpu_custom_call" | custom-call | flops 1000000 | bytes 2097152 | tf_op jit(solution)/shard_map/pallas_call | solution.py:593
  45.7 0.3 collective-permute-done.10.piece_2
  45.9 0.1 collective-permute-done.9.piece_1
  46.0 2.3 %shard_map.117 = f32[32,32,32]{2,1,0:T(8,128)} custom-call(f32[32,32,128]{2,1,0:T(8,128)S(1)} %shard_map.115.base, f32[4,16,128]{2,1,0:T(8,128)S(1)} %shard_map.116.piece_0, f32[4,16,128]{2,1,0:T(8,128)S(1)} %collective-permute-done.9.piece_1, f32[4,16,128]{2,1,0:T(8,128)S(1)} %collective-permute-done.10.piece_2, ...), custom_call_target="tpu_custom_call" | custom-call | flops 1000000 | bytes 2097152 | tf_op jit(solution)/shard_map/pallas_call | solution.py:593
  (18 shorter events, 0.0 us)
Async XLA Ops:
  0.7 0.9 %copy-start.1 = (f32[384,128]{1,0:T(8,128)S(1)}, f32[384,128]{1,0:T(8,128)}, u32[]{:S(2)}) copy-start(f32[384,128]{1,0:T(8,128)} %charges_hbm.1) | copy-start | bytes 589828
  1.6 18.9 %copy-start.5 = (f32[5,5,5]{2,1,0:T(8,128)S(1)}, f32[5,5,5]{2,1,0:T(8,128)}, u32[]{:S(2)}) copy-start(f32[5,5,5]{2,1,0:T(8,128)} %kernel_1.1) | copy-start | bytes 1504
  1.6 18.9 %copy-start.6 = (f32[5,5,5]{2,1,0:T(8,128)S(1)}, f32[5,5,5]{2,1,0:T(8,128)}, u32[]{:S(2)}) copy-start(f32[5,5,5]{2,1,0:T(8,128)} %kernel_2.1) | copy-start | bytes 1504
  1.6 18.9 %copy-start.7 = (f32[5,5,5]{2,1,0:T(8,128)S(1)}, f32[5,5,5]{2,1,0:T(8,128)}, u32[]{:S(2)}) copy-start(f32[5,5,5]{2,1,0:T(8,128)} %kernel_3.1) | copy-start | bytes 1504
  1.6 41.2 %copy-start.3 = (bf16[128,128]{1,0:T(8,128)(2,1)S(1)}, bf16[128,128]{1,0:T(8,128)(2,1)}, u32[]{:S(2)}) copy-start(bf16[128,128]{1,0:T(8,128)(2,1)} %constant.12.clone.prol_1) | copy-start | bytes 98308
  1.6 41.2 %copy-start.4 = (bf16[128,128]{1,0:T(8,128)(2,1)S(1)}, bf16[128,128]{1,0:T(8,128)(2,1)}, u32[]{:S(2)}) copy-start(bf16[128,128]{1,0:T(8,128)(2,1)} %constant.11.clone.prol_2) | copy-start | bytes 98308
  6.3 1.3 %collective-permute-start = (f32[88,128]{1,0:T(8,128)S(1)}, f32[88,128]{1,0:T(8,128)S(1)}, u32[]{:S(2)}, u32[]{:S(2)}) collective-permute-start(f32[88,128]{1,0:T(8,128)S(1)} %get-tuple-element.27), channel_id=1, source_target_pairs={{0,16},{16,0},{32,48},{48,32},{1,17},{17,1},{33,49},{49,33},{2,18}... | collective-permute-start | bytes 135176 | tf_op jit(solution)/shard_map/ppermute | solution.py:611
  7.7 8.2 %collective-permute-start.1 = (f32[48,128]{1,0:T(8,128)S(1)}, f32[48,128]{1,0:T(8,128)S(1)}, u32[]{:S(2)}, u32[]{:S(2)}) collective-permute-start(f32[48,128]{1,0:T(8,128)S(1)} %shard_map.110.own), channel_id=1, source_target_pairs={{0,32},{16,48},{32,0},{48,16},{1,33},{17,49},{33,1},{49,17},{2,34}... | collective-permute-start | bytes 73736 | tf_op jit(solution)/shard_map/ppermute | solution.py:611
  14.0 0.9 %copy-start.2 = (f32[8,32,128]{2,1,0:T(8,128)S(1)}, f32[8,32,128]{2,1,0:T(8,128)}, u32[]{:S(2)}) copy-start(f32[8,32,128]{2,1,0:T(8,128)} %constant.10.clone.factors) | copy-start | bytes 393220
  15.9 30.1 %copy-start = (bf16[8,128,128]{2,1,0:T(8,128)(2,1)S(1)}, bf16[8,128,128]{2,1,0:T(8,128)(2,1)}, u32[]{:S(2)}) copy-start(bf16[8,128,128]{2,1,0:T(8,128)(2,1)} %constant.13.clone.qz) | copy-start | bytes 786436
  16.3 8.8 %collective-permute-start.2 = (f32[72,128]{1,0:T(8,128)S(1)}, f32[72,128]{1,0:T(8,128)S(1)}, u32[]{:S(2)}, u32[]{:S(2)}) collective-permute-start(f32[72,128]{1,0:T(8,128)S(1)} %get-tuple-element.31), channel_id=1, source_target_pairs={{0,64},{64,0},{128,192},{192,128},{1,65},{65,1},{129,193},{193,129... | collective-permute-start | bytes 110600 | tf_op jit(solution)/shard_map/ppermute | solution.py:611
  17.8 7.2 %collective-permute-start.3 = (f32[72,128]{1,0:T(8,128)S(1)}, f32[72,128]{1,0:T(8,128)S(1)}, u32[]{:S(2)}, u32[]{:S(2)}) collective-permute-start(f32[72,128]{1,0:T(8,128)S(1)} %get-tuple-element.32), channel_id=1, source_target_pairs={{0,192},{64,128},{128,64},{192,0},{1,193},{65,129},{129,65},{193,1... | collective-permute-start | bytes 110600 | tf_op jit(solution)/shard_map/ppermute | solution.py:611
  19.9 5.1 %collective-permute-start.4 = (f32[8,128]{1,0:T(8,128)S(1)}, f32[8,128]{1,0:T(8,128)S(1)}, u32[]{:S(2)}, u32[]{:S(2)}) collective-permute-start(f32[8,128]{1,0:T(8,128)S(1)} %get-tuple-element.30.own), channel_id=1, source_target_pairs={{0,128},{64,192},{128,0},{192,64},{1,129},{65,193},{129,1},{193,65... | collective-permute-start | bytes 12296 | tf_op jit(solution)/shard_map/ppermute | solution.py:611
  25.8 13.1 %collective-permute-start.5 = (f32[96,128]{1,0:T(8,128)S(1)}, f32[96,128]{1,0:T(8,128)S(1)}, u32[]{:S(2)}, u32[]{:S(2)}) collective-permute-start(f32[96,128]{1,0:T(8,128)S(1)} %get-tuple-element.35), channel_id=1, source_target_pairs={{0,1},{1,0},{2,3},{3,2},{4,5},{5,4},{6,7},{7,6},{8,9},{9,8},{10,11... | collective-permute-start | bytes 147464 | tf_op jit(solution)/shard_map/ppermute | solution.py:611
  27.5 15.3 %collective-permute-start.6 = (f32[80,128]{1,0:T(8,128)S(1)}, f32[80,128]{1,0:T(8,128)S(1)}, u32[]{:S(2)}, u32[]{:S(2)}) collective-permute-start(f32[80,128]{1,0:T(8,128)S(1)} %get-tuple-element.36), channel_id=1, source_target_pairs={{0,0},{15,15},{1,2},{2,1},{3,4},{4,3},{5,6},{6,5},{7,8},{8,7},{9,1... | collective-permute-start | bytes 122888 | tf_op jit(solution)/shard_map/ppermute | solution.py:621
  32.0 4.9 %collective-permute-start.8 = (f32[16,128]{1,0:T(8,128)S(1)}, f32[16,128]{1,0:T(8,128)S(1)}, u32[]{:S(2)}, u32[]{:S(2)}) collective-permute-start(f32[16,128]{1,0:T(8,128)S(1)} %get-tuple-element.42.own), channel_id=1, source_target_pairs={{0,3},{1,2},{2,1},{3,0},{4,7},{5,6},{6,5},{7,4},{8,11},{9,10},{10,... | collective-permute-start | bytes 24584 | tf_op jit(solution)/shard_map/ppermute | solution.py:611
  33.7 5.2 %collective-permute-start.7 = (f32[16,128]{1,0:T(8,128)S(1)}, f32[16,128]{1,0:T(8,128)S(1)}, u32[]{:S(2)}, u32[]{:S(2)}) collective-permute-start(f32[16,128]{1,0:T(8,128)S(1)} %get-tuple-element.42.own), channel_id=1, source_target_pairs={{0,2},{1,3},{2,0},{3,1},{4,6},{5,7},{6,4},{7,5},{8,10},{9,11},{10,... | collective-permute-start | bytes 24584 | tf_op jit(solution)/shard_map/ppermute | solution.py:611
  39.3 6.4 %collective-permute-start.11 = (f32[4,16,128]{2,1,0:T(8,128)S(1)}, f32[4,16,128]{2,1,0:T(8,128)S(1)}, u32[]{:S(2)}, u32[]{:S(2)}) collective-permute-start(f32[4,16,128]{2,1,0:T(8,128)S(1)} %shard_map.116.piece_0), channel_id=1, source_target_pairs={{0,12},{1,13},{2,14},{3,15},{4,8},{5,9},{6,10},{7,11},{8,4},{9,5},... | collective-permute-start | bytes 98312 | tf_op jit(solution)/shard_map/ppermute | solution.py:611
  41.1 4.8 %collective-permute-start.10 = (f32[4,16,128]{2,1,0:T(8,128)S(1)}, f32[4,16,128]{2,1,0:T(8,128)S(1)}, u32[]{:S(2)}, u32[]{:S(2)}) collective-permute-start(f32[4,16,128]{2,1,0:T(8,128)S(1)} %shard_map.116.piece_0), channel_id=1, source_target_pairs={{0,8},{1,9},{2,10},{3,11},{4,12},{5,13},{6,14},{7,15},{8,0},{9,1},... | collective-permute-start | bytes 98312 | tf_op jit(solution)/shard_map/ppermute | solution.py:611
  42.1 3.9 %collective-permute-start.9 = (f32[4,16,128]{2,1,0:T(8,128)S(1)}, f32[4,16,128]{2,1,0:T(8,128)S(1)}, u32[]{:S(2)}, u32[]{:S(2)}) collective-permute-start(f32[4,16,128]{2,1,0:T(8,128)S(1)} %shard_map.116.piece_0), channel_id=1, source_target_pairs={{0,4},{1,5},{2,6},{3,7},{4,0},{5,1},{6,2},{7,3},{8,12},{9,13},{10,... | collective-permute-start | bytes 98312 | tf_op jit(solution)/shard_map/ppermute | solution.py:611

commit v3 on v2

--- a/solution.py
+++ b/solution.py
@@ -333,7 +333,7 @@
         ref[64:72, :] = total
 
 
-def widen_x_kernel(wide_y, own, got_1, got_3, got_2, after, out, raw_out, face_1, face_2):
+def widen_x_kernel(wide_y, own, got_1, got_3, got_2, after, out, raw_out, to_high, to_low):
     index, _ = place()
     even, one, two = nearest(index[0])
     total = None
@@ -358,22 +358,30 @@
             out[at[1] + k, 0:24, :] += lanes_of(roll(face[40:64], SEC - 18 * k), SEC, 18)
         for k in range(5):
             out[at[2] + k, 0:16, :] += lanes_of(roll(face[0:16], -11 * k), THI, 11)
+    for ref, high in ((to_high, True), (to_low, False)):
+        pack_z(out, ref, high)
+        ref[80:96, :] = total
+
+
+def pack_z(source, face, to_high):
+    for base, rows, planes, count, lane, high in (
+        (0, 40, 36, 2, 0, 30),
+        (40, 24, 22, 4, SEC, 14),
+        (64, 16, 15, 5, THI, 6),
+    ):
+        first = lane + high if to_high else lane
+        total = jnp.zeros((rows, 128), F32)
+        for x in range(planes):
+            kept = roll(source[x, 0:rows, :], count * x - first)
+            total = total + lanes_of(kept, count * x, count)
+        face[base : base + rows, :] = total
+
+
+def window_kernel(own, from_low, from_high, got_2, got_3, out):
+    index, _ = place()
     even, _, _ = nearest(index[2])
-    for base, rows, planes, count, lane in ((0, 40, 36, 2, 0), (40, 24, 22, 4, SEC), (64, 16, 15, 5, THI)):
-        at = {2: 30, 4: 14, 5: 6}[count]
-        sums = [jnp.zeros((rows, 128), F32) for _ in range(2)]
-        for x in range(planes):
-            slab = out[x, 0:rows, :]
-            for n, start in enumerate((lane, lane + at)):
-                sums[n] = sums[n] + lanes_of(roll(slab, count * x - start), count * x, count)
-        face_1[base : base + rows, :] = jnp.where(even, sums[1], sums[0])
-        face_2[base : base + rows, :] = jnp.where(even, sums[0], sums[1])
-    face_1[80:96, :] = total
-
-
-def window_kernel(own, got_1, got_2, got_3, out):
-    index, _ = place()
-    pieces = (own[...], got_1[80:96, :], got_2[...], got_3[...])
+    next_one = jnp.where(even, from_high[80:96, :], from_low[80:96, :])
+    pieces = (own[...], next_one, got_2[...], got_3[...])
     for group in range(4):
         total = None
         for step, piece in enumerate(pieces):
@@ -481,16 +489,14 @@
 
 
 def near_kernel(
-    wide, got_1, got_2, b1h, b1l, b2h, b2l, b3h, b3l, prol_2, prol_1,
+    wide, from_low, from_high, b1h, b1l, b2h, b2l, b3h, b3l, prol_2, prol_1,
     out,
     near_1, near_2, near_3, tall_3, tall_3y, tall_2, tall_2y,
 ):
     where = place()
     index, sizes = where
-    even, _, _ = nearest(index[2])
-    swapped, matched = got_1[0:80, :], got_2[...]
-    low_msg = jnp.where(index[2] == 0, 0.0, jnp.where(even, matched, swapped))
-    high_msg = jnp.where(index[2] == sizes[2] - 1, 0.0, jnp.where(even, swapped, matched))
+    low_msg = jnp.where(index[2] == 0, 0.0, from_low[...])
+    high_msg = jnp.where(index[2] == sizes[2] - 1, 0.0, from_high[...])
 
     def halo(x, rows, base, count, low_at, high_at):
         low = roll(low_msg[base : base + rows], low_at - count * x)
@@ -613,12 +619,9 @@
     ]
 
 
-def match(value, axis):
+def shift(value, axis, by):
     size = lax.axis_size(axis)
-    pairs = [(0, 0), (size - 1, size - 1)]
-    for i in range(1, size - 1, 2):
-        pairs += [(i, i + 1), (i + 1, i)]
-    return lax.ppermute(value, axis, pairs)
+    return lax.ppermute(value, axis, [(i, (i + by) % size) for i in range(size)])
 
 
 ANY = pl.BlockSpec(memory_space=pl.ANY)
@@ -668,27 +671,27 @@
         (packed, relay, got_1, got_2, rise),
         spaces={4: ANY},
     )
-    got_1, got_3, got_2 = exchange((face_1, face_3, raw), "gx", (1, 3, 2))
+    got_2, got_3, got_1 = exchange((raw, face_3, face_1), "gx", (2, 3, 1))
     bands = call(
         bands_kernel,
         tuple(shape(band[0], band[1], dtype=BF16) for band in BANDS for _ in range(2)),
         (kernel_fine, kernel_mid, kernel_coarse),
         spaces={0: SMEM, 1: SMEM, 2: SMEM},
     )
-    wide_x, raw, face_1, face_2 = call(
+    wide_x, raw, to_high, to_low = call(
         widen_x_kernel,
-        (shape(36, 40, 128), shape(16, 128), shape(96, 128), shape(80, 128)),
+        (shape(36, 40, 128), shape(16, 128), shape(96, 128), shape(96, 128)),
         (wide_y, raw, got_1, got_3, got_2, bands[0]),
         spaces={5: ANY},
     )
-    got_1, got_3, got_2 = exchange((face_1, raw, raw), "gz", (1, 3, 2))
-    matched = match(face_2, "gz")
-    window = call(window_kernel, shape(4, 16, 128), (raw, got_1, got_2, got_3))
+    from_low, from_high = shift(to_high, "gz", 1), shift(to_low, "gz", -1)
+    got_2, got_3 = exchange((raw, raw), "gz", (2, 3))
+    window = call(window_kernel, shape(4, 16, 128), (raw, from_low, from_high, got_2, got_3))
     pieces = [window] + exchange((window, window, window), "gz", (4, 8, 12))
     base = call(
         near_kernel,
         shape(32, 32, 128),
-        (wide_x, got_1, matched, *bands, jnp.asarray(PROL_2, BF16), jnp.asarray(PROL_1, BF16)),
+        (wide_x, from_low, from_high, *bands, jnp.asarray(PROL_2, BF16), jnp.asarray(PROL_1, BF16)),
         (
             pltpu.VMEM((32, 40, 256), F32),
             pltpu.VMEM((SPAN_2, 32, 128), F32),

time: 48.6 us -> 48.3 us (level)
  the two profiles are of different devices: /device:TPU:32 before, /device:TPU:24 now
where the time goes in v3:
time: 48.3 us; the launch traced here: 48.1 us
  starting transfers between devices  22.3 us (46%)
  Pallas kernels  14.6 us (30%)
  waiting for transfers between devices  8.5 us (18%)
  local copies, waits for them, and re-layouts  1.86 us (4%)
  other arithmetic  0.7 us (1%)
    ppermute x10, starting transfers between devices, exchange(): lax.ppermute(value, axis, [(i, i ^ step) for i in range(size)])  20.2 us
    pallas_call x9, Pallas kernels, call(): pl.pallas_call(kernel, out_shape=outs, in_specs=[spaces.get(i, VMEM) for...  14.6 us
    ppermute x10, waiting for transfers between devices, exchange(): lax.ppermute(value, axis, [(i, i ^ step) for i in range(size)])  8.5 us
    ppermute x2, starting transfers between devices, shift(): lax.ppermute(value, axis, [(i, (i + by) % size) for i in range(size)])  2.1 us
    unnamed x16, local copies, waits for them, and re-layouts  1.86 us
  transfers between devices with their start and end apart: 12, of which 4 were waited for; matrix products, arithmetic and copies ran while one was open for 0% of the time, Pallas kernels for 13%

profile of v3, /device:TPU:24, one launch (start us, length us, event | category | flops | bytes accessed | tf_op | source)
XLA Modules:
  0.0 48.1 jit_solution(3035583158713917839)
XLA Ops:
  0.0 0.7 %multiply_add_fusion.codes = s32[384]{0:T(512)S(1)} fusion(s32[384]{0:T(512)} %param.12, s32[384]{0:T(512)} %param.13), kind=kLoop, calls=%fused_computation | loop fusion | flops 768 | bytes 4608 | tf_op jit(solution)/shard_map/add | solution.py:635
  0.7 0.9 %copy-done.1 = f32[384,128]{1,0:T(8,128)S(1)} copy-done((f32[384,128]{1,0:T(8,128)S(1)}, f32[384,128]{1,0:T(8,128)}, u32[]{:S(2)}) %copy-start.1) | copy-done | bytes 196632
  1.6 0.0 copy-start.4
  1.7 4.7 %shard_map.109 = (f32[32,32,128]{2,1,0:T(8,128)S(1)}, f32[8,128]{1,0:T(8,128)S(1)}, f32[88,128]{1,0:T(8,128)S(1)}) custom-call(s32[384]{0:T(512)S(1)} %multiply_add_fusion.codes, f32[384,128]{1,0:T(8,128)S(1)} %copy-done.1, bf16[4608,128]{1,0:T(8,128)(2,1)} %bitcast.1), custom_call_target="tpu_custom_call" | custom-call | flops 1000000 | bytes 2097152 | tf_op jit(solution)/shard_map/pallas_call | solution.py:599
  6.3 0.1 collective-permute-start
  6.4 1.2 %collective-permute-done.got.got_1 = f32[88,128]{1,0:T(8,128)S(1)} collective-permute-done((f32[88,128]{1,0:T(8,128)S(1)}, f32[88,128]{1,0:T(8,128)S(1)}, u32[]{:S(2)}, u32[]{:S(2)}) %collective-permute-start) | collective-permute-done | bytes 45088 | tf_op jit(solution)/shard_map/ppermute | solution.py:617
  7.6 0.1 shard_map.110.own
  7.7 7.2 %collective-permute-start.1 = (f32[48,128]{1,0:T(8,128)S(1)}, f32[48,128]{1,0:T(8,128)S(1)}, u32[]{:S(2)}, u32[]{:S(2)}) collective-permute-start(f32[48,128]{1,0:T(8,128)S(1)} %shard_map.110.own), channel_id=1, source_target_pairs={{0,32},{16,48},{32,0},{48,16},{1,33},{17,49},{33,1},{49,17},{2,34}... | collective-permute-start | bytes 73736 | tf_op jit(solution)/shard_map/ppermute | solution.py:617
  14.9 0.9 %copy-done.2 = f32[8,32,128]{2,1,0:T(8,128)S(1)} copy-done((f32[8,32,128]{2,1,0:T(8,128)S(1)}, f32[8,32,128]{2,1,0:T(8,128)}, u32[]{:S(2)}) %copy-start.2) | copy-done | bytes 131096
  15.8 1.0 %shard_map.111 = (bf16[1024,896]{1,0:T(8,128)(2,1)S(1)}, bf16[1024,896]{1,0:T(8,128)(2,1)S(1)}, bf16[1024,256]{1,0:T(8,128)(2,1)S(1)}) custom-call(f32[8,32,128]{2,1,0:T(8,128)S(1)} %copy-done.2), custom_call_target="tpu_custom_call" | custom-call | flops 1000000 | bytes 2097152 | tf_op jit(solution)/shard_map/pallas_call | solution.py:599
  16.8 0.0 copy-start
  16.8 0.3 shard_map.112
  17.2 1.6 %collective-permute-start.2 = (f32[72,128]{1,0:T(8,128)S(1)}, f32[72,128]{1,0:T(8,128)S(1)}, u32[]{:S(2)}, u32[]{:S(2)}) collective-permute-start(f32[72,128]{1,0:T(8,128)S(1)} %get-tuple-element.31), channel_id=1, source_target_pairs={{0,64},{64,0},{128,192},{192,128},{1,65},{65,1},{129,193},{193,129... | collective-permute-start | bytes 110600 | tf_op jit(solution)/shard_map/ppermute | solution.py:617
  18.7 2.1 %collective-permute-start.3 = (f32[72,128]{1,0:T(8,128)S(1)}, f32[72,128]{1,0:T(8,128)S(1)}, u32[]{:S(2)}, u32[]{:S(2)}) collective-permute-start(f32[72,128]{1,0:T(8,128)S(1)} %get-tuple-element.32), channel_id=1, source_target_pairs={{0,192},{64,128},{128,64},{192,0},{1,193},{65,129},{129,65},{193,1... | collective-permute-start | bytes 110600 | tf_op jit(solution)/shard_map/ppermute | solution.py:617
  20.8 0.6 %collective-permute-start.4 = (f32[8,128]{1,0:T(8,128)S(1)}, f32[8,128]{1,0:T(8,128)S(1)}, u32[]{:S(2)}, u32[]{:S(2)}) collective-permute-start(f32[8,128]{1,0:T(8,128)S(1)} %get-tuple-element.30.own), channel_id=1, source_target_pairs={{0,128},{64,192},{128,0},{192,64},{1,129},{65,193},{129,1},{193,65... | collective-permute-start | bytes 12296 | tf_op jit(solution)/shard_map/ppermute | solution.py:617
  21.5 2.3 %shard_map.113 = (bf16[256,256]{1,0:T(8,128)(2,1)S(1)}, bf16[256,256]{1,0:T(8,128)(2,1)S(1)}, bf16[256,128]{1,0:T(8,128)(2,1)S(1)}, bf16[256,128]{1,0:T(8,128)(2...) custom-call(f32[5,5,5]{2,1,0:T(8,128)S(1)} %copy-done.5, f32[5,5,5]{2,1,0:T(8,128)S(1)} %copy-done.6, ...), custom_call_target="tpu_custom_call" | custom-call | flops 1000000 | bytes 2097152 | tf_op jit(solution)/shard_map/pallas_call | solution.py:599
  23.8 2.1 %collective-permute-done.4.got_2 = f32[8,128]{1,0:T(8,128)S(1)} collective-permute-done((f32[8,128]{1,0:T(8,128)S(1)}, f32[8,128]{1,0:T(8,128)S(1)}, u32[]{:S(2)}, u32[]{:S(2)}) %collective-permute-start.4) | collective-permute-done | bytes 4128 | tf_op jit(solution)/shard_map/ppermute | solution.py:617
  26.0 0.7 %shard_map.114 = (f32[36,40,128]{2,1,0:T(8,128)S(1)}, f32[16,128]{1,0:T(8,128)S(1)}, f32[96,128]{1,0:T(8,128)S(1)}, f32[96,128]{1,0:T(8,128)S(1)}) custom-call(f32[32,40,128]{2,1,0:T(8,128)S(1)} %get-tuple-element.29.wide_y, f32[8,128]{1,0:T(8,128)S(1)} %get-tuple-element.30.own, f32[72,128]{1,0:T(8,128)S(1)} %collective-permute-done.2.got_1, ...), custom_call_target="tpu_custom_call" | custom-call | flops 1000000 | bytes 2097152 | tf_op jit(solution)/shard_map/pallas_call | solution.py:599
  26.7 0.8 %collective-permute-start.5 = (f32[96,128]{1,0:T(8,128)S(1)}, f32[96,128]{1,0:T(8,128)S(1)}, u32[]{:S(2)}, u32[]{:S(2)}) collective-permute-start(f32[96,128]{1,0:T(8,128)S(1)} %get-tuple-element.35), channel_id=1, source_target_pairs={{0,1},{1,2},{2,3},{3,4},{4,5},{5,6},{6,7},{7,8},{8,9},{9,10},{10,1... | collective-permute-start | bytes 147464 | tf_op jit(solution)/shard_map/ppermute | solution.py:624
  27.4 1.3 %collective-permute-start.6 = (f32[96,128]{1,0:T(8,128)S(1)}, f32[96,128]{1,0:T(8,128)S(1)}, u32[]{:S(2)}, u32[]{:S(2)}) collective-permute-start(f32[96,128]{1,0:T(8,128)S(1)} %get-tuple-element.36), channel_id=1, source_target_pairs={{0,15},{1,0},{2,1},{3,2},{4,3},{5,4},{6,5},{7,6},{8,7},{9,8},{10,9... | collective-permute-start | bytes 147464 | tf_op jit(solution)/shard_map/ppermute | solution.py:624
  28.8 4.1 %collective-permute-start.8 = (f32[16,128]{1,0:T(8,128)S(1)}, f32[16,128]{1,0:T(8,128)S(1)}, u32[]{:S(2)}, u32[]{:S(2)}) collective-permute-start(f32[16,128]{1,0:T(8,128)S(1)} %get-tuple-element.42.own), channel_id=1, source_target_pairs={{0,3},{1,2},{2,1},{3,0},{4,7},{5,6},{6,5},{7,4},{8,11},{9,10},{10,... | collective-permute-start | bytes 24584 | tf_op jit(solution)/shard_map/ppermute | solution.py:617
  32.9 0.0 collective-permute-start.7
  32.9 1.6 %collective-permute-done.8.got_3 = f32[16,128]{1,0:T(8,128)S(1)} collective-permute-done((f32[16,128]{1,0:T(8,128)S(1)}, f32[16,128]{1,0:T(8,128)S(1)}, u32[]{:S(2)}, u32[]{:S(2)}) %collective-permute-start.8) | collective-permute-done | bytes 8224 | tf_op jit(solution)/shard_map/ppermute | solution.py:617
  34.6 3.5 %collective-permute-done.7.got_2 = f32[16,128]{1,0:T(8,128)S(1)} collective-permute-done((f32[16,128]{1,0:T(8,128)S(1)}, f32[16,128]{1,0:T(8,128)S(1)}, u32[]{:S(2)}, u32[]{:S(2)}) %collective-permute-start.7) | collective-permute-done | bytes 8224 | tf_op jit(solution)/shard_map/ppermute | solution.py:617
  38.1 0.0 collective-permute-done.5.from_low
  38.1 0.4 shard_map.116.piece_0
  38.5 1.5 %collective-permute-start.11 = (f32[4,16,128]{2,1,0:T(8,128)S(1)}, f32[4,16,128]{2,1,0:T(8,128)S(1)}, u32[]{:S(2)}, u32[]{:S(2)}) collective-permute-start(f32[4,16,128]{2,1,0:T(8,128)S(1)} %shard_map.116.piece_0), channel_id=1, source_target_pairs={{0,12},{1,13},{2,14},{3,15},{4,8},{5,9},{6,10},{7,11},{8,4},{9,5},... | collective-permute-start | bytes 98312 | tf_op jit(solution)/shard_map/ppermute | solution.py:617
  40.0 0.0 collective-permute-start.10
  40.0 2.9 %collective-permute-start.9 = (f32[4,16,128]{2,1,0:T(8,128)S(1)}, f32[4,16,128]{2,1,0:T(8,128)S(1)}, u32[]{:S(2)}, u32[]{:S(2)}) collective-permute-start(f32[4,16,128]{2,1,0:T(8,128)S(1)} %shard_map.116.piece_0), channel_id=1, source_target_pairs={{0,4},{1,5},{2,6},{3,7},{4,0},{5,1},{6,2},{7,3},{8,12},{9,13},{10,... | collective-permute-start | bytes 98312 | tf_op jit(solution)/shard_map/ppermute | solution.py:617
  42.9 2.8 %shard_map.115.base = f32[32,32,128]{2,1,0:T(8,128)S(1)} custom-call(f32[36,40,128]{2,1,0:T(8,128)S(1)} %get-tuple-element.34.wide, f32[96,128]{1,0:T(8,128)S(1)} %collective-permute-done.5.from_low, f32[96,128]{1,0:T(8,128)S(1)} %collective-permute-done.6.from_high, bf16[256,256]{1,0:T(8,128)(2,1)S(1)} %get-tuple-element.33.after.b1h, ...), custom_call_target="tpu_custom_call" | custom-call | flops 1000000 | bytes 2097152 | tf_op jit(solution)/shard_map/pallas_call | solution.py:599
  45.8 0.0 collective-permute-done.9.piece_1
  45.8 2.3 %shard_map.117 = f32[32,32,32]{2,1,0:T(8,128)} custom-call(f32[32,32,128]{2,1,0:T(8,128)S(1)} %shard_map.115.base, f32[4,16,128]{2,1,0:T(8,128)S(1)} %shard_map.116.piece_0, f32[4,16,128]{2,1,0:T(8,128)S(1)} %collective-permute-done.9.piece_1, f32[4,16,128]{2,1,0:T(8,128)S(1)} %collective-permute-done.10.piece_2, ...), custom_call_target="tpu_custom_call" | custom-call | flops 1000000 | bytes 2097152 | tf_op jit(solution)/shard_map/pallas_call | solution.py:599
  (18 shorter events, 0.0 us)
Async XLA Ops:
  0.7 0.9 %copy-start.1 = (f32[384,128]{1,0:T(8,128)S(1)}, f32[384,128]{1,0:T(8,128)}, u32[]{:S(2)}) copy-start(f32[384,128]{1,0:T(8,128)} %charges_hbm.1) | copy-start | bytes 589828
  1.6 19.8 %copy-start.5 = (f32[5,5,5]{2,1,0:T(8,128)S(1)}, f32[5,5,5]{2,1,0:T(8,128)}, u32[]{:S(2)}) copy-start(f32[5,5,5]{2,1,0:T(8,128)} %kernel_1.1) | copy-start | bytes 1504
  1.6 19.8 %copy-start.6 = (f32[5,5,5]{2,1,0:T(8,128)S(1)}, f32[5,5,5]{2,1,0:T(8,128)}, u32[]{:S(2)}) copy-start(f32[5,5,5]{2,1,0:T(8,128)} %kernel_2.1) | copy-start | bytes 1504
  1.6 19.8 %copy-start.7 = (f32[5,5,5]{2,1,0:T(8,128)S(1)}, f32[5,5,5]{2,1,0:T(8,128)}, u32[]{:S(2)}) copy-start(f32[5,5,5]{2,1,0:T(8,128)} %kernel_3.1) | copy-start | bytes 1504
  1.6 41.3 %copy-start.3 = (bf16[128,128]{1,0:T(8,128)(2,1)S(1)}, bf16[128,128]{1,0:T(8,128)(2,1)}, u32[]{:S(2)}) copy-start(bf16[128,128]{1,0:T(8,128)(2,1)} %constant.12.clone.prol_1) | copy-start | bytes 98308
  1.6 41.3 %copy-start.4 = (bf16[128,128]{1,0:T(8,128)(2,1)S(1)}, bf16[128,128]{1,0:T(8,128)(2,1)}, u32[]{:S(2)}) copy-start(bf16[128,128]{1,0:T(8,128)(2,1)} %constant.11.clone.prol_2) | copy-start | bytes 98308
  6.3 1.3 %collective-permute-start = (f32[88,128]{1,0:T(8,128)S(1)}, f32[88,128]{1,0:T(8,128)S(1)}, u32[]{:S(2)}, u32[]{:S(2)}) collective-permute-start(f32[88,128]{1,0:T(8,128)S(1)} %get-tuple-element.27), channel_id=1, source_target_pairs={{0,16},{16,0},{32,48},{48,32},{1,17},{17,1},{33,49},{49,33},{2,18}... | collective-permute-start | bytes 135176 | tf_op jit(solution)/shard_map/ppermute | solution.py:617
  7.7 9.1 %collective-permute-start.1 = (f32[48,128]{1,0:T(8,128)S(1)}, f32[48,128]{1,0:T(8,128)S(1)}, u32[]{:S(2)}, u32[]{:S(2)}) collective-permute-start(f32[48,128]{1,0:T(8,128)S(1)} %shard_map.110.own), channel_id=1, source_target_pairs={{0,32},{16,48},{32,0},{48,16},{1,33},{17,49},{33,1},{49,17},{2,34}... | collective-permute-start | bytes 73736 | tf_op jit(solution)/shard_map/ppermute | solution.py:617
  14.9 0.9 %copy-start.2 = (f32[8,32,128]{2,1,0:T(8,128)S(1)}, f32[8,32,128]{2,1,0:T(8,128)}, u32[]{:S(2)}) copy-start(f32[8,32,128]{2,1,0:T(8,128)} %constant.10.clone.factors) | copy-start | bytes 393220
  16.8 29.0 %copy-start = (bf16[8,128,128]{2,1,0:T(8,128)(2,1)S(1)}, bf16[8,128,128]{2,1,0:T(8,128)(2,1)}, u32[]{:S(2)}) copy-start(bf16[8,128,128]{2,1,0:T(8,128)(2,1)} %constant.13.clone.qz) | copy-start | bytes 786436
  17.2 8.8 %collective-permute-start.2 = (f32[72,128]{1,0:T(8,128)S(1)}, f32[72,128]{1,0:T(8,128)S(1)}, u32[]{:S(2)}, u32[]{:S(2)}) collective-permute-start(f32[72,128]{1,0:T(8,128)S(1)} %get-tuple-element.31), channel_id=1, source_target_pairs={{0,64},{64,0},{128,192},{192,128},{1,65},{65,1},{129,193},{193,129... | collective-permute-start | bytes 110600 | tf_op jit(solution)/shard_map/ppermute | solution.py:617
  18.7 7.2 %collective-permute-start.3 = (f32[72,128]{1,0:T(8,128)S(1)}, f32[72,128]{1,0:T(8,128)S(1)}, u32[]{:S(2)}, u32[]{:S(2)}) collective-permute-start(f32[72,128]{1,0:T(8,128)S(1)} %get-tuple-element.32), channel_id=1, source_target_pairs={{0,192},{64,128},{128,64},{192,0},{1,193},{65,129},{129,65},{193,1... | collective-permute-start | bytes 110600 | tf_op jit(solution)/shard_map/ppermute | solution.py:617
  20.8 5.1 %collective-permute-start.4 = (f32[8,128]{1,0:T(8,128)S(1)}, f32[8,128]{1,0:T(8,128)S(1)}, u32[]{:S(2)}, u32[]{:S(2)}) collective-permute-start(f32[8,128]{1,0:T(8,128)S(1)} %get-tuple-element.30.own), channel_id=1, source_target_pairs={{0,128},{64,192},{128,0},{192,64},{1,129},{65,193},{129,1},{193,65... | collective-permute-start | bytes 12296 | tf_op jit(solution)/shard_map/ppermute | solution.py:617
  26.7 11.4 %collective-permute-start.5 = (f32[96,128]{1,0:T(8,128)S(1)}, f32[96,128]{1,0:T(8,128)S(1)}, u32[]{:S(2)}, u32[]{:S(2)}) collective-permute-start(f32[96,128]{1,0:T(8,128)S(1)} %get-tuple-element.35), channel_id=1, source_target_pairs={{0,1},{1,2},{2,3},{3,4},{4,5},{5,6},{6,7},{7,8},{8,9},{9,10},{10,1... | collective-permute-start | bytes 147464 | tf_op jit(solution)/shard_map/ppermute | solution.py:624
  27.4 10.6 %collective-permute-start.6 = (f32[96,128]{1,0:T(8,128)S(1)}, f32[96,128]{1,0:T(8,128)S(1)}, u32[]{:S(2)}, u32[]{:S(2)}) collective-permute-start(f32[96,128]{1,0:T(8,128)S(1)} %get-tuple-element.36), channel_id=1, source_target_pairs={{0,15},{1,0},{2,1},{3,2},{4,3},{5,4},{6,5},{7,6},{8,7},{9,8},{10,9... | collective-permute-start | bytes 147464 | tf_op jit(solution)/shard_map/ppermute | solution.py:624
  28.8 5.8 %collective-permute-start.8 = (f32[16,128]{1,0:T(8,128)S(1)}, f32[16,128]{1,0:T(8,128)S(1)}, u32[]{:S(2)}, u32[]{:S(2)}) collective-permute-start(f32[16,128]{1,0:T(8,128)S(1)} %get-tuple-element.42.own), channel_id=1, source_target_pairs={{0,3},{1,2},{2,1},{3,0},{4,7},{5,6},{6,5},{7,4},{8,11},{9,10},{10,... | collective-permute-start | bytes 24584 | tf_op jit(solution)/shard_map/ppermute | solution.py:617
  32.9 5.2 %collective-permute-start.7 = (f32[16,128]{1,0:T(8,128)S(1)}, f32[16,128]{1,0:T(8,128)S(1)}, u32[]{:S(2)}, u32[]{:S(2)}) collective-permute-start(f32[16,128]{1,0:T(8,128)S(1)} %get-tuple-element.42.own), channel_id=1, source_target_pairs={{0,2},{1,3},{2,0},{3,1},{4,6},{5,7},{6,4},{7,5},{8,10},{9,11},{10,... | collective-permute-start | bytes 24584 | tf_op jit(solution)/shard_map/ppermute | solution.py:617
  38.5 7.3 %collective-permute-start.11 = (f32[4,16,128]{2,1,0:T(8,128)S(1)}, f32[4,16,128]{2,1,0:T(8,128)S(1)}, u32[]{:S(2)}, u32[]{:S(2)}) collective-permute-start(f32[4,16,128]{2,1,0:T(8,128)S(1)} %shard_map.116.piece_0), channel_id=1, source_target_pairs={{0,12},{1,13},{2,14},{3,15},{4,8},{5,9},{6,10},{7,11},{8,4},{9,5},... | collective-permute-start | bytes 98312 | tf_op jit(solution)/shard_map/ppermute | solution.py:617
  40.0 5.8 %collective-permute-start.10 = (f32[4,16,128]{2,1,0:T(8,128)S(1)}, f32[4,16,128]{2,1,0:T(8,128)S(1)}, u32[]{:S(2)}, u32[]{:S(2)}) collective-permute-start(f32[4,16,128]{2,1,0:T(8,128)S(1)} %shard_map.116.piece_0), channel_id=1, source_target_pairs={{0,8},{1,9},{2,10},{3,11},{4,12},{5,13},{6,14},{7,15},{8,0},{9,1},... | collective-permute-start | bytes 98312 | tf_op jit(solution)/shard_map/ppermute | solution.py:617
  40.0 5.8 %collective-permute-start.9 = (f32[4,16,128]{2,1,0:T(8,128)S(1)}, f32[4,16,128]{2,1,0:T(8,128)S(1)}, u32[]{:S(2)}, u32[]{:S(2)}) collective-permute-start(f32[4,16,128]{2,1,0:T(8,128)S(1)} %shard_map.116.piece_0), channel_id=1, source_target_pairs={{0,4},{1,5},{2,6},{3,7},{4,0},{5,1},{6,2},{7,3},{8,12},{9,13},{10,... | collective-permute-start | bytes 98312 | tf_op jit(solution)/shard_map/ppermute | solution.py:617

commit v4 on v3

--- a/solution.py
+++ b/solution.py
@@ -301,13 +301,11 @@
     out[40:48, :] = place_y(raw[...], index[1]) + place_y(got[80:88, :], partner)
 
 
-def widen_y_kernel(packed, own, got_1, got_2, after, out, raw_out, face_1, face_3):
+def widen_y_kernel(framed, own, got_1, got_2, after, out, raw_out, face_1, face_3):
     index, _ = place()
     even, one, two = nearest(index[1])
     total = own[40:48, :] + got_2[40:48, :]
     raw_out[...] = total
-    out[...] = jnp.zeros_like(out)
-    out[:, 2:34, :] = packed[...]
     a, b = got_1[0:40, :], got_2[0:40, :]
     low = jnp.where(even, 0.0, a) + jnp.where(two, b, 0.0)
     high = jnp.where(even, a, 0.0) + jnp.where(one, b, 0.0)
@@ -370,10 +368,12 @@
         (64, 16, 15, 5, THI, 6),
     ):
         first = lane + high if to_high else lane
+        at = iota((rows, 128), 1)
+        wanted = (at >= first) & (at < first + count)
         total = jnp.zeros((rows, 128), F32)
         for x in range(planes):
-            kept = roll(source[x, 0:rows, :], count * x - first)
-            total = total + lanes_of(kept, count * x, count)
+            kept = jnp.where(wanted, source[x, 0:rows, :], 0.0)
+            total = total + roll(kept, count * x - first)
         face[base : base + rows, :] = total
 
 
@@ -442,7 +442,7 @@
         low_ref[...] = low
 
 
-def green_kernel(factors, green_high, green_low, rise, block_high, block_low):
+def green_kernel(factors, packed, green_high, green_low, rise, framed, block_high, block_low):
     index, sizes = place()
     row, lane = iota((64, 128), 0), iota((64, 128), 1)
     delta_x = (lane // 8).astype(F32)
@@ -467,6 +467,9 @@
     high, low = split(kept)
     rise[:, 0:128] = (high.astype(F32) + roll(low.astype(F32), 64)).astype(BF16)
     rise[:, 128:256] = high
+    framed[:, 0:2, :] = jnp.zeros((32, 2, 128), F32)
+    framed[:, 34:40, :] = jnp.zeros((32, 6, 128), F32)
+    framed[:, 2:34, :] = packed[...]
 
 
 def prolong_rows(source, target, count, whole):
@@ -594,7 +597,7 @@
     out[...] = (base[...] + far.reshape(32, 32, 128))[:, :, 0:32]
 
 
-def call(kernel, outs, ins, scratch=(), megabytes=16, flops=1000000, spaces=None):
+def call(kernel, outs, ins, scratch=(), megabytes=16, spaces=None, aliases=None):
     spaces = spaces or {}
     return pl.pallas_call(
         kernel,
@@ -602,8 +605,9 @@
         in_specs=[spaces.get(i, VMEM) for i in range(len(ins))],
         out_specs=jax.tree.map(lambda _: VMEM, outs),
         scratch_shapes=list(scratch),
-        compiler_params=pltpu.CompilerParams(vmem_limit_bytes=megabytes * 2**20),
-        cost_estimate=pl.CostEstimate(flops=flops, bytes_accessed=2**21, transcendentals=0),
+        input_output_aliases=aliases or {},
+        compiler_params=pltpu.CompilerParams(vmem_limit_bytes=int(megabytes * 2**20)),
+        cost_estimate=pl.CostEstimate(flops=1000000, bytes_accessed=2**21, transcendentals=0),
     )(*ins)
 
 
@@ -619,9 +623,14 @@
     ]
 
 
-def shift(value, axis, by):
-    size = lax.axis_size(axis)
-    return lax.ppermute(value, axis, [(i, (i + by) % size) for i in range(size)])
+def shift(value, by):
+    size_y, size_z = lax.axis_size("gy"), lax.axis_size("gz")
+    half = size_y // 2
+    pairs = []
+    for core in range(half):
+        ring = [(high * half + core) * size_z + z for high in range(2) for z in range(size_z)]
+        pairs += [(ring[n], ring[(n + by) % len(ring)]) for n in range(len(ring))]
+    return lax.ppermute(value, ("gy", "gz"), pairs)
 
 
 ANY = pl.BlockSpec(memory_space=pl.ANY)
@@ -647,7 +656,7 @@
             pltpu.SemaphoreType.DMA((4,)),
         ),
         spaces={1: HBM, 2: HBM},
-        megabytes=53,
+        megabytes=53.75,
     )
     (got_1,) = exchange((face,), "gy", (1,))
     relay = call(relay_kernel, shape(48, 128), (raw, got_1))
@@ -655,21 +664,23 @@
     qx, qy, qz = composites()
     qz_high = qz.astype(BF16)
     qz_low = (qz - qz_high.astype(np.float32)).astype(BF16)
-    green_high, green_low, rise = call(
+    green_high, green_low, rise, framed = call(
         green_kernel,
         (
             shape(1024, 128 * SPAN_4, dtype=BF16),
             shape(1024, 128 * SPAN_4, dtype=BF16),
             shape(1024, 256, dtype=BF16),
+            shape(32, 40, 128),
         ),
-        (jnp.asarray(np.concatenate([qx, qy])),),
+        (jnp.asarray(np.concatenate([qx, qy])), packed),
         (pltpu.VMEM((18, 64, 128), BF16), pltpu.VMEM((18, 64, 128), BF16)),
     )
     wide_y, raw, face_1, face_3 = call(
         widen_y_kernel,
         (shape(32, 40, 128), shape(8, 128), shape(72, 128), shape(72, 128)),
-        (packed, relay, got_1, got_2, rise),
+        (framed, relay, got_1, got_2, rise),
         spaces={4: ANY},
+        aliases={0: 0},
     )
     got_2, got_3, got_1 = exchange((raw, face_3, face_1), "gx", (2, 3, 1))
     bands = call(
@@ -684,7 +695,7 @@
         (wide_y, raw, got_1, got_3, got_2, bands[0]),
         spaces={5: ANY},
     )
-    from_low, from_high = shift(to_high, "gz", 1), shift(to_low, "gz", -1)
+    from_low, from_high = shift(to_high, 1), shift(to_low, -1)
     got_2, got_3 = exchange((raw, raw), "gz", (2, 3))
     window = call(window_kernel, shape(4, 16, 128), (raw, from_low, from_high, got_2, got_3))
     pieces = [window] + exchange((window, window, window), "gz", (4, 8, 12))

time: 48.3 us -> 49.1 us (1.017)
  Pallas kernels: 14.6 us -> 15.2 us
    pallas_call x9, Pallas kernels: 14.6 us -> 15.2 us  [call(): pl.pallas_call(kernel, out_shape=outs, in_specs=[spaces.get(i, VMEM) for...]
where the time goes in v4:
time: 49.1 us; the launch traced here: 48.9 us
  starting transfers between devices  22.3 us (45%)
  Pallas kernels  15.2 us (31%)
  waiting for transfers between devices  8.5 us (17%)
  local copies, waits for them, and re-layouts  1.98 us (4%)
  other arithmetic  0.73 us (1%)
    ppermute x10, starting transfers between devices, exchange(): lax.ppermute(value, axis, [(i, i ^ step) for i in range(size)])  20.2 us
    pallas_call x9, Pallas kernels, call(): pl.pallas_call(kernel, out_shape=outs, in_specs=[spaces.get(i, VMEM) for...  15.2 us
    ppermute x10, waiting for transfers between devices, exchange(): lax.ppermute(value, axis, [(i, i ^ step) for i in range(size)])  8.5 us
    ppermute x2, starting transfers between devices, shift(): return lax.ppermute(value, ('gy', 'gz'), pairs)  2.1 us
    unnamed x16, local copies, waits for them, and re-layouts  1.98 us
  transfers between devices with their start and end apart: 12, of which 4 were waited for; matrix products, arithmetic and copies ran while one was open for 0% of the time, Pallas kernels for 13%

profile of v4, /device:TPU:24, one launch (start us, length us, event | category | flops | bytes accessed | tf_op | source)
XLA Modules:
  0.0 48.9 jit_solution(4397974353126860387)
XLA Ops:
  0.0 0.7 %multiply_add_fusion.codes = s32[384]{0:T(512)S(1)} fusion(s32[384]{0:T(512)} %param.12, s32[384]{0:T(512)} %param.13), kind=kLoop, calls=%fused_computation | loop fusion | flops 768 | bytes 4608 | tf_op jit(solution)/shard_map/add | solution.py:644
  0.7 5.2 %shard_map.109 = (f32[32,32,128]{2,1,0:T(8,128)}, f32[8,128]{1,0:T(8,128)S(1)}, f32[88,128]{1,0:T(8,128)S(1)}) custom-call(s32[384]{0:T(512)S(1)} %multiply_add_fusion.codes, f32[384,128]{1,0:T(8,128)} %charges_hbm.1, bf16[4608,128]{1,0:T(8,128)(2,1)} %bitcast.1), custom_call_target="tpu_custom_call" | custom-call | flops 1000000 | bytes 2097152 | tf_op jit(solution)/shard_map/pallas_call | solution.py:602
  6.0 0.0 copy-start.3
  6.0 0.0 copy-start.4
  6.0 0.1 collective-permute-start
  6.1 1.2 %collective-permute-done.got.got_1 = f32[88,128]{1,0:T(8,128)S(1)} collective-permute-done((f32[88,128]{1,0:T(8,128)S(1)}, f32[88,128]{1,0:T(8,128)S(1)}, u32[]{:S(2)}, u32[]{:S(2)}) %collective-permute-start) | collective-permute-done | bytes 45088 | tf_op jit(solution)/shard_map/ppermute | solution.py:621
  7.3 0.1 shard_map.111.own
  7.4 7.2 %collective-permute-start.1 = (f32[48,128]{1,0:T(8,128)S(1)}, f32[48,128]{1,0:T(8,128)S(1)}, u32[]{:S(2)}, u32[]{:S(2)}) collective-permute-start(f32[48,128]{1,0:T(8,128)S(1)} %shard_map.111.own), channel_id=1, source_target_pairs={{0,32},{16,48},{32,0},{48,16},{1,33},{17,49},{33,1},{49,17},{2,34}... | collective-permute-start | bytes 73736 | tf_op jit(solution)/shard_map/ppermute | solution.py:621
  14.6 1.0 %copy-done = f32[32,32,128]{2,1,0:T(8,128)S(1)} copy-done((f32[32,32,128]{2,1,0:T(8,128)S(1)}, f32[32,32,128]{2,1,0:T(8,128)}, u32[]{:S(2)}) %copy-start) | copy-done | bytes 524312
  15.7 0.9 %copy-done.2 = f32[8,32,128]{2,1,0:T(8,128)S(1)} copy-done((f32[8,32,128]{2,1,0:T(8,128)S(1)}, f32[8,32,128]{2,1,0:T(8,128)}, u32[]{:S(2)}) %copy-start.2) | copy-done | bytes 131096
  16.6 1.0 %shard_map.110 = (bf16[1024,896]{1,0:T(8,128)(2,1)S(1)}, bf16[1024,896]{1,0:T(8,128)(2,1)S(1)}, bf16[1024,256]{1,0:T(8,128)(2,1)S(1)}, f32[32,40,128]{2,1,0:T(8,128)S(1)}) custom-call(f32[8,32,128]{2,1,0:T(8,128)S(1)} %copy-done.2, f32[32,32,128]{2,1,0:T(8,128)S(1)} %copy-done), custom_call_target="tpu_custom_call" | custom-call | flops 1000000 | bytes 2097152 | tf_op jit(solution)/shard_map/pallas_call | solution.py:602
  17.5 0.0 collective-permute-done.1.got_2
  17.6 0.0 copy-start.1
  17.6 0.3 shard_map.112
  17.9 1.6 %collective-permute-start.2 = (f32[72,128]{1,0:T(8,128)S(1)}, f32[72,128]{1,0:T(8,128)S(1)}, u32[]{:S(2)}, u32[]{:S(2)}) collective-permute-start(f32[72,128]{1,0:T(8,128)S(1)} %get-tuple-element.33), channel_id=1, source_target_pairs={{0,64},{64,0},{128,192},{192,128},{1,65},{65,1},{129,193},{193,129... | collective-permute-start | bytes 110600 | tf_op jit(solution)/shard_map/ppermute | solution.py:621
  19.5 2.1 %collective-permute-start.3 = (f32[72,128]{1,0:T(8,128)S(1)}, f32[72,128]{1,0:T(8,128)S(1)}, u32[]{:S(2)}, u32[]{:S(2)}) collective-permute-start(f32[72,128]{1,0:T(8,128)S(1)} %get-tuple-element.34), channel_id=1, source_target_pairs={{0,192},{64,128},{128,64},{192,0},{1,193},{65,129},{129,65},{193,1... | collective-permute-start | bytes 110600 | tf_op jit(solution)/shard_map/ppermute | solution.py:621
  21.6 0.6 %collective-permute-start.4 = (f32[8,128]{1,0:T(8,128)S(1)}, f32[8,128]{1,0:T(8,128)S(1)}, u32[]{:S(2)}, u32[]{:S(2)}) collective-permute-start(f32[8,128]{1,0:T(8,128)S(1)} %get-tuple-element.32.own), channel_id=1, source_target_pairs={{0,128},{64,192},{128,0},{192,64},{1,129},{65,193},{129,1},{193,65... | collective-permute-start | bytes 12296 | tf_op jit(solution)/shard_map/ppermute | solution.py:621
  22.2 2.3 %shard_map.113 = (bf16[256,256]{1,0:T(8,128)(2,1)S(1)}, bf16[256,256]{1,0:T(8,128)(2,1)S(1)}, bf16[256,128]{1,0:T(8,128)(2,1)S(1)}, bf16[256,128]{1,0:T(8,128)(2...) custom-call(f32[5,5,5]{2,1,0:T(8,128)S(1)} %copy-done.5, f32[5,5,5]{2,1,0:T(8,128)S(1)} %copy-done.6, ...), custom_call_target="tpu_custom_call" | custom-call | flops 1000000 | bytes 2097152 | tf_op jit(solution)/shard_map/pallas_call | solution.py:602
  24.6 2.1 %collective-permute-done.4.got_2 = f32[8,128]{1,0:T(8,128)S(1)} collective-permute-done((f32[8,128]{1,0:T(8,128)S(1)}, f32[8,128]{1,0:T(8,128)S(1)}, u32[]{:S(2)}, u32[]{:S(2)}) %collective-permute-start.4) | collective-permute-done | bytes 4128 | tf_op jit(solution)/shard_map/ppermute | solution.py:621
  26.7 0.7 %shard_map.114 = (f32[36,40,128]{2,1,0:T(8,128)S(1)}, f32[16,128]{1,0:T(8,128)S(1)}, f32[96,128]{1,0:T(8,128)S(1)}, f32[96,128]{1,0:T(8,128)S(1)}) custom-call(f32[32,40,128]{2,1,0:T(8,128)S(1)} %get-tuple-element.31.wide_y, f32[8,128]{1,0:T(8,128)S(1)} %get-tuple-element.32.own, f32[72,128]{1,0:T(8,128)S(1)} %collective-permute-done.2.got_1, ...), custom_call_target="tpu_custom_call" | custom-call | flops 1000000 | bytes 2097152 | tf_op jit(solution)/shard_map/pallas_call | solution.py:602
  27.4 0.8 %collective-permute-start.5 = (f32[96,128]{1,0:T(8,128)S(1)}, f32[96,128]{1,0:T(8,128)S(1)}, u32[]{:S(2)}, u32[]{:S(2)}) collective-permute-start(f32[96,128]{1,0:T(8,128)S(1)} %get-tuple-element.37), channel_id=1, source_target_pairs={{0,1},{1,2},{2,3},{3,4},{4,5},{5,6},{6,7},{7,8},{8,9},{9,10},{10,1... | collective-permute-start | bytes 147464 | tf_op jit(solution)/shard_map/ppermute | solution.py:633
  28.2 1.3 %collective-permute-start.6 = (f32[96,128]{1,0:T(8,128)S(1)}, f32[96,128]{1,0:T(8,128)S(1)}, u32[]{:S(2)}, u32[]{:S(2)}) collective-permute-start(f32[96,128]{1,0:T(8,128)S(1)} %get-tuple-element.38), channel_id=1, source_target_pairs={{0,47},{1,0},{2,1},{3,2},{4,3},{5,4},{6,5},{7,6},{8,7},{9,8},{10,9... | collective-permute-start | bytes 147464 | tf_op jit(solution)/shard_map/ppermute | solution.py:633
  29.5 4.2 %collective-permute-start.8 = (f32[16,128]{1,0:T(8,128)S(1)}, f32[16,128]{1,0:T(8,128)S(1)}, u32[]{:S(2)}, u32[]{:S(2)}) collective-permute-start(f32[16,128]{1,0:T(8,128)S(1)} %get-tuple-element.44.own), channel_id=1, source_target_pairs={{0,3},{1,2},{2,1},{3,0},{4,7},{5,6},{6,5},{7,4},{8,11},{9,10},{10,... | collective-permute-start | bytes 24584 | tf_op jit(solution)/shard_map/ppermute | solution.py:621
  33.7 1.6 %collective-permute-done.8.got_3 = f32[16,128]{1,0:T(8,128)S(1)} collective-permute-done((f32[16,128]{1,0:T(8,128)S(1)}, f32[16,128]{1,0:T(8,128)S(1)}, u32[]{:S(2)}, u32[]{:S(2)}) %collective-permute-start.8) | collective-permute-done | bytes 8224 | tf_op jit(solution)/shard_map/ppermute | solution.py:621
  35.3 3.5 %collective-permute-done.7.got_2 = f32[16,128]{1,0:T(8,128)S(1)} collective-permute-done((f32[16,128]{1,0:T(8,128)S(1)}, f32[16,128]{1,0:T(8,128)S(1)}, u32[]{:S(2)}, u32[]{:S(2)}) %collective-permute-start.7) | collective-permute-done | bytes 8224 | tf_op jit(solution)/shard_map/ppermute | solution.py:621
  38.9 0.0 collective-permute-done.5.from_low
  38.9 0.4 shard_map.116.piece_0
  39.3 1.1 %collective-permute-start.11 = (f32[4,16,128]{2,1,0:T(8,128)S(1)}, f32[4,16,128]{2,1,0:T(8,128)S(1)}, u32[]{:S(2)}, u32[]{:S(2)}) collective-permute-start(f32[4,16,128]{2,1,0:T(8,128)S(1)} %shard_map.116.piece_0), channel_id=1, source_target_pairs={{0,12},{1,13},{2,14},{3,15},{4,8},{5,9},{6,10},{7,11},{8,4},{9,5},... | collective-permute-start | bytes 98312 | tf_op jit(solution)/shard_map/ppermute | solution.py:621
  40.4 0.0 collective-permute-start.10
  40.4 3.3 %collective-permute-start.9 = (f32[4,16,128]{2,1,0:T(8,128)S(1)}, f32[4,16,128]{2,1,0:T(8,128)S(1)}, u32[]{:S(2)}, u32[]{:S(2)}) collective-permute-start(f32[4,16,128]{2,1,0:T(8,128)S(1)} %shard_map.116.piece_0), channel_id=1, source_target_pairs={{0,4},{1,5},{2,6},{3,7},{4,0},{5,1},{6,2},{7,3},{8,12},{9,13},{10,... | collective-permute-start | bytes 98312 | tf_op jit(solution)/shard_map/ppermute | solution.py:621
  43.7 2.8 %shard_map.115.base = f32[32,32,128]{2,1,0:T(8,128)S(1)} custom-call(f32[36,40,128]{2,1,0:T(8,128)S(1)} %get-tuple-element.36.wide, f32[96,128]{1,0:T(8,128)S(1)} %collective-permute-done.5.from_low, f32[96,128]{1,0:T(8,128)S(1)} %collective-permute-done.6.from_high, bf16[256,256]{1,0:T(8,128)(2,1)S(1)} %get-tuple-element.35.after.b1h, ...), custom_call_target="tpu_custom_call" | custom-call | flops 1000000 | bytes 2097152 | tf_op jit(solution)/shard_map/pallas_call | solution.py:602
  46.6 2.3 %shard_map.117 = f32[32,32,32]{2,1,0:T(8,128)} custom-call(f32[32,32,128]{2,1,0:T(8,128)S(1)} %shard_map.115.base, f32[4,16,128]{2,1,0:T(8,128)S(1)} %shard_map.116.piece_0, f32[4,16,128]{2,1,0:T(8,128)S(1)} %collective-permute-done.9.piece_1, f32[4,16,128]{2,1,0:T(8,128)S(1)} %collective-permute-done.10.piece_2, ...), custom_call_target="tpu_custom_call" | custom-call | flops 1000000 | bytes 2097152 | tf_op jit(solution)/shard_map/pallas_call | solution.py:602
  (18 shorter events, 0.0 us)
Async XLA Ops:
  0.0 22.2 %copy-start.7 = (f32[5,5,5]{2,1,0:T(8,128)S(1)}, f32[5,5,5]{2,1,0:T(8,128)}, u32[]{:S(2)}) copy-start(f32[5,5,5]{2,1,0:T(8,128)} %kernel_3.1) | copy-start | bytes 1504
  0.0 22.2 %copy-start.6 = (f32[5,5,5]{2,1,0:T(8,128)S(1)}, f32[5,5,5]{2,1,0:T(8,128)}, u32[]{:S(2)}) copy-start(f32[5,5,5]{2,1,0:T(8,128)} %kernel_2.1) | copy-start | bytes 1504
  0.0 22.2 %copy-start.5 = (f32[5,5,5]{2,1,0:T(8,128)S(1)}, f32[5,5,5]{2,1,0:T(8,128)}, u32[]{:S(2)}) copy-start(f32[5,5,5]{2,1,0:T(8,128)} %kernel_1.1) | copy-start | bytes 1504
  6.0 37.7 %copy-start.3 = (bf16[128,128]{1,0:T(8,128)(2,1)S(1)}, bf16[128,128]{1,0:T(8,128)(2,1)}, u32[]{:S(2)}) copy-start(bf16[128,128]{1,0:T(8,128)(2,1)} %constant.12.clone.prol_1) | copy-start | bytes 98308
  6.0 37.7 %copy-start.4 = (bf16[128,128]{1,0:T(8,128)(2,1)S(1)}, bf16[128,128]{1,0:T(8,128)(2,1)}, u32[]{:S(2)}) copy-start(bf16[128,128]{1,0:T(8,128)(2,1)} %constant.11.clone.prol_2) | copy-start | bytes 98308
  6.0 1.3 %collective-permute-start = (f32[88,128]{1,0:T(8,128)S(1)}, f32[88,128]{1,0:T(8,128)S(1)}, u32[]{:S(2)}, u32[]{:S(2)}) collective-permute-start(f32[88,128]{1,0:T(8,128)S(1)} %get-tuple-element.29), channel_id=1, source_target_pairs={{0,16},{16,0},{32,48},{48,32},{1,17},{17,1},{33,49},{49,33},{2,18}... | collective-permute-start | bytes 135176 | tf_op jit(solution)/shard_map/ppermute | solution.py:621
  7.4 10.1 %collective-permute-start.1 = (f32[48,128]{1,0:T(8,128)S(1)}, f32[48,128]{1,0:T(8,128)S(1)}, u32[]{:S(2)}, u32[]{:S(2)}) collective-permute-start(f32[48,128]{1,0:T(8,128)S(1)} %shard_map.111.own), channel_id=1, source_target_pairs={{0,32},{16,48},{32,0},{48,16},{1,33},{17,49},{33,1},{49,17},{2,34}... | collective-permute-start | bytes 73736 | tf_op jit(solution)/shard_map/ppermute | solution.py:621
  14.6 1.0 %copy-start = (f32[32,32,128]{2,1,0:T(8,128)S(1)}, f32[32,32,128]{2,1,0:T(8,128)}, u32[]{:S(2)}) copy-start(f32[32,32,128]{2,1,0:T(8,128)} %get-tuple-element.26.packed) | copy-start | bytes 1572868
  15.7 0.9 %copy-start.2 = (f32[8,32,128]{2,1,0:T(8,128)S(1)}, f32[8,32,128]{2,1,0:T(8,128)}, u32[]{:S(2)}) copy-start(f32[8,32,128]{2,1,0:T(8,128)} %constant.10.clone.factors) | copy-start | bytes 393220
  17.6 29.0 %copy-start.1 = (bf16[8,128,128]{2,1,0:T(8,128)(2,1)S(1)}, bf16[8,128,128]{2,1,0:T(8,128)(2,1)}, u32[]{:S(2)}) copy-start(bf16[8,128,128]{2,1,0:T(8,128)(2,1)} %constant.13.clone.qz) | copy-start | bytes 786436
  17.9 8.8 %collective-permute-start.2 = (f32[72,128]{1,0:T(8,128)S(1)}, f32[72,128]{1,0:T(8,128)S(1)}, u32[]{:S(2)}, u32[]{:S(2)}) collective-permute-start(f32[72,128]{1,0:T(8,128)S(1)} %get-tuple-element.33), channel_id=1, source_target_pairs={{0,64},{64,0},{128,192},{192,128},{1,65},{65,1},{129,193},{193,129... | collective-permute-start | bytes 110600 | tf_op jit(solution)/shard_map/ppermute | solution.py:621
  19.5 7.2 %collective-permute-start.3 = (f32[72,128]{1,0:T(8,128)S(1)}, f32[72,128]{1,0:T(8,128)S(1)}, u32[]{:S(2)}, u32[]{:S(2)}) collective-permute-start(f32[72,128]{1,0:T(8,128)S(1)} %get-tuple-element.34), channel_id=1, source_target_pairs={{0,192},{64,128},{128,64},{192,0},{1,193},{65,129},{129,65},{193,1... | collective-permute-start | bytes 110600 | tf_op jit(solution)/shard_map/ppermute | solution.py:621
  21.6 5.1 %collective-permute-start.4 = (f32[8,128]{1,0:T(8,128)S(1)}, f32[8,128]{1,0:T(8,128)S(1)}, u32[]{:S(2)}, u32[]{:S(2)}) collective-permute-start(f32[8,128]{1,0:T(8,128)S(1)} %get-tuple-element.32.own), channel_id=1, source_target_pairs={{0,128},{64,192},{128,0},{192,64},{1,129},{65,193},{129,1},{193,65... | collective-permute-start | bytes 12296 | tf_op jit(solution)/shard_map/ppermute | solution.py:621
  27.4 11.4 %collective-permute-start.5 = (f32[96,128]{1,0:T(8,128)S(1)}, f32[96,128]{1,0:T(8,128)S(1)}, u32[]{:S(2)}, u32[]{:S(2)}) collective-permute-start(f32[96,128]{1,0:T(8,128)S(1)} %get-tuple-element.37), channel_id=1, source_target_pairs={{0,1},{1,2},{2,3},{3,4},{4,5},{5,6},{6,7},{7,8},{8,9},{9,10},{10,1... | collective-permute-start | bytes 147464 | tf_op jit(solution)/shard_map/ppermute | solution.py:633
  28.2 10.7 %collective-permute-start.6 = (f32[96,128]{1,0:T(8,128)S(1)}, f32[96,128]{1,0:T(8,128)S(1)}, u32[]{:S(2)}, u32[]{:S(2)}) collective-permute-start(f32[96,128]{1,0:T(8,128)S(1)} %get-tuple-element.38), channel_id=1, source_target_pairs={{0,47},{1,0},{2,1},{3,2},{4,3},{5,4},{6,5},{7,6},{8,7},{9,8},{10,9... | collective-permute-start | bytes 147464 | tf_op jit(solution)/shard_map/ppermute | solution.py:633
  29.5 5.8 %collective-permute-start.8 = (f32[16,128]{1,0:T(8,128)S(1)}, f32[16,128]{1,0:T(8,128)S(1)}, u32[]{:S(2)}, u32[]{:S(2)}) collective-permute-start(f32[16,128]{1,0:T(8,128)S(1)} %get-tuple-element.44.own), channel_id=1, source_target_pairs={{0,3},{1,2},{2,1},{3,0},{4,7},{5,6},{6,5},{7,4},{8,11},{9,10},{10,... | collective-permute-start | bytes 24584 | tf_op jit(solution)/shard_map/ppermute | solution.py:621
  33.7 5.2 %collective-permute-start.7 = (f32[16,128]{1,0:T(8,128)S(1)}, f32[16,128]{1,0:T(8,128)S(1)}, u32[]{:S(2)}, u32[]{:S(2)}) collective-permute-start(f32[16,128]{1,0:T(8,128)S(1)} %get-tuple-element.44.own), channel_id=1, source_target_pairs={{0,2},{1,3},{2,0},{3,1},{4,6},{5,7},{6,4},{7,5},{8,10},{9,11},{10,... | collective-permute-start | bytes 24584 | tf_op jit(solution)/shard_map/ppermute | solution.py:621
  39.3 7.3 %collective-permute-start.11 = (f32[4,16,128]{2,1,0:T(8,128)S(1)}, f32[4,16,128]{2,1,0:T(8,128)S(1)}, u32[]{:S(2)}, u32[]{:S(2)}) collective-permute-start(f32[4,16,128]{2,1,0:T(8,128)S(1)} %shard_map.116.piece_0), channel_id=1, source_target_pairs={{0,12},{1,13},{2,14},{3,15},{4,8},{5,9},{6,10},{7,11},{8,4},{9,5},... | collective-permute-start | bytes 98312 | tf_op jit(solution)/shard_map/ppermute | solution.py:621
  40.4 6.2 %collective-permute-start.10 = (f32[4,16,128]{2,1,0:T(8,128)S(1)}, f32[4,16,128]{2,1,0:T(8,128)S(1)}, u32[]{:S(2)}, u32[]{:S(2)}) collective-permute-start(f32[4,16,128]{2,1,0:T(8,128)S(1)} %shard_map.116.piece_0), channel_id=1, source_target_pairs={{0,8},{1,9},{2,10},{3,11},{4,12},{5,13},{6,14},{7,15},{8,0},{9,1},... | collective-permute-start | bytes 98312 | tf_op jit(solution)/shard_map/ppermute | solution.py:621
  40.4 6.2 %collective-permute-start.9 = (f32[4,16,128]{2,1,0:T(8,128)S(1)}, f32[4,16,128]{2,1,0:T(8,128)S(1)}, u32[]{:S(2)}, u32[]{:S(2)}) collective-permute-start(f32[4,16,128]{2,1,0:T(8,128)S(1)} %shard_map.116.piece_0), channel_id=1, source_target_pairs={{0,4},{1,5},{2,6},{3,7},{4,0},{5,1},{6,2},{7,3},{8,12},{9,13},{10,... | collective-permute-start | bytes 98312 | tf_op jit(solution)/shard_map/ppermute | solution.py:621

commit v5 on v4

--- a/solution.py
+++ b/solution.py
@@ -377,20 +377,24 @@
         face[base : base + rows, :] = total
 
 
-def window_kernel(own, from_low, from_high, got_2, got_3, out):
+def window_kernel(own, from_low, from_high, got_2, out):
     index, _ = place()
-    even, _, _ = nearest(index[2])
-    next_one = jnp.where(even, from_high[80:96, :], from_low[80:96, :])
-    pieces = (own[...], next_one, got_2[...], got_3[...])
+    early = lax.rem(index[2], 4) < 2
+    ends = got_2[...]
+    first, second, third = from_low[80:96, :], own[...], from_high[80:96, :]
+    pieces = (
+        jnp.where(early, first, ends),
+        jnp.where(early, second, first),
+        jnp.where(early, third, second),
+        jnp.where(early, ends, third),
+    )
     for group in range(4):
         total = None
-        for step, piece in enumerate(pieces):
-            apart = taps(
-                [(1.0, lanes_of(roll(piece, 24 * q - 32 * group), 32 * q, 8)) for q in range(4)]
-            )
-            at = 4 * lax.rem(jnp.bitwise_xor(index[2], step), 4)
-            moved = pltpu.roll(apart, at, 1)
-            total = moved if total is None else total + moved
+        for q in range(4):
+            for d, piece in enumerate(pieces):
+                to = 32 * q + 4 * d
+                moved = lanes_of(roll(piece, to - 32 * group - 8 * q), to, 8)
+                total = moved if total is None else total + moved
         out[group] = total
 
 
@@ -563,7 +567,9 @@
 ):
     index, sizes = place()
     lane = iota((8, 128), 1)
-    sources = [lax.rem(16 * (jnp.bitwise_xor(index[2], 4 * s) // 4) + 127, 128) for s in range(4)]
+    ring = lax.rem(index[2], 4)
+    first = 4 * (ring == 3).astype(jnp.int32) - 4 * (ring == 0).astype(jnp.int32) + 127
+    sources = [lax.rem(16 * lax.rem(index[2] // 4 + step, 4) + first, 128) for step in (0, 3, 1, 2)]
     for x in range(16):
         total = None
         for piece, at in zip((piece_0, piece_1, piece_2, piece_3), sources):
@@ -623,7 +629,7 @@
     ]
 
 
-def shift(value, by):
+def turn(value, by):
     size_y, size_z = lax.axis_size("gy"), lax.axis_size("gz")
     half = size_y // 2
     pairs = []
@@ -695,10 +701,10 @@
         (wide_y, raw, got_1, got_3, got_2, bands[0]),
         spaces={5: ANY},
     )
-    from_low, from_high = shift(to_high, 1), shift(to_low, -1)
-    got_2, got_3 = exchange((raw, raw), "gz", (2, 3))
-    window = call(window_kernel, shape(4, 16, 128), (raw, from_low, from_high, got_2, got_3))
-    pieces = [window] + exchange((window, window, window), "gz", (4, 8, 12))
+    from_low, from_high = turn(to_high, 1), turn(to_low, -1)
+    (got_2,) = exchange((raw,), "gz", (2,))
+    window = call(window_kernel, shape(4, 16, 128), (raw, from_low, from_high, got_2))
+    pieces = [window] + [turn(window, by) for by in (4, -4, 8)]
     base = call(
         near_kernel,
         shape(32, 32, 128),

time: 49.1 us -> 47.8 us (0.974)
  the two profiles are of different devices: /device:TPU:24 before, /device:TPU:32 now
where the time goes in v5:
time: 47.8 us; the launch traced here: 47.5 us
  starting transfers between devices  22.2 us (46%)
  Pallas kernels  15 us (31%)
  waiting for transfers between devices  7.42 us (16%)
  local copies, waits for them, and re-layouts  1.98 us (4%)
  other arithmetic  0.73 us (2%)
    pallas_call x9, Pallas kernels, call(): pl.pallas_call(kernel, out_shape=outs, in_specs=[spaces.get(i, VMEM) for...  15 us
    ppermute x6, starting transfers between devices, exchange(): lax.ppermute(value, axis, [(i, i ^ step) for i in range(size)])  11.8 us
    ppermute x5, starting transfers between devices, turn(): return lax.ppermute(value, ('gy', 'gz'), pairs)  10.4 us
    ppermute x6, waiting for transfers between devices, exchange(): lax.ppermute(value, axis, [(i, i ^ step) for i in range(size)])  7.41 us
    unnamed x16, local copies, waits for them, and re-layouts  1.98 us
  transfers between devices with their start and end apart: 11, of which 3 were waited for; matrix products, arithmetic and copies ran while one was open for 0% of the time, Pallas kernels for 13%

profile of v5, /device:TPU:32, one launch (start us, length us, event | category | flops | bytes accessed | tf_op | source)
XLA Modules:
  0.0 47.5 jit_solution(5452680453008643751)
XLA Ops:
  0.0 0.7 %multiply_add_fusion.codes = s32[384]{0:T(512)S(1)} fusion(s32[384]{0:T(512)} %param.12, s32[384]{0:T(512)} %param.13), kind=kLoop, calls=%fused_computation | loop fusion | flops 768 | bytes 4608 | tf_op jit(solution)/shard_map/add | solution.py:650
  0.7 5.2 %shard_map.109 = (f32[32,32,128]{2,1,0:T(8,128)}, f32[8,128]{1,0:T(8,128)S(1)}, f32[88,128]{1,0:T(8,128)S(1)}) custom-call(s32[384]{0:T(512)S(1)} %multiply_add_fusion.codes, f32[384,128]{1,0:T(8,128)} %charges_hbm.1, bf16[4608,128]{1,0:T(8,128)(2,1)} %bitcast.1), custom_call_target="tpu_custom_call" | custom-call | flops 1000000 | bytes 2097152 | tf_op jit(solution)/shard_map/pallas_call | solution.py:608
  6.0 0.0 copy-start.3
  6.0 0.0 copy-start.4
  6.0 0.1 collective-permute-start
  6.1 1.2 %collective-permute-done.got.got_1 = f32[88,128]{1,0:T(8,128)S(1)} collective-permute-done((f32[88,128]{1,0:T(8,128)S(1)}, f32[88,128]{1,0:T(8,128)S(1)}, u32[]{:S(2)}, u32[]{:S(2)}) %collective-permute-start) | collective-permute-done | bytes 45088 | tf_op jit(solution)/shard_map/ppermute | solution.py:627
  7.3 0.1 shard_map.111.own
  7.4 6.3 %collective-permute-start.1 = (f32[48,128]{1,0:T(8,128)S(1)}, f32[48,128]{1,0:T(8,128)S(1)}, u32[]{:S(2)}, u32[]{:S(2)}) collective-permute-start(f32[48,128]{1,0:T(8,128)S(1)} %shard_map.111.own), channel_id=1, source_target_pairs={{0,32},{16,48},{32,0},{48,16},{1,33},{17,49},{33,1},{49,17},{2,34}... | collective-permute-start | bytes 73736 | tf_op jit(solution)/shard_map/ppermute | solution.py:627
  13.7 1.0 %copy-done = f32[32,32,128]{2,1,0:T(8,128)S(1)} copy-done((f32[32,32,128]{2,1,0:T(8,128)S(1)}, f32[32,32,128]{2,1,0:T(8,128)}, u32[]{:S(2)}) %copy-start) | copy-done | bytes 524312
  14.8 0.9 %copy-done.2 = f32[8,32,128]{2,1,0:T(8,128)S(1)} copy-done((f32[8,32,128]{2,1,0:T(8,128)S(1)}, f32[8,32,128]{2,1,0:T(8,128)}, u32[]{:S(2)}) %copy-start.2) | copy-done | bytes 131096
  15.7 1.0 %shard_map.110 = (bf16[1024,896]{1,0:T(8,128)(2,1)S(1)}, bf16[1024,896]{1,0:T(8,128)(2,1)S(1)}, bf16[1024,256]{1,0:T(8,128)(2,1)S(1)}, f32[32,40,128]{2,1,0:T(8,128)S(1)}) custom-call(f32[8,32,128]{2,1,0:T(8,128)S(1)} %copy-done.2, f32[32,32,128]{2,1,0:T(8,128)S(1)} %copy-done), custom_call_target="tpu_custom_call" | custom-call | flops 1000000 | bytes 2097152 | tf_op jit(solution)/shard_map/pallas_call | solution.py:608
  16.6 0.0 copy-start.1
  16.7 0.3 shard_map.112
  17.0 1.6 %collective-permute-start.2 = (f32[72,128]{1,0:T(8,128)S(1)}, f32[72,128]{1,0:T(8,128)S(1)}, u32[]{:S(2)}, u32[]{:S(2)}) collective-permute-start(f32[72,128]{1,0:T(8,128)S(1)} %get-tuple-element.33), channel_id=1, source_target_pairs={{0,64},{64,0},{128,192},{192,128},{1,65},{65,1},{129,193},{193,129... | collective-permute-start | bytes 110600 | tf_op jit(solution)/shard_map/ppermute | solution.py:627
  18.6 2.1 %collective-permute-start.3 = (f32[72,128]{1,0:T(8,128)S(1)}, f32[72,128]{1,0:T(8,128)S(1)}, u32[]{:S(2)}, u32[]{:S(2)}) collective-permute-start(f32[72,128]{1,0:T(8,128)S(1)} %get-tuple-element.34), channel_id=1, source_target_pairs={{0,192},{64,128},{128,64},{192,0},{1,193},{65,129},{129,65},{193,1... | collective-permute-start | bytes 110600 | tf_op jit(solution)/shard_map/ppermute | solution.py:627
  20.7 0.6 %collective-permute-start.4 = (f32[8,128]{1,0:T(8,128)S(1)}, f32[8,128]{1,0:T(8,128)S(1)}, u32[]{:S(2)}, u32[]{:S(2)}) collective-permute-start(f32[8,128]{1,0:T(8,128)S(1)} %get-tuple-element.32.own), channel_id=1, source_target_pairs={{0,128},{64,192},{128,0},{192,64},{1,129},{65,193},{129,1},{193,65... | collective-permute-start | bytes 12296 | tf_op jit(solution)/shard_map/ppermute | solution.py:627
  21.3 2.3 %shard_map.113 = (bf16[256,256]{1,0:T(8,128)(2,1)S(1)}, bf16[256,256]{1,0:T(8,128)(2,1)S(1)}, bf16[256,128]{1,0:T(8,128)(2,1)S(1)}, bf16[256,128]{1,0:T(8,128)(2...) custom-call(f32[5,5,5]{2,1,0:T(8,128)S(1)} %copy-done.5, f32[5,5,5]{2,1,0:T(8,128)S(1)} %copy-done.6, ...), custom_call_target="tpu_custom_call" | custom-call | flops 1000000 | bytes 2097152 | tf_op jit(solution)/shard_map/pallas_call | solution.py:608
  23.7 2.1 %collective-permute-done.4.got_2 = f32[8,128]{1,0:T(8,128)S(1)} collective-permute-done((f32[8,128]{1,0:T(8,128)S(1)}, f32[8,128]{1,0:T(8,128)S(1)}, u32[]{:S(2)}, u32[]{:S(2)}) %collective-permute-start.4) | collective-permute-done | bytes 4128 | tf_op jit(solution)/shard_map/ppermute | solution.py:627
  25.8 0.0 collective-permute-done.3.got_3
  25.8 0.7 %shard_map.114 = (f32[36,40,128]{2,1,0:T(8,128)S(1)}, f32[16,128]{1,0:T(8,128)S(1)}, f32[96,128]{1,0:T(8,128)S(1)}, f32[96,128]{1,0:T(8,128)S(1)}) custom-call(f32[32,40,128]{2,1,0:T(8,128)S(1)} %get-tuple-element.31.wide_y, f32[8,128]{1,0:T(8,128)S(1)} %get-tuple-element.32.own, f32[72,128]{1,0:T(8,128)S(1)} %collective-permute-done.2.got_1, ...), custom_call_target="tpu_custom_call" | custom-call | flops 1000000 | bytes 2097152 | tf_op jit(solution)/shard_map/pallas_call | solution.py:608
  26.5 1.7 %collective-permute-start.5 = (f32[96,128]{1,0:T(8,128)S(1)}, f32[96,128]{1,0:T(8,128)S(1)}, u32[]{:S(2)}, u32[]{:S(2)}) collective-permute-start(f32[96,128]{1,0:T(8,128)S(1)} %get-tuple-element.37), channel_id=1, source_target_pairs={{0,1},{1,2},{2,3},{3,4},{4,5},{5,6},{6,7},{7,8},{8,9},{9,10},{10,1... | collective-permute-start | bytes 147464 | tf_op jit(solution)/shard_map/ppermute | solution.py:639
  28.2 2.6 %collective-permute-start.6 = (f32[96,128]{1,0:T(8,128)S(1)}, f32[96,128]{1,0:T(8,128)S(1)}, u32[]{:S(2)}, u32[]{:S(2)}) collective-permute-start(f32[96,128]{1,0:T(8,128)S(1)} %get-tuple-element.38), channel_id=1, source_target_pairs={{0,47},{1,0},{2,1},{3,2},{4,3},{5,4},{6,5},{7,6},{8,7},{9,8},{10,9... | collective-permute-start | bytes 147464 | tf_op jit(solution)/shard_map/ppermute | solution.py:639
  30.7 1.1 %collective-permute-start.7 = (f32[16,128]{1,0:T(8,128)S(1)}, f32[16,128]{1,0:T(8,128)S(1)}, u32[]{:S(2)}, u32[]{:S(2)}) collective-permute-start(f32[16,128]{1,0:T(8,128)S(1)} %get-tuple-element.44.own), channel_id=1, source_target_pairs={{0,2},{1,3},{2,0},{3,1},{4,6},{5,7},{6,4},{7,5},{8,10},{9,11},{10,... | collective-permute-start | bytes 24584 | tf_op jit(solution)/shard_map/ppermute | solution.py:627
  31.8 4.1 %collective-permute-done.7.got_2 = f32[16,128]{1,0:T(8,128)S(1)} collective-permute-done((f32[16,128]{1,0:T(8,128)S(1)}, f32[16,128]{1,0:T(8,128)S(1)}, u32[]{:S(2)}, u32[]{:S(2)}) %collective-permute-start.7) | collective-permute-done | bytes 8224 | tf_op jit(solution)/shard_map/ppermute | solution.py:627
  35.9 0.0 collective-permute-done.5.from_low
  35.9 0.0 collective-permute-done.6.from_high
  35.9 0.2 shard_map.116.piece_0
  36.1 1.8 %collective-permute-start.10 = (f32[4,16,128]{2,1,0:T(8,128)S(1)}, f32[4,16,128]{2,1,0:T(8,128)S(1)}, u32[]{:S(2)}, u32[]{:S(2)}) collective-permute-start(f32[4,16,128]{2,1,0:T(8,128)S(1)} %shard_map.116.piece_0), channel_id=1, source_target_pairs={{0,8},{1,9},{2,10},{3,11},{4,12},{5,13},{6,14},{7,15},{8,32},{9,33... | collective-permute-start | bytes 98312 | tf_op jit(solution)/shard_map/ppermute | solution.py:639
  37.9 1.4 %collective-permute-start.9 = (f32[4,16,128]{2,1,0:T(8,128)S(1)}, f32[4,16,128]{2,1,0:T(8,128)S(1)}, u32[]{:S(2)}, u32[]{:S(2)}) collective-permute-start(f32[4,16,128]{2,1,0:T(8,128)S(1)} %shard_map.116.piece_0), channel_id=1, source_target_pairs={{0,44},{1,45},{2,46},{3,47},{4,0},{5,1},{6,2},{7,3},{8,4},{9,5},{1... | collective-permute-start | bytes 98312 | tf_op jit(solution)/shard_map/ppermute | solution.py:639
  39.3 3.0 %collective-permute-start.8 = (f32[4,16,128]{2,1,0:T(8,128)S(1)}, f32[4,16,128]{2,1,0:T(8,128)S(1)}, u32[]{:S(2)}, u32[]{:S(2)}) collective-permute-start(f32[4,16,128]{2,1,0:T(8,128)S(1)} %shard_map.116.piece_0), channel_id=1, source_target_pairs={{0,4},{1,5},{2,6},{3,7},{4,8},{5,9},{6,10},{7,11},{8,12},{9,13},{1... | collective-permute-start | bytes 98312 | tf_op jit(solution)/shard_map/ppermute | solution.py:639
  42.3 2.9 %shard_map.115.base = f32[32,32,128]{2,1,0:T(8,128)S(1)} custom-call(f32[36,40,128]{2,1,0:T(8,128)S(1)} %get-tuple-element.36.wide, f32[96,128]{1,0:T(8,128)S(1)} %collective-permute-done.5.from_low, f32[96,128]{1,0:T(8,128)S(1)} %collective-permute-done.6.from_high, bf16[256,256]{1,0:T(8,128)(2,1)S(1)} %get-tuple-element.35.after.b1h, ...), custom_call_target="tpu_custom_call" | custom-call | flops 1000000 | bytes 2097152 | tf_op jit(solution)/shard_map/pallas_call | solution.py:608
  45.2 2.3 %shard_map.117 = f32[32,32,32]{2,1,0:T(8,128)} custom-call(f32[32,32,128]{2,1,0:T(8,128)S(1)} %shard_map.115.base, f32[4,16,128]{2,1,0:T(8,128)S(1)} %shard_map.116.piece_0, f32[4,16,128]{2,1,0:T(8,128)S(1)} %collective-permute-done.8.piece_1, f32[4,16,128]{2,1,0:T(8,128)S(1)} %collective-permute-done.9.piece_2, ...), custom_call_target="tpu_custom_call" | custom-call | flops 1000000 | bytes 2097152 | tf_op jit(solution)/shard_map/pallas_call | solution.py:608
  (16 shorter events, 0.0 us)
Async XLA Ops:
  0.0 21.3 %copy-start.7 = (f32[5,5,5]{2,1,0:T(8,128)S(1)}, f32[5,5,5]{2,1,0:T(8,128)}, u32[]{:S(2)}) copy-start(f32[5,5,5]{2,1,0:T(8,128)} %kernel_3.1) | copy-start | bytes 1504
  0.0 21.3 %copy-start.6 = (f32[5,5,5]{2,1,0:T(8,128)S(1)}, f32[5,5,5]{2,1,0:T(8,128)}, u32[]{:S(2)}) copy-start(f32[5,5,5]{2,1,0:T(8,128)} %kernel_2.1) | copy-start | bytes 1504
  0.0 21.3 %copy-start.5 = (f32[5,5,5]{2,1,0:T(8,128)S(1)}, f32[5,5,5]{2,1,0:T(8,128)}, u32[]{:S(2)}) copy-start(f32[5,5,5]{2,1,0:T(8,128)} %kernel_1.1) | copy-start | bytes 1504
  6.0 36.3 %copy-start.3 = (bf16[128,128]{1,0:T(8,128)(2,1)S(1)}, bf16[128,128]{1,0:T(8,128)(2,1)}, u32[]{:S(2)}) copy-start(bf16[128,128]{1,0:T(8,128)(2,1)} %constant.12.clone.prol_1) | copy-start | bytes 98308
  6.0 36.3 %copy-start.4 = (bf16[128,128]{1,0:T(8,128)(2,1)S(1)}, bf16[128,128]{1,0:T(8,128)(2,1)}, u32[]{:S(2)}) copy-start(bf16[128,128]{1,0:T(8,128)(2,1)} %constant.11.clone.prol_2) | copy-start | bytes 98308
  6.0 1.3 %collective-permute-start = (f32[88,128]{1,0:T(8,128)S(1)}, f32[88,128]{1,0:T(8,128)S(1)}, u32[]{:S(2)}, u32[]{:S(2)}) collective-permute-start(f32[88,128]{1,0:T(8,128)S(1)} %get-tuple-element.29), channel_id=1, source_target_pairs={{0,16},{16,0},{32,48},{48,32},{1,17},{17,1},{33,49},{49,33},{2,18}... | collective-permute-start | bytes 135176 | tf_op jit(solution)/shard_map/ppermute | solution.py:627
  7.4 9.2 %collective-permute-start.1 = (f32[48,128]{1,0:T(8,128)S(1)}, f32[48,128]{1,0:T(8,128)S(1)}, u32[]{:S(2)}, u32[]{:S(2)}) collective-permute-start(f32[48,128]{1,0:T(8,128)S(1)} %shard_map.111.own), channel_id=1, source_target_pairs={{0,32},{16,48},{32,0},{48,16},{1,33},{17,49},{33,1},{49,17},{2,34}... | collective-permute-start | bytes 73736 | tf_op jit(solution)/shard_map/ppermute | solution.py:627
  13.7 1.0 %copy-start = (f32[32,32,128]{2,1,0:T(8,128)S(1)}, f32[32,32,128]{2,1,0:T(8,128)}, u32[]{:S(2)}) copy-start(f32[32,32,128]{2,1,0:T(8,128)} %get-tuple-element.26.packed) | copy-start | bytes 1572868
  14.7 0.9 %copy-start.2 = (f32[8,32,128]{2,1,0:T(8,128)S(1)}, f32[8,32,128]{2,1,0:T(8,128)}, u32[]{:S(2)}) copy-start(f32[8,32,128]{2,1,0:T(8,128)} %constant.10.clone.factors) | copy-start | bytes 393220
  16.6 28.6 %copy-start.1 = (bf16[8,128,128]{2,1,0:T(8,128)(2,1)S(1)}, bf16[8,128,128]{2,1,0:T(8,128)(2,1)}, u32[]{:S(2)}) copy-start(bf16[8,128,128]{2,1,0:T(8,128)(2,1)} %constant.13.clone.qz) | copy-start | bytes 786436
  17.0 8.8 %collective-permute-start.2 = (f32[72,128]{1,0:T(8,128)S(1)}, f32[72,128]{1,0:T(8,128)S(1)}, u32[]{:S(2)}, u32[]{:S(2)}) collective-permute-start(f32[72,128]{1,0:T(8,128)S(1)} %get-tuple-element.33), channel_id=1, source_target_pairs={{0,64},{64,0},{128,192},{192,128},{1,65},{65,1},{129,193},{193,129... | collective-permute-start | bytes 110600 | tf_op jit(solution)/shard_map/ppermute | solution.py:627
  18.6 7.2 %collective-permute-start.3 = (f32[72,128]{1,0:T(8,128)S(1)}, f32[72,128]{1,0:T(8,128)S(1)}, u32[]{:S(2)}, u32[]{:S(2)}) collective-permute-start(f32[72,128]{1,0:T(8,128)S(1)} %get-tuple-element.34), channel_id=1, source_target_pairs={{0,192},{64,128},{128,64},{192,0},{1,193},{65,129},{129,65},{193,1... | collective-permute-start | bytes 110600 | tf_op jit(solution)/shard_map/ppermute | solution.py:627
  20.7 5.1 %collective-permute-start.4 = (f32[8,128]{1,0:T(8,128)S(1)}, f32[8,128]{1,0:T(8,128)S(1)}, u32[]{:S(2)}, u32[]{:S(2)}) collective-permute-start(f32[8,128]{1,0:T(8,128)S(1)} %get-tuple-element.32.own), channel_id=1, source_target_pairs={{0,128},{64,192},{128,0},{192,64},{1,129},{65,193},{129,1},{193,65... | collective-permute-start | bytes 12296 | tf_op jit(solution)/shard_map/ppermute | solution.py:627
  26.5 9.4 %collective-permute-start.5 = (f32[96,128]{1,0:T(8,128)S(1)}, f32[96,128]{1,0:T(8,128)S(1)}, u32[]{:S(2)}, u32[]{:S(2)}) collective-permute-start(f32[96,128]{1,0:T(8,128)S(1)} %get-tuple-element.37), channel_id=1, source_target_pairs={{0,1},{1,2},{2,3},{3,4},{4,5},{5,6},{6,7},{7,8},{8,9},{9,10},{10,1... | collective-permute-start | bytes 147464 | tf_op jit(solution)/shard_map/ppermute | solution.py:639
  28.2 7.7 %collective-permute-start.6 = (f32[96,128]{1,0:T(8,128)S(1)}, f32[96,128]{1,0:T(8,128)S(1)}, u32[]{:S(2)}, u32[]{:S(2)}) collective-permute-start(f32[96,128]{1,0:T(8,128)S(1)} %get-tuple-element.38), channel_id=1, source_target_pairs={{0,47},{1,0},{2,1},{3,2},{4,3},{5,4},{6,5},{7,6},{8,7},{9,8},{10,9... | collective-permute-start | bytes 147464 | tf_op jit(solution)/shard_map/ppermute | solution.py:639
  30.7 5.2 %collective-permute-start.7 = (f32[16,128]{1,0:T(8,128)S(1)}, f32[16,128]{1,0:T(8,128)S(1)}, u32[]{:S(2)}, u32[]{:S(2)}) collective-permute-start(f32[16,128]{1,0:T(8,128)S(1)} %get-tuple-element.44.own), channel_id=1, source_target_pairs={{0,2},{1,3},{2,0},{3,1},{4,6},{5,7},{6,4},{7,5},{8,10},{9,11},{10,... | collective-permute-start | bytes 24584 | tf_op jit(solution)/shard_map/ppermute | solution.py:627
  36.1 9.1 %collective-permute-start.10 = (f32[4,16,128]{2,1,0:T(8,128)S(1)}, f32[4,16,128]{2,1,0:T(8,128)S(1)}, u32[]{:S(2)}, u32[]{:S(2)}) collective-permute-start(f32[4,16,128]{2,1,0:T(8,128)S(1)} %shard_map.116.piece_0), channel_id=1, source_target_pairs={{0,8},{1,9},{2,10},{3,11},{4,12},{5,13},{6,14},{7,15},{8,32},{9,33... | collective-permute-start | bytes 98312 | tf_op jit(solution)/shard_map/ppermute | solution.py:639
  37.9 7.3 %collective-permute-start.9 = (f32[4,16,128]{2,1,0:T(8,128)S(1)}, f32[4,16,128]{2,1,0:T(8,128)S(1)}, u32[]{:S(2)}, u32[]{:S(2)}) collective-permute-start(f32[4,16,128]{2,1,0:T(8,128)S(1)} %shard_map.116.piece_0), channel_id=1, source_target_pairs={{0,44},{1,45},{2,46},{3,47},{4,0},{5,1},{6,2},{7,3},{8,4},{9,5},{1... | collective-permute-start | bytes 98312 | tf_op jit(solution)/shard_map/ppermute | solution.py:639
  39.3 5.9 %collective-permute-start.8 = (f32[4,16,128]{2,1,0:T(8,128)S(1)}, f32[4,16,128]{2,1,0:T(8,128)S(1)}, u32[]{:S(2)}, u32[]{:S(2)}) collective-permute-start(f32[4,16,128]{2,1,0:T(8,128)S(1)} %shard_map.116.piece_0), channel_id=1, source_target_pairs={{0,4},{1,5},{2,6},{3,7},{4,8},{5,9},{6,10},{7,11},{8,12},{9,13},{1... | collective-permute-start | bytes 98312 | tf_op jit(solution)/shard_map/ppermute | solution.py:639

commit v6 on v5

--- a/solution.py
+++ b/solution.py
@@ -19,6 +19,7 @@
 VMEM = pl.BlockSpec(memory_space=pltpu.VMEM)
 SMEM = pl.BlockSpec(memory_space=pltpu.SMEM)
 HBM = pl.BlockSpec(memory_space=pltpu.HBM)
+ANY = pl.BlockSpec(memory_space=pl.ANY)
 
 
 def weight(t):
@@ -155,8 +156,8 @@
 
 def deposit_kernel(
     codes, charges_hbm, spline_hbm,
-    packed, raw_out, face,
-    charges, spline, wide, patch, fine, buf_2, buf_3, buf_4, second_ref, third_ref, sems,
+    packed_hbm, raw_out, face,
+    packed, charges, spline, wide, patch, fine, buf_2, buf_3, buf_4, sems,
 ):
     where = place()
     index, sizes = where
@@ -230,13 +231,16 @@
     second = taps([(W[t], buf_2[:, pl.ds(t, 24, stride=2), :]) for t in range(5)])
     second = dot_exact(as_rows(second), rest_2).reshape(SPAN_2, 24, 128)
     second = jnp.where(inside_mask(second.shape, SPAN_2, 17, where), second, 0.0)
-    second_ref[...] = second
     for p, plane in enumerate(restrict_planes(lambda x: second[x], SPAN_3, SPAN_2, 3)):
         buf_3[p, 3:27, :] = plane
     third = taps([(W[t], buf_3[:, pl.ds(t, 16, stride=2), :]) for t in range(5)])
     third = dot_exact(as_rows(third), rest_3).reshape(SPAN_3, 16, 128)
     third = jnp.where(inside_mask(third.shape, SPAN_3, 9, where), third, 0.0)
-    third_ref[...] = third
+    packed[...] = fine[...]
+    packed[0:SPAN_2, 0:24, :] += roll(second, SEC)
+    packed[0:SPAN_3, 0:16, :] += roll(third, THI)
+    leave = pltpu.make_async_copy(packed, packed_hbm, sems.at[4])
+    leave.start()
     for p, plane in enumerate(restrict_planes(lambda x: third[x], SPAN_4, SPAN_3, 3)):
         buf_4[p, 3:19, :] = plane
     last = taps([(W[t], buf_4[:, pl.ds(t, 8, stride=2), :]) for t in range(5)])
@@ -245,16 +249,14 @@
     raw = taps([(1.0, roll(last[x], 8 * x)) for x in range(SPAN_4)])
     raw_out[...] = raw
 
-    packed[...] = fine[...]
-    packed[0:SPAN_2, 0:24, :] += roll(second, SEC)
-    packed[0:SPAN_3, 0:16, :] += roll(third, THI)
     even, _, _ = nearest(index[1])
-    low = pack_y(packed, (0, 0, 0))
-    high = pack_y(packed, (30, 14, 6))
-    for v in range(5):
+    low = pack_y(packed, FIRST_ROWS)
+    high = pack_y(packed, LAST_ROWS)
+    for v in range(4):
         face[8 * v : 8 * v + 8, :] = jnp.where(even, high[v], low[v])
-        face[40 + 8 * v : 48 + 8 * v, :] = jnp.where(even, low[v], high[v])
-    face[80:88, :] = raw
+        face[FACE + 8 * v : FACE + 8 * v + 8, :] = jnp.where(even, low[v], high[v])
+    face[2 * FACE : 2 * FACE + 8, :] = raw
+    leave.wait()
 
 
 def spot_1(p):
@@ -266,14 +268,27 @@
 
 
 def spot_3(p):
-    return 4, 0, p * 11
-
-
-LEVELS = ((32, 2, 0, 32, spot_1), (SPAN_2, 4, SEC, 18, spot_2), (SPAN_3, 5, THI, 11, spot_3))
+    return 3, 4, p * 11
+
+
+def spot_4(p):
+    return 3, p // 5, 72 + p % 5 * 11
+
+
+FACE = 32
+LEVELS = (
+    (32, 2, 0, 32, spot_1),
+    (SPAN_2, 4, SEC, 18, spot_2),
+    (SPAN_3, 4, THI, 11, spot_3),
+    (SPAN_3, 1, THI, 11, spot_4),
+)
+FIRST_ROWS = (0, 0, 0, 4)
+LAST_ROWS = (30, 14, 6, 10)
+ROWS_ABOVE = (34, 18, 10, 14)
 
 
 def pack_y(source, at):
-    tiles = [jnp.zeros((8, 128), F32) for _ in range(5)]
+    tiles = [jnp.zeros((8, 128), F32) for _ in range(4)]
     row, at_lane = iota((8, 128), 0), iota((8, 128), 1)
     for (planes, count, lane, width, spot), start in zip(LEVELS, at):
         for p in range(planes):
@@ -296,20 +311,21 @@
 
 def relay_kernel(raw, got, out):
     index, _ = place()
-    out[0:40, :] = got[40:80, :]
+    out[0:FACE, :] = got[FACE : 2 * FACE, :]
     partner = jnp.bitwise_xor(index[1], 1)
-    out[40:48, :] = place_y(raw[...], index[1]) + place_y(got[80:88, :], partner)
+    other = got[2 * FACE : 2 * FACE + 8, :]
+    out[FACE : FACE + 8, :] = place_y(raw[...], index[1]) + place_y(other, partner)
 
 
 def widen_y_kernel(framed, own, got_1, got_2, after, out, raw_out, face_1, face_3):
     index, _ = place()
     even, one, two = nearest(index[1])
-    total = own[40:48, :] + got_2[40:48, :]
+    total = own[FACE : FACE + 8, :] + got_2[FACE : FACE + 8, :]
     raw_out[...] = total
-    a, b = got_1[0:40, :], got_2[0:40, :]
+    a, b = got_1[0:FACE, :], got_2[0:FACE, :]
     low = jnp.where(even, 0.0, a) + jnp.where(two, b, 0.0)
     high = jnp.where(even, a, 0.0) + jnp.where(one, b, 0.0)
-    for face, at in ((low, (0, 0, 0)), (high, (34, 18, 10))):
+    for face, at in ((low, FIRST_ROWS), (high, ROWS_ABOVE)):
         for (planes, count, lane, width, spot), start in zip(LEVELS, at):
             for p in range(planes):
                 v, r, to = spot(p)
@@ -358,15 +374,12 @@
             out[at[2] + k, 0:16, :] += lanes_of(roll(face[0:16], -11 * k), THI, 11)
     for ref, high in ((to_high, True), (to_low, False)):
         pack_z(out, ref, high)
-        ref[80:96, :] = total
+        ref[64:80, :] = total
 
 
 def pack_z(source, face, to_high):
-    for base, rows, planes, count, lane, high in (
-        (0, 40, 36, 2, 0, 30),
-        (40, 24, 22, 4, SEC, 14),
-        (64, 16, 15, 5, THI, 6),
-    ):
+    sums = []
+    for rows, planes, count, lane, high in ((40, 36, 2, 0, 30), (24, 22, 4, SEC, 14), (16, 15, 5, THI, 6)):
         first = lane + high if to_high else lane
         at = iota((rows, 128), 1)
         wanted = (at >= first) & (at < first + count)
@@ -374,26 +387,35 @@
         for x in range(planes):
             kept = jnp.where(wanted, source[x, 0:rows, :], 0.0)
             total = total + roll(kept, count * x - first)
-        face[base : base + rows, :] = total
+        sums.append(total)
+    face[0:40, :] = sums[0]
+    face[40:64, :] = sums[1]
+    face[0:16, :] += lanes_of(roll(sums[2], 72), 72, 55)
+    face[40:56, :] += lanes_of(roll(sums[2], 88 - 55), 88, 20)
+
+
+def unpack_z(message):
+    third = lanes_of(roll(message[0:16], -72), 0, 55) + lanes_of(roll(message[40:56], 55 - 88), 55, 20)
+    return message[0:40], message[40:64], third
 
 
 def window_kernel(own, from_low, from_high, got_2, out):
     index, _ = place()
     early = lax.rem(index[2], 4) < 2
     ends = got_2[...]
-    first, second, third = from_low[80:96, :], own[...], from_high[80:96, :]
+    first, second, third = from_low[64:80, :], own[...], from_high[64:80, :]
     pieces = (
         jnp.where(early, first, ends),
         jnp.where(early, second, first),
         jnp.where(early, third, second),
         jnp.where(early, ends, third),
     )
-    for group in range(4):
+    for group in range(3):
         total = None
-        for q in range(4):
+        for q in range(min(6, 16 - 6 * group)):
             for d, piece in enumerate(pieces):
-                to = 32 * q + 4 * d
-                moved = lanes_of(roll(piece, to - 32 * group - 8 * q), to, 8)
+                to = 20 * q + 4 * d
+                moved = lanes_of(roll(piece, to - 48 * group - 8 * q), to, 8)
                 total = moved if total is None else total + moved
         out[group] = total
 
@@ -502,19 +524,19 @@
 ):
     where = place()
     index, sizes = where
-    low_msg = jnp.where(index[2] == 0, 0.0, from_low[...])
-    high_msg = jnp.where(index[2] == sizes[2] - 1, 0.0, from_high[...])
-
-    def halo(x, rows, base, count, low_at, high_at):
-        low = roll(low_msg[base : base + rows], low_at - count * x)
-        high = roll(high_msg[base : base + rows], high_at - count * x)
+    low_faces = unpack_z(jnp.where(index[2] == 0, 0.0, from_low[0:64, :]))
+    high_faces = unpack_z(jnp.where(index[2] == sizes[2] - 1, 0.0, from_high[0:64, :]))
+
+    def halo(x, level, count, low_at, high_at):
+        low = roll(low_faces[level], low_at - count * x)
+        high = roll(high_faces[level], high_at - count * x)
         return lanes_of(low, low_at, 5 * count) + lanes_of(high, high_at, 5 * count)
 
     planes = [lanes_of(wide[x, 0:16, :], THI, 11) for x in range(15)]
     left = []
     for x in range(SPAN_3):
         main = taps([(1.0, roll(planes[x + a], 11 * a - THI)) for a in range(5)])
-        left.append(main + halo(x, 16, 64, 5, 64, 96))
+        left.append(main + halo(x, 2, 5, 64, 96))
     left = jnp.concatenate(left, axis=0)
     near_3[...] = jnp.zeros_like(near_3)
     near_3[:, 0:16, :] = dot_split(left, b3h[...], b3l[...]).reshape(SPAN_3, 16, 128)
@@ -528,7 +550,7 @@
     left_a, left_b = [], []
     for x in range(SPAN_2):
         left_a.append(taps([(1.0, roll(planes[x + a], 18 * a - SEC)) for a in range(5)]))
-        left_b.append(halo(x, 24, 40, 4, 0, 32))
+        left_b.append(halo(x, 1, 4, 0, 32))
     left = jnp.concatenate(
         [jnp.concatenate(left_a, axis=0), jnp.concatenate(left_b, axis=0)], axis=1
     )
@@ -547,7 +569,7 @@
     left_a, left_b = [], []
     for x in range(32):
         left_a.append(taps([(1.0, roll(planes[x + a], 32 * a)) for a in range(4)]))
-        left_b.append(planes[x + 4] + halo(x, 40, 0, 2, 32, 64))
+        left_b.append(planes[x + 4] + halo(x, 0, 2, 32, 64))
     left = jnp.concatenate(
         [jnp.concatenate(left_a, axis=0), jnp.concatenate(left_b, axis=0)], axis=1
     )
@@ -562,8 +584,8 @@
 
 def top_kernel(
     base, piece_0, piece_1, piece_2, piece_3, green_high, green_low, rise, qz,
-    out,
-    fourth,
+    out_hbm,
+    fourth, out, sems,
 ):
     index, sizes = place()
     lane = iota((8, 128), 1)
@@ -573,8 +595,8 @@
     for x in range(16):
         total = None
         for piece, at in zip((piece_0, piece_1, piece_2, piece_3), sources):
-            kept = lanes_of(piece[x // 4], 32 * (x % 4), 32)
-            moved = pltpu.roll(kept, lax.rem(at + 128 - 32 * (x % 4), 128), 1)
+            kept = lanes_of(piece[x // 6], 20 * (x % 6), 20)
+            moved = pltpu.roll(kept, lax.rem(at + 128 - 20 * (x % 6), 128), 1)
             total = moved if total is None else total + moved
         total = total + roll(total, 64)
         fourth[x] = jnp.where(lane < 64, total[0:8], total[8:16])
@@ -599,17 +621,26 @@
     variant = jnp.where(index[2] == 0, 1, 0) + jnp.where(index[2] == sizes[2] - 1, 2, 0)
     high, low = split(dot_split(tops, qz[variant], qz[4 + variant]))
     right = jnp.concatenate([high, high, low, jnp.zeros_like(low)], axis=0)
-    far = dot(rise[...], right)
-    out[...] = (base[...] + far.reshape(32, 32, 128))[:, :, 0:32]
-
-
-def call(kernel, outs, ins, scratch=(), megabytes=16, spaces=None, aliases=None):
-    spaces = spaces or {}
+    copies = []
+    for part in range(4):
+        planes = slice(8 * part, 8 * part + 8)
+        far = dot(rise[256 * part : 256 * part + 256, :], right)
+        out[planes] = (base[planes] + far.reshape(8, 32, 128))[:, :, 0:32]
+        copies.append(pltpu.make_async_copy(out.at[planes], out_hbm.at[planes], sems.at[part]))
+        copies[-1].start()
+    for copy in copies:
+        copy.wait()
+
+
+def call(kernel, outs, ins, scratch=(), megabytes=16, spaces=None, out_spaces=None, aliases=None):
+    spaces, out_spaces = spaces or {}, out_spaces or {}
+    single = not isinstance(outs, tuple)
+    out_specs = [out_spaces.get(i, VMEM) for i in range(1 if single else len(outs))]
     return pl.pallas_call(
         kernel,
         out_shape=outs,
         in_specs=[spaces.get(i, VMEM) for i in range(len(ins))],
-        out_specs=jax.tree.map(lambda _: VMEM, outs),
+        out_specs=out_specs[0] if single else out_specs,
         scratch_shapes=list(scratch),
         input_output_aliases=aliases or {},
         compiler_params=pltpu.CompilerParams(vmem_limit_bytes=int(megabytes * 2**20)),
@@ -639,16 +670,14 @@
     return lax.ppermute(value, ("gy", "gz"), pairs)
 
 
-ANY = pl.BlockSpec(memory_space=pl.ANY)
-
-
 def shards(charges, counts, slots, spline, kernel_fine, kernel_mid, kernel_coarse):
     cells = charges.shape[0]
     packed, raw, face = call(
         deposit_kernel,
-        (shape(32, 32, 128), shape(8, 128), shape(88, 128)),
+        (shape(32, 32, 128), shape(8, 128), shape(2 * FACE + 8, 128)),
         (256 * slots + counts, charges, spline.reshape(cells * 12, ATOMS)),
         (
+            pltpu.VMEM((32, 32, 128), F32),
             pltpu.VMEM((cells, ATOMS), F32),
             pltpu.VMEM((cells * 12, 128), BF16),
             pltpu.VMEM((cells * 12, 128), F32),
@@ -657,15 +686,14 @@
             pltpu.VMEM((SPAN_2, 56, 128), F32),
             pltpu.VMEM((SPAN_3, 40, 128), F32),
             pltpu.VMEM((SPAN_4, 24, 128), F32),
-            pltpu.VMEM((SPAN_2, 24, 128), F32),
-            pltpu.VMEM((SPAN_3, 16, 128), F32),
-            pltpu.SemaphoreType.DMA((4,)),
+            pltpu.SemaphoreType.DMA((5,)),
         ),
         spaces={1: HBM, 2: HBM},
+        out_spaces={0: ANY},
         megabytes=53.75,
     )
     (got_1,) = exchange((face,), "gy", (1,))
-    relay = call(relay_kernel, shape(48, 128), (raw, got_1))
+    relay = call(relay_kernel, shape(FACE + 8, 128), (raw, got_1))
     (got_2,) = exchange((relay,), "gy", (2,))
     qx, qy, qz = composites()
     qz_high = qz.astype(BF16)
@@ -697,13 +725,13 @@
     )
     wide_x, raw, to_high, to_low = call(
         widen_x_kernel,
-        (shape(36, 40, 128), shape(16, 128), shape(96, 128), shape(96, 128)),
+        (shape(36, 40, 128), shape(16, 128), shape(80, 128), shape(80, 128)),
         (wide_y, raw, got_1, got_3, got_2, bands[0]),
         spaces={5: ANY},
     )
     from_low, from_high = turn(to_high, 1), turn(to_low, -1)
     (got_2,) = exchange((raw,), "gz", (2,))
-    window = call(window_kernel, shape(4, 16, 128), (raw, from_low, from_high, got_2))
+    window = call(window_kernel, shape(3, 16, 128), (raw, from_low, from_high, got_2))
     pieces = [window] + [turn(window, by) for by in (4, -4, 8)]
     base = call(
         near_kernel,
@@ -723,7 +751,12 @@
         top_kernel,
         shape(32, 32, 32),
         (base, *pieces, green_high, green_low, rise, jnp.asarray(np.concatenate([qz_high, qz_low]))),
-        (pltpu.VMEM((16, 8, 128), F32),),
+        (
+            pltpu.VMEM((16, 8, 128), F32),
+            pltpu.VMEM((32, 32, 32), F32),
+            pltpu.SemaphoreType.DMA((4,)),
+        ),
+        out_spaces={0: ANY},
     )
 
 

time: 47.8 us -> 47.7 us (level)
  no operation moved by 1% of the time
where the time goes in v6:
time: 47.7 us; the launch traced here: 47.4 us
  starting transfers between devices  22.1 us (46%)
  Pallas kernels  14.9 us (31%)
  waiting for transfers between devices  7.41 us (16%)
  local copies, waits for them, and re-layouts  1.98 us (4%)
  other arithmetic  0.73 us (2%)
    pallas_call x9, Pallas kernels, call(): pl.pallas_call(kernel, out_shape=outs, in_specs=[spaces.get(i, VMEM) for...  14.9 us
    ppermute x6, starting transfers between devices, exchange(): lax.ppermute(value, axis, [(i, i ^ step) for i in range(size)])  11.8 us
    ppermute x5, starting transfers between devices, turn(): return lax.ppermute(value, ('gy', 'gz'), pairs)  10.3 us
    ppermute x6, waiting for transfers between devices, exchange(): lax.ppermute(value, axis, [(i, i ^ step) for i in range(size)])  7.39 us
    unnamed x16, local copies, waits for them, and re-layouts  1.98 us
  transfers between devices with their start and end apart: 11, of which 3 were waited for; matrix products, arithmetic and copies ran while one was open for 0% of the time, Pallas kernels for 13%

profile of v6, /device:TPU:32, one launch (start us, length us, event | category | flops | bytes accessed | tf_op | source)
XLA Modules:
  0.0 47.4 jit_solution(9168683514293869249)
XLA Ops:
  0.0 0.7 %multiply_add_fusion.codes = s32[384]{0:T(512)S(1)} fusion(s32[384]{0:T(512)} %param.12, s32[384]{0:T(512)} %param.13), kind=kLoop, calls=%fused_computation | loop fusion | flops 768 | bytes 4608 | tf_op jit(solution)/shard_map/add | solution.py:678
  0.7 5.2 %shard_map.109 = (f32[32,32,128]{2,1,0:T(8,128)}, f32[8,128]{1,0:T(8,128)S(1)}, f32[72,128]{1,0:T(8,128)S(1)}) custom-call(s32[384]{0:T(512)S(1)} %multiply_add_fusion.codes, f32[384,128]{1,0:T(8,128)} %charges_hbm.1, bf16[4608,128]{1,0:T(8,128)(2,1)} %bitcast.1), custom_call_target="tpu_custom_call" | custom-call | flops 1000000 | bytes 2097152 | tf_op jit(solution)/shard_map/pallas_call | solution.py:639
  6.0 0.0 copy-start.3
  6.0 0.0 copy-start.4
  6.0 0.1 collective-permute-start
  6.1 1.2 %collective-permute-done.got.got_1 = f32[72,128]{1,0:T(8,128)S(1)} collective-permute-done((f32[72,128]{1,0:T(8,128)S(1)}, f32[72,128]{1,0:T(8,128)S(1)}, u32[]{:S(2)}, u32[]{:S(2)}) %collective-permute-start) | collective-permute-done | bytes 36896 | tf_op jit(solution)/shard_map/ppermute | solution.py:658
  7.3 0.1 shard_map.111.own
  7.4 6.3 %collective-permute-start.1 = (f32[40,128]{1,0:T(8,128)S(1)}, f32[40,128]{1,0:T(8,128)S(1)}, u32[]{:S(2)}, u32[]{:S(2)}) collective-permute-start(f32[40,128]{1,0:T(8,128)S(1)} %shard_map.111.own), channel_id=1, source_target_pairs={{0,32},{16,48},{32,0},{48,16},{1,33},{17,49},{33,1},{49,17},{2,34}... | collective-permute-start | bytes 61448 | tf_op jit(solution)/shard_map/ppermute | solution.py:658
  13.7 1.0 %copy-done = f32[32,32,128]{2,1,0:T(8,128)S(1)} copy-done((f32[32,32,128]{2,1,0:T(8,128)S(1)}, f32[32,32,128]{2,1,0:T(8,128)}, u32[]{:S(2)}) %copy-start) | copy-done | bytes 524312
  14.7 0.9 %copy-done.2 = f32[8,32,128]{2,1,0:T(8,128)S(1)} copy-done((f32[8,32,128]{2,1,0:T(8,128)S(1)}, f32[8,32,128]{2,1,0:T(8,128)}, u32[]{:S(2)}) %copy-start.2) | copy-done | bytes 131096
  15.6 1.0 %shard_map.110 = (bf16[1024,896]{1,0:T(8,128)(2,1)S(1)}, bf16[1024,896]{1,0:T(8,128)(2,1)S(1)}, bf16[1024,256]{1,0:T(8,128)(2,1)S(1)}, f32[32,40,128]{2,1,0:T(8,128)S(1)}) custom-call(f32[8,32,128]{2,1,0:T(8,128)S(1)} %copy-done.2, f32[32,32,128]{2,1,0:T(8,128)S(1)} %copy-done), custom_call_target="tpu_custom_call" | custom-call | flops 1000000 | bytes 2097152 | tf_op jit(solution)/shard_map/pallas_call | solution.py:639
  16.6 0.0 copy-start.1
  16.6 0.4 shard_map.112
  17.0 1.6 %collective-permute-start.2 = (f32[72,128]{1,0:T(8,128)S(1)}, f32[72,128]{1,0:T(8,128)S(1)}, u32[]{:S(2)}, u32[]{:S(2)}) collective-permute-start(f32[72,128]{1,0:T(8,128)S(1)} %get-tuple-element.33), channel_id=1, source_target_pairs={{0,64},{64,0},{128,192},{192,128},{1,65},{65,1},{129,193},{193,129... | collective-permute-start | bytes 110600 | tf_op jit(solution)/shard_map/ppermute | solution.py:658
  18.6 2.1 %collective-permute-start.3 = (f32[72,128]{1,0:T(8,128)S(1)}, f32[72,128]{1,0:T(8,128)S(1)}, u32[]{:S(2)}, u32[]{:S(2)}) collective-permute-start(f32[72,128]{1,0:T(8,128)S(1)} %get-tuple-element.34), channel_id=1, source_target_pairs={{0,192},{64,128},{128,64},{192,0},{1,193},{65,129},{129,65},{193,1... | collective-permute-start | bytes 110600 | tf_op jit(solution)/shard_map/ppermute | solution.py:658
  20.7 0.6 %collective-permute-start.4 = (f32[8,128]{1,0:T(8,128)S(1)}, f32[8,128]{1,0:T(8,128)S(1)}, u32[]{:S(2)}, u32[]{:S(2)}) collective-permute-start(f32[8,128]{1,0:T(8,128)S(1)} %get-tuple-element.32.own), channel_id=1, source_target_pairs={{0,128},{64,192},{128,0},{192,64},{1,129},{65,193},{129,1},{193,65... | collective-permute-start | bytes 12296 | tf_op jit(solution)/shard_map/ppermute | solution.py:658
  21.3 2.3 %shard_map.113 = (bf16[256,256]{1,0:T(8,128)(2,1)S(1)}, bf16[256,256]{1,0:T(8,128)(2,1)S(1)}, bf16[256,128]{1,0:T(8,128)(2,1)S(1)}, bf16[256,128]{1,0:T(8,128)(2...) custom-call(f32[5,5,5]{2,1,0:T(8,128)S(1)} %copy-done.5, f32[5,5,5]{2,1,0:T(8,128)S(1)} %copy-done.6, ...), custom_call_target="tpu_custom_call" | custom-call | flops 1000000 | bytes 2097152 | tf_op jit(solution)/shard_map/pallas_call | solution.py:639
  23.7 2.1 %collective-permute-done.4.got_2 = f32[8,128]{1,0:T(8,128)S(1)} collective-permute-done((f32[8,128]{1,0:T(8,128)S(1)}, f32[8,128]{1,0:T(8,128)S(1)}, u32[]{:S(2)}, u32[]{:S(2)}) %collective-permute-start.4) | collective-permute-done | bytes 4128 | tf_op jit(solution)/shard_map/ppermute | solution.py:658
  25.8 0.0 collective-permute-done.3.got_3
  25.8 0.8 %shard_map.114 = (f32[36,40,128]{2,1,0:T(8,128)S(1)}, f32[16,128]{1,0:T(8,128)S(1)}, f32[80,128]{1,0:T(8,128)S(1)}, f32[80,128]{1,0:T(8,128)S(1)}) custom-call(f32[32,40,128]{2,1,0:T(8,128)S(1)} %get-tuple-element.31.wide_y, f32[8,128]{1,0:T(8,128)S(1)} %get-tuple-element.32.own, f32[72,128]{1,0:T(8,128)S(1)} %collective-permute-done.2.got_1, ...), custom_call_target="tpu_custom_call" | custom-call | flops 1000000 | bytes 2097152 | tf_op jit(solution)/shard_map/pallas_call | solution.py:639
  26.6 1.6 %collective-permute-start.5 = (f32[80,128]{1,0:T(8,128)S(1)}, f32[80,128]{1,0:T(8,128)S(1)}, u32[]{:S(2)}, u32[]{:S(2)}) collective-permute-start(f32[80,128]{1,0:T(8,128)S(1)} %get-tuple-element.37), channel_id=1, source_target_pairs={{0,1},{1,2},{2,3},{3,4},{4,5},{5,6},{6,7},{7,8},{8,9},{9,10},{10,1... | collective-permute-start | bytes 122888 | tf_op jit(solution)/shard_map/ppermute | solution.py:670
  28.3 2.6 %collective-permute-start.6 = (f32[80,128]{1,0:T(8,128)S(1)}, f32[80,128]{1,0:T(8,128)S(1)}, u32[]{:S(2)}, u32[]{:S(2)}) collective-permute-start(f32[80,128]{1,0:T(8,128)S(1)} %get-tuple-element.38), channel_id=1, source_target_pairs={{0,47},{1,0},{2,1},{3,2},{4,3},{5,4},{6,5},{7,6},{8,7},{9,8},{10,9... | collective-permute-start | bytes 122888 | tf_op jit(solution)/shard_map/ppermute | solution.py:670
  30.8 1.1 %collective-permute-start.7 = (f32[16,128]{1,0:T(8,128)S(1)}, f32[16,128]{1,0:T(8,128)S(1)}, u32[]{:S(2)}, u32[]{:S(2)}) collective-permute-start(f32[16,128]{1,0:T(8,128)S(1)} %get-tuple-element.44.own), channel_id=1, source_target_pairs={{0,2},{1,3},{2,0},{3,1},{4,6},{5,7},{6,4},{7,5},{8,10},{9,11},{10,... | collective-permute-start | bytes 24584 | tf_op jit(solution)/shard_map/ppermute | solution.py:658
  31.9 4.1 %collective-permute-done.7.got_2 = f32[16,128]{1,0:T(8,128)S(1)} collective-permute-done((f32[16,128]{1,0:T(8,128)S(1)}, f32[16,128]{1,0:T(8,128)S(1)}, u32[]{:S(2)}, u32[]{:S(2)}) %collective-permute-start.7) | collective-permute-done | bytes 8224 | tf_op jit(solution)/shard_map/ppermute | solution.py:658
  36.0 0.0 collective-permute-done.5.from_low
  36.0 0.0 collective-permute-done.6.from_high
  36.0 0.2 shard_map.116.piece_0
  36.2 1.8 %collective-permute-start.10 = (f32[3,16,128]{2,1,0:T(8,128)S(1)}, f32[3,16,128]{2,1,0:T(8,128)S(1)}, u32[]{:S(2)}, u32[]{:S(2)}) collective-permute-start(f32[3,16,128]{2,1,0:T(8,128)S(1)} %shard_map.116.piece_0), channel_id=1, source_target_pairs={{0,8},{1,9},{2,10},{3,11},{4,12},{5,13},{6,14},{7,15},{8,32},{9,33... | collective-permute-start | bytes 73736 | tf_op jit(solution)/shard_map/ppermute | solution.py:670
  38.0 1.4 %collective-permute-start.9 = (f32[3,16,128]{2,1,0:T(8,128)S(1)}, f32[3,16,128]{2,1,0:T(8,128)S(1)}, u32[]{:S(2)}, u32[]{:S(2)}) collective-permute-start(f32[3,16,128]{2,1,0:T(8,128)S(1)} %shard_map.116.piece_0), channel_id=1, source_target_pairs={{0,44},{1,45},{2,46},{3,47},{4,0},{5,1},{6,2},{7,3},{8,4},{9,5},{1... | collective-permute-start | bytes 73736 | tf_op jit(solution)/shard_map/ppermute | solution.py:670
  39.4 3.0 %collective-permute-start.8 = (f32[3,16,128]{2,1,0:T(8,128)S(1)}, f32[3,16,128]{2,1,0:T(8,128)S(1)}, u32[]{:S(2)}, u32[]{:S(2)}) collective-permute-start(f32[3,16,128]{2,1,0:T(8,128)S(1)} %shard_map.116.piece_0), channel_id=1, source_target_pairs={{0,4},{1,5},{2,6},{3,7},{4,8},{5,9},{6,10},{7,11},{8,12},{9,13},{1... | collective-permute-start | bytes 73736 | tf_op jit(solution)/shard_map/ppermute | solution.py:670
  42.3 2.7 %shard_map.115.base = f32[32,32,128]{2,1,0:T(8,128)S(1)} custom-call(f32[36,40,128]{2,1,0:T(8,128)S(1)} %get-tuple-element.36.wide, f32[80,128]{1,0:T(8,128)S(1)} %collective-permute-done.5.from_low, f32[80,128]{1,0:T(8,128)S(1)} %collective-permute-done.6.from_high, bf16[256,256]{1,0:T(8,128)(2,1)S(1)} %get-tuple-element.35.after.b1h, ...), custom_call_target="tpu_custom_call" | custom-call | flops 1000000 | bytes 2097152 | tf_op jit(solution)/shard_map/pallas_call | solution.py:639
  45.1 2.2 %shard_map.117 = f32[32,32,32]{2,1,0:T(8,128)} custom-call(f32[32,32,128]{2,1,0:T(8,128)S(1)} %shard_map.115.base, f32[3,16,128]{2,1,0:T(8,128)S(1)} %shard_map.116.piece_0, f32[3,16,128]{2,1,0:T(8,128)S(1)} %collective-permute-done.8.piece_1, f32[3,16,128]{2,1,0:T(8,128)S(1)} %collective-permute-done.9.piece_2, ...), custom_call_target="tpu_custom_call" | custom-call | flops 1000000 | bytes 2097152 | tf_op jit(solution)/shard_map/pallas_call | solution.py:639
  (16 shorter events, 0.0 us)
Async XLA Ops:
  0.0 21.3 %copy-start.7 = (f32[5,5,5]{2,1,0:T(8,128)S(1)}, f32[5,5,5]{2,1,0:T(8,128)}, u32[]{:S(2)}) copy-start(f32[5,5,5]{2,1,0:T(8,128)} %kernel_3.1) | copy-start | bytes 1504
  0.0 21.3 %copy-start.6 = (f32[5,5,5]{2,1,0:T(8,128)S(1)}, f32[5,5,5]{2,1,0:T(8,128)}, u32[]{:S(2)}) copy-start(f32[5,5,5]{2,1,0:T(8,128)} %kernel_2.1) | copy-start | bytes 1504
  0.0 21.3 %copy-start.5 = (f32[5,5,5]{2,1,0:T(8,128)S(1)}, f32[5,5,5]{2,1,0:T(8,128)}, u32[]{:S(2)}) copy-start(f32[5,5,5]{2,1,0:T(8,128)} %kernel_1.1) | copy-start | bytes 1504
  6.0 36.3 %copy-start.3 = (bf16[128,128]{1,0:T(8,128)(2,1)S(1)}, bf16[128,128]{1,0:T(8,128)(2,1)}, u32[]{:S(2)}) copy-start(bf16[128,128]{1,0:T(8,128)(2,1)} %constant.12.clone.prol_1) | copy-start | bytes 98308
  6.0 36.3 %copy-start.4 = (bf16[128,128]{1,0:T(8,128)(2,1)S(1)}, bf16[128,128]{1,0:T(8,128)(2,1)}, u32[]{:S(2)}) copy-start(bf16[128,128]{1,0:T(8,128)(2,1)} %constant.11.clone.prol_2) | copy-start | bytes 98308
  6.0 1.3 %collective-permute-start = (f32[72,128]{1,0:T(8,128)S(1)}, f32[72,128]{1,0:T(8,128)S(1)}, u32[]{:S(2)}, u32[]{:S(2)}) collective-permute-start(f32[72,128]{1,0:T(8,128)S(1)} %get-tuple-element.29), channel_id=1, source_target_pairs={{0,16},{16,0},{32,48},{48,32},{1,17},{17,1},{33,49},{49,33},{2,18}... | collective-permute-start | bytes 110600 | tf_op jit(solution)/shard_map/ppermute | solution.py:658
  7.4 9.2 %collective-permute-start.1 = (f32[40,128]{1,0:T(8,128)S(1)}, f32[40,128]{1,0:T(8,128)S(1)}, u32[]{:S(2)}, u32[]{:S(2)}) collective-permute-start(f32[40,128]{1,0:T(8,128)S(1)} %shard_map.111.own), channel_id=1, source_target_pairs={{0,32},{16,48},{32,0},{48,16},{1,33},{17,49},{33,1},{49,17},{2,34}... | collective-permute-start | bytes 61448 | tf_op jit(solution)/shard_map/ppermute | solution.py:658
  13.7 1.0 %copy-start = (f32[32,32,128]{2,1,0:T(8,128)S(1)}, f32[32,32,128]{2,1,0:T(8,128)}, u32[]{:S(2)}) copy-start(f32[32,32,128]{2,1,0:T(8,128)} %get-tuple-element.26.packed) | copy-start | bytes 1572868
  14.7 0.9 %copy-start.2 = (f32[8,32,128]{2,1,0:T(8,128)S(1)}, f32[8,32,128]{2,1,0:T(8,128)}, u32[]{:S(2)}) copy-start(f32[8,32,128]{2,1,0:T(8,128)} %constant.10.clone.factors) | copy-start | bytes 393220
  16.6 28.4 %copy-start.1 = (bf16[8,128,128]{2,1,0:T(8,128)(2,1)S(1)}, bf16[8,128,128]{2,1,0:T(8,128)(2,1)}, u32[]{:S(2)}) copy-start(bf16[8,128,128]{2,1,0:T(8,128)(2,1)} %constant.13.clone.qz) | copy-start | bytes 786436
  17.0 8.8 %collective-permute-start.2 = (f32[72,128]{1,0:T(8,128)S(1)}, f32[72,128]{1,0:T(8,128)S(1)}, u32[]{:S(2)}, u32[]{:S(2)}) collective-permute-start(f32[72,128]{1,0:T(8,128)S(1)} %get-tuple-element.33), channel_id=1, source_target_pairs={{0,64},{64,0},{128,192},{192,128},{1,65},{65,1},{129,193},{193,129... | collective-permute-start | bytes 110600 | tf_op jit(solution)/shard_map/ppermute | solution.py:658
  18.6 7.2 %collective-permute-start.3 = (f32[72,128]{1,0:T(8,128)S(1)}, f32[72,128]{1,0:T(8,128)S(1)}, u32[]{:S(2)}, u32[]{:S(2)}) collective-permute-start(f32[72,128]{1,0:T(8,128)S(1)} %get-tuple-element.34), channel_id=1, source_target_pairs={{0,192},{64,128},{128,64},{192,0},{1,193},{65,129},{129,65},{193,1... | collective-permute-start | bytes 110600 | tf_op jit(solution)/shard_map/ppermute | solution.py:658
  20.7 5.1 %collective-permute-start.4 = (f32[8,128]{1,0:T(8,128)S(1)}, f32[8,128]{1,0:T(8,128)S(1)}, u32[]{:S(2)}, u32[]{:S(2)}) collective-permute-start(f32[8,128]{1,0:T(8,128)S(1)} %get-tuple-element.32.own), channel_id=1, source_target_pairs={{0,128},{64,192},{128,0},{192,64},{1,129},{65,193},{129,1},{193,65... | collective-permute-start | bytes 12296 | tf_op jit(solution)/shard_map/ppermute | solution.py:658
  26.6 9.4 %collective-permute-start.5 = (f32[80,128]{1,0:T(8,128)S(1)}, f32[80,128]{1,0:T(8,128)S(1)}, u32[]{:S(2)}, u32[]{:S(2)}) collective-permute-start(f32[80,128]{1,0:T(8,128)S(1)} %get-tuple-element.37), channel_id=1, source_target_pairs={{0,1},{1,2},{2,3},{3,4},{4,5},{5,6},{6,7},{7,8},{8,9},{9,10},{10,1... | collective-permute-start | bytes 122888 | tf_op jit(solution)/shard_map/ppermute | solution.py:670
  28.3 7.7 %collective-permute-start.6 = (f32[80,128]{1,0:T(8,128)S(1)}, f32[80,128]{1,0:T(8,128)S(1)}, u32[]{:S(2)}, u32[]{:S(2)}) collective-permute-start(f32[80,128]{1,0:T(8,128)S(1)} %get-tuple-element.38), channel_id=1, source_target_pairs={{0,47},{1,0},{2,1},{3,2},{4,3},{5,4},{6,5},{7,6},{8,7},{9,8},{10,9... | collective-permute-start | bytes 122888 | tf_op jit(solution)/shard_map/ppermute | solution.py:670
  30.8 5.2 %collective-permute-start.7 = (f32[16,128]{1,0:T(8,128)S(1)}, f32[16,128]{1,0:T(8,128)S(1)}, u32[]{:S(2)}, u32[]{:S(2)}) collective-permute-start(f32[16,128]{1,0:T(8,128)S(1)} %get-tuple-element.44.own), channel_id=1, source_target_pairs={{0,2},{1,3},{2,0},{3,1},{4,6},{5,7},{6,4},{7,5},{8,10},{9,11},{10,... | collective-permute-start | bytes 24584 | tf_op jit(solution)/shard_map/ppermute | solution.py:658
  36.2 8.8 %collective-permute-start.10 = (f32[3,16,128]{2,1,0:T(8,128)S(1)}, f32[3,16,128]{2,1,0:T(8,128)S(1)}, u32[]{:S(2)}, u32[]{:S(2)}) collective-permute-start(f32[3,16,128]{2,1,0:T(8,128)S(1)} %shard_map.116.piece_0), channel_id=1, source_target_pairs={{0,8},{1,9},{2,10},{3,11},{4,12},{5,13},{6,14},{7,15},{8,32},{9,33... | collective-permute-start | bytes 73736 | tf_op jit(solution)/shard_map/ppermute | solution.py:670
  38.0 7.1 %collective-permute-start.9 = (f32[3,16,128]{2,1,0:T(8,128)S(1)}, f32[3,16,128]{2,1,0:T(8,128)S(1)}, u32[]{:S(2)}, u32[]{:S(2)}) collective-permute-start(f32[3,16,128]{2,1,0:T(8,128)S(1)} %shard_map.116.piece_0), channel_id=1, source_target_pairs={{0,44},{1,45},{2,46},{3,47},{4,0},{5,1},{6,2},{7,3},{8,4},{9,5},{1... | collective-permute-start | bytes 73736 | tf_op jit(solution)/shard_map/ppermute | solution.py:670
  39.4 5.7 %collective-permute-start.8 = (f32[3,16,128]{2,1,0:T(8,128)S(1)}, f32[3,16,128]{2,1,0:T(8,128)S(1)}, u32[]{:S(2)}, u32[]{:S(2)}) collective-permute-start(f32[3,16,128]{2,1,0:T(8,128)S(1)} %shard_map.116.piece_0), channel_id=1, source_target_pairs={{0,4},{1,5},{2,6},{3,7},{4,8},{5,9},{6,10},{7,11},{8,12},{9,13},{1... | collective-permute-start | bytes 73736 | tf_op jit(solution)/shard_map/ppermute | solution.py:670

commit v7 on v6

--- a/solution.py
+++ b/solution.py
@@ -1,3 +1,5 @@
+import functools
+
 import jax
 import jax.numpy as jnp
 import numpy as np
@@ -347,7 +349,7 @@
         ref[64:72, :] = total
 
 
-def widen_x_kernel(wide_y, own, got_1, got_3, got_2, after, out, raw_out, to_high, to_low):
+def widen_x_kernel(wide_y, own, got_2, got_1, got_3, after, out, raw_out, to_high, to_low):
     index, _ = place()
     even, one, two = nearest(index[0])
     total = None
@@ -399,7 +401,7 @@
     return message[0:40], message[40:64], third
 
 
-def window_kernel(own, from_low, from_high, got_2, out):
+def window_kernel(own, got_2, from_low, from_high, after, out):
     index, _ = place()
     early = lax.rem(index[2], 4) < 2
     ends = got_2[...]
@@ -460,12 +462,12 @@
     return total_high.astype(BF16), total_low.astype(BF16)
 
 
-def bands_kernel(kernel_1, kernel_2, kernel_3, b1h, b1l, b2h, b2l, b3h, b3l):
-    outs = ((b1h, b1l), (b2h, b2l), (b3h, b3l))
-    for kernel, band, (high_ref, low_ref) in zip((kernel_1, kernel_2, kernel_3), BANDS, outs):
+def bands_kernel(bands, *refs):
+    kernels, outs = refs[: len(bands)], refs[len(bands) :]
+    for n, (kernel, band) in enumerate(zip(kernels, bands)):
         high, low = build_bands(kernel, band)
-        high_ref[...] = high
-        low_ref[...] = low
+        outs[2 * n][...] = high
+        outs[2 * n + 1][...] = low
 
 
 def green_kernel(factors, packed, green_high, green_low, rise, framed, block_high, block_low):
@@ -591,7 +593,7 @@
     lane = iota((8, 128), 1)
     ring = lax.rem(index[2], 4)
     first = 4 * (ring == 3).astype(jnp.int32) - 4 * (ring == 0).astype(jnp.int32) + 127
-    sources = [lax.rem(16 * lax.rem(index[2] // 4 + step, 4) + first, 128) for step in (0, 3, 1, 2)]
+    sources = [lax.rem(16 * lax.rem(index[2] // 4 + step, 4) + first, 128) for step in (0, 2, 3, 1)]
     for x in range(16):
         total = None
         for piece, at in zip((piece_0, piece_1, piece_2, piece_3), sources):
@@ -632,7 +634,7 @@
         copy.wait()
 
 
-def call(kernel, outs, ins, scratch=(), megabytes=16, spaces=None, out_spaces=None, aliases=None):
+def call(kernel, outs, ins, scratch=(), megabytes=16, spaces=None, out_spaces=None, aliases=None, flops=1000000):
     spaces, out_spaces = spaces or {}, out_spaces or {}
     single = not isinstance(outs, tuple)
     out_specs = [out_spaces.get(i, VMEM) for i in range(1 if single else len(outs))]
@@ -644,7 +646,7 @@
         scratch_shapes=list(scratch),
         input_output_aliases=aliases or {},
         compiler_params=pltpu.CompilerParams(vmem_limit_bytes=int(megabytes * 2**20)),
-        cost_estimate=pl.CostEstimate(flops=1000000, bytes_accessed=2**21, transcendentals=0),
+        cost_estimate=pl.CostEstimate(flops=flops, bytes_accessed=2**21, transcendentals=0),
     )(*ins)
 
 
@@ -668,6 +670,16 @@
         ring = [(high * half + core) * size_z + z for high in range(2) for z in range(size_z)]
         pairs += [(ring[n], ring[(n + by) % len(ring)]) for n in range(len(ring))]
     return lax.ppermute(value, ("gy", "gz"), pairs)
+
+
+def banded(bands, *kernels, flops=10**9):
+    return call(
+        functools.partial(bands_kernel, bands),
+        tuple(shape(band[0], band[1], dtype=BF16) for band in bands for _ in range(2)),
+        kernels,
+        spaces={n: SMEM for n in range(len(kernels))},
+        flops=flops,
+    )
 
 
 def shards(charges, counts, slots, spline, kernel_fine, kernel_mid, kernel_coarse):
@@ -716,27 +728,28 @@
         spaces={4: ANY},
         aliases={0: 0},
     )
-    got_2, got_3, got_1 = exchange((raw, face_3, face_1), "gx", (2, 3, 1))
-    bands = call(
-        bands_kernel,
-        tuple(shape(band[0], band[1], dtype=BF16) for band in BANDS for _ in range(2)),
-        (kernel_fine, kernel_mid, kernel_coarse),
-        spaces={0: SMEM, 1: SMEM, 2: SMEM},
-    )
+    got_3, got_1, got_2 = exchange((face_3, face_1, raw), "gx", (3, 1, 2))
+    bands_1 = banded(BANDS[:1], kernel_fine)
     wide_x, raw, to_high, to_low = call(
         widen_x_kernel,
         (shape(36, 40, 128), shape(16, 128), shape(80, 128), shape(80, 128)),
-        (wide_y, raw, got_1, got_3, got_2, bands[0]),
+        (wide_y, raw, got_2, got_1, got_3, bands_1[0]),
         spaces={5: ANY},
     )
     from_low, from_high = turn(to_high, 1), turn(to_low, -1)
     (got_2,) = exchange((raw,), "gz", (2,))
-    window = call(window_kernel, shape(3, 16, 128), (raw, from_low, from_high, got_2))
-    pieces = [window] + [turn(window, by) for by in (4, -4, 8)]
+    bands_2 = banded(BANDS[1:], kernel_mid, kernel_coarse)
+    window = call(
+        window_kernel,
+        shape(3, 16, 128),
+        (raw, got_2, from_low, from_high, bands_2[0]),
+        spaces={4: ANY},
+    )
+    pieces = [window] + [turn(window, by) for by in (8, 4, -4)]
     base = call(
         near_kernel,
         shape(32, 32, 128),
-        (wide_x, from_low, from_high, *bands, jnp.asarray(PROL_2, BF16), jnp.asarray(PROL_1, BF16)),
+        (wide_x, from_low, from_high, *bands_1, *bands_2, jnp.asarray(PROL_2, BF16), jnp.asarray(PROL_1, BF16)),
         (
             pltpu.VMEM((32, 40, 256), F32),
             pltpu.VMEM((SPAN_2, 32, 128), F32),

time: 47.7 us -> 48.7 us (1.021)
  Pallas kernels: 14.9 us -> 15.5 us
  waiting for transfers between devices: 7.41 us -> 7.92 us
    ppermute x5, waiting for transfers between devices: 0.01 us -> 1.07 us  [turn(): return lax.ppermute(value, ('gy', 'gz'), pairs)]
    pallas_call x9 -> x10, Pallas kernels: 14.9 us -> 15.5 us  [call(): pl.pallas_call(kernel, out_shape=outs, in_specs=[spaces.get(i, VMEM) for...]
    ppermute x6, waiting for transfers between devices: 7.39 us -> 6.85 us  [exchange(): lax.ppermute(value, axis, [(i, i ^ step) for i in range(size)])]
  transfers between devices with their start and end apart: 11 -> 11, of which waited for: 3 -> 5; matrix products, arithmetic and copies ran while one was open for 0% -> 0% of each run, Pallas kernels for 13% -> 14%
where the time goes in v7:
time: 48.7 us; the launch traced here: 48.5 us
  starting transfers between devices  22.1 us (45%)
  Pallas kernels  15.5 us (32%)
  waiting for transfers between devices  7.92 us (16%)
  local copies, waits for them, and re-layouts  1.97 us (4%)
  other arithmetic  0.71 us (1%)
    pallas_call x10, Pallas kernels, call(): pl.pallas_call(kernel, out_shape=outs, in_specs=[spaces.get(i, VMEM) for...  15.5 us
    ppermute x6, starting transfers between devices, exchange(): lax.ppermute(value, axis, [(i, i ^ step) for i in range(size)])  11.7 us
    ppermute x5, starting transfers between devices, turn(): return lax.ppermute(value, ('gy', 'gz'), pairs)  10.3 us
    ppermute x6, waiting for transfers between devices, exchange(): lax.ppermute(value, axis, [(i, i ^ step) for i in range(size)])  6.85 us
    unnamed x16, local copies, waits for them, and re-layouts  1.97 us
    ppermute x5, waiting for transfers between devices, turn(): return lax.ppermute(value, ('gy', 'gz'), pairs)  1.07 us
  transfers between devices with their start and end apart: 11, of which 5 were waited for; matrix products, arithmetic and copies ran while one was open for 0% of the time, Pallas kernels for 14%

profile of v7, /device:TPU:32, one launch (start us, length us, event | category | flops | bytes accessed | tf_op | source)
XLA Modules:
  0.0 48.5 jit_solution(4974980757132348270)
XLA Ops:
  0.0 0.7 %multiply_add_fusion.codes = s32[384]{0:T(512)S(1)} fusion(s32[384]{0:T(512)} %param.12, s32[384]{0:T(512)} %param.13), kind=kLoop, calls=%fused_computation | loop fusion | flops 768 | bytes 4608 | tf_op jit(solution)/shard_map/add | solution.py:690
  0.7 5.2 %shard_map.109 = (f32[32,32,128]{2,1,0:T(8,128)}, f32[8,128]{1,0:T(8,128)S(1)}, f32[72,128]{1,0:T(8,128)S(1)}) custom-call(s32[384]{0:T(512)S(1)} %multiply_add_fusion.codes, f32[384,128]{1,0:T(8,128)} %charges_hbm.1, bf16[4608,128]{1,0:T(8,128)(2,1)} %bitcast.1), custom_call_target="tpu_custom_call" | custom-call | flops 1000000 | bytes 2097152 | tf_op jit(solution)/shard_map/pallas_call | solution.py:641
  6.0 0.1 collective-permute-start
  6.1 1.2 %collective-permute-done.got.got_1 = f32[72,128]{1,0:T(8,128)S(1)} collective-permute-done((f32[72,128]{1,0:T(8,128)S(1)}, f32[72,128]{1,0:T(8,128)S(1)}, u32[]{:S(2)}, u32[]{:S(2)}) %collective-permute-start) | collective-permute-done | bytes 36896 | tf_op jit(solution)/shard_map/ppermute | solution.py:660
  7.3 0.1 shard_map.111.own
  7.3 6.3 %collective-permute-start.1 = (f32[40,128]{1,0:T(8,128)S(1)}, f32[40,128]{1,0:T(8,128)S(1)}, u32[]{:S(2)}, u32[]{:S(2)}) collective-permute-start(f32[40,128]{1,0:T(8,128)S(1)} %shard_map.111.own), channel_id=1, source_target_pairs={{0,32},{16,48},{32,0},{48,16},{1,33},{17,49},{33,1},{49,17},{2,34}... | collective-permute-start | bytes 61448 | tf_op jit(solution)/shard_map/ppermute | solution.py:660
  13.6 1.0 %copy-done = f32[32,32,128]{2,1,0:T(8,128)S(1)} copy-done((f32[32,32,128]{2,1,0:T(8,128)S(1)}, f32[32,32,128]{2,1,0:T(8,128)}, u32[]{:S(2)}) %copy-start) | copy-done | bytes 524312
  14.7 0.9 %copy-done.2 = f32[8,32,128]{2,1,0:T(8,128)S(1)} copy-done((f32[8,32,128]{2,1,0:T(8,128)S(1)}, f32[8,32,128]{2,1,0:T(8,128)}, u32[]{:S(2)}) %copy-start.2) | copy-done | bytes 131096
  15.6 1.0 %shard_map.110 = (bf16[1024,896]{1,0:T(8,128)(2,1)S(1)}, bf16[1024,896]{1,0:T(8,128)(2,1)S(1)}, bf16[1024,256]{1,0:T(8,128)(2,1)S(1)}, f32[32,40,128]{2,1,0:T(8,128)S(1)}) custom-call(f32[8,32,128]{2,1,0:T(8,128)S(1)} %copy-done.2, f32[32,32,128]{2,1,0:T(8,128)S(1)} %copy-done), custom_call_target="tpu_custom_call" | custom-call | flops 1000000 | bytes 2097152 | tf_op jit(solution)/shard_map/pallas_call | solution.py:641
  16.6 0.4 shard_map.112
  16.9 3.1 %collective-permute-start.2 = (f32[8,128]{1,0:T(8,128)S(1)}, f32[8,128]{1,0:T(8,128)S(1)}, u32[]{:S(2)}, u32[]{:S(2)}) collective-permute-start(f32[8,128]{1,0:T(8,128)S(1)} %get-tuple-element.32.own), channel_id=1, source_target_pairs={{0,128},{64,192},{128,0},{192,64},{1,129},{65,193},{129,1},{193,65... | collective-permute-start | bytes 12296 | tf_op jit(solution)/shard_map/ppermute | solution.py:660
  20.1 0.6 %collective-permute-start.3 = (f32[72,128]{1,0:T(8,128)S(1)}, f32[72,128]{1,0:T(8,128)S(1)}, u32[]{:S(2)}, u32[]{:S(2)}) collective-permute-start(f32[72,128]{1,0:T(8,128)S(1)} %get-tuple-element.33), channel_id=1, source_target_pairs={{0,64},{64,0},{128,192},{192,128},{1,65},{65,1},{129,193},{193,129... | collective-permute-start | bytes 110600 | tf_op jit(solution)/shard_map/ppermute | solution.py:660
  20.7 0.5 %collective-permute-start.4 = (f32[72,128]{1,0:T(8,128)S(1)}, f32[72,128]{1,0:T(8,128)S(1)}, u32[]{:S(2)}, u32[]{:S(2)}) collective-permute-start(f32[72,128]{1,0:T(8,128)S(1)} %get-tuple-element.34), channel_id=1, source_target_pairs={{0,192},{64,128},{128,64},{192,0},{1,193},{65,129},{129,65},{193,1... | collective-permute-start | bytes 110600 | tf_op jit(solution)/shard_map/ppermute | solution.py:660
  21.2 1.4 %shard_map.113 = (bf16[256,256]{1,0:T(8,128)(2,1)S(1)}, bf16[256,256]{1,0:T(8,128)(2,1)S(1)}) custom-call(f32[5,5,5]{2,1,0:T(8,128)S(1)} %copy-done.5), custom_call_target="tpu_custom_call" | custom-call | flops 1000000000 | bytes 2097152 | tf_op jit(solution)/shard_map/pallas_call | solution.py:641
  22.6 1.4 %collective-permute-done.3.got_1 = f32[72,128]{1,0:T(8,128)S(1)} collective-permute-done((f32[72,128]{1,0:T(8,128)S(1)}, f32[72,128]{1,0:T(8,128)S(1)}, u32[]{:S(2)}, u32[]{:S(2)}) %collective-permute-start.3) | collective-permute-done | bytes 36896 | tf_op jit(solution)/shard_map/ppermute | solution.py:660
  24.0 1.8 %collective-permute-done.4.got_3 = f32[72,128]{1,0:T(8,128)S(1)} collective-permute-done((f32[72,128]{1,0:T(8,128)S(1)}, f32[72,128]{1,0:T(8,128)S(1)}, u32[]{:S(2)}, u32[]{:S(2)}) %collective-permute-start.4) | collective-permute-done | bytes 36896 | tf_op jit(solution)/shard_map/ppermute | solution.py:660
  25.8 0.8 %shard_map.114 = (f32[36,40,128]{2,1,0:T(8,128)S(1)}, f32[16,128]{1,0:T(8,128)S(1)}, f32[80,128]{1,0:T(8,128)S(1)}, f32[80,128]{1,0:T(8,128)S(1)}) custom-call(f32[32,40,128]{2,1,0:T(8,128)S(1)} %get-tuple-element.31.wide_y, f32[8,128]{1,0:T(8,128)S(1)} %get-tuple-element.32.own, f32[8,128]{1,0:T(8,128)S(1)} %collective-permute-done.2.got_2, ...), custom_call_target="tpu_custom_call" | custom-call | flops 1000000 | bytes 2097152 | tf_op jit(solution)/shard_map/pallas_call | solution.py:641
  26.6 1.6 %collective-permute-start.5 = (f32[80,128]{1,0:T(8,128)S(1)}, f32[80,128]{1,0:T(8,128)S(1)}, u32[]{:S(2)}, u32[]{:S(2)}) collective-permute-start(f32[80,128]{1,0:T(8,128)S(1)} %get-tuple-element.37), channel_id=1, source_target_pairs={{0,1},{1,2},{2,3},{3,4},{4,5},{5,6},{6,7},{7,8},{8,9},{9,10},{10,1... | collective-permute-start | bytes 122888 | tf_op jit(solution)/shard_map/ppermute | solution.py:672
  28.3 2.6 %collective-permute-start.6 = (f32[80,128]{1,0:T(8,128)S(1)}, f32[80,128]{1,0:T(8,128)S(1)}, u32[]{:S(2)}, u32[]{:S(2)}) collective-permute-start(f32[80,128]{1,0:T(8,128)S(1)} %get-tuple-element.38), channel_id=1, source_target_pairs={{0,47},{1,0},{2,1},{3,2},{4,3},{5,4},{6,5},{7,6},{8,7},{9,8},{10,9... | collective-permute-start | bytes 122888 | tf_op jit(solution)/shard_map/ppermute | solution.py:672
  30.9 1.1 %collective-permute-start.7 = (f32[16,128]{1,0:T(8,128)S(1)}, f32[16,128]{1,0:T(8,128)S(1)}, u32[]{:S(2)}, u32[]{:S(2)}) collective-permute-start(f32[16,128]{1,0:T(8,128)S(1)} %get-tuple-element.44.own), channel_id=1, source_target_pairs={{0,2},{1,3},{2,0},{3,1},{4,6},{5,7},{6,4},{7,5},{8,10},{9,11},{10,... | collective-permute-start | bytes 24584 | tf_op jit(solution)/shard_map/ppermute | solution.py:660
  31.9 1.6 %shard_map.115 = (bf16[256,128]{1,0:T(8,128)(2,1)S(1)}, bf16[256,128]{1,0:T(8,128)(2,1)S(1)}, bf16[128,128]{1,0:T(8,128)(2,1)S(1)}, bf16[128,128]{1,0:T(8,128)(2,1)S(1)}) custom-call(f32[5,5,5]{2,1,0:T(8,128)S(1)} %copy-done.6, f32[5,5,5]{2,1,0:T(8,128)S(1)} %copy-done.7), custom_call_target="tpu_custom_call" | custom-call | flops 1000000000 | bytes 2097152 | tf_op jit(solution)/shard_map/pallas_call | solution.py:641
  33.6 0.0 copy-start.1
  33.6 2.4 %collective-permute-done.7.got_2 = f32[16,128]{1,0:T(8,128)S(1)} collective-permute-done((f32[16,128]{1,0:T(8,128)S(1)}, f32[16,128]{1,0:T(8,128)S(1)}, u32[]{:S(2)}, u32[]{:S(2)}) %collective-permute-start.7) | collective-permute-done | bytes 8224 | tf_op jit(solution)/shard_map/ppermute | solution.py:660
  36.0 0.0 collective-permute-done.5.from_low
  36.0 0.0 collective-permute-done.6.from_high
  36.0 0.2 shard_map.117.piece_0
  36.2 1.8 %collective-permute-start.8 = (f32[3,16,128]{2,1,0:T(8,128)S(1)}, f32[3,16,128]{2,1,0:T(8,128)S(1)}, u32[]{:S(2)}, u32[]{:S(2)}) collective-permute-start(f32[3,16,128]{2,1,0:T(8,128)S(1)} %shard_map.117.piece_0), channel_id=1, source_target_pairs={{0,8},{1,9},{2,10},{3,11},{4,12},{5,13},{6,14},{7,15},{8,32},{9,33... | collective-permute-start | bytes 73736 | tf_op jit(solution)/shard_map/ppermute | solution.py:672
  38.0 4.3 %collective-permute-start.9 = (f32[3,16,128]{2,1,0:T(8,128)S(1)}, f32[3,16,128]{2,1,0:T(8,128)S(1)}, u32[]{:S(2)}, u32[]{:S(2)}) collective-permute-start(f32[3,16,128]{2,1,0:T(8,128)S(1)} %shard_map.117.piece_0), channel_id=1, source_target_pairs={{0,4},{1,5},{2,6},{3,7},{4,8},{5,9},{6,10},{7,11},{8,12},{9,13},{1... | collective-permute-start | bytes 73736 | tf_op jit(solution)/shard_map/ppermute | solution.py:672
  42.3 0.0 collective-permute-start.10
  42.4 2.7 %shard_map.116.base = f32[32,32,128]{2,1,0:T(8,128)S(1)} custom-call(f32[36,40,128]{2,1,0:T(8,128)S(1)} %get-tuple-element.36.wide, f32[80,128]{1,0:T(8,128)S(1)} %collective-permute-done.5.from_low, f32[80,128]{1,0:T(8,128)S(1)} %collective-permute-done.6.from_high, bf16[256,256]{1,0:T(8,128)(2,1)S(1)} %get-tuple-element.35.after.b1h, ...), custom_call_target="tpu_custom_call" | custom-call | flops 1000000 | bytes 2097152 | tf_op jit(solution)/shard_map/pallas_call | solution.py:641
  45.1 1.1 %collective-permute-done.10.piece_3 = f32[3,16,128]{2,1,0:T(8,128)S(1)} collective-permute-done((f32[3,16,128]{2,1,0:T(8,128)S(1)}, f32[3,16,128]{2,1,0:T(8,128)S(1)}, u32[]{:S(2)}, u32[]{:S(2)}) %collective-permute-start.10) | collective-permute-done | bytes 24608 | tf_op jit(solution)/shard_map/ppermute | solution.py:672
  46.2 2.2 %shard_map.118 = f32[32,32,32]{2,1,0:T(8,128)} custom-call(f32[32,32,128]{2,1,0:T(8,128)S(1)} %shard_map.116.base, f32[3,16,128]{2,1,0:T(8,128)S(1)} %shard_map.117.piece_0, f32[3,16,128]{2,1,0:T(8,128)S(1)} %collective-permute-done.8.piece_1, f32[3,16,128]{2,1,0:T(8,128)S(1)} %collective-permute-done.9.piece_2, ...), custom_call_target="tpu_custom_call" | custom-call | flops 1000000 | bytes 2097152 | tf_op jit(solution)/shard_map/pallas_call | solution.py:641
  (17 shorter events, 0.0 us)
Async XLA Ops:
  0.0 21.2 %copy-start.5 = (f32[5,5,5]{2,1,0:T(8,128)S(1)}, f32[5,5,5]{2,1,0:T(8,128)}, u32[]{:S(2)}) copy-start(f32[5,5,5]{2,1,0:T(8,128)} %refs_0_.2) | copy-start | bytes 1504
  6.0 1.3 %collective-permute-start = (f32[72,128]{1,0:T(8,128)S(1)}, f32[72,128]{1,0:T(8,128)S(1)}, u32[]{:S(2)}, u32[]{:S(2)}) collective-permute-start(f32[72,128]{1,0:T(8,128)S(1)} %get-tuple-element.29), channel_id=1, source_target_pairs={{0,16},{16,0},{32,48},{48,32},{1,17},{17,1},{33,49},{49,33},{2,18}... | collective-permute-start | bytes 110600 | tf_op jit(solution)/shard_map/ppermute | solution.py:660
  7.3 9.2 %collective-permute-start.1 = (f32[40,128]{1,0:T(8,128)S(1)}, f32[40,128]{1,0:T(8,128)S(1)}, u32[]{:S(2)}, u32[]{:S(2)}) collective-permute-start(f32[40,128]{1,0:T(8,128)S(1)} %shard_map.111.own), channel_id=1, source_target_pairs={{0,32},{16,48},{32,0},{48,16},{1,33},{17,49},{33,1},{49,17},{2,34}... | collective-permute-start | bytes 61448 | tf_op jit(solution)/shard_map/ppermute | solution.py:660
  13.6 1.0 %copy-start = (f32[32,32,128]{2,1,0:T(8,128)S(1)}, f32[32,32,128]{2,1,0:T(8,128)}, u32[]{:S(2)}) copy-start(f32[32,32,128]{2,1,0:T(8,128)} %get-tuple-element.26.packed) | copy-start | bytes 1572868
  14.7 0.9 %copy-start.2 = (f32[8,32,128]{2,1,0:T(8,128)S(1)}, f32[8,32,128]{2,1,0:T(8,128)}, u32[]{:S(2)}) copy-start(f32[8,32,128]{2,1,0:T(8,128)} %constant.10.clone.factors) | copy-start | bytes 393220
  16.9 5.6 %collective-permute-start.2 = (f32[8,128]{1,0:T(8,128)S(1)}, f32[8,128]{1,0:T(8,128)S(1)}, u32[]{:S(2)}, u32[]{:S(2)}) collective-permute-start(f32[8,128]{1,0:T(8,128)S(1)} %get-tuple-element.32.own), channel_id=1, source_target_pairs={{0,128},{64,192},{128,0},{192,64},{1,129},{65,193},{129,1},{193,65... | collective-permute-start | bytes 12296 | tf_op jit(solution)/shard_map/ppermute | solution.py:660
  20.1 4.0 %collective-permute-start.3 = (f32[72,128]{1,0:T(8,128)S(1)}, f32[72,128]{1,0:T(8,128)S(1)}, u32[]{:S(2)}, u32[]{:S(2)}) collective-permute-start(f32[72,128]{1,0:T(8,128)S(1)} %get-tuple-element.33), channel_id=1, source_target_pairs={{0,64},{64,0},{128,192},{192,128},{1,65},{65,1},{129,193},{193,129... | collective-permute-start | bytes 110600 | tf_op jit(solution)/shard_map/ppermute | solution.py:660
  20.6 11.3 %copy-start.6 = (f32[5,5,5]{2,1,0:T(8,128)S(1)}, f32[5,5,5]{2,1,0:T(8,128)}, u32[]{:S(2)}) copy-start(f32[5,5,5]{2,1,0:T(8,128)} %refs_0_.3) | copy-start | bytes 1504
  20.6 11.3 %copy-start.7 = (f32[5,5,5]{2,1,0:T(8,128)S(1)}, f32[5,5,5]{2,1,0:T(8,128)}, u32[]{:S(2)}) copy-start(f32[5,5,5]{2,1,0:T(8,128)} %refs_1_.1) | copy-start | bytes 1504
  20.7 5.2 %collective-permute-start.4 = (f32[72,128]{1,0:T(8,128)S(1)}, f32[72,128]{1,0:T(8,128)S(1)}, u32[]{:S(2)}, u32[]{:S(2)}) collective-permute-start(f32[72,128]{1,0:T(8,128)S(1)} %get-tuple-element.34), channel_id=1, source_target_pairs={{0,192},{64,128},{128,64},{192,0},{1,193},{65,129},{129,65},{193,1... | collective-permute-start | bytes 110600 | tf_op jit(solution)/shard_map/ppermute | solution.py:660
  26.6 9.4 %collective-permute-start.5 = (f32[80,128]{1,0:T(8,128)S(1)}, f32[80,128]{1,0:T(8,128)S(1)}, u32[]{:S(2)}, u32[]{:S(2)}) collective-permute-start(f32[80,128]{1,0:T(8,128)S(1)} %get-tuple-element.37), channel_id=1, source_target_pairs={{0,1},{1,2},{2,3},{3,4},{4,5},{5,6},{6,7},{7,8},{8,9},{9,10},{10,1... | collective-permute-start | bytes 122888 | tf_op jit(solution)/shard_map/ppermute | solution.py:672
  28.3 7.7 %collective-permute-start.6 = (f32[80,128]{1,0:T(8,128)S(1)}, f32[80,128]{1,0:T(8,128)S(1)}, u32[]{:S(2)}, u32[]{:S(2)}) collective-permute-start(f32[80,128]{1,0:T(8,128)S(1)} %get-tuple-element.38), channel_id=1, source_target_pairs={{0,47},{1,0},{2,1},{3,2},{4,3},{5,4},{6,5},{7,6},{8,7},{9,8},{10,9... | collective-permute-start | bytes 122888 | tf_op jit(solution)/shard_map/ppermute | solution.py:672
  30.8 11.5 %copy-start.3 = (bf16[128,128]{1,0:T(8,128)(2,1)S(1)}, bf16[128,128]{1,0:T(8,128)(2,1)}, u32[]{:S(2)}) copy-start(bf16[128,128]{1,0:T(8,128)(2,1)} %constant.11.clone.prol_2) | copy-start | bytes 98308
  30.9 11.5 %copy-start.4 = (bf16[128,128]{1,0:T(8,128)(2,1)S(1)}, bf16[128,128]{1,0:T(8,128)(2,1)}, u32[]{:S(2)}) copy-start(bf16[128,128]{1,0:T(8,128)(2,1)} %constant.12.clone.prol_1) | copy-start | bytes 98308
  30.9 5.2 %collective-permute-start.7 = (f32[16,128]{1,0:T(8,128)S(1)}, f32[16,128]{1,0:T(8,128)S(1)}, u32[]{:S(2)}, u32[]{:S(2)}) collective-permute-start(f32[16,128]{1,0:T(8,128)S(1)} %get-tuple-element.44.own), channel_id=1, source_target_pairs={{0,2},{1,3},{2,0},{3,1},{4,6},{5,7},{6,4},{7,5},{8,10},{9,11},{10,... | collective-permute-start | bytes 24584 | tf_op jit(solution)/shard_map/ppermute | solution.py:660
  33.6 12.6 %copy-start.1 = (bf16[8,128,128]{2,1,0:T(8,128)(2,1)S(1)}, bf16[8,128,128]{2,1,0:T(8,128)(2,1)}, u32[]{:S(2)}) copy-start(bf16[8,128,128]{2,1,0:T(8,128)(2,1)} %constant.13.clone.qz) | copy-start | bytes 786436
  36.2 8.9 %collective-permute-start.8 = (f32[3,16,128]{2,1,0:T(8,128)S(1)}, f32[3,16,128]{2,1,0:T(8,128)S(1)}, u32[]{:S(2)}, u32[]{:S(2)}) collective-permute-start(f32[3,16,128]{2,1,0:T(8,128)S(1)} %shard_map.117.piece_0), channel_id=1, source_target_pairs={{0,8},{1,9},{2,10},{3,11},{4,12},{5,13},{6,14},{7,15},{8,32},{9,33... | collective-permute-start | bytes 73736 | tf_op jit(solution)/shard_map/ppermute | solution.py:672
  38.0 7.1 %collective-permute-start.9 = (f32[3,16,128]{2,1,0:T(8,128)S(1)}, f32[3,16,128]{2,1,0:T(8,128)S(1)}, u32[]{:S(2)}, u32[]{:S(2)}) collective-permute-start(f32[3,16,128]{2,1,0:T(8,128)S(1)} %shard_map.117.piece_0), channel_id=1, source_target_pairs={{0,4},{1,5},{2,6},{3,7},{4,8},{5,9},{6,10},{7,11},{8,12},{9,13},{1... | collective-permute-start | bytes 73736 | tf_op jit(solution)/shard_map/ppermute | solution.py:672
  42.3 3.8 %collective-permute-start.10 = (f32[3,16,128]{2,1,0:T(8,128)S(1)}, f32[3,16,128]{2,1,0:T(8,128)S(1)}, u32[]{:S(2)}, u32[]{:S(2)}) collective-permute-start(f32[3,16,128]{2,1,0:T(8,128)S(1)} %shard_map.117.piece_0), channel_id=1, source_target_pairs={{0,44},{1,45},{2,46},{3,47},{4,0},{5,1},{6,2},{7,3},{8,4},{9,5},{1... | collective-permute-start | bytes 73736 | tf_op jit(solution)/shard_map/ppermute | solution.py:672

commit v8 on v7

--- a/solution.py
+++ b/solution.py
@@ -319,7 +319,7 @@
     out[FACE : FACE + 8, :] = place_y(raw[...], index[1]) + place_y(other, partner)
 
 
-def widen_y_kernel(framed, own, got_1, got_2, after, out, raw_out, face_1, face_3):
+def widen_y_kernel(framed, own, got_1, got_2, after, out, raw_out, slots):
     index, _ = place()
     even, one, two = nearest(index[1])
     total = own[FACE : FACE + 8, :] + got_2[FACE : FACE + 8, :]
@@ -334,11 +334,12 @@
                 slab = roll(roll(face[8 * v : 8 * v + 8], -r, 0), lane - to)
                 slab = lanes_of(slab, lane, width)
                 out[p, start : start + count, :] += slab[0:count]
-    even, one, _ = nearest(index[0])
-    for ref, to_high in ((face_1, even), (face_3, one)):
+    for n in range(4):
+        to_high = index[0] < n
         f = jnp.where(to_high, 30, 0)
         s = jnp.where(to_high, 14, 0)
         t = jnp.where(to_high, 6, 0)
+        ref = slots.at[n]
         ref[0:40, :] = lanes_of(out[f], 0, 32) + lanes_of(roll(out[f + 1], 32), 32, 32)
         ref[0:16, :] += taps(
             [(1.0, lanes_of(roll(out[t + k, 0:16, :], 11 * k), THI + 11 * k, 11)) for k in range(5)]
@@ -349,21 +350,19 @@
         ref[64:72, :] = total
 
 
-def widen_x_kernel(wide_y, own, got_2, got_1, got_3, after, out, raw_out, to_high, to_low):
+def widen_x_kernel(wide_y, own, got, after, out, raw_out, to_high, to_low):
     index, _ = place()
-    even, one, two = nearest(index[0])
     total = None
     lane = iota((16, 128), 1)
-    for step, tile in ((0, own[...]), (1, got_1[64:72, :]), (2, got_2[...]), (3, got_3[64:72, :])):
+    for n in range(4):
+        tile = jnp.where(index[0] == n, own[...], got[n, 64:72, :])
         tall = jnp.concatenate([tile, roll(tile, 64)], axis=0)
         tall = jnp.where(lane < 64, tall, 0.0)
-        at = lax.rem(32 * jnp.bitwise_xor(index[0], step) + 120, 128)
-        moved = pltpu.roll(tall, at, 1)
+        moved = roll(tall, 32 * n - 8)
         total = moved if total is None else total + moved
     raw_out[...] = total
-    a, b = got_1[...], got_3[...]
-    low = jnp.where(even, 0.0, a) + jnp.where(two, b, 0.0)
-    high = jnp.where(even, a, 0.0) + jnp.where(one, b, 0.0)
+    low = jnp.where(index[0] == 0, 0.0, got[jnp.maximum(index[0] - 1, 0)])
+    high = jnp.where(index[0] == 3, 0.0, got[jnp.minimum(index[0] + 1, 3)])
     out[0:2] = jnp.zeros((2, 40, 128), F32)
     out[34:36] = jnp.zeros((2, 40, 128), F32)
     out[2:34] = wide_y[...]
@@ -721,20 +720,20 @@
         (jnp.asarray(np.concatenate([qx, qy])), packed),
         (pltpu.VMEM((18, 64, 128), BF16), pltpu.VMEM((18, 64, 128), BF16)),
     )
-    wide_y, raw, face_1, face_3 = call(
+    wide_y, raw, slots = call(
         widen_y_kernel,
-        (shape(32, 40, 128), shape(8, 128), shape(72, 128), shape(72, 128)),
+        (shape(32, 40, 128), shape(8, 128), shape(4, 72, 128)),
         (framed, relay, got_1, got_2, rise),
         spaces={4: ANY},
         aliases={0: 0},
     )
-    got_3, got_1, got_2 = exchange((face_3, face_1, raw), "gx", (3, 1, 2))
+    got = lax.all_to_all(slots, "gx", split_axis=0, concat_axis=0, tiled=True)
     bands_1 = banded(BANDS[:1], kernel_fine)
     wide_x, raw, to_high, to_low = call(
         widen_x_kernel,
         (shape(36, 40, 128), shape(16, 128), shape(80, 128), shape(80, 128)),
-        (wide_y, raw, got_2, got_1, got_3, bands_1[0]),
-        spaces={5: ANY},
+        (wide_y, raw, got, bands_1[0]),
+        spaces={3: ANY},
     )
     from_low, from_high = turn(to_high, 1), turn(to_low, -1)
     (got_2,) = exchange((raw,), "gz", (2,))

time: 48.7 us -> 51 us (1.047)
  waiting for transfers between devices: 7.92 us -> 9.38 us
  local copies, waits for them, and re-layouts: 1.97 us -> 3.22 us
  starting transfers between devices: 22.1 us -> 20.9 us
  Pallas kernels: 15.5 us -> 16.2 us
    all_to_all x0 -> x1, waiting for transfers between devices: none -> 4.68 us  [shards(): got = lax.all_to_all(slots, 'gx', split_axis=0, concat_axis=0, tiled=True)]
    all_to_all x0 -> x1, starting transfers between devices: none -> 4.3 us  [shards(): got = lax.all_to_all(slots, 'gx', split_axis=0, concat_axis=0, tiled=True)]
    ppermute x6 -> x3, starting transfers between devices: 11.7 us -> 7.48 us  [exchange(): lax.ppermute(value, axis, [(i, i ^ step) for i in range(size)])]
    ppermute x6 -> x3, waiting for transfers between devices: 6.85 us -> 3.61 us  [exchange(): lax.ppermute(value, axis, [(i, i ^ step) for i in range(size)])]
    unnamed x16 -> x20, local copies, waits for them, and re-layouts: 1.97 us -> 3.22 us
    ppermute x5, starting transfers between devices: 10.3 us -> 9.1 us  [turn(): return lax.ppermute(value, ('gy', 'gz'), pairs)]
    pallas_call x10, Pallas kernels: 15.5 us -> 16.2 us  [call(): pl.pallas_call(kernel, out_shape=outs, in_specs=[spaces.get(i, VMEM) for...]
  transfers between devices with their start and end apart: 11 -> 9, of which waited for: 5 -> 4; matrix products, arithmetic and copies ran while one was open for 0% -> 0% of each run, Pallas kernels for 14% -> 13%
where the time goes in v8:
time: 51 us; the launch traced here: 50.7 us
  starting transfers between devices  20.9 us (41%)
  Pallas kernels  16.2 us (32%)
  waiting for transfers between devices  9.38 us (18%)
  local copies, waits for them, and re-layouts  3.22 us (6%)
  other arithmetic  0.71 us (1%)
    pallas_call x10, Pallas kernels, call(): pl.pallas_call(kernel, out_shape=outs, in_specs=[spaces.get(i, VMEM) for...  16.2 us
    ppermute x5, starting transfers between devices, turn(): return lax.ppermute(value, ('gy', 'gz'), pairs)  9.1 us
    ppermute x3, starting transfers between devices, exchange(): lax.ppermute(value, axis, [(i, i ^ step) for i in range(size)])  7.48 us
    all_to_all x1, waiting for transfers between devices, shards(): got = lax.all_to_all(slots, 'gx', split_axis=0, concat_axis=0, tiled=True)  4.68 us
    all_to_all x1, starting transfers between devices, shards(): got = lax.all_to_all(slots, 'gx', split_axis=0, concat_axis=0, tiled=True)  4.3 us
    ppermute x3, waiting for transfers between devices, exchange(): lax.ppermute(value, axis, [(i, i ^ step) for i in range(size)])  3.61 us
    unnamed x20, local copies, waits for them, and re-layouts  3.22 us
    ppermute x5, waiting for transfers between devices, turn(): return lax.ppermute(value, ('gy', 'gz'), pairs)  1.09 us
  transfers between devices with their start and end apart: 9, of which 4 were waited for; matrix products, arithmetic and copies ran while one was open for 0% of the time, Pallas kernels for 13%

profile of v8, /device:TPU:32, one launch (start us, length us, event | category | flops | bytes accessed | tf_op | source)
XLA Modules:
  0.0 50.7 jit_solution(3302883230188400158)
XLA Ops:
  0.0 0.7 %multiply_add_fusion.codes = s32[384]{0:T(512)S(1)} fusion(s32[384]{0:T(512)} %param.12, s32[384]{0:T(512)} %param.13), kind=kLoop, calls=%fused_computation | loop fusion | flops 768 | bytes 4608 | tf_op jit(solution)/shard_map/add | solution.py:689
  0.7 5.2 %shard_map.109 = (f32[32,32,128]{2,1,0:T(8,128)}, f32[8,128]{1,0:T(8,128)S(1)}, f32[72,128]{1,0:T(8,128)S(1)}) custom-call(s32[384]{0:T(512)S(1)} %multiply_add_fusion.codes, f32[384,128]{1,0:T(8,128)} %charges_hbm.1, bf16[4608,128]{1,0:T(8,128)(2,1)} %bitcast.1), custom_call_target="tpu_custom_call" | custom-call | flops 1000000 | bytes 2097152 | tf_op jit(solution)/shard_map/pallas_call | solution.py:640
  6.0 0.1 collective-permute-start
  6.1 1.2 %collective-permute-done.got.got_1 = f32[72,128]{1,0:T(8,128)S(1)} collective-permute-done((f32[72,128]{1,0:T(8,128)S(1)}, f32[72,128]{1,0:T(8,128)S(1)}, u32[]{:S(2)}, u32[]{:S(2)}) %collective-permute-start) | collective-permute-done | bytes 36896 | tf_op jit(solution)/shard_map/ppermute | solution.py:659
  7.3 0.1 shard_map.111.own
  7.3 6.3 %collective-permute-start.1 = (f32[40,128]{1,0:T(8,128)S(1)}, f32[40,128]{1,0:T(8,128)S(1)}, u32[]{:S(2)}, u32[]{:S(2)}) collective-permute-start(f32[40,128]{1,0:T(8,128)S(1)} %shard_map.111.own), channel_id=1, source_target_pairs={{0,32},{16,48},{32,0},{48,16},{1,33},{17,49},{33,1},{49,17},{2,34}... | collective-permute-start | bytes 61448 | tf_op jit(solution)/shard_map/ppermute | solution.py:659
  13.7 1.0 %copy-done.2 = f32[32,32,128]{2,1,0:T(8,128)S(1)} copy-done((f32[32,32,128]{2,1,0:T(8,128)S(1)}, f32[32,32,128]{2,1,0:T(8,128)}, u32[]{:S(2)}) %copy-start.2) | copy-done | bytes 524312
  14.7 0.9 %copy-done.4 = f32[8,32,128]{2,1,0:T(8,128)S(1)} copy-done((f32[8,32,128]{2,1,0:T(8,128)S(1)}, f32[8,32,128]{2,1,0:T(8,128)}, u32[]{:S(2)}) %copy-start.4) | copy-done | bytes 131096
  15.6 1.0 %shard_map.110 = (bf16[1024,896]{1,0:T(8,128)(2,1)S(1)}, bf16[1024,896]{1,0:T(8,128)(2,1)S(1)}, bf16[1024,256]{1,0:T(8,128)(2,1)S(1)}, f32[32,40,128]{2,1,0:T(8,128)S(1)}) custom-call(f32[8,32,128]{2,1,0:T(8,128)S(1)} %copy-done.4, f32[32,32,128]{2,1,0:T(8,128)S(1)} %copy-done.2), custom_call_target="tpu_custom_call" | custom-call | flops 1000000 | bytes 2097152 | tf_op jit(solution)/shard_map/pallas_call | solution.py:640
  16.6 1.3 %copy-done = bf16[1024,896]{1,0:T(8,128)(2,1)} copy-done((bf16[1024,896]{1,0:T(8,128)(2,1)}, bf16[1024,896]{1,0:T(8,128)(2,1)S(1)}, u32[]{:S(2)}) %copy-start) | copy-done | bytes 1835032
  17.8 0.0 collective-permute-done.1.got_2
  17.8 1.1 %shard_map.112 = (f32[32,40,128]{2,1,0:T(8,128)S(1)}, f32[8,128]{1,0:T(8,128)S(1)}, f32[4,72,128]{2,1,0:T(8,128)}) custom-call(f32[32,40,128]{2,1,0:T(8,128)S(1)} %get-tuple-element.26.framed, f32[40,128]{1,0:T(8,128)S(1)} %shard_map.111.own, f32[72,128]{1,0:T(8,128)S(1)} %collective-permute-done.got.got_1, ...), custom_call_target="tpu_custom_call", output_to_operand_aliasing={{0}: (0, {})} | custom-call | flops 1000000 | bytes 2097152 | tf_op jit(solution)/shard_map/pallas_call | solution.py:640
  18.9 4.3 %all-to-all-start = ((f32[4,72,128]{2,1,0:T(8,128)}), f32[4,72,128]{2,1,0:T(8,128)S(1)}, u32[]{:S(2)}, u32[]{:S(2)}) async-start(f32[4,72,128]{2,1,0:T(8,128)} %get-tuple-element.32), calls=%async_computation | async-start | bytes 294912 | tf_op jit(solution)/shard_map/all_to_all | solution.py:730
  23.2 1.4 %shard_map.113 = (bf16[256,256]{1,0:T(8,128)(2,1)S(1)}, bf16[256,256]{1,0:T(8,128)(2,1)S(1)}) custom-call(f32[5,5,5]{2,1,0:T(8,128)S(1)} %copy-done.7), custom_call_target="tpu_custom_call" | custom-call | flops 1000000000 | bytes 2097152 | tf_op jit(solution)/shard_map/pallas_call | solution.py:640
  24.6 4.7 %all-to-all-done.got = f32[4,72,128]{2,1,0:T(8,128)S(1)} async-done(((f32[4,72,128]{2,1,0:T(8,128)}), f32[4,72,128]{2,1,0:T(8,128)S(1)}, u32[]{:S(2)}, u32[]{:S(2)}) %all-to-all-start) | async-done | bytes 147488 | tf_op jit(solution)/shard_map/all_to_all | solution.py:730
  29.3 0.8 %shard_map.114 = (f32[36,40,128]{2,1,0:T(8,128)S(1)}, f32[16,128]{1,0:T(8,128)S(1)}, f32[80,128]{1,0:T(8,128)S(1)}, f32[80,128]{1,0:T(8,128)S(1)}) custom-call(f32[32,40,128]{2,1,0:T(8,128)S(1)} %get-tuple-element.30.wide_y, f32[8,128]{1,0:T(8,128)S(1)} %get-tuple-element.31.own, f32[4,72,128]{2,1,0:T(8,128)S(1)} %all-to-all-done.got, ...), custom_call_target="tpu_custom_call" | custom-call | flops 1000000 | bytes 2097152 | tf_op jit(solution)/shard_map/pallas_call | solution.py:640
  30.1 1.6 %collective-permute-start.2 = (f32[80,128]{1,0:T(8,128)S(1)}, f32[80,128]{1,0:T(8,128)S(1)}, u32[]{:S(2)}, u32[]{:S(2)}) collective-permute-start(f32[80,128]{1,0:T(8,128)S(1)} %get-tuple-element.35), channel_id=1, source_target_pairs={{0,1},{1,2},{2,3},{3,4},{4,5},{5,6},{6,7},{7,8},{8,9},{9,10},{10,1... | collective-permute-start | bytes 122888 | tf_op jit(solution)/shard_map/ppermute | solution.py:671
  31.7 2.6 %collective-permute-start.3 = (f32[80,128]{1,0:T(8,128)S(1)}, f32[80,128]{1,0:T(8,128)S(1)}, u32[]{:S(2)}, u32[]{:S(2)}) collective-permute-start(f32[80,128]{1,0:T(8,128)S(1)} %get-tuple-element.36), channel_id=1, source_target_pairs={{0,47},{1,0},{2,1},{3,2},{4,3},{5,4},{6,5},{7,6},{8,7},{9,8},{10,9... | collective-permute-start | bytes 122888 | tf_op jit(solution)/shard_map/ppermute | solution.py:671
  34.3 1.1 %collective-permute-start.4 = (f32[16,128]{1,0:T(8,128)S(1)}, f32[16,128]{1,0:T(8,128)S(1)}, u32[]{:S(2)}, u32[]{:S(2)}) collective-permute-start(f32[16,128]{1,0:T(8,128)S(1)} %get-tuple-element.42.own), channel_id=1, source_target_pairs={{0,2},{1,3},{2,0},{3,1},{4,6},{5,7},{6,4},{7,5},{8,10},{9,11},{10,... | collective-permute-start | bytes 24584 | tf_op jit(solution)/shard_map/ppermute | solution.py:659
  35.4 1.6 %shard_map.115 = (bf16[256,128]{1,0:T(8,128)(2,1)S(1)}, bf16[256,128]{1,0:T(8,128)(2,1)S(1)}, bf16[128,128]{1,0:T(8,128)(2,1)S(1)}, bf16[128,128]{1,0:T(8,128)(2,1)S(1)}) custom-call(f32[5,5,5]{2,1,0:T(8,128)S(1)} %copy-done.8, f32[5,5,5]{2,1,0:T(8,128)S(1)} %copy-done.9), custom_call_target="tpu_custom_call" | custom-call | flops 1000000000 | bytes 2097152 | tf_op jit(solution)/shard_map/pallas_call | solution.py:640
  37.0 2.4 %collective-permute-done.4.got_2 = f32[16,128]{1,0:T(8,128)S(1)} collective-permute-done((f32[16,128]{1,0:T(8,128)S(1)}, f32[16,128]{1,0:T(8,128)S(1)}, u32[]{:S(2)}, u32[]{:S(2)}) %collective-permute-start.4) | collective-permute-done | bytes 8224 | tf_op jit(solution)/shard_map/ppermute | solution.py:659
  39.4 0.0 collective-permute-done.2.from_low
  39.5 0.0 collective-permute-done.3.from_high
  39.5 0.2 shard_map.117.piece_0
  39.6 1.5 %collective-permute-start.5 = (f32[3,16,128]{2,1,0:T(8,128)S(1)}, f32[3,16,128]{2,1,0:T(8,128)S(1)}, u32[]{:S(2)}, u32[]{:S(2)}) collective-permute-start(f32[3,16,128]{2,1,0:T(8,128)S(1)} %shard_map.117.piece_0), channel_id=1, source_target_pairs={{0,8},{1,9},{2,10},{3,11},{4,12},{5,13},{6,14},{7,15},{8,32},{9,33... | collective-permute-start | bytes 73736 | tf_op jit(solution)/shard_map/ppermute | solution.py:671
  41.2 3.3 %collective-permute-start.6 = (f32[3,16,128]{2,1,0:T(8,128)S(1)}, f32[3,16,128]{2,1,0:T(8,128)S(1)}, u32[]{:S(2)}, u32[]{:S(2)}) collective-permute-start(f32[3,16,128]{2,1,0:T(8,128)S(1)} %shard_map.117.piece_0), channel_id=1, source_target_pairs={{0,4},{1,5},{2,6},{3,7},{4,8},{5,9},{6,10},{7,11},{8,12},{9,13},{1... | collective-permute-start | bytes 73736 | tf_op jit(solution)/shard_map/ppermute | solution.py:671
  44.5 0.0 collective-permute-start.7
  44.6 2.7 %shard_map.116.base = f32[32,32,128]{2,1,0:T(8,128)S(1)} custom-call(f32[36,40,128]{2,1,0:T(8,128)S(1)} %get-tuple-element.34.wide, f32[80,128]{1,0:T(8,128)S(1)} %collective-permute-done.2.from_low, f32[80,128]{1,0:T(8,128)S(1)} %collective-permute-done.3.from_high, bf16[256,256]{1,0:T(8,128)(2,1)S(1)} %get-tuple-element.33.after.b1h, ...), custom_call_target="tpu_custom_call" | custom-call | flops 1000000 | bytes 2097152 | tf_op jit(solution)/shard_map/pallas_call | solution.py:640
  47.3 0.0 collective-permute-done.5.piece_1
  47.3 0.0 collective-permute-done.6.piece_2
  47.3 1.1 %collective-permute-done.7.piece_3 = f32[3,16,128]{2,1,0:T(8,128)S(1)} collective-permute-done((f32[3,16,128]{2,1,0:T(8,128)S(1)}, f32[3,16,128]{2,1,0:T(8,128)S(1)}, u32[]{:S(2)}, u32[]{:S(2)}) %collective-permute-start.7) | collective-permute-done | bytes 24608 | tf_op jit(solution)/shard_map/ppermute | solution.py:671
  48.4 2.2 %shard_map.118 = f32[32,32,32]{2,1,0:T(8,128)} custom-call(f32[32,32,128]{2,1,0:T(8,128)S(1)} %shard_map.116.base, f32[3,16,128]{2,1,0:T(8,128)S(1)} %shard_map.117.piece_0, f32[3,16,128]{2,1,0:T(8,128)S(1)} %collective-permute-done.5.piece_1, f32[3,16,128]{2,1,0:T(8,128)S(1)} %collective-permute-done.6.piece_2, ...), custom_call_target="tpu_custom_call" | custom-call | flops 1000000 | bytes 2097152 | tf_op jit(solution)/shard_map/pallas_call | solution.py:640
  (17 shorter events, 0.0 us)
Async XLA Ops:
  0.0 23.2 %copy-start.7 = (f32[5,5,5]{2,1,0:T(8,128)S(1)}, f32[5,5,5]{2,1,0:T(8,128)}, u32[]{:S(2)}) copy-start(f32[5,5,5]{2,1,0:T(8,128)} %refs_0_.2) | copy-start | bytes 1504
  6.0 1.3 %collective-permute-start = (f32[72,128]{1,0:T(8,128)S(1)}, f32[72,128]{1,0:T(8,128)S(1)}, u32[]{:S(2)}, u32[]{:S(2)}) collective-permute-start(f32[72,128]{1,0:T(8,128)S(1)} %get-tuple-element.28), channel_id=1, source_target_pairs={{0,16},{16,0},{32,48},{48,32},{1,17},{17,1},{33,49},{49,33},{2,18}... | collective-permute-start | bytes 110600 | tf_op jit(solution)/shard_map/ppermute | solution.py:659
  7.3 10.5 %collective-permute-start.1 = (f32[40,128]{1,0:T(8,128)S(1)}, f32[40,128]{1,0:T(8,128)S(1)}, u32[]{:S(2)}, u32[]{:S(2)}) collective-permute-start(f32[40,128]{1,0:T(8,128)S(1)} %shard_map.111.own), channel_id=1, source_target_pairs={{0,32},{16,48},{32,0},{48,16},{1,33},{17,49},{33,1},{49,17},{2,34}... | collective-permute-start | bytes 61448 | tf_op jit(solution)/shard_map/ppermute | solution.py:659
  13.6 1.0 %copy-start.2 = (f32[32,32,128]{2,1,0:T(8,128)S(1)}, f32[32,32,128]{2,1,0:T(8,128)}, u32[]{:S(2)}) copy-start(f32[32,32,128]{2,1,0:T(8,128)} %get-tuple-element.25.packed) | copy-start | bytes 1572868
  14.7 0.9 %copy-start.4 = (f32[8,32,128]{2,1,0:T(8,128)S(1)}, f32[8,32,128]{2,1,0:T(8,128)}, u32[]{:S(2)}) copy-start(f32[8,32,128]{2,1,0:T(8,128)} %constant.10.clone.factors) | copy-start | bytes 393220
  16.6 1.3 %copy-start = (bf16[1024,896]{1,0:T(8,128)(2,1)}, bf16[1024,896]{1,0:T(8,128)(2,1)S(1)}, u32[]{:S(2)}) copy-start(bf16[1024,896]{1,0:T(8,128)(2,1)S(1)} %get-tuple-element.44.green_low) | copy-start | bytes 5505028
  18.9 10.4 %all-to-all-start = ((f32[4,72,128]{2,1,0:T(8,128)}), f32[4,72,128]{2,1,0:T(8,128)S(1)}, u32[]{:S(2)}, u32[]{:S(2)}) async-start(f32[4,72,128]{2,1,0:T(8,128)} %get-tuple-element.32), calls=%async_computation | async-start | bytes 294912 | tf_op jit(solution)/shard_map/all_to_all | solution.py:730
  23.2 12.2 %copy-start.8 = (f32[5,5,5]{2,1,0:T(8,128)S(1)}, f32[5,5,5]{2,1,0:T(8,128)}, u32[]{:S(2)}) copy-start(f32[5,5,5]{2,1,0:T(8,128)} %refs_0_.3) | copy-start | bytes 1504
  23.2 12.2 %copy-start.9 = (f32[5,5,5]{2,1,0:T(8,128)S(1)}, f32[5,5,5]{2,1,0:T(8,128)}, u32[]{:S(2)}) copy-start(f32[5,5,5]{2,1,0:T(8,128)} %refs_1_.1) | copy-start | bytes 1504
  30.1 9.4 %collective-permute-start.2 = (f32[80,128]{1,0:T(8,128)S(1)}, f32[80,128]{1,0:T(8,128)S(1)}, u32[]{:S(2)}, u32[]{:S(2)}) collective-permute-start(f32[80,128]{1,0:T(8,128)S(1)} %get-tuple-element.35), channel_id=1, source_target_pairs={{0,1},{1,2},{2,3},{3,4},{4,5},{5,6},{6,7},{7,8},{8,9},{9,10},{10,1... | collective-permute-start | bytes 122888 | tf_op jit(solution)/shard_map/ppermute | solution.py:671
  31.7 7.7 %collective-permute-start.3 = (f32[80,128]{1,0:T(8,128)S(1)}, f32[80,128]{1,0:T(8,128)S(1)}, u32[]{:S(2)}, u32[]{:S(2)}) collective-permute-start(f32[80,128]{1,0:T(8,128)S(1)} %get-tuple-element.36), channel_id=1, source_target_pairs={{0,47},{1,0},{2,1},{3,2},{4,3},{5,4},{6,5},{7,6},{8,7},{9,8},{10,9... | collective-permute-start | bytes 122888 | tf_op jit(solution)/shard_map/ppermute | solution.py:671
  34.3 10.3 %copy-start.5 = (bf16[128,128]{1,0:T(8,128)(2,1)S(1)}, bf16[128,128]{1,0:T(8,128)(2,1)}, u32[]{:S(2)}) copy-start(bf16[128,128]{1,0:T(8,128)(2,1)} %constant.11.clone.prol_2) | copy-start | bytes 98308
  34.3 10.3 %copy-start.6 = (bf16[128,128]{1,0:T(8,128)(2,1)S(1)}, bf16[128,128]{1,0:T(8,128)(2,1)}, u32[]{:S(2)}) copy-start(bf16[128,128]{1,0:T(8,128)(2,1)} %constant.12.clone.prol_1) | copy-start | bytes 98308
  34.3 5.2 %collective-permute-start.4 = (f32[16,128]{1,0:T(8,128)S(1)}, f32[16,128]{1,0:T(8,128)S(1)}, u32[]{:S(2)}, u32[]{:S(2)}) collective-permute-start(f32[16,128]{1,0:T(8,128)S(1)} %get-tuple-element.42.own), channel_id=1, source_target_pairs={{0,2},{1,3},{2,0},{3,1},{4,6},{5,7},{6,4},{7,5},{8,10},{9,11},{10,... | collective-permute-start | bytes 24584 | tf_op jit(solution)/shard_map/ppermute | solution.py:659
  35.4 13.0 %copy-start.3 = (bf16[8,128,128]{2,1,0:T(8,128)(2,1)S(1)}, bf16[8,128,128]{2,1,0:T(8,128)(2,1)}, u32[]{:S(2)}) copy-start(bf16[8,128,128]{2,1,0:T(8,128)(2,1)} %constant.13.clone.qz) | copy-start | bytes 786436
  37.0 11.3 %copy-start.1 = (bf16[1024,896]{1,0:T(8,128)(2,1)S(1)}, bf16[1024,896]{1,0:T(8,128)(2,1)}, u32[]{:S(2)}) copy-start(bf16[1024,896]{1,0:T(8,128)(2,1)} %copy-done) | copy-start | bytes 5505028
  39.6 7.6 %collective-permute-start.5 = (f32[3,16,128]{2,1,0:T(8,128)S(1)}, f32[3,16,128]{2,1,0:T(8,128)S(1)}, u32[]{:S(2)}, u32[]{:S(2)}) collective-permute-start(f32[3,16,128]{2,1,0:T(8,128)S(1)} %shard_map.117.piece_0), channel_id=1, source_target_pairs={{0,8},{1,9},{2,10},{3,11},{4,12},{5,13},{6,14},{7,15},{8,32},{9,33... | collective-permute-start | bytes 73736 | tf_op jit(solution)/shard_map/ppermute | solution.py:671
  41.2 6.1 %collective-permute-start.6 = (f32[3,16,128]{2,1,0:T(8,128)S(1)}, f32[3,16,128]{2,1,0:T(8,128)S(1)}, u32[]{:S(2)}, u32[]{:S(2)}) collective-permute-start(f32[3,16,128]{2,1,0:T(8,128)S(1)} %shard_map.117.piece_0), channel_id=1, source_target_pairs={{0,4},{1,5},{2,6},{3,7},{4,8},{5,9},{6,10},{7,11},{8,12},{9,13},{1... | collective-permute-start | bytes 73736 | tf_op jit(solution)/shard_map/ppermute | solution.py:671
  44.5 3.8 %collective-permute-start.7 = (f32[3,16,128]{2,1,0:T(8,128)S(1)}, f32[3,16,128]{2,1,0:T(8,128)S(1)}, u32[]{:S(2)}, u32[]{:S(2)}) collective-permute-start(f32[3,16,128]{2,1,0:T(8,128)S(1)} %shard_map.117.piece_0), channel_id=1, source_target_pairs={{0,44},{1,45},{2,46},{3,47},{4,0},{5,1},{6,2},{7,3},{8,4},{9,5},{1... | collective-permute-start | bytes 73736 | tf_op jit(solution)/shard_map/ppermute | solution.py:671

commit v9 on v7

--- a/solution.py
+++ b/solution.py
@@ -349,9 +349,55 @@
         ref[64:72, :] = total
 
 
-def widen_x_kernel(wide_y, own, got_2, got_1, got_3, after, out, raw_out, to_high, to_low):
+def x_faces(index, got_1, got_3):
+    even, one, two = nearest(index)
+    a, b = got_1[0:64, :], got_3[0:64, :]
+    low = jnp.where(even, 0.0, a) + jnp.where(two, b, 0.0)
+    high = jnp.where(even, a, 0.0) + jnp.where(one, b, 0.0)
+    planes = []
+    for face, at in ((low, (0, 0, 0)), (high, (34, 18, 10))):
+        for k in range(2):
+            planes.append((0, at[0] + k, lanes_of(roll(face[0:40], -32 * k), 0, 32)))
+        for k in range(4):
+            planes.append((1, at[1] + k, lanes_of(roll(face[40:64], -18 * k), 0, 18)))
+        for k in range(5):
+            planes.append((2, at[2] + k, lanes_of(roll(face[0:16], -THI - 11 * k), 0, 11)))
+    return planes
+
+
+def widen_x_kernel(wide_y, after, got_1, got_3, out):
     index, _ = place()
-    even, one, two = nearest(index[0])
+    out[0:2] = jnp.zeros((2, 40, 128), F32)
+    out[34:36] = jnp.zeros((2, 40, 128), F32)
+    out[2:34] = wide_y[...]
+    for level, at, values in x_faces(index[0], got_1, got_3):
+        rows = values.shape[0]
+        out[at, 0:rows, :] += roll(values, (0, SEC, THI)[level])
+
+
+Z_LEVELS = ((40, 2, 0, 30), (24, 4, SEC, 14), (16, 5, THI, 6))
+
+
+def chosen_lanes(values, first, count):
+    at = iota(values.shape, 1)
+    return jnp.where((at >= first) & (at < first + count), values, 0.0)
+
+
+def own_z_kernel(wide_y, after, high, low):
+    for ref, to_high in ((high, True), (low, False)):
+        start = 0
+        for (rows, count, lane, top), planes in zip(Z_LEVELS, (32, SPAN_2, SPAN_3)):
+            first = lane + top if to_high else lane
+            total = jnp.zeros((rows, 128), F32)
+            for x in range(planes):
+                kept = chosen_lanes(wide_y[x, 0:rows, :], first, count)
+                total = total + roll(kept, count * (x + 2) - first)
+            ref[start : start + rows, :] = total
+            start += rows
+
+
+def edge_x_kernel(own, got_2, got_1, got_3, high, low, raw_out, to_high, to_low):
+    index, _ = place()
     total = None
     lane = iota((16, 128), 1)
     for step, tile in ((0, own[...]), (1, got_1[64:72, :]), (2, got_2[...]), (3, got_3[64:72, :])):
@@ -361,39 +407,19 @@
         moved = pltpu.roll(tall, at, 1)
         total = moved if total is None else total + moved
     raw_out[...] = total
-    a, b = got_1[...], got_3[...]
-    low = jnp.where(even, 0.0, a) + jnp.where(two, b, 0.0)
-    high = jnp.where(even, a, 0.0) + jnp.where(one, b, 0.0)
-    out[0:2] = jnp.zeros((2, 40, 128), F32)
-    out[34:36] = jnp.zeros((2, 40, 128), F32)
-    out[2:34] = wide_y[...]
-    for face, at in ((low, (0, 0, 0)), (high, (34, 18, 10))):
-        for k in range(2):
-            out[at[0] + k] += lanes_of(roll(face[0:40], -32 * k), 0, 32)
-        for k in range(4):
-            out[at[1] + k, 0:24, :] += lanes_of(roll(face[40:64], SEC - 18 * k), SEC, 18)
-        for k in range(5):
-            out[at[2] + k, 0:16, :] += lanes_of(roll(face[0:16], -11 * k), THI, 11)
-    for ref, high in ((to_high, True), (to_low, False)):
-        pack_z(out, ref, high)
-        ref[64:80, :] = total
-
-
-def pack_z(source, face, to_high):
-    sums = []
-    for rows, planes, count, lane, high in ((40, 36, 2, 0, 30), (24, 22, 4, SEC, 14), (16, 15, 5, THI, 6)):
-        first = lane + high if to_high else lane
-        at = iota((rows, 128), 1)
-        wanted = (at >= first) & (at < first + count)
-        total = jnp.zeros((rows, 128), F32)
-        for x in range(planes):
-            kept = jnp.where(wanted, source[x, 0:rows, :], 0.0)
-            total = total + roll(kept, count * x - first)
-        sums.append(total)
-    face[0:40, :] = sums[0]
-    face[40:64, :] = sums[1]
-    face[0:16, :] += lanes_of(roll(sums[2], 72), 72, 55)
-    face[40:56, :] += lanes_of(roll(sums[2], 88 - 55), 88, 20)
+    planes = x_faces(index[0], got_1, got_3)
+    for face, own_face, is_high in ((to_high, high, True), (to_low, low, False)):
+        sums = [own_face[0:40, :], own_face[40:64, :], own_face[64:80, :]]
+        for level, at, values in planes:
+            _, count, _, top = Z_LEVELS[level]
+            first = top if is_high else 0
+            kept = chosen_lanes(values, first, count)
+            sums[level] = sums[level] + roll(kept, count * at - first)
+        face[0:40, :] = sums[0]
+        face[40:64, :] = sums[1]
+        face[0:16, :] += lanes_of(roll(sums[2], 72), 72, 55)
+        face[40:56, :] += lanes_of(roll(sums[2], 88 - 55), 88, 20)
+        face[64:80, :] = total
 
 
 def unpack_z(message):
@@ -401,7 +427,7 @@
     return message[0:40], message[40:64], third
 
 
-def window_kernel(own, got_2, from_low, from_high, after, out):
+def window_kernel(own, got_2, from_low, from_high, after_1, after_2, out):
     index, _ = place()
     early = lax.rem(index[2], 4) < 2
     ends = got_2[...]
@@ -470,7 +496,7 @@
         outs[2 * n + 1][...] = low
 
 
-def green_kernel(factors, packed, green_high, green_low, rise, framed, block_high, block_low):
+def green_kernel(factors, packed, green, rise, framed, block_high, block_low):
     index, sizes = place()
     row, lane = iota((64, 128), 0), iota((64, 128), 1)
     delta_x = (lane // 8).astype(F32)
@@ -482,11 +508,12 @@
         block_low[apart] = low
     for ty in range(SPAN_4):
         columns = slice(128 * ty, 128 * ty + 128)
+        lows = slice(128 * (SPAN_4 + ty), 128 * (SPAN_4 + ty) + 128)
         for sy in range(16):
             apart = jnp.abs(4 * index[1] - 1 + ty - sy)
             first = sy % 8 * 128 + sy // 8 * 64
-            green_high[first : first + 64, columns] = block_high[apart]
-            green_low[first : first + 64, columns] = block_low[apart]
+            green[first : first + 64, columns] = block_high[apart]
+            green[first : first + 64, lows] = block_low[apart]
     variant = [
         jnp.where(index[d] == 0, 1, 0) + jnp.where(index[d] == sizes[d] - 1, 2, 0) for d in range(3)
     ]
@@ -585,7 +612,7 @@
 
 
 def top_kernel(
-    base, piece_0, piece_1, piece_2, piece_3, green_high, green_low, rise, qz,
+    base, piece_0, piece_1, piece_2, piece_3, green, rise, qz,
     out_hbm,
     fourth, out, sems,
 ):
@@ -602,15 +629,14 @@
             total = moved if total is None else total + moved
         total = total + roll(total, 64)
         fourth[x] = jnp.where(lane < 64, total[0:8], total[8:16])
-    total = jnp.zeros((32, 128 * SPAN_4), F32)
-    extra = jnp.zeros((16, 128 * SPAN_4), F32)
+    width = 128 * SPAN_4
+    total = jnp.zeros((32, 2 * width), F32)
     for s in range(0, 8, 2):
         left = jnp.concatenate([fourth[:, s, :], fourth[:, s + 1, :]], axis=1)
         high, low = split(left)
         rows = slice(128 * s, 128 * s + 256)
-        total = total + dot(jnp.concatenate([high, low], axis=0), green_high[rows, :])
-        extra = extra + dot(high, green_low[rows, :])
-    sums = total[0:16] + (total[16:32] + extra)
+        total = total + dot(jnp.concatenate([high, low], axis=0), green[rows, :])
+    sums = total[0:16, :width] + (total[16:32, :width] + total[0:16, width:])
     row, lane = iota((16, 128), 0), iota((16, 128), 1)
     tops = []
     for tx in range(SPAN_4):
@@ -710,11 +736,10 @@
     qx, qy, qz = composites()
     qz_high = qz.astype(BF16)
     qz_low = (qz - qz_high.astype(np.float32)).astype(BF16)
-    green_high, green_low, rise, framed = call(
+    green, rise, framed = call(
         green_kernel,
         (
-            shape(1024, 128 * SPAN_4, dtype=BF16),
-            shape(1024, 128 * SPAN_4, dtype=BF16),
+            shape(1024, 256 * SPAN_4, dtype=BF16),
             shape(1024, 256, dtype=BF16),
             shape(32, 40, 128),
         ),
@@ -730,11 +755,16 @@
     )
     got_3, got_1, got_2 = exchange((face_3, face_1, raw), "gx", (3, 1, 2))
     bands_1 = banded(BANDS[:1], kernel_fine)
-    wide_x, raw, to_high, to_low = call(
-        widen_x_kernel,
-        (shape(36, 40, 128), shape(16, 128), shape(80, 128), shape(80, 128)),
-        (wide_y, raw, got_2, got_1, got_3, bands_1[0]),
-        spaces={5: ANY},
+    own_high, own_low = call(
+        own_z_kernel, (shape(80, 128), shape(80, 128)), (wide_y, bands_1[0]), spaces={1: ANY}
+    )
+    wide_x = call(
+        widen_x_kernel, shape(36, 40, 128), (wide_y, got_2, got_1, got_3), spaces={1: ANY}
+    )
+    raw, to_high, to_low = call(
+        edge_x_kernel,
+        (shape(16, 128), shape(80, 128), shape(80, 128)),
+        (raw, got_2, got_1, got_3, own_high, own_low),
     )
     from_low, from_high = turn(to_high, 1), turn(to_low, -1)
     (got_2,) = exchange((raw,), "gz", (2,))
@@ -742,8 +772,8 @@
     window = call(
         window_kernel,
         shape(3, 16, 128),
-        (raw, got_2, from_low, from_high, bands_2[0]),
-        spaces={4: ANY},
+        (raw, got_2, from_low, from_high, bands_2[0], wide_x),
+        spaces={4: ANY, 5: ANY},
     )
     pieces = [window] + [turn(window, by) for by in (8, 4, -4)]
     base = call(
@@ -763,7 +793,7 @@
     return call(
         top_kernel,
         shape(32, 32, 32),
-        (base, *pieces, green_high, green_low, rise, jnp.asarray(np.concatenate([qz_high, qz_low]))),
+        (base, *pieces, green, rise, jnp.asarray(np.concatenate([qz_high, qz_low]))),
         (
             pltpu.VMEM((16, 8, 128), F32),
             pltpu.VMEM((32, 32, 32), F32),

time: 48.7 us -> 48.4 us (level)
  waiting for transfers between devices: 7.92 us -> 6.41 us
  local copies, waits for them, and re-layouts: 1.97 us -> 2.7 us
    ppermute x6, waiting for transfers between devices: 6.85 us -> 5.33 us  [exchange(): lax.ppermute(value, axis, [(i, i ^ step) for i in range(size)])]
    unnamed x16, local copies, waits for them, and re-layouts: 1.97 us -> 2.7 us
    pallas_call x10 -> x12, Pallas kernels: 15.5 us -> 15.9 us  [call(): pl.pallas_call(kernel, out_shape=outs, in_specs=[spaces.get(i, VMEM) for...]
  transfers between devices with their start and end apart: 11 -> 11, of which waited for: 5 -> 5; matrix products, arithmetic and copies ran while one was open for 0% -> 0% of each run, Pallas kernels for 14% -> 15%
where the time goes in v9:
time: 48.4 us; the launch traced here: 48.1 us
  starting transfers between devices  22.1 us (46%)
  Pallas kernels  15.9 us (33%)
  waiting for transfers between devices  6.41 us (13%)
  local copies, waits for them, and re-layouts  2.7 us (6%)
  other arithmetic  0.7 us (1%)
    pallas_call x12, Pallas kernels, call(): pl.pallas_call(kernel, out_shape=outs, in_specs=[spaces.get(i, VMEM) for...  15.9 us
    ppermute x6, starting transfers between devices, exchange(): lax.ppermute(value, axis, [(i, i ^ step) for i in range(size)])  11.7 us
    ppermute x5, starting transfers between devices, turn(): return lax.ppermute(value, ('gy', 'gz'), pairs)  10.4 us
    ppermute x6, waiting for transfers between devices, exchange(): lax.ppermute(value, axis, [(i, i ^ step) for i in range(size)])  5.33 us
    unnamed x16, local copies, waits for them, and re-layouts  2.7 us
    ppermute x5, waiting for transfers between devices, turn(): return lax.ppermute(value, ('gy', 'gz'), pairs)  1.08 us
  transfers between devices with their start and end apart: 11, of which 5 were waited for; matrix products, arithmetic and copies ran while one was open for 0% of the time, Pallas kernels for 15%

profile of v9, /device:TPU:32, one launch (start us, length us, event | category | flops | bytes accessed | tf_op | source)
XLA Modules:
  0.0 48.1 jit_solution(11126132629385573012)
XLA Ops:
  0.0 0.7 %multiply_add_fusion.codes = s32[384]{0:T(512)S(1)} fusion(s32[384]{0:T(512)} %param.12, s32[384]{0:T(512)} %param.13), kind=kLoop, calls=%fused_computation | loop fusion | flops 768 | bytes 4608 | tf_op jit(solution)/shard_map/add | solution.py:716
  0.7 5.2 %shard_map.109 = (f32[32,32,128]{2,1,0:T(8,128)}, f32[8,128]{1,0:T(8,128)S(1)}, f32[72,128]{1,0:T(8,128)S(1)}) custom-call(s32[384]{0:T(512)S(1)} %multiply_add_fusion.codes, f32[384,128]{1,0:T(8,128)} %charges_hbm.1, bf16[4608,128]{1,0:T(8,128)(2,1)} %bitcast.1), custom_call_target="tpu_custom_call" | custom-call | flops 1000000 | bytes 2097152 | tf_op jit(solution)/shard_map/pallas_call | solution.py:667
  6.0 0.1 collective-permute-start
  6.1 1.2 %collective-permute-done.got.got_1 = f32[72,128]{1,0:T(8,128)S(1)} collective-permute-done((f32[72,128]{1,0:T(8,128)S(1)}, f32[72,128]{1,0:T(8,128)S(1)}, u32[]{:S(2)}, u32[]{:S(2)}) %collective-permute-start) | collective-permute-done | bytes 36896 | tf_op jit(solution)/shard_map/ppermute | solution.py:686
  7.3 0.1 shard_map.111.own
  7.3 6.3 %collective-permute-start.1 = (f32[40,128]{1,0:T(8,128)S(1)}, f32[40,128]{1,0:T(8,128)S(1)}, u32[]{:S(2)}, u32[]{:S(2)}) collective-permute-start(f32[40,128]{1,0:T(8,128)S(1)} %shard_map.111.own), channel_id=1, source_target_pairs={{0,32},{16,48},{32,0},{48,16},{1,33},{17,49},{33,1},{49,17},{2,34}... | collective-permute-start | bytes 61448 | tf_op jit(solution)/shard_map/ppermute | solution.py:686
  13.7 1.0 %copy-done = f32[32,32,128]{2,1,0:T(8,128)S(1)} copy-done((f32[32,32,128]{2,1,0:T(8,128)S(1)}, f32[32,32,128]{2,1,0:T(8,128)}, u32[]{:S(2)}) %copy-start) | copy-done | bytes 524312
  14.7 0.9 %copy-done.2 = f32[8,32,128]{2,1,0:T(8,128)S(1)} copy-done((f32[8,32,128]{2,1,0:T(8,128)S(1)}, f32[8,32,128]{2,1,0:T(8,128)}, u32[]{:S(2)}) %copy-start.2) | copy-done | bytes 131096
  15.6 1.0 %shard_map.110 = (bf16[1024,1792]{1,0:T(8,128)(2,1)S(1)}, bf16[1024,256]{1,0:T(8,128)(2,1)S(1)}, f32[32,40,128]{2,1,0:T(8,128)S(1)}) custom-call(f32[8,32,128]{2,1,0:T(8,128)S(1)} %copy-done.2, f32[32,32,128]{2,1,0:T(8,128)S(1)} %copy-done), custom_call_target="tpu_custom_call" | custom-call | flops 1000000 | bytes 2097152 | tf_op jit(solution)/shard_map/pallas_call | solution.py:667
  16.6 0.4 shard_map.112
  16.9 3.1 %collective-permute-start.2 = (f32[8,128]{1,0:T(8,128)S(1)}, f32[8,128]{1,0:T(8,128)S(1)}, u32[]{:S(2)}, u32[]{:S(2)}) collective-permute-start(f32[8,128]{1,0:T(8,128)S(1)} %get-tuple-element.32.own), channel_id=1, source_target_pairs={{0,128},{64,192},{128,0},{192,64},{1,129},{65,193},{129,1},{193,65... | collective-permute-start | bytes 12296 | tf_op jit(solution)/shard_map/ppermute | solution.py:686
  20.1 0.6 %collective-permute-start.3 = (f32[72,128]{1,0:T(8,128)S(1)}, f32[72,128]{1,0:T(8,128)S(1)}, u32[]{:S(2)}, u32[]{:S(2)}) collective-permute-start(f32[72,128]{1,0:T(8,128)S(1)} %get-tuple-element.33), channel_id=1, source_target_pairs={{0,64},{64,0},{128,192},{192,128},{1,65},{65,1},{129,193},{193,129... | collective-permute-start | bytes 110600 | tf_op jit(solution)/shard_map/ppermute | solution.py:686
  20.7 0.6 %collective-permute-start.4 = (f32[72,128]{1,0:T(8,128)S(1)}, f32[72,128]{1,0:T(8,128)S(1)}, u32[]{:S(2)}, u32[]{:S(2)}) collective-permute-start(f32[72,128]{1,0:T(8,128)S(1)} %get-tuple-element.34), channel_id=1, source_target_pairs={{0,192},{64,128},{128,64},{192,0},{1,193},{65,129},{129,65},{193,1... | collective-permute-start | bytes 110600 | tf_op jit(solution)/shard_map/ppermute | solution.py:686
  21.2 0.7 %copy-done.5 = f32[5,5,5]{2,1,0:T(8,128)S(1)} copy-done((f32[5,5,5]{2,1,0:T(8,128)S(1)}, f32[5,5,5]{2,1,0:T(8,128)}, u32[]{:S(2)}) %copy-start.5) | copy-done | bytes 524
  21.9 1.4 %shard_map.114 = (bf16[256,256]{1,0:T(8,128)(2,1)S(1)}, bf16[256,256]{1,0:T(8,128)(2,1)S(1)}) custom-call(f32[5,5,5]{2,1,0:T(8,128)S(1)} %copy-done.5), custom_call_target="tpu_custom_call" | custom-call | flops 1000000000 | bytes 2097152 | tf_op jit(solution)/shard_map/pallas_call | solution.py:667
  23.3 0.0 copy-start.3
  23.3 0.6 %shard_map.115 = (f32[80,128]{1,0:T(8,128)S(1)}, f32[80,128]{1,0:T(8,128)S(1)}) custom-call(f32[32,40,128]{2,1,0:T(8,128)S(1)} %get-tuple-element.31.wide_y, bf16[256,256]{1,0:T(8,128)(2,1)S(1)} %get-tuple-element.35.after.b1h), custom_call_target="tpu_custom_call" | custom-call | flops 1000000 | bytes 2097152 | tf_op jit(solution)/shard_map/pallas_call | solution.py:667
  23.9 0.1 collective-permute-done.3.got_1
  24.0 1.8 %collective-permute-done.4.got_3 = f32[72,128]{1,0:T(8,128)S(1)} collective-permute-done((f32[72,128]{1,0:T(8,128)S(1)}, f32[72,128]{1,0:T(8,128)S(1)}, u32[]{:S(2)}, u32[]{:S(2)}) %collective-permute-start.4) | collective-permute-done | bytes 36896 | tf_op jit(solution)/shard_map/ppermute | solution.py:686
  25.8 0.3 shard_map.116
  26.1 1.7 %collective-permute-start.5 = (f32[80,128]{1,0:T(8,128)S(1)}, f32[80,128]{1,0:T(8,128)S(1)}, u32[]{:S(2)}, u32[]{:S(2)}) collective-permute-start(f32[80,128]{1,0:T(8,128)S(1)} %get-tuple-element.38), channel_id=1, source_target_pairs={{0,1},{1,2},{2,3},{3,4},{4,5},{5,6},{6,7},{7,8},{8,9},{9,10},{10,1... | collective-permute-start | bytes 122888 | tf_op jit(solution)/shard_map/ppermute | solution.py:698
  27.8 2.6 %collective-permute-start.6 = (f32[80,128]{1,0:T(8,128)S(1)}, f32[80,128]{1,0:T(8,128)S(1)}, u32[]{:S(2)}, u32[]{:S(2)}) collective-permute-start(f32[80,128]{1,0:T(8,128)S(1)} %get-tuple-element.39), channel_id=1, source_target_pairs={{0,47},{1,0},{2,1},{3,2},{4,3},{5,4},{6,5},{7,6},{8,7},{9,8},{10,9... | collective-permute-start | bytes 122888 | tf_op jit(solution)/shard_map/ppermute | solution.py:698
  30.4 1.1 %collective-permute-start.7 = (f32[16,128]{1,0:T(8,128)S(1)}, f32[16,128]{1,0:T(8,128)S(1)}, u32[]{:S(2)}, u32[]{:S(2)}) collective-permute-start(f32[16,128]{1,0:T(8,128)S(1)} %get-tuple-element.45.own), channel_id=1, source_target_pairs={{0,2},{1,3},{2,0},{3,1},{4,6},{5,7},{6,4},{7,5},{8,10},{9,11},{10,... | collective-permute-start | bytes 24584 | tf_op jit(solution)/shard_map/ppermute | solution.py:686
  31.4 1.6 %shard_map.117 = (bf16[256,128]{1,0:T(8,128)(2,1)S(1)}, bf16[256,128]{1,0:T(8,128)(2,1)S(1)}, bf16[128,128]{1,0:T(8,128)(2,1)S(1)}, bf16[128,128]{1,0:T(8,128)(2,1)S(1)}) custom-call(f32[5,5,5]{2,1,0:T(8,128)S(1)} %copy-done.6, f32[5,5,5]{2,1,0:T(8,128)S(1)} %copy-done.7), custom_call_target="tpu_custom_call" | custom-call | flops 1000000000 | bytes 2097152 | tf_op jit(solution)/shard_map/pallas_call | solution.py:667
  33.1 0.2 shard_map.113.wide.after_2
  33.3 2.2 %collective-permute-done.7.got_2 = f32[16,128]{1,0:T(8,128)S(1)} collective-permute-done((f32[16,128]{1,0:T(8,128)S(1)}, f32[16,128]{1,0:T(8,128)S(1)}, u32[]{:S(2)}, u32[]{:S(2)}) %collective-permute-start.7) | collective-permute-done | bytes 8224 | tf_op jit(solution)/shard_map/ppermute | solution.py:686
  35.5 0.2 shard_map.119.piece_0
  35.7 1.8 %collective-permute-start.8 = (f32[3,16,128]{2,1,0:T(8,128)S(1)}, f32[3,16,128]{2,1,0:T(8,128)S(1)}, u32[]{:S(2)}, u32[]{:S(2)}) collective-permute-start(f32[3,16,128]{2,1,0:T(8,128)S(1)} %shard_map.119.piece_0), channel_id=1, source_target_pairs={{0,8},{1,9},{2,10},{3,11},{4,12},{5,13},{6,14},{7,15},{8,32},{9,33... | collective-permute-start | bytes 73736 | tf_op jit(solution)/shard_map/ppermute | solution.py:698
  37.5 4.3 %collective-permute-start.9 = (f32[3,16,128]{2,1,0:T(8,128)S(1)}, f32[3,16,128]{2,1,0:T(8,128)S(1)}, u32[]{:S(2)}, u32[]{:S(2)}) collective-permute-start(f32[3,16,128]{2,1,0:T(8,128)S(1)} %shard_map.119.piece_0), channel_id=1, source_target_pairs={{0,4},{1,5},{2,6},{3,7},{4,8},{5,9},{6,10},{7,11},{8,12},{9,13},{1... | collective-permute-start | bytes 73736 | tf_op jit(solution)/shard_map/ppermute | solution.py:698
  41.9 2.7 %shard_map.118.base = f32[32,32,128]{2,1,0:T(8,128)S(1)} custom-call(f32[36,40,128]{2,1,0:T(8,128)S(1)} %shard_map.113.wide.after_2, f32[80,128]{1,0:T(8,128)S(1)} %collective-permute-done.5.from_low, f32[80,128]{1,0:T(8,128)S(1)} %collective-permute-done.6.from_high, bf16[256,256]{1,0:T(8,128)(2,1)S(1)} %get-tuple-element.35.after.b1h, ...), custom_call_target="tpu_custom_call" | custom-call | flops 1000000 | bytes 2097152 | tf_op jit(solution)/shard_map/pallas_call | solution.py:667
  44.6 1.1 %collective-permute-done.10.piece_3 = f32[3,16,128]{2,1,0:T(8,128)S(1)} collective-permute-done((f32[3,16,128]{2,1,0:T(8,128)S(1)}, f32[3,16,128]{2,1,0:T(8,128)S(1)}, u32[]{:S(2)}, u32[]{:S(2)}) %collective-permute-start.10) | collective-permute-done | bytes 24608 | tf_op jit(solution)/shard_map/ppermute | solution.py:698
  45.7 2.3 %shard_map.120 = f32[32,32,32]{2,1,0:T(8,128)} custom-call(f32[32,32,128]{2,1,0:T(8,128)S(1)} %shard_map.118.base, f32[3,16,128]{2,1,0:T(8,128)S(1)} %shard_map.119.piece_0, f32[3,16,128]{2,1,0:T(8,128)S(1)} %collective-permute-done.8.piece_1, f32[3,16,128]{2,1,0:T(8,128)S(1)} %collective-permute-done.9.piece_2, ...), custom_call_target="tpu_custom_call" | custom-call | flops 1000000 | bytes 2097152 | tf_op jit(solution)/shard_map/pallas_call | solution.py:667
  (19 shorter events, 0.0 us)
Async XLA Ops:
  5.9 25.5 %copy-start.6 = (f32[5,5,5]{2,1,0:T(8,128)S(1)}, f32[5,5,5]{2,1,0:T(8,128)}, u32[]{:S(2)}) copy-start(f32[5,5,5]{2,1,0:T(8,128)} %refs_0_.3) | copy-start | bytes 1504
  6.0 25.5 %copy-start.7 = (f32[5,5,5]{2,1,0:T(8,128)S(1)}, f32[5,5,5]{2,1,0:T(8,128)}, u32[]{:S(2)}) copy-start(f32[5,5,5]{2,1,0:T(8,128)} %refs_1_.1) | copy-start | bytes 1504
  6.0 1.3 %collective-permute-start = (f32[72,128]{1,0:T(8,128)S(1)}, f32[72,128]{1,0:T(8,128)S(1)}, u32[]{:S(2)}, u32[]{:S(2)}) collective-permute-start(f32[72,128]{1,0:T(8,128)S(1)} %get-tuple-element.29), channel_id=1, source_target_pairs={{0,16},{16,0},{32,48},{48,32},{1,17},{17,1},{33,49},{49,33},{2,18}... | collective-permute-start | bytes 110600 | tf_op jit(solution)/shard_map/ppermute | solution.py:686
  7.3 9.2 %collective-permute-start.1 = (f32[40,128]{1,0:T(8,128)S(1)}, f32[40,128]{1,0:T(8,128)S(1)}, u32[]{:S(2)}, u32[]{:S(2)}) collective-permute-start(f32[40,128]{1,0:T(8,128)S(1)} %shard_map.111.own), channel_id=1, source_target_pairs={{0,32},{16,48},{32,0},{48,16},{1,33},{17,49},{33,1},{49,17},{2,34}... | collective-permute-start | bytes 61448 | tf_op jit(solution)/shard_map/ppermute | solution.py:686
  13.7 1.0 %copy-start = (f32[32,32,128]{2,1,0:T(8,128)S(1)}, f32[32,32,128]{2,1,0:T(8,128)}, u32[]{:S(2)}) copy-start(f32[32,32,128]{2,1,0:T(8,128)} %get-tuple-element.26.packed) | copy-start | bytes 1572868
  14.7 0.9 %copy-start.2 = (f32[8,32,128]{2,1,0:T(8,128)S(1)}, f32[8,32,128]{2,1,0:T(8,128)}, u32[]{:S(2)}) copy-start(f32[8,32,128]{2,1,0:T(8,128)} %constant.10.clone.factors) | copy-start | bytes 393220
  16.9 7.0 %collective-permute-start.2 = (f32[8,128]{1,0:T(8,128)S(1)}, f32[8,128]{1,0:T(8,128)S(1)}, u32[]{:S(2)}, u32[]{:S(2)}) collective-permute-start(f32[8,128]{1,0:T(8,128)S(1)} %get-tuple-element.32.own), channel_id=1, source_target_pairs={{0,128},{64,192},{128,0},{192,64},{1,129},{65,193},{129,1},{193,65... | collective-permute-start | bytes 12296 | tf_op jit(solution)/shard_map/ppermute | solution.py:686
  20.1 4.0 %collective-permute-start.3 = (f32[72,128]{1,0:T(8,128)S(1)}, f32[72,128]{1,0:T(8,128)S(1)}, u32[]{:S(2)}, u32[]{:S(2)}) collective-permute-start(f32[72,128]{1,0:T(8,128)S(1)} %get-tuple-element.33), channel_id=1, source_target_pairs={{0,64},{64,0},{128,192},{192,128},{1,65},{65,1},{129,193},{193,129... | collective-permute-start | bytes 110600 | tf_op jit(solution)/shard_map/ppermute | solution.py:686
  20.7 5.2 %collective-permute-start.4 = (f32[72,128]{1,0:T(8,128)S(1)}, f32[72,128]{1,0:T(8,128)S(1)}, u32[]{:S(2)}, u32[]{:S(2)}) collective-permute-start(f32[72,128]{1,0:T(8,128)S(1)} %get-tuple-element.34), channel_id=1, source_target_pairs={{0,192},{64,128},{128,64},{192,0},{1,193},{65,129},{129,65},{193,1... | collective-permute-start | bytes 110600 | tf_op jit(solution)/shard_map/ppermute | solution.py:686
  21.2 0.7 %copy-start.5 = (f32[5,5,5]{2,1,0:T(8,128)S(1)}, f32[5,5,5]{2,1,0:T(8,128)}, u32[]{:S(2)}) copy-start(f32[5,5,5]{2,1,0:T(8,128)} %refs_0_.2) | copy-start | bytes 1504
  23.3 18.6 %copy-start.3 = (bf16[128,128]{1,0:T(8,128)(2,1)S(1)}, bf16[128,128]{1,0:T(8,128)(2,1)}, u32[]{:S(2)}) copy-start(bf16[128,128]{1,0:T(8,128)(2,1)} %constant.11.clone.prol_2) | copy-start | bytes 98308
  23.3 18.5 %copy-start.4 = (bf16[128,128]{1,0:T(8,128)(2,1)S(1)}, bf16[128,128]{1,0:T(8,128)(2,1)}, u32[]{:S(2)}) copy-start(bf16[128,128]{1,0:T(8,128)(2,1)} %constant.12.clone.prol_1) | copy-start | bytes 98308
  26.1 9.4 %collective-permute-start.5 = (f32[80,128]{1,0:T(8,128)S(1)}, f32[80,128]{1,0:T(8,128)S(1)}, u32[]{:S(2)}, u32[]{:S(2)}) collective-permute-start(f32[80,128]{1,0:T(8,128)S(1)} %get-tuple-element.38), channel_id=1, source_target_pairs={{0,1},{1,2},{2,3},{3,4},{4,5},{5,6},{6,7},{7,8},{8,9},{9,10},{10,1... | collective-permute-start | bytes 122888 | tf_op jit(solution)/shard_map/ppermute | solution.py:698
  27.8 7.7 %collective-permute-start.6 = (f32[80,128]{1,0:T(8,128)S(1)}, f32[80,128]{1,0:T(8,128)S(1)}, u32[]{:S(2)}, u32[]{:S(2)}) collective-permute-start(f32[80,128]{1,0:T(8,128)S(1)} %get-tuple-element.39), channel_id=1, source_target_pairs={{0,47},{1,0},{2,1},{3,2},{4,3},{5,4},{6,5},{7,6},{8,7},{9,8},{10,9... | collective-permute-start | bytes 122888 | tf_op jit(solution)/shard_map/ppermute | solution.py:698
  30.4 15.3 %copy-start.1 = (bf16[8,128,128]{2,1,0:T(8,128)(2,1)S(1)}, bf16[8,128,128]{2,1,0:T(8,128)(2,1)}, u32[]{:S(2)}) copy-start(bf16[8,128,128]{2,1,0:T(8,128)(2,1)} %constant.13.clone.qz) | copy-start | bytes 786436
  30.4 5.2 %collective-permute-start.7 = (f32[16,128]{1,0:T(8,128)S(1)}, f32[16,128]{1,0:T(8,128)S(1)}, u32[]{:S(2)}, u32[]{:S(2)}) collective-permute-start(f32[16,128]{1,0:T(8,128)S(1)} %get-tuple-element.45.own), channel_id=1, source_target_pairs={{0,2},{1,3},{2,0},{3,1},{4,6},{5,7},{6,4},{7,5},{8,10},{9,11},{10,... | collective-permute-start | bytes 24584 | tf_op jit(solution)/shard_map/ppermute | solution.py:686
  35.7 8.9 %collective-permute-start.8 = (f32[3,16,128]{2,1,0:T(8,128)S(1)}, f32[3,16,128]{2,1,0:T(8,128)S(1)}, u32[]{:S(2)}, u32[]{:S(2)}) collective-permute-start(f32[3,16,128]{2,1,0:T(8,128)S(1)} %shard_map.119.piece_0), channel_id=1, source_target_pairs={{0,8},{1,9},{2,10},{3,11},{4,12},{5,13},{6,14},{7,15},{8,32},{9,33... | collective-permute-start | bytes 73736 | tf_op jit(solution)/shard_map/ppermute | solution.py:698
  37.5 7.1 %collective-permute-start.9 = (f32[3,16,128]{2,1,0:T(8,128)S(1)}, f32[3,16,128]{2,1,0:T(8,128)S(1)}, u32[]{:S(2)}, u32[]{:S(2)}) collective-permute-start(f32[3,16,128]{2,1,0:T(8,128)S(1)} %shard_map.119.piece_0), channel_id=1, source_target_pairs={{0,4},{1,5},{2,6},{3,7},{4,8},{5,9},{6,10},{7,11},{8,12},{9,13},{1... | collective-permute-start | bytes 73736 | tf_op jit(solution)/shard_map/ppermute | solution.py:698
  41.9 3.8 %collective-permute-start.10 = (f32[3,16,128]{2,1,0:T(8,128)S(1)}, f32[3,16,128]{2,1,0:T(8,128)S(1)}, u32[]{:S(2)}, u32[]{:S(2)}) collective-permute-start(f32[3,16,128]{2,1,0:T(8,128)S(1)} %shard_map.119.piece_0), channel_id=1, source_target_pairs={{0,44},{1,45},{2,46},{3,47},{4,0},{5,1},{6,2},{7,3},{8,4},{9,5},{1... | collective-permute-start | bytes 73736 | tf_op jit(solution)/shard_map/ppermute | solution.py:698

commit v10 on v9

--- a/solution.py
+++ b/solution.py
@@ -496,7 +496,7 @@
         outs[2 * n + 1][...] = low
 
 
-def green_kernel(factors, packed, green, rise, framed, block_high, block_low):
+def green_kernel(factors, packed, green_high, green_low, rise, framed, block_high, block_low):
     index, sizes = place()
     row, lane = iota((64, 128), 0), iota((64, 128), 1)
     delta_x = (lane // 8).astype(F32)
@@ -508,12 +508,11 @@
         block_low[apart] = low
     for ty in range(SPAN_4):
         columns = slice(128 * ty, 128 * ty + 128)
-        lows = slice(128 * (SPAN_4 + ty), 128 * (SPAN_4 + ty) + 128)
         for sy in range(16):
             apart = jnp.abs(4 * index[1] - 1 + ty - sy)
             first = sy % 8 * 128 + sy // 8 * 64
-            green[first : first + 64, columns] = block_high[apart]
-            green[first : first + 64, lows] = block_low[apart]
+            green_high[first : first + 64, columns] = block_high[apart]
+            green_low[first : first + 64, columns] = block_low[apart]
     variant = [
         jnp.where(index[d] == 0, 1, 0) + jnp.where(index[d] == sizes[d] - 1, 2, 0) for d in range(3)
     ]
@@ -612,7 +611,7 @@
 
 
 def top_kernel(
-    base, piece_0, piece_1, piece_2, piece_3, green, rise, qz,
+    base, piece_0, piece_1, piece_2, piece_3, green_high, green_low, rise, qz,
     out_hbm,
     fourth, out, sems,
 ):
@@ -620,7 +619,7 @@
     lane = iota((8, 128), 1)
     ring = lax.rem(index[2], 4)
     first = 4 * (ring == 3).astype(jnp.int32) - 4 * (ring == 0).astype(jnp.int32) + 127
-    sources = [lax.rem(16 * lax.rem(index[2] // 4 + step, 4) + first, 128) for step in (0, 2, 3, 1)]
+    sources = [lax.rem(16 * lax.rem(index[2] // 4 + step, 4) + first, 128) for step in (0, 2, 1, 3)]
     for x in range(16):
         total = None
         for piece, at in zip((piece_0, piece_1, piece_2, piece_3), sources):
@@ -629,14 +628,15 @@
             total = moved if total is None else total + moved
         total = total + roll(total, 64)
         fourth[x] = jnp.where(lane < 64, total[0:8], total[8:16])
-    width = 128 * SPAN_4
-    total = jnp.zeros((32, 2 * width), F32)
+    total = jnp.zeros((32, 128 * SPAN_4), F32)
+    extra = jnp.zeros((16, 128 * SPAN_4), F32)
     for s in range(0, 8, 2):
         left = jnp.concatenate([fourth[:, s, :], fourth[:, s + 1, :]], axis=1)
         high, low = split(left)
         rows = slice(128 * s, 128 * s + 256)
-        total = total + dot(jnp.concatenate([high, low], axis=0), green[rows, :])
-    sums = total[0:16, :width] + (total[16:32, :width] + total[0:16, width:])
+        total = total + dot(jnp.concatenate([high, low], axis=0), green_high[rows, :])
+        extra = extra + dot(high, green_low[rows, :])
+    sums = total[0:16] + (total[16:32] + extra)
     row, lane = iota((16, 128), 0), iota((16, 128), 1)
     tops = []
     for tx in range(SPAN_4):
@@ -736,10 +736,11 @@
     qx, qy, qz = composites()
     qz_high = qz.astype(BF16)
     qz_low = (qz - qz_high.astype(np.float32)).astype(BF16)
-    green, rise, framed = call(
+    green_high, green_low, rise, framed = call(
         green_kernel,
         (
-            shape(1024, 256 * SPAN_4, dtype=BF16),
+            shape(1024, 128 * SPAN_4, dtype=BF16),
+            shape(1024, 128 * SPAN_4, dtype=BF16),
             shape(1024, 256, dtype=BF16),
             shape(32, 40, 128),
         ),
@@ -775,7 +776,7 @@
         (raw, got_2, from_low, from_high, bands_2[0], wide_x),
         spaces={4: ANY, 5: ANY},
     )
-    pieces = [window] + [turn(window, by) for by in (8, 4, -4)]
+    pieces = [window] + [turn(window, by) for by in (8, -4, 4)]
     base = call(
         near_kernel,
         shape(32, 32, 128),
@@ -793,7 +794,7 @@
     return call(
         top_kernel,
         shape(32, 32, 32),
-        (base, *pieces, green, rise, jnp.asarray(np.concatenate([qz_high, qz_low]))),
+        (base, *pieces, green_high, green_low, rise, jnp.asarray(np.concatenate([qz_high, qz_low]))),
         (
             pltpu.VMEM((16, 8, 128), F32),
             pltpu.VMEM((32, 32, 32), F32),

time: 48.4 us -> 47.3 us (0.977)
  local copies, waits for them, and re-layouts: 2.7 us -> 1.98 us
    ppermute x5, waiting for transfers between devices: 1.08 us -> 0.01 us  [turn(): return lax.ppermute(value, ('gy', 'gz'), pairs)]
    unnamed x16, local copies, waits for them, and re-layouts: 2.7 us -> 1.98 us
    ppermute x6, waiting for transfers between devices: 5.33 us -> 6.06 us  [exchange(): lax.ppermute(value, axis, [(i, i ^ step) for i in range(size)])]
  transfers between devices with their start and end apart: 11 -> 11, of which waited for: 5 -> 4; matrix products, arithmetic and copies ran while one was open for 0% -> 0% of each run, Pallas kernels for 15% -> 16%
where the time goes in v10:
time: 47.3 us; the launch traced here: 46.9 us
  starting transfers between devices  22.1 us (47%)
  Pallas kernels  15.8 us (33%)
  waiting for transfers between devices  6.07 us (13%)
  local copies, waits for them, and re-layouts  1.98 us (4%)
  other arithmetic  0.71 us (2%)
    pallas_call x12, Pallas kernels, call(): pl.pallas_call(kernel, out_shape=outs, in_specs=[spaces.get(i, VMEM) for...  15.8 us
    ppermute x6, starting transfers between devices, exchange(): lax.ppermute(value, axis, [(i, i ^ step) for i in range(size)])  11.7 us
    ppermute x5, starting transfers between devices, turn(): return lax.ppermute(value, ('gy', 'gz'), pairs)  10.4 us
    ppermute x6, waiting for transfers between devices, exchange(): lax.ppermute(value, axis, [(i, i ^ step) for i in range(size)])  6.06 us
    unnamed x16, local copies, waits for them, and re-layouts  1.98 us
  transfers between devices with their start and end apart: 11, of which 4 were waited for; matrix products, arithmetic and copies ran while one was open for 0% of the time, Pallas kernels for 16%

profile of v10, /device:TPU:32, one launch (start us, length us, event | category | flops | bytes accessed | tf_op | source)
XLA Modules:
  0.0 46.9 jit_solution(6878903490116465999)
XLA Ops:
  0.0 0.7 %multiply_add_fusion.codes = s32[384]{0:T(512)S(1)} fusion(s32[384]{0:T(512)} %param.12, s32[384]{0:T(512)} %param.13), kind=kLoop, calls=%fused_computation | loop fusion | flops 768 | bytes 4608 | tf_op jit(solution)/shard_map/add | solution.py:716
  0.7 5.2 %shard_map.109 = (f32[32,32,128]{2,1,0:T(8,128)}, f32[8,128]{1,0:T(8,128)S(1)}, f32[72,128]{1,0:T(8,128)S(1)}) custom-call(s32[384]{0:T(512)S(1)} %multiply_add_fusion.codes, f32[384,128]{1,0:T(8,128)} %charges_hbm.1, bf16[4608,128]{1,0:T(8,128)(2,1)} %bitcast.1), custom_call_target="tpu_custom_call" | custom-call | flops 1000000 | bytes 2097152 | tf_op jit(solution)/shard_map/pallas_call | solution.py:667
  6.0 0.1 collective-permute-start
  6.1 1.2 %collective-permute-done.got.got_1 = f32[72,128]{1,0:T(8,128)S(1)} collective-permute-done((f32[72,128]{1,0:T(8,128)S(1)}, f32[72,128]{1,0:T(8,128)S(1)}, u32[]{:S(2)}, u32[]{:S(2)}) %collective-permute-start) | collective-permute-done | bytes 36896 | tf_op jit(solution)/shard_map/ppermute | solution.py:686
  7.3 0.1 shard_map.111.own
  7.3 6.3 %collective-permute-start.1 = (f32[40,128]{1,0:T(8,128)S(1)}, f32[40,128]{1,0:T(8,128)S(1)}, u32[]{:S(2)}, u32[]{:S(2)}) collective-permute-start(f32[40,128]{1,0:T(8,128)S(1)} %shard_map.111.own), channel_id=1, source_target_pairs={{0,32},{16,48},{32,0},{48,16},{1,33},{17,49},{33,1},{49,17},{2,34}... | collective-permute-start | bytes 61448 | tf_op jit(solution)/shard_map/ppermute | solution.py:686
  13.7 1.0 %copy-done = f32[32,32,128]{2,1,0:T(8,128)S(1)} copy-done((f32[32,32,128]{2,1,0:T(8,128)S(1)}, f32[32,32,128]{2,1,0:T(8,128)}, u32[]{:S(2)}) %copy-start) | copy-done | bytes 524312
  14.7 0.9 %copy-done.2 = f32[8,32,128]{2,1,0:T(8,128)S(1)} copy-done((f32[8,32,128]{2,1,0:T(8,128)S(1)}, f32[8,32,128]{2,1,0:T(8,128)}, u32[]{:S(2)}) %copy-start.2) | copy-done | bytes 131096
  15.6 1.0 %shard_map.110 = (bf16[1024,896]{1,0:T(8,128)(2,1)S(1)}, bf16[1024,896]{1,0:T(8,128)(2,1)S(1)}, bf16[1024,256]{1,0:T(8,128)(2,1)S(1)}, f32[32,40,128]{2,1,0:T(8,128)S(1)}) custom-call(f32[8,32,128]{2,1,0:T(8,128)S(1)} %copy-done.2, f32[32,32,128]{2,1,0:T(8,128)S(1)} %copy-done), custom_call_target="tpu_custom_call" | custom-call | flops 1000000 | bytes 2097152 | tf_op jit(solution)/shard_map/pallas_call | solution.py:667
  16.6 0.4 shard_map.112
  16.9 3.1 %collective-permute-start.2 = (f32[8,128]{1,0:T(8,128)S(1)}, f32[8,128]{1,0:T(8,128)S(1)}, u32[]{:S(2)}, u32[]{:S(2)}) collective-permute-start(f32[8,128]{1,0:T(8,128)S(1)} %get-tuple-element.33.own), channel_id=1, source_target_pairs={{0,128},{64,192},{128,0},{192,64},{1,129},{65,193},{129,1},{193,65... | collective-permute-start | bytes 12296 | tf_op jit(solution)/shard_map/ppermute | solution.py:686
  20.1 0.6 %collective-permute-start.3 = (f32[72,128]{1,0:T(8,128)S(1)}, f32[72,128]{1,0:T(8,128)S(1)}, u32[]{:S(2)}, u32[]{:S(2)}) collective-permute-start(f32[72,128]{1,0:T(8,128)S(1)} %get-tuple-element.34), channel_id=1, source_target_pairs={{0,64},{64,0},{128,192},{192,128},{1,65},{65,1},{129,193},{193,129... | collective-permute-start | bytes 110600 | tf_op jit(solution)/shard_map/ppermute | solution.py:686
  20.7 0.5 %collective-permute-start.4 = (f32[72,128]{1,0:T(8,128)S(1)}, f32[72,128]{1,0:T(8,128)S(1)}, u32[]{:S(2)}, u32[]{:S(2)}) collective-permute-start(f32[72,128]{1,0:T(8,128)S(1)} %get-tuple-element.35), channel_id=1, source_target_pairs={{0,192},{64,128},{128,64},{192,0},{1,193},{65,129},{129,65},{193,1... | collective-permute-start | bytes 110600 | tf_op jit(solution)/shard_map/ppermute | solution.py:686
  21.2 1.4 %shard_map.114 = (bf16[256,256]{1,0:T(8,128)(2,1)S(1)}, bf16[256,256]{1,0:T(8,128)(2,1)S(1)}) custom-call(f32[5,5,5]{2,1,0:T(8,128)S(1)} %copy-done.5), custom_call_target="tpu_custom_call" | custom-call | flops 1000000000 | bytes 2097152 | tf_op jit(solution)/shard_map/pallas_call | solution.py:667
  22.6 0.6 %shard_map.115 = (f32[80,128]{1,0:T(8,128)S(1)}, f32[80,128]{1,0:T(8,128)S(1)}) custom-call(f32[32,40,128]{2,1,0:T(8,128)S(1)} %get-tuple-element.32.wide_y, bf16[256,256]{1,0:T(8,128)(2,1)S(1)} %get-tuple-element.36.after.b1h), custom_call_target="tpu_custom_call" | custom-call | flops 1000000 | bytes 2097152 | tf_op jit(solution)/shard_map/pallas_call | solution.py:667
  23.1 0.9 %collective-permute-done.3.got_1 = f32[72,128]{1,0:T(8,128)S(1)} collective-permute-done((f32[72,128]{1,0:T(8,128)S(1)}, f32[72,128]{1,0:T(8,128)S(1)}, u32[]{:S(2)}, u32[]{:S(2)}) %collective-permute-start.3) | collective-permute-done | bytes 36896 | tf_op jit(solution)/shard_map/ppermute | solution.py:686
  24.0 1.8 %collective-permute-done.4.got_3 = f32[72,128]{1,0:T(8,128)S(1)} collective-permute-done((f32[72,128]{1,0:T(8,128)S(1)}, f32[72,128]{1,0:T(8,128)S(1)}, u32[]{:S(2)}, u32[]{:S(2)}) %collective-permute-start.4) | collective-permute-done | bytes 36896 | tf_op jit(solution)/shard_map/ppermute | solution.py:686
  25.8 0.3 shard_map.116
  26.1 1.7 %collective-permute-start.5 = (f32[80,128]{1,0:T(8,128)S(1)}, f32[80,128]{1,0:T(8,128)S(1)}, u32[]{:S(2)}, u32[]{:S(2)}) collective-permute-start(f32[80,128]{1,0:T(8,128)S(1)} %get-tuple-element.39), channel_id=1, source_target_pairs={{0,1},{1,2},{2,3},{3,4},{4,5},{5,6},{6,7},{7,8},{8,9},{9,10},{10,1... | collective-permute-start | bytes 122888 | tf_op jit(solution)/shard_map/ppermute | solution.py:698
  27.8 2.6 %collective-permute-start.6 = (f32[80,128]{1,0:T(8,128)S(1)}, f32[80,128]{1,0:T(8,128)S(1)}, u32[]{:S(2)}, u32[]{:S(2)}) collective-permute-start(f32[80,128]{1,0:T(8,128)S(1)} %get-tuple-element.40), channel_id=1, source_target_pairs={{0,47},{1,0},{2,1},{3,2},{4,3},{5,4},{6,5},{7,6},{8,7},{9,8},{10,9... | collective-permute-start | bytes 122888 | tf_op jit(solution)/shard_map/ppermute | solution.py:698
  30.4 1.1 %collective-permute-start.7 = (f32[16,128]{1,0:T(8,128)S(1)}, f32[16,128]{1,0:T(8,128)S(1)}, u32[]{:S(2)}, u32[]{:S(2)}) collective-permute-start(f32[16,128]{1,0:T(8,128)S(1)} %get-tuple-element.46.own), channel_id=1, source_target_pairs={{0,2},{1,3},{2,0},{3,1},{4,6},{5,7},{6,4},{7,5},{8,10},{9,11},{10,... | collective-permute-start | bytes 24584 | tf_op jit(solution)/shard_map/ppermute | solution.py:686
  31.4 1.6 %shard_map.117 = (bf16[256,128]{1,0:T(8,128)(2,1)S(1)}, bf16[256,128]{1,0:T(8,128)(2,1)S(1)}, bf16[128,128]{1,0:T(8,128)(2,1)S(1)}, bf16[128,128]{1,0:T(8,128)(2,1)S(1)}) custom-call(f32[5,5,5]{2,1,0:T(8,128)S(1)} %copy-done.6, f32[5,5,5]{2,1,0:T(8,128)S(1)} %copy-done.7), custom_call_target="tpu_custom_call" | custom-call | flops 1000000000 | bytes 2097152 | tf_op jit(solution)/shard_map/pallas_call | solution.py:667
  33.1 0.0 copy-start.3
  33.1 0.0 copy-start.4
  33.1 0.2 shard_map.113.wide.after_2
  33.3 2.2 %collective-permute-done.7.got_2 = f32[16,128]{1,0:T(8,128)S(1)} collective-permute-done((f32[16,128]{1,0:T(8,128)S(1)}, f32[16,128]{1,0:T(8,128)S(1)}, u32[]{:S(2)}, u32[]{:S(2)}) %collective-permute-start.7) | collective-permute-done | bytes 8224 | tf_op jit(solution)/shard_map/ppermute | solution.py:686
  35.5 0.2 shard_map.119.piece_0
  35.7 1.8 %collective-permute-start.8 = (f32[3,16,128]{2,1,0:T(8,128)S(1)}, f32[3,16,128]{2,1,0:T(8,128)S(1)}, u32[]{:S(2)}, u32[]{:S(2)}) collective-permute-start(f32[3,16,128]{2,1,0:T(8,128)S(1)} %shard_map.119.piece_0), channel_id=1, source_target_pairs={{0,8},{1,9},{2,10},{3,11},{4,12},{5,13},{6,14},{7,15},{8,32},{9,33... | collective-permute-start | bytes 73736 | tf_op jit(solution)/shard_map/ppermute | solution.py:698
  37.5 1.4 %collective-permute-start.9 = (f32[3,16,128]{2,1,0:T(8,128)S(1)}, f32[3,16,128]{2,1,0:T(8,128)S(1)}, u32[]{:S(2)}, u32[]{:S(2)}) collective-permute-start(f32[3,16,128]{2,1,0:T(8,128)S(1)} %shard_map.119.piece_0), channel_id=1, source_target_pairs={{0,44},{1,45},{2,46},{3,47},{4,0},{5,1},{6,2},{7,3},{8,4},{9,5},{1... | collective-permute-start | bytes 73736 | tf_op jit(solution)/shard_map/ppermute | solution.py:698
  38.9 3.0 %collective-permute-start.10 = (f32[3,16,128]{2,1,0:T(8,128)S(1)}, f32[3,16,128]{2,1,0:T(8,128)S(1)}, u32[]{:S(2)}, u32[]{:S(2)}) collective-permute-start(f32[3,16,128]{2,1,0:T(8,128)S(1)} %shard_map.119.piece_0), channel_id=1, source_target_pairs={{0,4},{1,5},{2,6},{3,7},{4,8},{5,9},{6,10},{7,11},{8,12},{9,13},{1... | collective-permute-start | bytes 73736 | tf_op jit(solution)/shard_map/ppermute | solution.py:698
  41.9 2.7 %shard_map.118.base = f32[32,32,128]{2,1,0:T(8,128)S(1)} custom-call(f32[36,40,128]{2,1,0:T(8,128)S(1)} %shard_map.113.wide.after_2, f32[80,128]{1,0:T(8,128)S(1)} %collective-permute-done.5.from_low, f32[80,128]{1,0:T(8,128)S(1)} %collective-permute-done.6.from_high, bf16[256,256]{1,0:T(8,128)(2,1)S(1)} %get-tuple-element.36.after.b1h, ...), custom_call_target="tpu_custom_call" | custom-call | flops 1000000 | bytes 2097152 | tf_op jit(solution)/shard_map/pallas_call | solution.py:667
  44.6 2.2 %shard_map.120 = f32[32,32,32]{2,1,0:T(8,128)} custom-call(f32[32,32,128]{2,1,0:T(8,128)S(1)} %shard_map.118.base, f32[3,16,128]{2,1,0:T(8,128)S(1)} %shard_map.119.piece_0, f32[3,16,128]{2,1,0:T(8,128)S(1)} %collective-permute-done.8.piece_1, f32[3,16,128]{2,1,0:T(8,128)S(1)} %collective-permute-done.9.piece_2, ...), custom_call_target="tpu_custom_call" | custom-call | flops 1000000 | bytes 2097152 | tf_op jit(solution)/shard_map/pallas_call | solution.py:667
  (19 shorter events, 0.0 us)
Async XLA Ops:
  0.0 21.2 %copy-start.5 = (f32[5,5,5]{2,1,0:T(8,128)S(1)}, f32[5,5,5]{2,1,0:T(8,128)}, u32[]{:S(2)}) copy-start(f32[5,5,5]{2,1,0:T(8,128)} %refs_0_.2) | copy-start | bytes 1504
  6.0 1.3 %collective-permute-start = (f32[72,128]{1,0:T(8,128)S(1)}, f32[72,128]{1,0:T(8,128)S(1)}, u32[]{:S(2)}, u32[]{:S(2)}) collective-permute-start(f32[72,128]{1,0:T(8,128)S(1)} %get-tuple-element.30), channel_id=1, source_target_pairs={{0,16},{16,0},{32,48},{48,32},{1,17},{17,1},{33,49},{49,33},{2,18}... | collective-permute-start | bytes 110600 | tf_op jit(solution)/shard_map/ppermute | solution.py:686
  7.3 9.2 %collective-permute-start.1 = (f32[40,128]{1,0:T(8,128)S(1)}, f32[40,128]{1,0:T(8,128)S(1)}, u32[]{:S(2)}, u32[]{:S(2)}) collective-permute-start(f32[40,128]{1,0:T(8,128)S(1)} %shard_map.111.own), channel_id=1, source_target_pairs={{0,32},{16,48},{32,0},{48,16},{1,33},{17,49},{33,1},{49,17},{2,34}... | collective-permute-start | bytes 61448 | tf_op jit(solution)/shard_map/ppermute | solution.py:686
  13.6 1.0 %copy-start = (f32[32,32,128]{2,1,0:T(8,128)S(1)}, f32[32,32,128]{2,1,0:T(8,128)}, u32[]{:S(2)}) copy-start(f32[32,32,128]{2,1,0:T(8,128)} %get-tuple-element.27.packed) | copy-start | bytes 1572868
  14.7 0.9 %copy-start.2 = (f32[8,32,128]{2,1,0:T(8,128)S(1)}, f32[8,32,128]{2,1,0:T(8,128)}, u32[]{:S(2)}) copy-start(f32[8,32,128]{2,1,0:T(8,128)} %constant.10.clone.factors) | copy-start | bytes 393220
  16.9 6.2 %collective-permute-start.2 = (f32[8,128]{1,0:T(8,128)S(1)}, f32[8,128]{1,0:T(8,128)S(1)}, u32[]{:S(2)}, u32[]{:S(2)}) collective-permute-start(f32[8,128]{1,0:T(8,128)S(1)} %get-tuple-element.33.own), channel_id=1, source_target_pairs={{0,128},{64,192},{128,0},{192,64},{1,129},{65,193},{129,1},{193,65... | collective-permute-start | bytes 12296 | tf_op jit(solution)/shard_map/ppermute | solution.py:686
  20.1 4.0 %collective-permute-start.3 = (f32[72,128]{1,0:T(8,128)S(1)}, f32[72,128]{1,0:T(8,128)S(1)}, u32[]{:S(2)}, u32[]{:S(2)}) collective-permute-start(f32[72,128]{1,0:T(8,128)S(1)} %get-tuple-element.34), channel_id=1, source_target_pairs={{0,64},{64,0},{128,192},{192,128},{1,65},{65,1},{129,193},{193,129... | collective-permute-start | bytes 110600 | tf_op jit(solution)/shard_map/ppermute | solution.py:686
  20.6 10.8 %copy-start.6 = (f32[5,5,5]{2,1,0:T(8,128)S(1)}, f32[5,5,5]{2,1,0:T(8,128)}, u32[]{:S(2)}) copy-start(f32[5,5,5]{2,1,0:T(8,128)} %refs_0_.3) | copy-start | bytes 1504
  20.6 10.8 %copy-start.7 = (f32[5,5,5]{2,1,0:T(8,128)S(1)}, f32[5,5,5]{2,1,0:T(8,128)}, u32[]{:S(2)}) copy-start(f32[5,5,5]{2,1,0:T(8,128)} %refs_1_.1) | copy-start | bytes 1504
  20.7 5.2 %collective-permute-start.4 = (f32[72,128]{1,0:T(8,128)S(1)}, f32[72,128]{1,0:T(8,128)S(1)}, u32[]{:S(2)}, u32[]{:S(2)}) collective-permute-start(f32[72,128]{1,0:T(8,128)S(1)} %get-tuple-element.35), channel_id=1, source_target_pairs={{0,192},{64,128},{128,64},{192,0},{1,193},{65,129},{129,65},{193,1... | collective-permute-start | bytes 110600 | tf_op jit(solution)/shard_map/ppermute | solution.py:686
  26.1 9.4 %collective-permute-start.5 = (f32[80,128]{1,0:T(8,128)S(1)}, f32[80,128]{1,0:T(8,128)S(1)}, u32[]{:S(2)}, u32[]{:S(2)}) collective-permute-start(f32[80,128]{1,0:T(8,128)S(1)} %get-tuple-element.39), channel_id=1, source_target_pairs={{0,1},{1,2},{2,3},{3,4},{4,5},{5,6},{6,7},{7,8},{8,9},{9,10},{10,1... | collective-permute-start | bytes 122888 | tf_op jit(solution)/shard_map/ppermute | solution.py:698
  27.8 7.7 %collective-permute-start.6 = (f32[80,128]{1,0:T(8,128)S(1)}, f32[80,128]{1,0:T(8,128)S(1)}, u32[]{:S(2)}, u32[]{:S(2)}) collective-permute-start(f32[80,128]{1,0:T(8,128)S(1)} %get-tuple-element.40), channel_id=1, source_target_pairs={{0,47},{1,0},{2,1},{3,2},{4,3},{5,4},{6,5},{7,6},{8,7},{9,8},{10,9... | collective-permute-start | bytes 122888 | tf_op jit(solution)/shard_map/ppermute | solution.py:698
  30.4 5.2 %collective-permute-start.7 = (f32[16,128]{1,0:T(8,128)S(1)}, f32[16,128]{1,0:T(8,128)S(1)}, u32[]{:S(2)}, u32[]{:S(2)}) collective-permute-start(f32[16,128]{1,0:T(8,128)S(1)} %get-tuple-element.46.own), channel_id=1, source_target_pairs={{0,2},{1,3},{2,0},{3,1},{4,6},{5,7},{6,4},{7,5},{8,10},{9,11},{10,... | collective-permute-start | bytes 24584 | tf_op jit(solution)/shard_map/ppermute | solution.py:686
  33.1 8.8 %copy-start.3 = (bf16[128,128]{1,0:T(8,128)(2,1)S(1)}, bf16[128,128]{1,0:T(8,128)(2,1)}, u32[]{:S(2)}) copy-start(bf16[128,128]{1,0:T(8,128)(2,1)} %constant.11.clone.prol_2) | copy-start | bytes 98308
  33.1 8.8 %copy-start.4 = (bf16[128,128]{1,0:T(8,128)(2,1)S(1)}, bf16[128,128]{1,0:T(8,128)(2,1)}, u32[]{:S(2)}) copy-start(bf16[128,128]{1,0:T(8,128)(2,1)} %constant.12.clone.prol_1) | copy-start | bytes 98308
  33.1 11.5 %copy-start.1 = (bf16[8,128,128]{2,1,0:T(8,128)(2,1)S(1)}, bf16[8,128,128]{2,1,0:T(8,128)(2,1)}, u32[]{:S(2)}) copy-start(bf16[8,128,128]{2,1,0:T(8,128)(2,1)} %constant.13.clone.qz) | copy-start | bytes 786436
  35.7 8.9 %collective-permute-start.8 = (f32[3,16,128]{2,1,0:T(8,128)S(1)}, f32[3,16,128]{2,1,0:T(8,128)S(1)}, u32[]{:S(2)}, u32[]{:S(2)}) collective-permute-start(f32[3,16,128]{2,1,0:T(8,128)S(1)} %shard_map.119.piece_0), channel_id=1, source_target_pairs={{0,8},{1,9},{2,10},{3,11},{4,12},{5,13},{6,14},{7,15},{8,32},{9,33... | collective-permute-start | bytes 73736 | tf_op jit(solution)/shard_map/ppermute | solution.py:698
  37.5 7.1 %collective-permute-start.9 = (f32[3,16,128]{2,1,0:T(8,128)S(1)}, f32[3,16,128]{2,1,0:T(8,128)S(1)}, u32[]{:S(2)}, u32[]{:S(2)}) collective-permute-start(f32[3,16,128]{2,1,0:T(8,128)S(1)} %shard_map.119.piece_0), channel_id=1, source_target_pairs={{0,44},{1,45},{2,46},{3,47},{4,0},{5,1},{6,2},{7,3},{8,4},{9,5},{1... | collective-permute-start | bytes 73736 | tf_op jit(solution)/shard_map/ppermute | solution.py:698
  38.9 5.7 %collective-permute-start.10 = (f32[3,16,128]{2,1,0:T(8,128)S(1)}, f32[3,16,128]{2,1,0:T(8,128)S(1)}, u32[]{:S(2)}, u32[]{:S(2)}) collective-permute-start(f32[3,16,128]{2,1,0:T(8,128)S(1)} %shard_map.119.piece_0), channel_id=1, source_target_pairs={{0,4},{1,5},{2,6},{3,7},{4,8},{5,9},{6,10},{7,11},{8,12},{9,13},{1... | collective-permute-start | bytes 73736 | tf_op jit(solution)/shard_map/ppermute | solution.py:698

commit v11 on v10

--- a/solution.py
+++ b/solution.py
@@ -610,22 +610,36 @@
         out[x] = first + prolong_plane(lambda q: tall_2y[q], x, False)
 
 
+def window_starts(index):
+    ring = lax.rem(index, 4)
+    first = 4 * (ring == 3).astype(jnp.int32) - 4 * (ring == 0).astype(jnp.int32) + 127
+    return [lax.rem(16 * lax.rem(index // 4 + step, 4) + first, 128) for step in (0, 2, 1, 3)]
+
+
+def placed_row(piece, at, x):
+    kept = lanes_of(piece[x // 6], 20 * (x % 6), 20)
+    return pltpu.roll(kept, lax.rem(at + 128 - 20 * (x % 6), 128), 1)
+
+
+def place_kernel(piece_0, piece_1, piece_2, after, out):
+    index, _ = place()
+    starts = window_starts(index[2])
+    for x in range(16):
+        out[x] = taps(
+            [(1.0, placed_row(p, at, x)) for p, at in zip((piece_0, piece_1, piece_2), starts)]
+        )
+
+
 def top_kernel(
-    base, piece_0, piece_1, piece_2, piece_3, green_high, green_low, rise, qz,
+    base, early, piece_3, green_high, green_low, rise, qz,
     out_hbm,
     fourth, out, sems,
 ):
     index, sizes = place()
     lane = iota((8, 128), 1)
-    ring = lax.rem(index[2], 4)
-    first = 4 * (ring == 3).astype(jnp.int32) - 4 * (ring == 0).astype(jnp.int32) + 127
-    sources = [lax.rem(16 * lax.rem(index[2] // 4 + step, 4) + first, 128) for step in (0, 2, 1, 3)]
+    at = window_starts(index[2])[3]
     for x in range(16):
-        total = None
-        for piece, at in zip((piece_0, piece_1, piece_2, piece_3), sources):
-            kept = lanes_of(piece[x // 6], 20 * (x % 6), 20)
-            moved = pltpu.roll(kept, lax.rem(at + 128 - 20 * (x % 6), 128), 1)
-            total = moved if total is None else total + moved
+        total = early[x] + placed_row(piece_3, at, x)
         total = total + roll(total, 64)
         fourth[x] = jnp.where(lane < 64, total[0:8], total[8:16])
     total = jnp.zeros((32, 128 * SPAN_4), F32)
@@ -791,10 +805,11 @@
             pltpu.VMEM((SPAN_2, 32, 128), F32),
         ),
     )
+    early = call(place_kernel, shape(16, 16, 128), (*pieces[:3], base), spaces={3: ANY})
     return call(
         top_kernel,
         shape(32, 32, 32),
-        (base, *pieces, green_high, green_low, rise, jnp.asarray(np.concatenate([qz_high, qz_low]))),
+        (base, early, pieces[3], green_high, green_low, rise, jnp.asarray(np.concatenate([qz_high, qz_low]))),
         (
             pltpu.VMEM((16, 8, 128), F32),
             pltpu.VMEM((32, 32, 32), F32),

time: 47.3 us -> 47.3 us (level)
    pallas_call x12 -> x13, Pallas kernels: 15.8 us -> 15.8 us  [call(): pl.pallas_call(kernel, out_shape=outs, in_specs=[spaces.get(i, VMEM) for...]
where the time goes in v11:
time: 47.3 us; the launch traced here: 47 us
  starting transfers between devices  22.1 us (47%)
  Pallas kernels  15.8 us (33%)
  waiting for transfers between devices  6.07 us (13%)
  local copies, waits for them, and re-layouts  1.98 us (4%)
  other arithmetic  0.71 us (2%)
    pallas_call x13, Pallas kernels, call(): pl.pallas_call(kernel, out_shape=outs, in_specs=[spaces.get(i, VMEM) for...  15.8 us
    ppermute x6, starting transfers between devices, exchange(): lax.ppermute(value, axis, [(i, i ^ step) for i in range(size)])  11.7 us
    ppermute x5, starting transfers between devices, turn(): return lax.ppermute(value, ('gy', 'gz'), pairs)  10.4 us
    ppermute x6, waiting for transfers between devices, exchange(): lax.ppermute(value, axis, [(i, i ^ step) for i in range(size)])  6.06 us
    unnamed x16, local copies, waits for them, and re-layouts  1.98 us
  transfers between devices with their start and end apart: 11, of which 4 were waited for; matrix products, arithmetic and copies ran while one was open for 0% of the time, Pallas kernels for 16%

profile of v11, /device:TPU:32, one launch (start us, length us, event | category | flops | bytes accessed | tf_op | source)
XLA Modules:
  0.0 47.0 jit_solution(4752607270494629156)
XLA Ops:
  0.0 0.7 %multiply_add_fusion.codes = s32[384]{0:T(512)S(1)} fusion(s32[384]{0:T(512)} %param.12, s32[384]{0:T(512)} %param.13), kind=kLoop, calls=%fused_computation | loop fusion | flops 768 | bytes 4608 | tf_op jit(solution)/shard_map/add | solution.py:730
  0.7 5.2 %shard_map.109 = (f32[32,32,128]{2,1,0:T(8,128)}, f32[8,128]{1,0:T(8,128)S(1)}, f32[72,128]{1,0:T(8,128)S(1)}) custom-call(s32[384]{0:T(512)S(1)} %multiply_add_fusion.codes, f32[384,128]{1,0:T(8,128)} %charges_hbm.1, bf16[4608,128]{1,0:T(8,128)(2,1)} %bitcast.1), custom_call_target="tpu_custom_call" | custom-call | flops 1000000 | bytes 2097152 | tf_op jit(solution)/shard_map/pallas_call | solution.py:681
  6.0 0.1 collective-permute-start
  6.1 1.2 %collective-permute-done.got.got_1 = f32[72,128]{1,0:T(8,128)S(1)} collective-permute-done((f32[72,128]{1,0:T(8,128)S(1)}, f32[72,128]{1,0:T(8,128)S(1)}, u32[]{:S(2)}, u32[]{:S(2)}) %collective-permute-start) | collective-permute-done | bytes 36896 | tf_op jit(solution)/shard_map/ppermute | solution.py:700
  7.3 0.1 shard_map.111.own
  7.3 6.3 %collective-permute-start.1 = (f32[40,128]{1,0:T(8,128)S(1)}, f32[40,128]{1,0:T(8,128)S(1)}, u32[]{:S(2)}, u32[]{:S(2)}) collective-permute-start(f32[40,128]{1,0:T(8,128)S(1)} %shard_map.111.own), channel_id=1, source_target_pairs={{0,32},{16,48},{32,0},{48,16},{1,33},{17,49},{33,1},{49,17},{2,34}... | collective-permute-start | bytes 61448 | tf_op jit(solution)/shard_map/ppermute | solution.py:700
  13.7 1.0 %copy-done = f32[32,32,128]{2,1,0:T(8,128)S(1)} copy-done((f32[32,32,128]{2,1,0:T(8,128)S(1)}, f32[32,32,128]{2,1,0:T(8,128)}, u32[]{:S(2)}) %copy-start) | copy-done | bytes 524312
  14.7 0.9 %copy-done.2 = f32[8,32,128]{2,1,0:T(8,128)S(1)} copy-done((f32[8,32,128]{2,1,0:T(8,128)S(1)}, f32[8,32,128]{2,1,0:T(8,128)}, u32[]{:S(2)}) %copy-start.2) | copy-done | bytes 131096
  15.6 1.0 %shard_map.110 = (bf16[1024,896]{1,0:T(8,128)(2,1)S(1)}, bf16[1024,896]{1,0:T(8,128)(2,1)S(1)}, bf16[1024,256]{1,0:T(8,128)(2,1)S(1)}, f32[32,40,128]{2,1,0:T(8,128)S(1)}) custom-call(f32[8,32,128]{2,1,0:T(8,128)S(1)} %copy-done.2, f32[32,32,128]{2,1,0:T(8,128)S(1)} %copy-done), custom_call_target="tpu_custom_call" | custom-call | flops 1000000 | bytes 2097152 | tf_op jit(solution)/shard_map/pallas_call | solution.py:681
  16.6 0.4 shard_map.112
  16.9 3.1 %collective-permute-start.2 = (f32[8,128]{1,0:T(8,128)S(1)}, f32[8,128]{1,0:T(8,128)S(1)}, u32[]{:S(2)}, u32[]{:S(2)}) collective-permute-start(f32[8,128]{1,0:T(8,128)S(1)} %get-tuple-element.33.own), channel_id=1, source_target_pairs={{0,128},{64,192},{128,0},{192,64},{1,129},{65,193},{129,1},{193,65... | collective-permute-start | bytes 12296 | tf_op jit(solution)/shard_map/ppermute | solution.py:700
  20.1 0.6 %collective-permute-start.3 = (f32[72,128]{1,0:T(8,128)S(1)}, f32[72,128]{1,0:T(8,128)S(1)}, u32[]{:S(2)}, u32[]{:S(2)}) collective-permute-start(f32[72,128]{1,0:T(8,128)S(1)} %get-tuple-element.34), channel_id=1, source_target_pairs={{0,64},{64,0},{128,192},{192,128},{1,65},{65,1},{129,193},{193,129... | collective-permute-start | bytes 110600 | tf_op jit(solution)/shard_map/ppermute | solution.py:700
  20.7 0.5 %collective-permute-start.4 = (f32[72,128]{1,0:T(8,128)S(1)}, f32[72,128]{1,0:T(8,128)S(1)}, u32[]{:S(2)}, u32[]{:S(2)}) collective-permute-start(f32[72,128]{1,0:T(8,128)S(1)} %get-tuple-element.35), channel_id=1, source_target_pairs={{0,192},{64,128},{128,64},{192,0},{1,193},{65,129},{129,65},{193,1... | collective-permute-start | bytes 110600 | tf_op jit(solution)/shard_map/ppermute | solution.py:700
  21.2 1.4 %shard_map.114 = (bf16[256,256]{1,0:T(8,128)(2,1)S(1)}, bf16[256,256]{1,0:T(8,128)(2,1)S(1)}) custom-call(f32[5,5,5]{2,1,0:T(8,128)S(1)} %copy-done.5), custom_call_target="tpu_custom_call" | custom-call | flops 1000000000 | bytes 2097152 | tf_op jit(solution)/shard_map/pallas_call | solution.py:681
  22.6 0.6 %shard_map.115 = (f32[80,128]{1,0:T(8,128)S(1)}, f32[80,128]{1,0:T(8,128)S(1)}) custom-call(f32[32,40,128]{2,1,0:T(8,128)S(1)} %get-tuple-element.32.wide_y, bf16[256,256]{1,0:T(8,128)(2,1)S(1)} %get-tuple-element.36.after.b1h), custom_call_target="tpu_custom_call" | custom-call | flops 1000000 | bytes 2097152 | tf_op jit(solution)/shard_map/pallas_call | solution.py:681
  23.1 0.9 %collective-permute-done.3.got_1 = f32[72,128]{1,0:T(8,128)S(1)} collective-permute-done((f32[72,128]{1,0:T(8,128)S(1)}, f32[72,128]{1,0:T(8,128)S(1)}, u32[]{:S(2)}, u32[]{:S(2)}) %collective-permute-start.3) | collective-permute-done | bytes 36896 | tf_op jit(solution)/shard_map/ppermute | solution.py:700
  24.0 1.8 %collective-permute-done.4.got_3 = f32[72,128]{1,0:T(8,128)S(1)} collective-permute-done((f32[72,128]{1,0:T(8,128)S(1)}, f32[72,128]{1,0:T(8,128)S(1)}, u32[]{:S(2)}, u32[]{:S(2)}) %collective-permute-start.4) | collective-permute-done | bytes 36896 | tf_op jit(solution)/shard_map/ppermute | solution.py:700
  25.8 0.3 shard_map.116
  26.1 1.7 %collective-permute-start.5 = (f32[80,128]{1,0:T(8,128)S(1)}, f32[80,128]{1,0:T(8,128)S(1)}, u32[]{:S(2)}, u32[]{:S(2)}) collective-permute-start(f32[80,128]{1,0:T(8,128)S(1)} %get-tuple-element.39), channel_id=1, source_target_pairs={{0,1},{1,2},{2,3},{3,4},{4,5},{5,6},{6,7},{7,8},{8,9},{9,10},{10,1... | collective-permute-start | bytes 122888 | tf_op jit(solution)/shard_map/ppermute | solution.py:712
  27.8 2.6 %collective-permute-start.6 = (f32[80,128]{1,0:T(8,128)S(1)}, f32[80,128]{1,0:T(8,128)S(1)}, u32[]{:S(2)}, u32[]{:S(2)}) collective-permute-start(f32[80,128]{1,0:T(8,128)S(1)} %get-tuple-element.40), channel_id=1, source_target_pairs={{0,47},{1,0},{2,1},{3,2},{4,3},{5,4},{6,5},{7,6},{8,7},{9,8},{10,9... | collective-permute-start | bytes 122888 | tf_op jit(solution)/shard_map/ppermute | solution.py:712
  30.4 1.1 %collective-permute-start.7 = (f32[16,128]{1,0:T(8,128)S(1)}, f32[16,128]{1,0:T(8,128)S(1)}, u32[]{:S(2)}, u32[]{:S(2)}) collective-permute-start(f32[16,128]{1,0:T(8,128)S(1)} %get-tuple-element.46.own), channel_id=1, source_target_pairs={{0,2},{1,3},{2,0},{3,1},{4,6},{5,7},{6,4},{7,5},{8,10},{9,11},{10,... | collective-permute-start | bytes 24584 | tf_op jit(solution)/shard_map/ppermute | solution.py:700
  31.4 1.6 %shard_map.117 = (bf16[256,128]{1,0:T(8,128)(2,1)S(1)}, bf16[256,128]{1,0:T(8,128)(2,1)S(1)}, bf16[128,128]{1,0:T(8,128)(2,1)S(1)}, bf16[128,128]{1,0:T(8,128)(2,1)S(1)}) custom-call(f32[5,5,5]{2,1,0:T(8,128)S(1)} %copy-done.6, f32[5,5,5]{2,1,0:T(8,128)S(1)} %copy-done.7), custom_call_target="tpu_custom_call" | custom-call | flops 1000000000 | bytes 2097152 | tf_op jit(solution)/shard_map/pallas_call | solution.py:681
  33.1 0.0 copy-start.3
  33.1 0.2 shard_map.113.wide.after_2
  33.3 2.2 %collective-permute-done.7.got_2 = f32[16,128]{1,0:T(8,128)S(1)} collective-permute-done((f32[16,128]{1,0:T(8,128)S(1)}, f32[16,128]{1,0:T(8,128)S(1)}, u32[]{:S(2)}, u32[]{:S(2)}) %collective-permute-start.7) | collective-permute-done | bytes 8224 | tf_op jit(solution)/shard_map/ppermute | solution.py:700
  35.5 0.2 shard_map.119.piece_0
  35.7 1.8 %collective-permute-start.8 = (f32[3,16,128]{2,1,0:T(8,128)S(1)}, f32[3,16,128]{2,1,0:T(8,128)S(1)}, u32[]{:S(2)}, u32[]{:S(2)}) collective-permute-start(f32[3,16,128]{2,1,0:T(8,128)S(1)} %shard_map.119.piece_0), channel_id=1, source_target_pairs={{0,8},{1,9},{2,10},{3,11},{4,12},{5,13},{6,14},{7,15},{8,32},{9,33... | collective-permute-start | bytes 73736 | tf_op jit(solution)/shard_map/ppermute | solution.py:712
  37.5 1.4 %collective-permute-start.9 = (f32[3,16,128]{2,1,0:T(8,128)S(1)}, f32[3,16,128]{2,1,0:T(8,128)S(1)}, u32[]{:S(2)}, u32[]{:S(2)}) collective-permute-start(f32[3,16,128]{2,1,0:T(8,128)S(1)} %shard_map.119.piece_0), channel_id=1, source_target_pairs={{0,44},{1,45},{2,46},{3,47},{4,0},{5,1},{6,2},{7,3},{8,4},{9,5},{1... | collective-permute-start | bytes 73736 | tf_op jit(solution)/shard_map/ppermute | solution.py:712
  38.9 3.0 %collective-permute-start.10 = (f32[3,16,128]{2,1,0:T(8,128)S(1)}, f32[3,16,128]{2,1,0:T(8,128)S(1)}, u32[]{:S(2)}, u32[]{:S(2)}) collective-permute-start(f32[3,16,128]{2,1,0:T(8,128)S(1)} %shard_map.119.piece_0), channel_id=1, source_target_pairs={{0,4},{1,5},{2,6},{3,7},{4,8},{5,9},{6,10},{7,11},{8,12},{9,13},{1... | collective-permute-start | bytes 73736 | tf_op jit(solution)/shard_map/ppermute | solution.py:712
  41.9 2.7 %shard_map.118.after.base = f32[32,32,128]{2,1,0:T(8,128)S(1)} custom-call(f32[36,40,128]{2,1,0:T(8,128)S(1)} %shard_map.113.wide.after_2, f32[80,128]{1,0:T(8,128)S(1)} %collective-permute-done.5.from_low, f32[80,128]{1,0:T(8,128)S(1)} %collective-permute-done.6.from_high, bf16[256,256]{1,0:T(8,128)(2,1)S(1)} %get-tuple-element.36.after.b1h, ...), custom_call_target="tpu_custom_call" | custom-call | flops 1000000 | bytes 2097152 | tf_op jit(solution)/shard_map/pallas_call | solution.py:681
  44.6 0.2 shard_map.120.early
  44.8 2.1 %shard_map.121 = f32[32,32,32]{2,1,0:T(8,128)} custom-call(f32[32,32,128]{2,1,0:T(8,128)S(1)} %shard_map.118.after.base, f32[16,16,128]{2,1,0:T(8,128)S(1)} %shard_map.120.early, f32[3,16,128]{2,1,0:T(8,128)S(1)} %collective-permute-done.10.piece_3, bf16[1024,896]{1,0:T(8,128)(2,1)S(1)} %get-tuple-element.47.green_high, ...), custom_call_target="tpu_custom_call" | custom-call | flops 1000000 | bytes 2097152 | tf_op jit(solution)/shard_map/pallas_call | solution.py:681
  (20 shorter events, 0.0 us)
Async XLA Ops:
  0.0 21.2 %copy-start.5 = (f32[5,5,5]{2,1,0:T(8,128)S(1)}, f32[5,5,5]{2,1,0:T(8,128)}, u32[]{:S(2)}) copy-start(f32[5,5,5]{2,1,0:T(8,128)} %refs_0_.2) | copy-start | bytes 1504
  6.0 1.3 %collective-permute-start = (f32[72,128]{1,0:T(8,128)S(1)}, f32[72,128]{1,0:T(8,128)S(1)}, u32[]{:S(2)}, u32[]{:S(2)}) collective-permute-start(f32[72,128]{1,0:T(8,128)S(1)} %get-tuple-element.30), channel_id=1, source_target_pairs={{0,16},{16,0},{32,48},{48,32},{1,17},{17,1},{33,49},{49,33},{2,18}... | collective-permute-start | bytes 110600 | tf_op jit(solution)/shard_map/ppermute | solution.py:700
  7.3 9.2 %collective-permute-start.1 = (f32[40,128]{1,0:T(8,128)S(1)}, f32[40,128]{1,0:T(8,128)S(1)}, u32[]{:S(2)}, u32[]{:S(2)}) collective-permute-start(f32[40,128]{1,0:T(8,128)S(1)} %shard_map.111.own), channel_id=1, source_target_pairs={{0,32},{16,48},{32,0},{48,16},{1,33},{17,49},{33,1},{49,17},{2,34}... | collective-permute-start | bytes 61448 | tf_op jit(solution)/shard_map/ppermute | solution.py:700
  13.6 1.0 %copy-start = (f32[32,32,128]{2,1,0:T(8,128)S(1)}, f32[32,32,128]{2,1,0:T(8,128)}, u32[]{:S(2)}) copy-start(f32[32,32,128]{2,1,0:T(8,128)} %get-tuple-element.27.packed) | copy-start | bytes 1572868
  14.7 0.9 %copy-start.2 = (f32[8,32,128]{2,1,0:T(8,128)S(1)}, f32[8,32,128]{2,1,0:T(8,128)}, u32[]{:S(2)}) copy-start(f32[8,32,128]{2,1,0:T(8,128)} %constant.10.clone.factors) | copy-start | bytes 393220
  16.9 6.2 %collective-permute-start.2 = (f32[8,128]{1,0:T(8,128)S(1)}, f32[8,128]{1,0:T(8,128)S(1)}, u32[]{:S(2)}, u32[]{:S(2)}) collective-permute-start(f32[8,128]{1,0:T(8,128)S(1)} %get-tuple-element.33.own), channel_id=1, source_target_pairs={{0,128},{64,192},{128,0},{192,64},{1,129},{65,193},{129,1},{193,65... | collective-permute-start | bytes 12296 | tf_op jit(solution)/shard_map/ppermute | solution.py:700
  20.1 4.0 %collective-permute-start.3 = (f32[72,128]{1,0:T(8,128)S(1)}, f32[72,128]{1,0:T(8,128)S(1)}, u32[]{:S(2)}, u32[]{:S(2)}) collective-permute-start(f32[72,128]{1,0:T(8,128)S(1)} %get-tuple-element.34), channel_id=1, source_target_pairs={{0,64},{64,0},{128,192},{192,128},{1,65},{65,1},{129,193},{193,129... | collective-permute-start | bytes 110600 | tf_op jit(solution)/shard_map/ppermute | solution.py:700
  20.6 10.8 %copy-start.6 = (f32[5,5,5]{2,1,0:T(8,128)S(1)}, f32[5,5,5]{2,1,0:T(8,128)}, u32[]{:S(2)}) copy-start(f32[5,5,5]{2,1,0:T(8,128)} %refs_0_.3) | copy-start | bytes 1504
  20.6 10.8 %copy-start.7 = (f32[5,5,5]{2,1,0:T(8,128)S(1)}, f32[5,5,5]{2,1,0:T(8,128)}, u32[]{:S(2)}) copy-start(f32[5,5,5]{2,1,0:T(8,128)} %refs_1_.1) | copy-start | bytes 1504
  20.7 5.2 %collective-permute-start.4 = (f32[72,128]{1,0:T(8,128)S(1)}, f32[72,128]{1,0:T(8,128)S(1)}, u32[]{:S(2)}, u32[]{:S(2)}) collective-permute-start(f32[72,128]{1,0:T(8,128)S(1)} %get-tuple-element.35), channel_id=1, source_target_pairs={{0,192},{64,128},{128,64},{192,0},{1,193},{65,129},{129,65},{193,1... | collective-permute-start | bytes 110600 | tf_op jit(solution)/shard_map/ppermute | solution.py:700
  26.1 9.4 %collective-permute-start.5 = (f32[80,128]{1,0:T(8,128)S(1)}, f32[80,128]{1,0:T(8,128)S(1)}, u32[]{:S(2)}, u32[]{:S(2)}) collective-permute-start(f32[80,128]{1,0:T(8,128)S(1)} %get-tuple-element.39), channel_id=1, source_target_pairs={{0,1},{1,2},{2,3},{3,4},{4,5},{5,6},{6,7},{7,8},{8,9},{9,10},{10,1... | collective-permute-start | bytes 122888 | tf_op jit(solution)/shard_map/ppermute | solution.py:712
  27.8 7.7 %collective-permute-start.6 = (f32[80,128]{1,0:T(8,128)S(1)}, f32[80,128]{1,0:T(8,128)S(1)}, u32[]{:S(2)}, u32[]{:S(2)}) collective-permute-start(f32[80,128]{1,0:T(8,128)S(1)} %get-tuple-element.40), channel_id=1, source_target_pairs={{0,47},{1,0},{2,1},{3,2},{4,3},{5,4},{6,5},{7,6},{8,7},{9,8},{10,9... | collective-permute-start | bytes 122888 | tf_op jit(solution)/shard_map/ppermute | solution.py:712
  30.4 5.2 %collective-permute-start.7 = (f32[16,128]{1,0:T(8,128)S(1)}, f32[16,128]{1,0:T(8,128)S(1)}, u32[]{:S(2)}, u32[]{:S(2)}) collective-permute-start(f32[16,128]{1,0:T(8,128)S(1)} %get-tuple-element.46.own), channel_id=1, source_target_pairs={{0,2},{1,3},{2,0},{3,1},{4,6},{5,7},{6,4},{7,5},{8,10},{9,11},{10,... | collective-permute-start | bytes 24584 | tf_op jit(solution)/shard_map/ppermute | solution.py:700
  33.1 8.8 %copy-start.3 = (bf16[128,128]{1,0:T(8,128)(2,1)S(1)}, bf16[128,128]{1,0:T(8,128)(2,1)}, u32[]{:S(2)}) copy-start(bf16[128,128]{1,0:T(8,128)(2,1)} %constant.11.clone.prol_2) | copy-start | bytes 98308
  33.1 8.8 %copy-start.4 = (bf16[128,128]{1,0:T(8,128)(2,1)S(1)}, bf16[128,128]{1,0:T(8,128)(2,1)}, u32[]{:S(2)}) copy-start(bf16[128,128]{1,0:T(8,128)(2,1)} %constant.12.clone.prol_1) | copy-start | bytes 98308
  33.3 11.4 %copy-start.1 = (bf16[8,128,128]{2,1,0:T(8,128)(2,1)S(1)}, bf16[8,128,128]{2,1,0:T(8,128)(2,1)}, u32[]{:S(2)}) copy-start(bf16[8,128,128]{2,1,0:T(8,128)(2,1)} %constant.13.clone.qz) | copy-start | bytes 786436
  35.7 8.8 %collective-permute-start.8 = (f32[3,16,128]{2,1,0:T(8,128)S(1)}, f32[3,16,128]{2,1,0:T(8,128)S(1)}, u32[]{:S(2)}, u32[]{:S(2)}) collective-permute-start(f32[3,16,128]{2,1,0:T(8,128)S(1)} %shard_map.119.piece_0), channel_id=1, source_target_pairs={{0,8},{1,9},{2,10},{3,11},{4,12},{5,13},{6,14},{7,15},{8,32},{9,33... | collective-permute-start | bytes 73736 | tf_op jit(solution)/shard_map/ppermute | solution.py:712
  37.5 7.0 %collective-permute-start.9 = (f32[3,16,128]{2,1,0:T(8,128)S(1)}, f32[3,16,128]{2,1,0:T(8,128)S(1)}, u32[]{:S(2)}, u32[]{:S(2)}) collective-permute-start(f32[3,16,128]{2,1,0:T(8,128)S(1)} %shard_map.119.piece_0), channel_id=1, source_target_pairs={{0,44},{1,45},{2,46},{3,47},{4,0},{5,1},{6,2},{7,3},{8,4},{9,5},{1... | collective-permute-start | bytes 73736 | tf_op jit(solution)/shard_map/ppermute | solution.py:712
  38.9 5.9 %collective-permute-start.10 = (f32[3,16,128]{2,1,0:T(8,128)S(1)}, f32[3,16,128]{2,1,0:T(8,128)S(1)}, u32[]{:S(2)}, u32[]{:S(2)}) collective-permute-start(f32[3,16,128]{2,1,0:T(8,128)S(1)} %shard_map.119.piece_0), channel_id=1, source_target_pairs={{0,4},{1,5},{2,6},{3,7},{4,8},{5,9},{6,10},{7,11},{8,12},{9,13},{1... | collective-permute-start | bytes 73736 | tf_op jit(solution)/shard_map/ppermute | solution.py:712

commit v12 on v10

--- a/solution.py
+++ b/solution.py
@@ -619,7 +619,7 @@
     lane = iota((8, 128), 1)
     ring = lax.rem(index[2], 4)
     first = 4 * (ring == 3).astype(jnp.int32) - 4 * (ring == 0).astype(jnp.int32) + 127
-    sources = [lax.rem(16 * lax.rem(index[2] // 4 + step, 4) + first, 128) for step in (0, 2, 1, 3)]
+    sources = [lax.rem(16 * lax.rem(index[2] // 4 + step, 4) + first, 128) for step in (0, 1, 2, 3)]
     for x in range(16):
         total = None
         for piece, at in zip((piece_0, piece_1, piece_2, piece_3), sources):
@@ -776,7 +776,7 @@
         (raw, got_2, from_low, from_high, bands_2[0], wide_x),
         spaces={4: ANY, 5: ANY},
     )
-    pieces = [window] + [turn(window, by) for by in (8, -4, 4)]
+    pieces = [window] + [turn(window, by) for by in (-4, 8, 4)]
     base = call(
         near_kernel,
         shape(32, 32, 128),

time: 47.3 us -> 47.4 us (level)
  no operation moved by 1% of the time
where the time goes in v12:
time: 47.4 us; the launch traced here: 47.2 us
  starting transfers between devices  22.4 us (47%)
  Pallas kernels  15.8 us (33%)
  waiting for transfers between devices  6.07 us (13%)
  local copies, waits for them, and re-layouts  1.98 us (4%)
  other arithmetic  0.71 us (1%)
    pallas_call x12, Pallas kernels, call(): pl.pallas_call(kernel, out_shape=outs, in_specs=[spaces.get(i, VMEM) for...  15.8 us
    ppermute x6, starting transfers between devices, exchange(): lax.ppermute(value, axis, [(i, i ^ step) for i in range(size)])  11.7 us
    ppermute x5, starting transfers between devices, turn(): return lax.ppermute(value, ('gy', 'gz'), pairs)  10.6 us
    ppermute x6, waiting for transfers between devices, exchange(): lax.ppermute(value, axis, [(i, i ^ step) for i in range(size)])  6.06 us
    unnamed x16, local copies, waits for them, and re-layouts  1.98 us
  transfers between devices with their start and end apart: 11, of which 4 were waited for; matrix products, arithmetic and copies ran while one was open for 0% of the time, Pallas kernels for 16%

profile of v12, /device:TPU:32, one launch (start us, length us, event | category | flops | bytes accessed | tf_op | source)
XLA Modules:
  0.0 47.2 jit_solution(17617398630259552489)
XLA Ops:
  0.0 0.7 %multiply_add_fusion.codes = s32[384]{0:T(512)S(1)} fusion(s32[384]{0:T(512)} %param.12, s32[384]{0:T(512)} %param.13), kind=kLoop, calls=%fused_computation | loop fusion | flops 768 | bytes 4608 | tf_op jit(solution)/shard_map/add | solution.py:716
  0.7 5.2 %shard_map.109 = (f32[32,32,128]{2,1,0:T(8,128)}, f32[8,128]{1,0:T(8,128)S(1)}, f32[72,128]{1,0:T(8,128)S(1)}) custom-call(s32[384]{0:T(512)S(1)} %multiply_add_fusion.codes, f32[384,128]{1,0:T(8,128)} %charges_hbm.1, bf16[4608,128]{1,0:T(8,128)(2,1)} %bitcast.1), custom_call_target="tpu_custom_call" | custom-call | flops 1000000 | bytes 2097152 | tf_op jit(solution)/shard_map/pallas_call | solution.py:667
  6.0 0.1 collective-permute-start
  6.1 1.2 %collective-permute-done.got.got_1 = f32[72,128]{1,0:T(8,128)S(1)} collective-permute-done((f32[72,128]{1,0:T(8,128)S(1)}, f32[72,128]{1,0:T(8,128)S(1)}, u32[]{:S(2)}, u32[]{:S(2)}) %collective-permute-start) | collective-permute-done | bytes 36896 | tf_op jit(solution)/shard_map/ppermute | solution.py:686
  7.3 0.1 shard_map.111.own
  7.3 6.3 %collective-permute-start.1 = (f32[40,128]{1,0:T(8,128)S(1)}, f32[40,128]{1,0:T(8,128)S(1)}, u32[]{:S(2)}, u32[]{:S(2)}) collective-permute-start(f32[40,128]{1,0:T(8,128)S(1)} %shard_map.111.own), channel_id=1, source_target_pairs={{0,32},{16,48},{32,0},{48,16},{1,33},{17,49},{33,1},{49,17},{2,34}... | collective-permute-start | bytes 61448 | tf_op jit(solution)/shard_map/ppermute | solution.py:686
  13.7 1.0 %copy-done = f32[32,32,128]{2,1,0:T(8,128)S(1)} copy-done((f32[32,32,128]{2,1,0:T(8,128)S(1)}, f32[32,32,128]{2,1,0:T(8,128)}, u32[]{:S(2)}) %copy-start) | copy-done | bytes 524312
  14.7 0.9 %copy-done.2 = f32[8,32,128]{2,1,0:T(8,128)S(1)} copy-done((f32[8,32,128]{2,1,0:T(8,128)S(1)}, f32[8,32,128]{2,1,0:T(8,128)}, u32[]{:S(2)}) %copy-start.2) | copy-done | bytes 131096
  15.6 1.0 %shard_map.110 = (bf16[1024,896]{1,0:T(8,128)(2,1)S(1)}, bf16[1024,896]{1,0:T(8,128)(2,1)S(1)}, bf16[1024,256]{1,0:T(8,128)(2,1)S(1)}, f32[32,40,128]{2,1,0:T(8,128)S(1)}) custom-call(f32[8,32,128]{2,1,0:T(8,128)S(1)} %copy-done.2, f32[32,32,128]{2,1,0:T(8,128)S(1)} %copy-done), custom_call_target="tpu_custom_call" | custom-call | flops 1000000 | bytes 2097152 | tf_op jit(solution)/shard_map/pallas_call | solution.py:667
  16.6 0.4 shard_map.112
  16.9 3.1 %collective-permute-start.2 = (f32[8,128]{1,0:T(8,128)S(1)}, f32[8,128]{1,0:T(8,128)S(1)}, u32[]{:S(2)}, u32[]{:S(2)}) collective-permute-start(f32[8,128]{1,0:T(8,128)S(1)} %get-tuple-element.33.own), channel_id=1, source_target_pairs={{0,128},{64,192},{128,0},{192,64},{1,129},{65,193},{129,1},{193,65... | collective-permute-start | bytes 12296 | tf_op jit(solution)/shard_map/ppermute | solution.py:686
  20.1 0.6 %collective-permute-start.3 = (f32[72,128]{1,0:T(8,128)S(1)}, f32[72,128]{1,0:T(8,128)S(1)}, u32[]{:S(2)}, u32[]{:S(2)}) collective-permute-start(f32[72,128]{1,0:T(8,128)S(1)} %get-tuple-element.34), channel_id=1, source_target_pairs={{0,64},{64,0},{128,192},{192,128},{1,65},{65,1},{129,193},{193,129... | collective-permute-start | bytes 110600 | tf_op jit(solution)/shard_map/ppermute | solution.py:686
  20.7 0.5 %collective-permute-start.4 = (f32[72,128]{1,0:T(8,128)S(1)}, f32[72,128]{1,0:T(8,128)S(1)}, u32[]{:S(2)}, u32[]{:S(2)}) collective-permute-start(f32[72,128]{1,0:T(8,128)S(1)} %get-tuple-element.35), channel_id=1, source_target_pairs={{0,192},{64,128},{128,64},{192,0},{1,193},{65,129},{129,65},{193,1... | collective-permute-start | bytes 110600 | tf_op jit(solution)/shard_map/ppermute | solution.py:686
  21.2 1.4 %shard_map.114 = (bf16[256,256]{1,0:T(8,128)(2,1)S(1)}, bf16[256,256]{1,0:T(8,128)(2,1)S(1)}) custom-call(f32[5,5,5]{2,1,0:T(8,128)S(1)} %copy-done.5), custom_call_target="tpu_custom_call" | custom-call | flops 1000000000 | bytes 2097152 | tf_op jit(solution)/shard_map/pallas_call | solution.py:667
  22.6 0.6 %shard_map.115 = (f32[80,128]{1,0:T(8,128)S(1)}, f32[80,128]{1,0:T(8,128)S(1)}) custom-call(f32[32,40,128]{2,1,0:T(8,128)S(1)} %get-tuple-element.32.wide_y, bf16[256,256]{1,0:T(8,128)(2,1)S(1)} %get-tuple-element.36.after.b1h), custom_call_target="tpu_custom_call" | custom-call | flops 1000000 | bytes 2097152 | tf_op jit(solution)/shard_map/pallas_call | solution.py:667
  23.1 0.9 %collective-permute-done.3.got_1 = f32[72,128]{1,0:T(8,128)S(1)} collective-permute-done((f32[72,128]{1,0:T(8,128)S(1)}, f32[72,128]{1,0:T(8,128)S(1)}, u32[]{:S(2)}, u32[]{:S(2)}) %collective-permute-start.3) | collective-permute-done | bytes 36896 | tf_op jit(solution)/shard_map/ppermute | solution.py:686
  24.0 1.8 %collective-permute-done.4.got_3 = f32[72,128]{1,0:T(8,128)S(1)} collective-permute-done((f32[72,128]{1,0:T(8,128)S(1)}, f32[72,128]{1,0:T(8,128)S(1)}, u32[]{:S(2)}, u32[]{:S(2)}) %collective-permute-start.4) | collective-permute-done | bytes 36896 | tf_op jit(solution)/shard_map/ppermute | solution.py:686
  25.8 0.3 shard_map.116
  26.1 1.7 %collective-permute-start.5 = (f32[80,128]{1,0:T(8,128)S(1)}, f32[80,128]{1,0:T(8,128)S(1)}, u32[]{:S(2)}, u32[]{:S(2)}) collective-permute-start(f32[80,128]{1,0:T(8,128)S(1)} %get-tuple-element.39), channel_id=1, source_target_pairs={{0,1},{1,2},{2,3},{3,4},{4,5},{5,6},{6,7},{7,8},{8,9},{9,10},{10,1... | collective-permute-start | bytes 122888 | tf_op jit(solution)/shard_map/ppermute | solution.py:698
  27.8 2.6 %collective-permute-start.6 = (f32[80,128]{1,0:T(8,128)S(1)}, f32[80,128]{1,0:T(8,128)S(1)}, u32[]{:S(2)}, u32[]{:S(2)}) collective-permute-start(f32[80,128]{1,0:T(8,128)S(1)} %get-tuple-element.40), channel_id=1, source_target_pairs={{0,47},{1,0},{2,1},{3,2},{4,3},{5,4},{6,5},{7,6},{8,7},{9,8},{10,9... | collective-permute-start | bytes 122888 | tf_op jit(solution)/shard_map/ppermute | solution.py:698
  30.4 1.1 %collective-permute-start.7 = (f32[16,128]{1,0:T(8,128)S(1)}, f32[16,128]{1,0:T(8,128)S(1)}, u32[]{:S(2)}, u32[]{:S(2)}) collective-permute-start(f32[16,128]{1,0:T(8,128)S(1)} %get-tuple-element.46.own), channel_id=1, source_target_pairs={{0,2},{1,3},{2,0},{3,1},{4,6},{5,7},{6,4},{7,5},{8,10},{9,11},{10,... | collective-permute-start | bytes 24584 | tf_op jit(solution)/shard_map/ppermute | solution.py:686
  31.4 1.6 %shard_map.117 = (bf16[256,128]{1,0:T(8,128)(2,1)S(1)}, bf16[256,128]{1,0:T(8,128)(2,1)S(1)}, bf16[128,128]{1,0:T(8,128)(2,1)S(1)}, bf16[128,128]{1,0:T(8,128)(2,1)S(1)}) custom-call(f32[5,5,5]{2,1,0:T(8,128)S(1)} %copy-done.6, f32[5,5,5]{2,1,0:T(8,128)S(1)} %copy-done.7), custom_call_target="tpu_custom_call" | custom-call | flops 1000000000 | bytes 2097152 | tf_op jit(solution)/shard_map/pallas_call | solution.py:667
  33.1 0.0 copy-start.3
  33.1 0.0 copy-start.4
  33.1 0.0 copy-start.1
  33.1 0.2 shard_map.113.wide.after_2
  33.3 2.2 %collective-permute-done.7.got_2 = f32[16,128]{1,0:T(8,128)S(1)} collective-permute-done((f32[16,128]{1,0:T(8,128)S(1)}, f32[16,128]{1,0:T(8,128)S(1)}, u32[]{:S(2)}, u32[]{:S(2)}) %collective-permute-start.7) | collective-permute-done | bytes 8224 | tf_op jit(solution)/shard_map/ppermute | solution.py:686
  35.5 0.2 shard_map.119.piece_0
  35.7 2.9 %collective-permute-start.8 = (f32[3,16,128]{2,1,0:T(8,128)S(1)}, f32[3,16,128]{2,1,0:T(8,128)S(1)}, u32[]{:S(2)}, u32[]{:S(2)}) collective-permute-start(f32[3,16,128]{2,1,0:T(8,128)S(1)} %shard_map.119.piece_0), channel_id=1, source_target_pairs={{0,44},{1,45},{2,46},{3,47},{4,0},{5,1},{6,2},{7,3},{8,4},{9,5},{1... | collective-permute-start | bytes 73736 | tf_op jit(solution)/shard_map/ppermute | solution.py:698
  38.6 3.5 %collective-permute-start.10 = (f32[3,16,128]{2,1,0:T(8,128)S(1)}, f32[3,16,128]{2,1,0:T(8,128)S(1)}, u32[]{:S(2)}, u32[]{:S(2)}) collective-permute-start(f32[3,16,128]{2,1,0:T(8,128)S(1)} %shard_map.119.piece_0), channel_id=1, source_target_pairs={{0,4},{1,5},{2,6},{3,7},{4,8},{5,9},{6,10},{7,11},{8,12},{9,13},{1... | collective-permute-start | bytes 73736 | tf_op jit(solution)/shard_map/ppermute | solution.py:698
  42.1 2.7 %shard_map.118.base = f32[32,32,128]{2,1,0:T(8,128)S(1)} custom-call(f32[36,40,128]{2,1,0:T(8,128)S(1)} %shard_map.113.wide.after_2, f32[80,128]{1,0:T(8,128)S(1)} %collective-permute-done.5.from_low, f32[80,128]{1,0:T(8,128)S(1)} %collective-permute-done.6.from_high, bf16[256,256]{1,0:T(8,128)(2,1)S(1)} %get-tuple-element.36.after.b1h, ...), custom_call_target="tpu_custom_call" | custom-call | flops 1000000 | bytes 2097152 | tf_op jit(solution)/shard_map/pallas_call | solution.py:667
  44.9 2.2 %shard_map.120 = f32[32,32,32]{2,1,0:T(8,128)} custom-call(f32[32,32,128]{2,1,0:T(8,128)S(1)} %shard_map.118.base, f32[3,16,128]{2,1,0:T(8,128)S(1)} %shard_map.119.piece_0, f32[3,16,128]{2,1,0:T(8,128)S(1)} %collective-permute-done.8.piece_1, f32[3,16,128]{2,1,0:T(8,128)S(1)} %collective-permute-done.9.piece_2, ...), custom_call_target="tpu_custom_call" | custom-call | flops 1000000 | bytes 2097152 | tf_op jit(solution)/shard_map/pallas_call | solution.py:667
  (19 shorter events, 0.0 us)
Async XLA Ops:
  0.0 21.2 %copy-start.5 = (f32[5,5,5]{2,1,0:T(8,128)S(1)}, f32[5,5,5]{2,1,0:T(8,128)}, u32[]{:S(2)}) copy-start(f32[5,5,5]{2,1,0:T(8,128)} %refs_0_.2) | copy-start | bytes 1504
  6.0 1.3 %collective-permute-start = (f32[72,128]{1,0:T(8,128)S(1)}, f32[72,128]{1,0:T(8,128)S(1)}, u32[]{:S(2)}, u32[]{:S(2)}) collective-permute-start(f32[72,128]{1,0:T(8,128)S(1)} %get-tuple-element.30), channel_id=1, source_target_pairs={{0,16},{16,0},{32,48},{48,32},{1,17},{17,1},{33,49},{49,33},{2,18}... | collective-permute-start | bytes 110600 | tf_op jit(solution)/shard_map/ppermute | solution.py:686
  7.3 9.2 %collective-permute-start.1 = (f32[40,128]{1,0:T(8,128)S(1)}, f32[40,128]{1,0:T(8,128)S(1)}, u32[]{:S(2)}, u32[]{:S(2)}) collective-permute-start(f32[40,128]{1,0:T(8,128)S(1)} %shard_map.111.own), channel_id=1, source_target_pairs={{0,32},{16,48},{32,0},{48,16},{1,33},{17,49},{33,1},{49,17},{2,34}... | collective-permute-start | bytes 61448 | tf_op jit(solution)/shard_map/ppermute | solution.py:686
  13.6 1.0 %copy-start = (f32[32,32,128]{2,1,0:T(8,128)S(1)}, f32[32,32,128]{2,1,0:T(8,128)}, u32[]{:S(2)}) copy-start(f32[32,32,128]{2,1,0:T(8,128)} %get-tuple-element.27.packed) | copy-start | bytes 1572868
  14.7 0.9 %copy-start.2 = (f32[8,32,128]{2,1,0:T(8,128)S(1)}, f32[8,32,128]{2,1,0:T(8,128)}, u32[]{:S(2)}) copy-start(f32[8,32,128]{2,1,0:T(8,128)} %constant.10.clone.factors) | copy-start | bytes 393220
  16.9 6.2 %collective-permute-start.2 = (f32[8,128]{1,0:T(8,128)S(1)}, f32[8,128]{1,0:T(8,128)S(1)}, u32[]{:S(2)}, u32[]{:S(2)}) collective-permute-start(f32[8,128]{1,0:T(8,128)S(1)} %get-tuple-element.33.own), channel_id=1, source_target_pairs={{0,128},{64,192},{128,0},{192,64},{1,129},{65,193},{129,1},{193,65... | collective-permute-start | bytes 12296 | tf_op jit(solution)/shard_map/ppermute | solution.py:686
  20.1 4.0 %collective-permute-start.3 = (f32[72,128]{1,0:T(8,128)S(1)}, f32[72,128]{1,0:T(8,128)S(1)}, u32[]{:S(2)}, u32[]{:S(2)}) collective-permute-start(f32[72,128]{1,0:T(8,128)S(1)} %get-tuple-element.34), channel_id=1, source_target_pairs={{0,64},{64,0},{128,192},{192,128},{1,65},{65,1},{129,193},{193,129... | collective-permute-start | bytes 110600 | tf_op jit(solution)/shard_map/ppermute | solution.py:686
  20.6 10.8 %copy-start.6 = (f32[5,5,5]{2,1,0:T(8,128)S(1)}, f32[5,5,5]{2,1,0:T(8,128)}, u32[]{:S(2)}) copy-start(f32[5,5,5]{2,1,0:T(8,128)} %refs_0_.3) | copy-start | bytes 1504
  20.6 10.8 %copy-start.7 = (f32[5,5,5]{2,1,0:T(8,128)S(1)}, f32[5,5,5]{2,1,0:T(8,128)}, u32[]{:S(2)}) copy-start(f32[5,5,5]{2,1,0:T(8,128)} %refs_1_.1) | copy-start | bytes 1504
  20.7 5.2 %collective-permute-start.4 = (f32[72,128]{1,0:T(8,128)S(1)}, f32[72,128]{1,0:T(8,128)S(1)}, u32[]{:S(2)}, u32[]{:S(2)}) collective-permute-start(f32[72,128]{1,0:T(8,128)S(1)} %get-tuple-element.35), channel_id=1, source_target_pairs={{0,192},{64,128},{128,64},{192,0},{1,193},{65,129},{129,65},{193,1... | collective-permute-start | bytes 110600 | tf_op jit(solution)/shard_map/ppermute | solution.py:686
  26.1 9.4 %collective-permute-start.5 = (f32[80,128]{1,0:T(8,128)S(1)}, f32[80,128]{1,0:T(8,128)S(1)}, u32[]{:S(2)}, u32[]{:S(2)}) collective-permute-start(f32[80,128]{1,0:T(8,128)S(1)} %get-tuple-element.39), channel_id=1, source_target_pairs={{0,1},{1,2},{2,3},{3,4},{4,5},{5,6},{6,7},{7,8},{8,9},{9,10},{10,1... | collective-permute-start | bytes 122888 | tf_op jit(solution)/shard_map/ppermute | solution.py:698
  27.8 7.7 %collective-permute-start.6 = (f32[80,128]{1,0:T(8,128)S(1)}, f32[80,128]{1,0:T(8,128)S(1)}, u32[]{:S(2)}, u32[]{:S(2)}) collective-permute-start(f32[80,128]{1,0:T(8,128)S(1)} %get-tuple-element.40), channel_id=1, source_target_pairs={{0,47},{1,0},{2,1},{3,2},{4,3},{5,4},{6,5},{7,6},{8,7},{9,8},{10,9... | collective-permute-start | bytes 122888 | tf_op jit(solution)/shard_map/ppermute | solution.py:698
  30.4 5.2 %collective-permute-start.7 = (f32[16,128]{1,0:T(8,128)S(1)}, f32[16,128]{1,0:T(8,128)S(1)}, u32[]{:S(2)}, u32[]{:S(2)}) collective-permute-start(f32[16,128]{1,0:T(8,128)S(1)} %get-tuple-element.46.own), channel_id=1, source_target_pairs={{0,2},{1,3},{2,0},{3,1},{4,6},{5,7},{6,4},{7,5},{8,10},{9,11},{10,... | collective-permute-start | bytes 24584 | tf_op jit(solution)/shard_map/ppermute | solution.py:686
  33.1 9.0 %copy-start.3 = (bf16[128,128]{1,0:T(8,128)(2,1)S(1)}, bf16[128,128]{1,0:T(8,128)(2,1)}, u32[]{:S(2)}) copy-start(bf16[128,128]{1,0:T(8,128)(2,1)} %constant.11.clone.prol_2) | copy-start | bytes 98308
  33.1 9.0 %copy-start.4 = (bf16[128,128]{1,0:T(8,128)(2,1)S(1)}, bf16[128,128]{1,0:T(8,128)(2,1)}, u32[]{:S(2)}) copy-start(bf16[128,128]{1,0:T(8,128)(2,1)} %constant.12.clone.prol_1) | copy-start | bytes 98308
  33.1 11.8 %copy-start.1 = (bf16[8,128,128]{2,1,0:T(8,128)(2,1)S(1)}, bf16[8,128,128]{2,1,0:T(8,128)(2,1)}, u32[]{:S(2)}) copy-start(bf16[8,128,128]{2,1,0:T(8,128)(2,1)} %constant.13.clone.qz) | copy-start | bytes 786436
  35.7 9.1 %collective-permute-start.8 = (f32[3,16,128]{2,1,0:T(8,128)S(1)}, f32[3,16,128]{2,1,0:T(8,128)S(1)}, u32[]{:S(2)}, u32[]{:S(2)}) collective-permute-start(f32[3,16,128]{2,1,0:T(8,128)S(1)} %shard_map.119.piece_0), channel_id=1, source_target_pairs={{0,44},{1,45},{2,46},{3,47},{4,0},{5,1},{6,2},{7,3},{8,4},{9,5},{1... | collective-permute-start | bytes 73736 | tf_op jit(solution)/shard_map/ppermute | solution.py:698
  38.6 6.3 %collective-permute-start.9 = (f32[3,16,128]{2,1,0:T(8,128)S(1)}, f32[3,16,128]{2,1,0:T(8,128)S(1)}, u32[]{:S(2)}, u32[]{:S(2)}) collective-permute-start(f32[3,16,128]{2,1,0:T(8,128)S(1)} %shard_map.119.piece_0), channel_id=1, source_target_pairs={{0,8},{1,9},{2,10},{3,11},{4,12},{5,13},{6,14},{7,15},{8,32},{9,33... | collective-permute-start | bytes 73736 | tf_op jit(solution)/shard_map/ppermute | solution.py:698
  38.6 6.3 %collective-permute-start.10 = (f32[3,16,128]{2,1,0:T(8,128)S(1)}, f32[3,16,128]{2,1,0:T(8,128)S(1)}, u32[]{:S(2)}, u32[]{:S(2)}) collective-permute-start(f32[3,16,128]{2,1,0:T(8,128)S(1)} %shard_map.119.piece_0), channel_id=1, source_target_pairs={{0,4},{1,5},{2,6},{3,7},{4,8},{5,9},{6,10},{7,11},{8,12},{9,13},{1... | collective-permute-start | bytes 73736 | tf_op jit(solution)/shard_map/ppermute | solution.py:698
